TPU v7x, 128 devices: a whole 4x4x4 slice. The times are simulated.
128 devices in a mesh: rec: 8 (over z, core), seq: 16 (over y, x).
Axes of the slice: x: 4, y: 4, z: 4, core: 2. Of those that a mesh axis runs over, the one named last changes fastest.
Arguments:
- tokens: bfloat16 [8, 4096, 768], P('rec', 'seq'), may hold values from -6 to 6
- cotangent: bfloat16 [8, 4096, 768], P('rec', 'seq'), may hold values from -6 to 6
- log_decay: float32 [8, 24, 4096], P('rec', None, 'seq'), may hold values from -0.8 to 0
- w_in: bfloat16 [768, 1536], replicated, may hold values from -0.21875 to 0.21875
- w_bc: bfloat16 [768, 256], replicated, may hold values from -0.009765625 to 0.009765625
- w_out: bfloat16 [1536, 768], replicated, may hold values from -0.15625 to 0.15625
Outputs:
- d_tokens: bfloat16 [8, 4096, 768], P('rec', 'seq')
- grad_in: float32 [768, 1536], P(('rec', 'seq'))
- grad_bc: float32 [768, 256], P(('rec', 'seq'))
- grad_out: float32 [1536, 768], P(('rec', 'seq'))
All inputs are finite; a program needn't handle non-finite values.
Results may differ from a plain program's by a relative error of at most 0.0085.
Values sent between devices are 32-bit elements; how exact they have to be, the bound alone decides.
No kernel may reach another device: no remote copies, remote signals or barrier semaphores. Data moves between devices by JAX's collectives and lax.ppermute only.
A program may use at most 256 MiB of HBM per device.

v0:
```python
import jax
import jax.numpy as jnp
from jax import lax
from jax.sharding import PartitionSpec as P

BLOCK = 128


def prefix(value, axis, join, neutral, backward):
    count, mine = (lax.axis_size(axis), lax.axis_index(axis))
    pieces = jax.tree.map(lambda part: lax.all_gather(part, axis), value)
    if backward:
        pieces = jax.tree.map(lambda part: part[::-1], pieces)
        mine = count - 1 - mine
    subtotal = jax.tree.map(
        lambda part, zero: jnp.full_like(part, 0) + jnp.asarray(zero, part.dtype), value, neutral
    )

    def step(position, subtotal):
        longer = join(subtotal, jax.tree.map(lambda part: part[position], pieces))
        return jax.tree.map(lambda new, old: jnp.where(position < mine, new, old), longer, subtotal)

    return lax.fori_loop(0, count - 1, step, subtotal)


def ssd_block(state, segment_list):
    xs_b, b_b, c_b, la_b = segment_list
    width = la_b.shape[1]
    cum = jnp.cumsum(la_b, axis=1)
    diff = cum[:, :, None] - cum[:, None, :]
    lower = jnp.tril(jnp.ones((width, width), dtype=bool))
    decay = jnp.where(lower, jnp.exp(jnp.where(lower, diff, 0.0)), 0.0)
    scores = jnp.dot(c_b, b_b.T, precision=lax.Precision.HIGHEST)
    y_inner = jnp.einsum(
        "hts,shp->thp", decay * scores[None], xs_b, precision=lax.Precision.HIGHEST
    )
    y_carry = (
        jnp.einsum("tn,hnp->thp", c_b, state, precision=lax.Precision.HIGHEST)
        * jnp.exp(cum).T[:, :, None]
    )
    tail = jnp.exp(cum[:, -1:] - cum)
    new_state = jnp.exp(cum[:, -1])[:, None, None] * state + jnp.einsum(
        "sn,shp->hnp", b_b, xs_b * tail.T[:, :, None], precision=lax.Precision.HIGHEST
    )
    return (new_state, y_inner + y_carry)


def ssd_pass(xs3, bmat, cmat, decay_log, state):
    count = xs3.shape[0] // BLOCK
    blocks = (
        xs3.reshape(count, BLOCK, xs3.shape[1], xs3.shape[2]),
        bmat.reshape(count, BLOCK, bmat.shape[1]),
        cmat.reshape(count, BLOCK, cmat.shape[1]),
        decay_log.reshape(decay_log.shape[0], count, BLOCK).transpose(1, 0, 2),
    )
    final, ys = lax.scan(ssd_block, state, blocks)
    return (ys.reshape(xs3.shape), final)


def edge_terms(xs3, bmat, cmat, decay_log, dy3):
    cum = jnp.cumsum(decay_log, axis=1)
    tail = jnp.exp(cum[:, -1:] - cum)
    ends = jnp.einsum(
        "sn,shp->hnp", bmat, xs3 * tail.T[:, :, None], precision=lax.Precision.HIGHEST
    )
    pulled = jnp.einsum(
        "tn,thp->hnp", cmat, dy3 * jnp.exp(cum).T[:, :, None], precision=lax.Precision.HIGHEST
    )
    return (jnp.exp(cum[:, -1]), ends, pulled)


def combine(earlier, later):
    return (earlier[0] * later[0], later[0][:, None, None] * earlier[1] + later[1])


def square_total(shares):
    local = (
        jnp.sum(shares[0] * shares[0])
        + jnp.sum(shares[1] * shares[1])
        + jnp.sum(shares[2] * shares[2])
    )
    return lax.psum(local, ("rec", "seq"))


def body(tokens, cotangent, log_decay, w_in, w_bc, w_out):
    tok = tokens[0]
    grad_y = cotangent[0]
    decay_log = log_decay[0]
    steps_here = tok.shape[0]
    heads = decay_log.shape[0]
    nstate = w_bc.shape[1] // 2
    channels = w_in.shape[1] // heads
    xs = jnp.dot(tok, w_in, preferred_element_type=jnp.float32).astype(jnp.bfloat16)
    bc = jnp.dot(tok, w_bc, preferred_element_type=jnp.float32).astype(jnp.bfloat16)
    xs3 = xs.astype(jnp.float32).reshape(steps_here, heads, channels)
    bmat = bc[:, :nstate].astype(jnp.float32)
    cmat = bc[:, nstate:].astype(jnp.float32)
    dy3 = jnp.einsum("td,hd->th", grad_y, w_out, preferred_element_type=jnp.float32).reshape(
        steps_here, heads, channels
    )
    flip_log = decay_log[:, ::-1]
    zero_block = jnp.zeros((heads, nstate, channels), jnp.float32)
    identity = (jnp.ones((heads,), jnp.float32), zero_block)
    total, ends_fwd, _ = edge_terms(xs3, bmat, cmat, decay_log, dy3)
    _, ends_rev, _ = edge_terms(xs3[::-1], bmat[::-1], cmat[::-1], flip_log, dy3[::-1])
    primals_s_in = prefix((total, ends_fwd), "seq", combine, identity, False)[1]
    primals_r_in = prefix((total, ends_rev), "seq", combine, identity, True)[1]
    total, _, pull_fwd = edge_terms(xs3, bmat, cmat, decay_log, dy3)
    _, _, pull_rev = edge_terms(xs3[::-1], bmat[::-1], cmat[::-1], flip_log, dy3[::-1])
    d_fwd = prefix((total, pull_fwd), "seq", combine, identity, True)[1]
    d_rev = prefix((total, pull_rev), "seq", combine, identity, False)[1]
    d_fwd, d_rev = (d_fwd, d_rev)

    def mixer(xs_a, b_a, c_a):
        y_fwd, end_fwd = ssd_pass(xs_a, b_a, c_a, decay_log, primals_s_in)
        y_rev, backward_final_carry = ssd_pass(
            xs_a[::-1], b_a[::-1], c_a[::-1], flip_log, primals_r_in
        )
        return (y_fwd + y_rev[::-1], end_fwd, backward_final_carry)

    yfull, pullback = jax.vjp(mixer, xs3, bmat, cmat)
    dxs_f, d_b, d_c = pullback((dy3, d_fwd, d_rev))
    y16 = yfull[0].reshape(steps_here, heads * channels).astype(jnp.bfloat16)
    dxs = dxs_f.reshape(steps_here, heads * channels).astype(jnp.bfloat16)
    dbc = jnp.concatenate([d_b, d_c], axis=1).astype(jnp.bfloat16)
    d_tok = (
        jnp.einsum("th,dh->td", dxs, w_in, preferred_element_type=jnp.float32)
        + jnp.einsum("tn,dn->td", dbc, w_bc, preferred_element_type=jnp.float32)
    ).astype(jnp.bfloat16)
    raw_in = jnp.einsum("td,th->dh", tok, dxs, preferred_element_type=jnp.float32)
    raw_bc = jnp.einsum("td,tn->dn", tok, dbc, preferred_element_type=jnp.float32)
    raw_out = jnp.einsum("th,td->hd", y16, grad_y, preferred_element_type=jnp.float32)
    entries = raw_in.size + raw_bc.size + raw_out.size
    shares = (
        lax.psum_scatter(raw_in, ("rec", "seq"), scatter_dimension=0, tiled=True),
        lax.psum_scatter(raw_bc, ("rec", "seq"), scatter_dimension=0, tiled=True),
        lax.psum_scatter(raw_out, ("rec", "seq"), scatter_dimension=0, tiled=True),
    )
    total_sq = square_total(shares)
    factor = jnp.minimum(1.0, 1.0 / jnp.sqrt(total_sq / entries + 1e-06))
    return (d_tok[None], factor * shares[0], factor * shares[1], factor * shares[2])


def solution(mesh):
    in_specs = (P("rec", "seq", None), P("rec", "seq", None), P("rec", None, "seq"), P(), P(), P())
    out_specs = (
        P("rec", "seq", None),
        P(("rec", "seq"), None),
        P(("rec", "seq"), None),
        P(("rec", "seq"), None),
    )
    return jax.shard_map(body, mesh=mesh, in_specs=in_specs, out_specs=out_specs, check_vma=False)
```

profile of v0, /device:TPU:6, one launch (start us, length us, event | category | flops | bytes accessed | tf_op | source)
XLA Modules:
  0.0 1429.2 jit_solution(15862484426441988379)
XLA Ops:
  7.2 4.0 fusion.216
  11.2 4.1 rev.41
  18.2 3.7 fusion.192
  26.9 4.0 rev.45
  31.0 3.7 fusion.195
  55.7 33.5 %all-reduce = f32[384]{0:T(512)S(1)} all-reduce(f32[384]{0:T(512)S(1)} %dynamic-update-slice), channel_id=2, replica_groups=mesh['rec'=8,'seq'=16] {'seq'}, use_global_device_ids=true, to_apply=%add | all-reduce | flops 384 | bytes 3072
  92.2 22.1 %all-gather.10.cloned.1.call-done = f32[384,128,64]{1,2,0:T(8,128)} async-done(((f32[24,128,64]{1,2,0:T(8,128)}), f32[384,128,64]{1,2,0:T(8,128)}) %all-gather.10.cloned.1.call-update) | async-done | bytes 12582928 | tf_op jit(solution)/shard_map/all_gather | solution.py:11
  114.2 92.2 %while.164 = (s32[]{:T(128)}, f32[24,128,64]{2,1,0:T(8,128)}, s32[]{:T(128)}, f32[16,24]{1,0:T(8,128)S(1)}, f32[16,24,128,64]{2,3,1,0:T(8,128)}, /*index=5*/s32[]{:T(128)}, s32[]{:T(128)}) while((s32[]{:T(128)}, f32[24,128,64]{2,1,0:T(8,128)}, s32[]{:T(128)}, f32[16,24]{1,0:T(8,128)S(1)}, f32[16,24,128,64]{2,3,1,0:T(8,128)}, ...), condition=%wide.region_5.6_spmd.clone, body=%wide.region_4.5_spmd.clone.sunk | while | flops 786436 | bytes 5505425 | solution.py:23
  135.0 3.4 fusion.389
  153.5 3.5 fusion.389
  166.0 3.4 fusion.389
  178.4 3.4 fusion.389
  190.8 3.4 fusion.389
  209.2 17.7 %copy.116 = f32[16,24,128,64]{3,2,1,0:T(8,128)} copy(f32[16,24,128,64]{2,3,1,0:T(8,128)} %bitcast.653) | data formatting | bytes 25165824 | tf_op jit(solution)/shard_map/all_gather | solution.py:11
  226.9 17.7 %rev.47 = f32[16,24,128,64]{3,2,1,0:T(8,128)} reverse(f32[16,24,128,64]{3,2,1,0:T(8,128)} %copy.116), dimensions={0} | reverse | bytes 25165824 | tf_op jit(solution)/shard_map/rev | solution.py:13
  244.6 49.9 %while.165 = (s32[]{:T(128)}, f32[24,128,64]{2,1,0:T(8,128)}, s32[]{:T(128)}, f32[16,24]{1,0:T(8,128)S(1)}, f32[16,24,128,64]{3,2,1,0:T(8,128)}, /*index=5*/s32[]{:T(128)}, s32[]{:T(128)}) while((s32[]{:T(128)}, f32[24,128,64]{2,1,0:T(8,128)}, s32[]{:T(128)}, f32[16,24]{1,0:T(8,128)S(1)}, f32[16,24,128,64]{3,2,1,0:T(8,128)}, ...), condition=%wide.region_7.8_spmd.clone, body=%wide.region_6.7_spmd.clone.sunk | while | flops 786436 | bytes 2359697 | solution.py:23
  261.2 3.4 fusion.390
  264.6 3.4 fusion.390
  274.5 3.4 fusion.390
  277.9 3.4 fusion.390
  281.3 3.4 fusion.390
  307.6 68.2 %while.162 = (s32[]{:T(128)}, f32[24,128,64]{1,2,0:T(8,128)S(1)}, f32[2,128,24,64]{1,0,3,2:T(2,128)}, f32[2,128,128]{1,2,0:T(8,128)}, f32[2,24,128,128]{3,2,1,0:...) while((s32[]{:T(128)}, f32[24,128,64]{1,2,0:T(8,128)S(1)}, ...), condition=%wide.region_10.11_spmd.clone.clone, body=%wide.region_8.10_spmd.clone.clone.sunk | while | flops 935857152 | bytes 43502108 | solution.py:56
  313.7 4.1 fusion.376
  317.8 19.0 %dynamic_update_slice.256 = f32[2,128,24,64]{1,0,3,2:T(2,128)} dynamic-update-slice(f32[2,128,24,64]{1,0,3,2:T(2,128)} %get-tuple-element.2837, f32[1,128,24,64]{1,0,3,2:T(1,128)} %bitcast.646, s32[]{:T(128)S(6)} %copy.241, s32[]{:T(128)} %constant.302.clone.1..sunk.2, s32[]{:T(128)} %constant.302.clone.1..sunk.2, s32[]{:T(128)} %constant.302.clone.1..sunk.2) | dynamic-update-slice | bytes 1572868 | tf_op jit(solution)/shard_map/jvp()/while/body/jit(dynamic_update_index_in_dim)/dynamic_update_slice | solution.py:56
  347.8 4.1 fusion.376
  351.9 19.0 %dynamic_update_slice.256 = f32[2,128,24,64]{1,0,3,2:T(2,128)} dynamic-update-slice(f32[2,128,24,64]{1,0,3,2:T(2,128)} %get-tuple-element.2837, f32[1,128,24,64]{1,0,3,2:T(1,128)} %bitcast.646, s32[]{:T(128)S(6)} %copy.241, s32[]{:T(128)} %constant.302.clone.1..sunk.2, s32[]{:T(128)} %constant.302.clone.1..sunk.2, s32[]{:T(128)} %constant.302.clone.1..sunk.2) | dynamic-update-slice | bytes 1572868 | tf_op jit(solution)/shard_map/jvp()/while/body/jit(dynamic_update_index_in_dim)/dynamic_update_slice | solution.py:56
  379.0 76.2 %while.160 = (s32[]{:T(128)}, f32[24,128,64]{1,2,0:T(8,128)}, f32[2,128,24,64]{1,0,3,2:T(2,128)}, f32[2,128,128]{2,1,0:T(8,128)}, f32[2,128,128]{2,1,0:T(8,128)}...) while((s32[]{:T(128)}, f32[24,128,64]{1,2,0:T(8,128)}, ...), condition=%wide.region_13.14_spmd, body=%wide.region_11.13_spmd.sunk | while | flops 1864253440 | bytes 46030980 | solution.py:56
  391.2 19.0 %dynamic_update_slice.246 = f32[2,128,24,64]{1,0,3,2:T(2,128)} dynamic-update-slice(f32[2,128,24,64]{1,0,3,2:T(2,128)} %get-tuple-element.2894, f32[1,128,24,64]{1,0,3,2:T(1,128)} %bitcast.638, s32[]{:T(128)S(6)} %sub.293, s32[]{:T(128)} %constant.302.clone.1..sunk, s32[]{:T(128)} %constant.302.clone.1..sunk, s32[]{:T(128)} %constant.302.clone.1..sunk) | dynamic-update-slice | bytes 1572868 | tf_op jit(solution)/shard_map/transpose(jvp())/while/body/jit(dynamic_update_index_in_dim)/dynamic_update_slice | solution.py:56
  410.3 4.4 fusion.340
  429.1 19.0 %dynamic_update_slice.246 = f32[2,128,24,64]{1,0,3,2:T(2,128)} dynamic-update-slice(f32[2,128,24,64]{1,0,3,2:T(2,128)} %get-tuple-element.2894, f32[1,128,24,64]{1,0,3,2:T(1,128)} %bitcast.638, s32[]{:T(128)S(6)} %sub.293, s32[]{:T(128)} %constant.302.clone.1..sunk, s32[]{:T(128)} %constant.302.clone.1..sunk, s32[]{:T(128)} %constant.302.clone.1..sunk) | dynamic-update-slice | bytes 1572868 | tf_op jit(solution)/shard_map/transpose(jvp())/while/body/jit(dynamic_update_index_in_dim)/dynamic_update_slice | solution.py:56
  448.2 4.4 fusion.340
  458.6 4.1 rev.48
  462.7 17.5 %copy.127 = f32[16,24,128,64]{3,2,1,0:T(8,128)} copy(f32[16,24,128,64]{2,3,1,0:T(8,128)} %bitcast.652) | data formatting | bytes 25165824 | tf_op jit(solution)/shard_map/all_gather | solution.py:11
  480.2 17.4 %rev.49 = f32[16,24,128,64]{3,2,1,0:T(8,128)} reverse(f32[16,24,128,64]{3,2,1,0:T(8,128)} %copy.127), dimensions={0} | reverse | bytes 25165824 | tf_op jit(solution)/shard_map/rev | solution.py:13
  497.7 59.4 %while.166 = (s32[]{:T(128)}, f32[24,128,64]{2,1,0:T(8,128)}, s32[]{:T(128)}, f32[16,24]{1,0:T(8,128)}, f32[16,24,128,64]{3,2,1,0:T(8,128)}, /*index=5*/s32[]{:T(128)}, s32[]{:T(128)}) while((s32[]{:T(128)}, f32[24,128,64]{2,1,0:T(8,128)}, s32[]{:T(128)}, f32[16,24]{1,0:T(8,128)}, f32[16,24,128,64]{3,2,1,0:T(8,128)}, ...), condition=%wide.region_15.16_spmd.clone, body=%wide.region_14.15_spmd.clone.sunk | while | flops 786436 | bytes 2359697 | solution.py:23
  559.9 92.5 %while.167 = (s32[]{:T(128)}, f32[24,128,64]{2,1,0:T(8,128)}, s32[]{:T(128)}, f32[16,24]{1,0:T(8,128)S(1)}, f32[16,24,128,64]{2,3,1,0:T(8,128)}, /*index=5*/s32[]{:T(128)}, s32[]{:T(128)}) while((s32[]{:T(128)}, f32[24,128,64]{2,1,0:T(8,128)}, s32[]{:T(128)}, f32[16,24]{1,0:T(8,128)S(1)}, f32[16,24,128,64]{2,3,1,0:T(8,128)}, ...), condition=%wide.region_17.18_spmd.clone, body=%wide.region_16.17_spmd.clone.sunk | while | flops 786436 | bytes 5505425 | solution.py:23
  580.8 3.4 fusion.392
  587.0 3.4 fusion.392
  593.2 3.4 fusion.392
  664.9 68.2 %while.163 = (s32[]{:T(128)}, f32[24,128,64]{1,2,0:T(8,128)S(1)}, f32[2,128,24,64]{1,0,3,2:T(2,128)}, f32[2,128,128]{1,2,0:T(8,128)}, f32[2,24,128,128]{3,2,1,0:...) while((s32[]{:T(128)}, f32[24,128,64]{1,2,0:T(8,128)S(1)}, ...), condition=%wide.region_20.21_spmd.clone.clone, body=%wide.region_18.20_spmd.clone.clone.sunk | while | flops 935857152 | bytes 43697180 | solution.py:56
  670.9 4.1 fusion.388
  675.0 19.0 %dynamic_update_slice.263 = f32[2,128,24,64]{1,0,3,2:T(2,128)} dynamic-update-slice(f32[2,128,24,64]{1,0,3,2:T(2,128)} %get-tuple-element.2993, f32[1,128,24,64]{1,0,3,2:T(1,128)} %bitcast.647, s32[]{:T(128)S(6)} %copy.301, s32[]{:T(128)} %constant.302.clone.1..sunk.3, s32[]{:T(128)} %constant.302.clone.1..sunk.3, s32[]{:T(128)} %constant.302.clone.1..sunk.3) | dynamic-update-slice | bytes 1572868 | tf_op jit(solution)/shard_map/jvp()/while/body/jit(dynamic_update_index_in_dim)/dynamic_update_slice | solution.py:56
  705.0 4.1 fusion.388
  709.1 19.0 %dynamic_update_slice.263 = f32[2,128,24,64]{1,0,3,2:T(2,128)} dynamic-update-slice(f32[2,128,24,64]{1,0,3,2:T(2,128)} %get-tuple-element.2993, f32[1,128,24,64]{1,0,3,2:T(1,128)} %bitcast.647, s32[]{:T(128)S(6)} %copy.301, s32[]{:T(128)} %constant.302.clone.1..sunk.3, s32[]{:T(128)} %constant.302.clone.1..sunk.3, s32[]{:T(128)} %constant.302.clone.1..sunk.3) | dynamic-update-slice | bytes 1572868 | tf_op jit(solution)/shard_map/jvp()/while/body/jit(dynamic_update_index_in_dim)/dynamic_update_slice | solution.py:56
  736.3 74.6 %while.161 = (s32[]{:T(128)}, f32[24,128,64]{1,2,0:T(8,128)}, f32[2,128,24,64]{1,0,3,2:T(2,128)}, f32[2,128,128]{2,1,0:T(8,128)}, f32[2,128,128]{2,1,0:T(8,128)}...) while((s32[]{:T(128)}, f32[24,128,64]{1,2,0:T(8,128)}, ...), condition=%wide.region_23.24_spmd, body=%wide.region_21.23_spmd.sunk | while | flops 1864253440 | bytes 46030980 | solution.py:56
  747.6 19.0 %dynamic_update_slice.249 = f32[2,128,24,64]{1,0,3,2:T(2,128)} dynamic-update-slice(f32[2,128,24,64]{1,0,3,2:T(2,128)} %get-tuple-element.3050, f32[1,128,24,64]{1,0,3,2:T(1,128)} %bitcast.639, s32[]{:T(128)S(6)} %sub.294, s32[]{:T(128)} %constant.302.clone.1..sunk.1, s32[]{:T(128)} %constant.302.clone.1..sunk.1, s32[]{:T(128)} %constant.302.clone.1..sunk.1) | dynamic-update-slice | bytes 1572868 | tf_op jit(solution)/shard_map/transpose(jvp())/while/body/jit(dynamic_update_index_in_dim)/dynamic_update_slice | solution.py:56
  766.6 4.4 fusion.362
  784.8 19.0 %dynamic_update_slice.249 = f32[2,128,24,64]{1,0,3,2:T(2,128)} dynamic-update-slice(f32[2,128,24,64]{1,0,3,2:T(2,128)} %get-tuple-element.3050, f32[1,128,24,64]{1,0,3,2:T(1,128)} %bitcast.639, s32[]{:T(128)S(6)} %sub.294, s32[]{:T(128)} %constant.302.clone.1..sunk.1, s32[]{:T(128)} %constant.302.clone.1..sunk.1, s32[]{:T(128)} %constant.302.clone.1..sunk.1) | dynamic-update-slice | bytes 1572868 | tf_op jit(solution)/shard_map/transpose(jvp())/while/body/jit(dynamic_update_index_in_dim)/dynamic_update_slice | solution.py:56
  803.8 4.4 fusion.362
  810.9 3.4 reshape.281
  827.7 4.0 rev.52
  839.8 353.5 %fusion.4 = f32[16,768]{1,0:T(8,128)} fusion(f32[1536,768]{1,0:T(8,128)} %fusion.214), kind=kCustom, calls=%all-reduce-scatter | all-reduce-scatter fusion | flops 1572865 | bytes 4767744
  1199.2 7.7 collective-permute-start.28
  1218.9 13.1 collective-permute-start.21
  1232.0 3.4 collective-permute-start.20
  1249.0 3.8 collective-permute-start.12
  1260.2 3.7 collective-permute-start.8
  1265.3 5.5 collective-permute-start.6
  1270.8 4.0 collective-permute-start.5
  1274.8 4.4 collective-permute-start.4
  1283.5 3.7 collective-permute-start.1
  1287.3 4.0 collective-permute-start
  1293.6 48.6 %concatenate.5 = f32[524,768]{1,0:T(8,128)} concatenate(f32[12,768]{1,0:T(8,128)} %copy-done.57, f32[16,768]{1,0:T(8,128)} %collective-permute-done.30, f32[16,768]{1,0:T(8,128)} %collective-permute-done.29, f32[16,768]{1,0:T(8,128)} %collective-permute-done.28, f32[16,768]{1,0:T(8,128)} %collective-permute-done.27, f32[16,768]{1,0:T(8,128)} %collective-permute-done.26, ...), dimensions={0} | concatenate | bytes 3219456
  1351.6 64.1 %psum.7 = f32[]{:T(128)} all-reduce(f32[]{:T(128)S(6)} %add.210), channel_id=1, replica_groups=mesh['rec'=8,'seq'=16] {'rec','seq'}, use_global_device_ids=true, to_apply=%region_30.31 | all-reduce | flops 1 | bytes 8 | tf_op jit(solution)/shard_map/psum | solution.py:82
  (627 shorter events, 502.8 us)
Async XLA Ops:
  7.2 14.8 %copy-start = (bf16[768,1536]{1,0:T(8,128)(2,1)S(1)}, bf16[768,1536]{1,0:T(8,128)(2,1)}, u32[]{:S(2)}) copy-start(bf16[768,1536]{1,0:T(8,128)(2,1)} %param.25) | copy-start | bytes 7077892
  7.2 107.1 %all-gather.10.cloned.1.call-start = ((), (), s32[]{:S(2)}) async-start(), calls=%async_computation | async-start | bytes 13369344 | tf_op jit(solution)/shard_map/all_gather | solution.py:11
  11.2 4.1 copy-start.55
  11.2 6.6 copy-start.21
  11.2 6.6 copy-start.26
  18.1 12.8 copy-start.17
  21.9 187.3 %all-gather.12.cloned.1.call-start = ((), (), s32[]{:S(2)}) async-start(), calls=%async_computation.1 | async-start | bytes 13369344 | tf_op jit(solution)/shard_map/all_gather | solution.py:11
  26.9 4.1 copy-start.54
  34.8 427.9 %all-gather.14.cloned.1.call-start = ((), (), s32[]{:S(2)}) async-start(), calls=%async_computation.2 | async-start | bytes 13369344 | tf_op jit(solution)/shard_map/all_gather | solution.py:11
  34.9 4.4 copy-start.41
  39.3 520.6 %all-gather.16.cloned.1.call-start = ((), (), s32[]{:S(2)}) async-start(), calls=%async_computation.3 | async-start | bytes 13369344 | tf_op jit(solution)/shard_map/all_gather | solution.py:11
  42.5 1301.2 %all-reduce.8.cloned.1.call-start = ((), (), s32[]{:S(2)}) async-start(), calls=%async_computation.4 | async-start | bytes 11010048
  379.4 5.6 copy-start.10
  410.3 4.4 copy-start.35
  410.3 4.8 copy-start.11
  417.4 5.5 copy-start.10
  448.2 4.4 copy-start.35
  448.2 4.8 copy-start.11
  736.5 4.9 copy-start.9
  766.6 4.4 copy-start.31
  766.6 4.8 copy-start.14
  773.7 4.9 copy-start.9
  803.8 4.4 copy-start.31
  803.8 4.8 copy-start.14
  810.9 4.1 copy-start.37
  1193.3 18.0 %collective-permute-start.30 = (f32[16,768]{1,0:T(8,128)}, f32[16,768]{1,0:T(8,128)}, u32[]{:S(2)}, u32[]{:S(2)}) collective-permute-start(f32[16,768]{1,0:T(8,128)} %fusion.4), channel_id=1, source_target_pairs={{0,31},{1,32},{2,33},{3,34},{4,35},{5,36},{6,37},{7,38},{8,39},{9,... | collective-permute-start | bytes 147464
  1196.0 12.8 collective-permute-start.31
  1197.3 15.9 %collective-permute-start.29 = (f32[16,768]{1,0:T(8,128)}, f32[16,768]{1,0:T(8,128)}, u32[]{:S(2)}, u32[]{:S(2)}) collective-permute-start(f32[16,768]{1,0:T(8,128)} %fusion.4), channel_id=1, source_target_pairs={{0,30},{1,31},{2,32},{3,33},{4,34},{5,35},{6,36},{7,37},{8,38},{9,... | collective-permute-start | bytes 147464
  1199.2 15.9 %collective-permute-start.28 = (f32[16,768]{1,0:T(8,128)}, f32[16,768]{1,0:T(8,128)}, u32[]{:S(2)}, u32[]{:S(2)}) collective-permute-start(f32[16,768]{1,0:T(8,128)} %fusion.4), channel_id=1, source_target_pairs={{0,29},{1,30},{2,31},{3,32},{4,33},{5,34},{6,35},{7,36},{8,37},{9,... | collective-permute-start | bytes 147464
  1206.9 10.1 collective-permute-start.27
  1209.4 9.5 collective-permute-start.26
  1211.3 20.7 %collective-permute-start.25 = (f32[16,768]{1,0:T(8,128)}, f32[16,768]{1,0:T(8,128)}, u32[]{:S(2)}, u32[]{:S(2)}) collective-permute-start(f32[16,768]{1,0:T(8,128)} %fusion.4), channel_id=1, source_target_pairs={{0,26},{1,27},{2,28},{3,29},{4,30},{5,31},{6,32},{7,33},{8,34},{9,... | collective-permute-start | bytes 147464
  1213.2 22.2 %collective-permute-start.24 = (f32[16,768]{1,0:T(8,128)}, f32[16,768]{1,0:T(8,128)}, u32[]{:S(2)}, u32[]{:S(2)}) collective-permute-start(f32[16,768]{1,0:T(8,128)} %fusion.4), channel_id=1, source_target_pairs={{0,25},{1,26},{2,27},{3,28},{4,29},{5,30},{6,31},{7,32},{8,33},{9,... | collective-permute-start | bytes 147464
  1215.1 22.2 %collective-permute-start.23 = (f32[16,768]{1,0:T(8,128)}, f32[16,768]{1,0:T(8,128)}, u32[]{:S(2)}, u32[]{:S(2)}) collective-permute-start(f32[16,768]{1,0:T(8,128)} %fusion.4), channel_id=1, source_target_pairs={{0,24},{1,25},{2,26},{3,27},{4,28},{5,29},{6,30},{7,31},{8,32},{9,... | collective-permute-start | bytes 147464
  1217.0 22.3 %collective-permute-start.22 = (f32[16,768]{1,0:T(8,128)}, f32[16,768]{1,0:T(8,128)}, u32[]{:S(2)}, u32[]{:S(2)}) collective-permute-start(f32[16,768]{1,0:T(8,128)} %fusion.4), channel_id=1, source_target_pairs={{0,23},{1,24},{2,25},{3,26},{4,27},{5,28},{6,29},{7,30},{8,31},{9,... | collective-permute-start | bytes 147464
  1218.9 22.3 %collective-permute-start.21 = (f32[16,768]{1,0:T(8,128)}, f32[16,768]{1,0:T(8,128)}, u32[]{:S(2)}, u32[]{:S(2)}) collective-permute-start(f32[16,768]{1,0:T(8,128)} %fusion.4), channel_id=1, source_target_pairs={{0,22},{1,23},{2,24},{3,25},{4,26},{5,27},{6,28},{7,29},{8,30},{9,... | collective-permute-start | bytes 147464
  1232.0 11.0 collective-permute-start.20
  1235.4 9.5 collective-permute-start.19
  1237.3 9.5 collective-permute-start.18
  1239.2 9.8 collective-permute-start.17
  1241.1 11.6 collective-permute-start.16
  1243.0 11.9 collective-permute-start.15
  1244.9 12.2 collective-permute-start.14
  1246.8 13.4 collective-permute-start.13
  1249.0 14.9 %collective-permute-start.12 = (f32[16,768]{1,0:T(8,128)}, f32[16,768]{1,0:T(8,128)}, u32[]{:S(2)}, u32[]{:S(2)}) collective-permute-start(f32[16,768]{1,0:T(8,128)} %fusion.4), channel_id=1, source_target_pairs={{0,13},{1,14},{2,15},{3,16},{4,17},{5,18},{6,19},{7,20},{8,21},{9,... | collective-permute-start | bytes 147464
  1252.8 12.5 collective-permute-start.11
  1254.9 15.9 %collective-permute-start.10 = (f32[16,768]{1,0:T(8,128)}, f32[16,768]{1,0:T(8,128)}, u32[]{:S(2)}, u32[]{:S(2)}) collective-permute-start(f32[16,768]{1,0:T(8,128)} %fusion.4), channel_id=1, source_target_pairs={{0,11},{1,12},{2,13},{3,14},{4,15},{5,16},{6,17},{7,18},{8,19},{9,... | collective-permute-start | bytes 147464
  1257.1 17.7 %collective-permute-start.9 = (f32[16,768]{1,0:T(8,128)}, f32[16,768]{1,0:T(8,128)S(1)}, u32[]{:S(2)}, u32[]{:S(2)}) collective-permute-start(f32[16,768]{1,0:T(8,128)} %fusion.4), channel_id=1, source_target_pairs={{0,10},{1,11},{2,12},{3,13},{4,14},{5,15},{6,16},{7,17},{8,18},{9,... | collective-permute-start | bytes 147464
  1260.2 18.9 %collective-permute-start.8 = (f32[16,768]{1,0:T(8,128)}, f32[16,768]{1,0:T(8,128)S(1)}, u32[]{:S(2)}, u32[]{:S(2)}) collective-permute-start(f32[16,768]{1,0:T(8,128)} %fusion.4), channel_id=1, source_target_pairs={{0,9},{1,10},{2,11},{3,12},{4,13},{5,14},{6,15},{7,16},{8,17},{9,1... | collective-permute-start | bytes 147464
  1264.0 17.4 %collective-permute-start.7 = (f32[16,768]{1,0:T(8,128)}, f32[16,768]{1,0:T(8,128)S(1)}, u32[]{:S(2)}, u32[]{:S(2)}) collective-permute-start(f32[16,768]{1,0:T(8,128)} %fusion.4), channel_id=1, source_target_pairs={{0,8},{1,9},{2,10},{3,11},{4,12},{5,13},{6,14},{7,15},{8,16},{9,17... | collective-permute-start | bytes 147464
  1265.3 18.3 %collective-permute-start.6 = (f32[16,768]{1,0:T(8,128)}, f32[16,768]{1,0:T(8,128)S(1)}, u32[]{:S(2)}, u32[]{:S(2)}) collective-permute-start(f32[16,768]{1,0:T(8,128)} %fusion.4), channel_id=1, source_target_pairs={{0,7},{1,8},{2,9},{3,10},{4,11},{5,12},{6,13},{7,14},{8,15},{9,16}... | collective-permute-start | bytes 147464
  1270.8 16.5 %collective-permute-start.5 = (f32[16,768]{1,0:T(8,128)}, f32[16,768]{1,0:T(8,128)S(1)}, u32[]{:S(2)}, u32[]{:S(2)}) collective-permute-start(f32[16,768]{1,0:T(8,128)} %fusion.4), channel_id=1, source_target_pairs={{0,6},{1,7},{2,8},{3,9},{4,10},{5,11},{6,12},{7,13},{8,14},{9,15},... | collective-permute-start | bytes 147464
  1274.8 16.5 %copy-start.58 = (f32[16,768]{1,0:T(8,128)}, f32[16,768]{1,0:T(8,128)S(1)}, u32[]{:S(2)}) copy-start(f32[16,768]{1,0:T(8,128)S(1)} %collective-permute-done.9) | copy-start | bytes 147460
  1274.8 18.3 %collective-permute-start.4 = (f32[16,768]{1,0:T(8,128)}, f32[16,768]{1,0:T(8,128)}, u32[]{:S(2)}, u32[]{:S(2)}) collective-permute-start(f32[16,768]{1,0:T(8,128)} %fusion.4), channel_id=1, source_target_pairs={{0,5},{1,6},{2,7},{3,8},{4,9},{5,10},{6,11},{7,12},{8,13},{9,14},{... | collective-permute-start | bytes 147464
  1279.1 12.2 copy-start.59
  1279.1 13.9 collective-permute-start.3
  1281.3 10.0 copy-start.60
  1281.3 11.7 collective-permute-start.2
  1283.5 7.8 copy-start.61
  1283.5 9.6 collective-permute-start.1
  1287.3 4.0 copy-start.62
  1287.3 6.3 collective-permute-start
  1293.1 56.6 %copy-start.27 = (bf16[768,256]{1,0:T(8,128)(2,1)S(1)}, bf16[768,256]{1,0:T(8,128)(2,1)}, u32[]{:S(2)}) copy-start(bf16[768,256]{1,0:T(8,128)(2,1)} %param.26) | copy-start | bytes 1179652
  1293.1 56.6 %copy-start.28 = (f32[256,768]{1,0:T(8,128)S(1)}, f32[256,768]{1,0:T(8,128)}, u32[]{:S(2)}) copy-start(f32[256,768]{1,0:T(8,128)} %fusion.228) | copy-start | bytes 2359300
  (75 other events, 167.9 us)
Sparse Core Ops, SparseCore 0:
  22.0 92.1 all-gather.9
  116.4 90.0 all-gather.11
  208.6 89.5 all-gather.13
  300.3 89.5 all-gather.15
  834.8 159.7 all-reduce.7
where the time goes:
time: 1460 us; the launch traced here: 1430 us
  local copies, waits for them, and re-layouts  480 us (33%)
  blocking collectives  451 us (31%)
  other arithmetic  228 us (16%)
  matrix products  131 us (9%)
  starting transfers between devices  96.5 us (7%)
  waiting for transfers between devices  22.7 us (2%)
  between operations  18.1 us (1%)
    unnamed x2, blocking collectives  387 us
    select_n x60, other arithmetic, step(): jnp.where(position < mine, new, old)  199 us
    dynamic_update_slice x20, local copies, waits for them, and re-layouts, ssd_pass(): final, ys = lax.scan(ssd_block, state, blocks)  159 us
    unnamed x33, starting transfers between devices  96.4 us
    dynamic_slice x60, local copies, waits for them, and re-layouts, step(): longer = join(subtotal, jax.tree.map(lambda part: part[position], pieces))  84.6 us
    psum x1, blocking collectives, square_total(): return lax.psum(local, ('rec', 'seq'))  64.1 us
    unnamed x79, local copies, waits for them, and re-layouts  63.2 us
    dot_general x12, matrix products, ssd_block(): jnp.einsum('hts,shp->thp', decay * scores[None], xs_b, precision=lax.Prec...  43.9 us
  transfers between devices with their start and end apart: 37, of which 2 were waited for; matrix products, arithmetic and copies ran while one was open for 62% of the time, Pallas kernels for 0%

commit v1 on v0

v1 whole, which is shorter than its diff:
```python
import jax
import jax.numpy as jnp
from jax import lax
from jax.experimental import pallas as pl
from jax.experimental.pallas import tpu as pltpu
from jax.sharding import PartitionSpec as P

F32 = jnp.float32
BF16 = jnp.bfloat16
NX = 4
NY = 4
NZ = 4
SEG = 256
HALF = SEG // 2
DM = 768
NS = 128
NH = 6
HD = 64
HC = NH * HD
ROWS = DM // 2


def shift(axis, step, wrap=True):
    if axis == "c":
        return "rec", [(r, r ^ 1) for r in range(2 * NZ)]
    count, stride, total, name = {
        "x": (NX, 1, NX * NY, "seq"),
        "y": (NY, NX, NX * NY, "seq"),
        "z": (NZ, 2, 2 * NZ, "rec"),
    }[axis]
    pairs = []
    for i in range(total):
        at = (i // stride) % count
        to = at + step
        if not wrap and not 0 <= to < count:
            continue
        pairs.append((i, i + (to % count - at) * stride))
    return name, pairs


def move(value, axis, step, wrap=True):
    name, pairs = shift(axis, step, wrap)
    return lax.ppermute(value, name, pairs)


def dot(a, b, ca, cb):
    return lax.dot_general(a, b, (((ca,), (cb,)), ((), ())), preferred_element_type=F32)


def place(p, x):
    return lax.rem(p - x + NX, NX)


def vm(n):
    return [pl.BlockSpec(memory_space=pltpu.VMEM)] * n


SMEM = pl.BlockSpec(memory_space=pltpu.SMEM)
PARAMS = pltpu.CompilerParams(vmem_limit_bytes=56 * 2**20)


def tok_kernel(
    at, a0, b0, a1, b1, a2, b2, a3, b3, w_in, w_bc, ci, ce,
    tokb, xs, xfr, bc, pre, t_f, t_r, ends,
):
    x = at[0]
    for k, (a, b) in enumerate(((a0, b0), (a1, b1), (a2, b2), (a3, b3))):
        tokb[k, :HALF] = a[...].astype(BF16)
        tokb[k, HALF:] = b[...].astype(BF16)

    def segment(k, _):
        t = tokb[k]
        xv = dot(t, w_in[...], 1, 0).astype(BF16)
        bv = dot(t, w_bc[...], 1, 0).astype(BF16)
        xs[k] = xv
        bc[k] = bv
        xf = xv.astype(F32)
        last = ci[k, SEG - 1 : SEG, :]
        xfr[k, :, :HC] = (xf * jnp.exp(last - ci[k])).astype(BF16)
        xfr[k, :, HC:] = (xf * jnp.exp(ce[k])).astype(BF16)
        ends[k] = dot(bv[:, :NS], xfr[k], 0, 0)
        return 0

    lax.fori_loop(0, NX, segment, 0)
    acc = jnp.zeros((NS, HC), F32)
    for p in range(NX):
        k = place(p, x)
        pre[0, k] = acc
        acc = acc * jnp.exp(ci[k, SEG - 1 : SEG, :]) + ends[k, :, :HC]
    t_f[...] = acc
    acc = jnp.zeros((NS, HC), F32)
    for p in reversed(range(NX)):
        k = place(p, x)
        pre[1, k] = acc
        acc = acc * jnp.exp(ci[k, SEG - 1 : SEG, :]) + ends[k, :, HC:]
    t_r[...] = acc


def cot_kernel(
    at, a0, b0, a1, b1, a2, b2, a3, b3, w_out, ci, ce, bc,
    cotb, dy, dyfr, pre, t_f, t_r, ends,
):
    x = at[0]
    for k, (a, b) in enumerate(((a0, b0), (a1, b1), (a2, b2), (a3, b3))):
        cotb[k, :HALF] = a[...].astype(BF16)
        cotb[k, HALF:] = b[...].astype(BF16)

    def segment(k, _):
        d = dot(cotb[k], w_out[...], 1, 1)
        dy[k] = d.astype(BF16)
        last = ci[k, SEG - 1 : SEG, :]
        dyfr[k, :, :HC] = (d * jnp.exp(ci[k])).astype(BF16)
        dyfr[k, :, HC:] = (d * jnp.exp(last - ce[k])).astype(BF16)
        ends[k] = dot(bc[k, :, NS:], dyfr[k], 0, 0)
        return 0

    lax.fori_loop(0, NX, segment, 0)
    acc = jnp.zeros((NS, HC), F32)
    for p in reversed(range(NX)):
        k = place(p, x)
        pre[0, k] = acc
        acc = acc * jnp.exp(ci[k, SEG - 1 : SEG, :]) + ends[k, :, :HC]
    t_f[...] = acc
    acc = jnp.zeros((NS, HC), F32)
    for p in range(NX):
        k = place(p, x)
        pre[1, k] = acc
        acc = acc * jnp.exp(ci[k, SEG - 1 : SEG, :]) + ends[k, :, HC:]
    t_r[...] = acc


def enter(pre, which, q, ci, x, order, out, cols):
    log = jnp.zeros((1, HC), F32)
    for p in order:
        k = place(p, x)
        out[k, :, cols] = (pre[which, k] + q[...] * jnp.exp(log)).astype(BF16)
        log = log + ci[k, SEG - 1 : SEG, :]


def inner_kernel(
    at, xs, bc, dy, dyfr, cotb, ci, ce, cirow, cerow, pre, q_f, q_r,
    keep, send, dxi, dci, dbi, sr, yb, g,
):
    x, core = at[0], at[1]
    enter(pre, 0, q_f, ci, x, range(NX), sr, pl.ds(0, HC))
    enter(pre, 1, q_r, ci, x, reversed(range(NX)), sr, pl.ds(HC, HC))

    def segment(k, _):
        b, c = bc[k, :, :NS], bc[k, :, NS:]
        t = lax.broadcasted_iota(jnp.int32, (SEG, SEG), 0)
        s = lax.broadcasted_iota(jnp.int32, (SEG, SEG), 1)
        low, same = t > s, t == s
        scores = dot(c, b, 1, 1)
        scores = jnp.where(same, 2.0 * scores, scores)
        lane = lax.broadcasted_iota(jnp.int32, (SEG, 2 * HD), 1)
        carry = dot(c, sr[k], 1, 0)
        total = jnp.zeros((SEG, SEG), F32)
        for pair in range(NH // 2):
            cols = slice(pair * 2 * HD, (pair + 1) * 2 * HD)
            xp, dp = xs[k, :, cols], dy[k, :, cols]
            ws, xm, dm = [], [], []
            for i in range(2):
                h = 2 * pair + i
                at_t = slice(h * HD, h * HD + 1)
                diff = jnp.where(
                    low,
                    ci[k, :, at_t] - cirow[k, h : h + 1, :],
                    cerow[k, h : h + 1, :] - ce[k, :, at_t],
                )
                decay = jnp.exp(diff)
                mine = (lane < HD) if i == 0 else (lane >= HD)
                xm.append(jnp.where(mine, xp, jnp.zeros_like(xp)))
                dm.append(jnp.where(mine, dp, jnp.zeros_like(dp)))
                ws.append((decay * scores).astype(BF16))
                total = total + decay * dot(dm[i], xp, 1, 1)
            y = dot(ws[0], xm[0], 1, 0) + dot(ws[1], xm[1], 1, 0)
            last = ci[k, SEG - 1 : SEG, cols]
            y = y + carry[:, cols] * jnp.exp(ci[k, :, cols])
            y = y + carry[:, slice(HC + cols.start, HC + cols.stop)] * jnp.exp(last - ce[k, :, cols])
            yb[pl.ds(k * SEG, SEG), cols] = y.astype(BF16)
            dxi[k, :, cols] = dot(ws[0], dm[0], 0, 0) + dot(ws[1], dm[1], 0, 0)
        total = jnp.where(same, 2.0 * total, total).astype(BF16)
        dci[k] = dot(total, b, 1, 0) + dot(dyfr[k], sr[k], 1, 1)
        dbi[k] = dot(total, c, 0, 0)
        return 0

    lax.fori_loop(0, NX, segment, 0)
    raw = dot(yb[...], cotb[...].reshape(NX * SEG, DM), 0, 0)
    for j in range(2):
        for q in range(4):
            z, c = 2 * j + q // 2, q % 2
            g[c, 96 * z : 96 * z + 96, :] = raw[96 * q : 96 * q + 96, HC * j : HC * j + HC]
    keep[...] = g[core]
    send[...] = g[1 - core]


def outer_kernel(
    at, tokb, xfr, bc, ci, ce, pre, q_f, q_r, dxi, dci, dbi, w_in, w_bc,
    keep, send, d0, d1a, d1b, d2a, d2b, d3a, d3b, ds, dz, g,
):
    x, core = at[0], at[1]
    enter(pre, 0, q_f, ci, x, reversed(range(NX)), ds, pl.ds(0, HC))
    enter(pre, 1, q_r, ci, x, range(NX), ds, pl.ds(HC, HC))

    def segment(k, _):
        b = bc[k, :, :NS]
        last = ci[k, SEG - 1 : SEG, :]
        back = dot(b, ds[k], 1, 0)
        dx = dxi[k] + back[:, :HC] * jnp.exp(last - ci[k]) + back[:, HC:] * jnp.exp(ce[k])
        dz[k, :, :HC] = dx.astype(BF16)
        dz[k, :, HC : HC + NS] = (dbi[k] + dot(xfr[k], ds[k], 1, 1)).astype(BF16)
        dz[k, :, HC + NS :] = dci[k].astype(BF16)
        return 0

    lax.fori_loop(0, NX, segment, 0)

    def tokens_of(k):
        return dot(dz[k, :, :HC], w_in[...], 1, 1) + dot(dz[k, :, HC:], w_bc[...], 1, 1)

    for k, (lo, hi) in ((2, (d2a, d2b)), (1, (d1a, d1b)), (3, (d3a, d3b))):
        d = tokens_of(k)
        lo[...] = d[:HALF]
        hi[...] = d[HALF:]
    d0[...] = tokens_of(0)
    width = HC + 2 * NS
    raw = dot(tokb[...].reshape(NX * SEG, DM), dz[...].reshape(NX * SEG, width), 0, 0)
    for j in range(2 * NZ):
        z, c = j // 2, j % 2
        g[c, 96 * z : 96 * z + 96, :] = raw[96 * j : 96 * j + 96, :]
    keep[...] = g[core]
    send[...] = g[1 - core]


def call(kernel, outs, scratch, args, flops):
    moved = sum(a.size * a.dtype.itemsize for a in args)
    return pl.pallas_call(
        kernel,
        out_shape=[jax.ShapeDtypeStruct(*o) for o in outs],
        in_specs=[SMEM] + vm(len(args) - 1),
        out_specs=vm(len(outs)),
        scratch_shapes=[pltpu.VMEM(*s) for s in scratch],
        compiler_params=PARAMS,
        cost_estimate=pl.CostEstimate(flops=flops, bytes_accessed=moved, transcendentals=0),
    )(*args)


def along_y(t_up, t_down, lrow, l_up, l_down):
    f = move(t_up, "y", 1, False)
    r = move(t_down, "y", -1, False)
    two_f = t_up + jnp.exp(lrow) * f
    two_r = t_down + jnp.exp(lrow) * r
    far_f = move(two_f, "y", 2, False)
    far_r = move(two_r, "y", -2, False)
    return f + jnp.exp(l_up) * far_f, r + jnp.exp(l_down) * far_r


def pick(value, index):
    return lax.dynamic_index_in_dim(value, index, 0, keepdims=False)


def scatter_sum(part, first, second, at):
    if first == "y":
        part = jnp.swapaxes(part, 0, 1)
    for axis in (first, second):
        own = pick(part, at[axis])
        for step in (1, 3, 2):
            own = own + move(pick(part, (at[axis] + step) % 4), axis, step)
        part = own
    return part


def body(tokens, cotangent, log_decay, w_in, w_bc, w_out):
    seq, rec = lax.axis_index("seq"), lax.axis_index("rec")
    x, y = seq % NX, seq // NX
    core, z = rec % 2, rec // 2
    at = jnp.stack([x, core]).astype(jnp.int32)

    def gather(v):
        a, b = v[:HALF].astype(F32), v[HALF:].astype(F32)
        a3, b3 = move(a, "x", 1), move(b, "x", 1)
        a1, b1 = move(a, "x", -1), move(b, "x", -1)
        a2, b2 = move(a3, "x", 1), move(b1, "x", -1)
        return [a, b, a1, b1, a2, b2, a3, b3]

    la0 = log_decay[0]
    las = jnp.stack([la0, move(la0, "x", -1), move(la0, "x", 2), move(la0, "x", 1)])
    toks = gather(tokens[0])
    cots = gather(cotangent[0])
    la = lax.dynamic_slice(las, (0, x * NH, 0), (NX, NH, SEG))
    tri = jnp.triu(jnp.ones((SEG, SEG), F32))
    spread = jnp.repeat(jnp.eye(NH, dtype=F32), HD, axis=1)
    best = lax.Precision.HIGHEST
    cirow = jnp.einsum("khs,st->kht", la, tri, precision=best)
    cerow = cirow - la
    ci = jnp.einsum("kht,hj->ktj", cirow, spread, precision=best)
    ce = jnp.einsum("kht,hj->ktj", cerow, spread, precision=best)
    lrow = jnp.broadcast_to(jnp.sum(ci[:, -1, :], axis=0)[None], (8, HC))
    l_up, l_down = move(lrow, "y", 1)[:1], move(lrow, "y", -1)[:1]
    lrow = lrow[:1]
    wi = lax.dynamic_slice(w_in, (0, x * HC), (DM, HC))
    wo = lax.dynamic_slice(w_out, (x * HC, 0), (HC, DM))

    state = ((NS, HC), F32)
    edges = ((2, NX, NS, HC), F32)
    tokb, xs, xfr, bc, pre_s, t_f, t_r = call(
        tok_kernel,
        [((NX, SEG, DM), BF16), ((NX, SEG, HC), BF16), ((NX, SEG, 2 * HC), BF16), ((NX, SEG, 2 * NS), BF16),
         edges, state, state],
        [((NX, NS, 2 * HC), F32)],
        [at, *toks, wi, w_bc, ci, ce],
        2 * 1024 * (DM * (HC + 2 * NS) + NS * 2 * HC),
    )
    q_f, q_r = along_y(t_f, t_r, lrow, l_up, l_down)
    cotb, dy, dyfr, pre_d, u_f, u_r = call(
        cot_kernel,
        [((NX, SEG, DM), BF16), ((NX, SEG, HC), BF16), ((NX, SEG, 2 * HC), BF16), edges, state, state],
        [((NX, NS, 2 * HC), F32)],
        [at, *cots, wo, ci, ce, bc],
        2 * 1024 * (DM * HC + NS * 2 * HC),
    )
    p_r, p_f = along_y(u_r, u_f, lrow, l_up, l_down)
    keep_o, send_o, dxi, dci, dbi = call(
        inner_kernel,
        [((ROWS, HC), F32), ((ROWS, HC), F32), ((NX, SEG, HC), F32), ((NX, SEG, NS), F32), ((NX, SEG, NS), F32)],
        [((NX, NS, 2 * HC), BF16), ((NX * SEG, HC), BF16), ((2, ROWS, HC), F32)],
        [at, xs, bc, dy, dyfr, cotb, ci, ce, cirow, cerow, pre_s, q_f, q_r],
        2 * 1024 * (HC * DM + 5 * SEG * HC + 6 * NS * HC),
    )
    width = HC + 2 * NS
    half = ((HALF, DM), F32)
    keep_i, send_i, d0, d1a, d1b, d2a, d2b, d3a, d3b = call(
        outer_kernel,
        [((ROWS, width), F32), ((ROWS, width), F32), ((SEG, DM), F32), half, half, half, half, half, half],
        [((NX, NS, 2 * HC), BF16), ((NX, SEG, width), BF16), ((2, ROWS, width), F32)],
        [at, tokb, xfr, bc, ci, ce, pre_d, p_f, p_r, dxi, dci, dbi, wi, w_bc],
        2 * 1024 * (2 * width * DM + 4 * NS * HC),
    )
    from_a = d1a + move(d2a, "x", 1)
    from_b = d3b + move(d2b, "x", -1)
    top = d0[:HALF] + move(from_a, "x", 1) + move(d3a, "x", -1)
    bottom = d0[HALF:] + move(d1b, "x", 1) + move(from_b, "x", -1)
    d_tok = jnp.concatenate([top, bottom], axis=0).astype(BF16)

    place_of = {"z": z, "y": y}
    raw_o = (keep_o + move(send_o, "c", 1)).reshape(NZ, NY, 24, HC)
    raw_i = (keep_i + move(send_i, "c", 1)).reshape(NZ, NY, 24, width)
    raw_o = scatter_sum(raw_o, "z", "y", place_of)
    raw_i = jnp.concatenate(
        [
            scatter_sum(raw_i[..., :256], "z", "y", place_of),
            scatter_sum(raw_i[..., 256:], "y", "z", place_of),
        ],
        axis=-1,
    )
    blocks = raw_i.reshape(NX, 6, width)
    pieces = jnp.stack(
        [pick(blocks, x)] + [move(pick(blocks, (x + k) % NX), "x", k) for k in range(1, NX)]
    )
    sum_bc = jnp.sum(pieces[..., HC:], axis=0)
    all_in = jnp.concatenate([pick(pieces, (x - p) % NX)[:, :HC] for p in range(NX)], axis=1)
    left = z < 2
    upper, lower = raw_o[:12], raw_o[12:]
    one, two = [], []
    for r in range(2 * NZ):
        for s in range(NX * NY):
            zz, cc, yy, xx = r // 2, r % 2, s // NX, s % NX
            to = 32 * xx + 2 * ((zz % 2) * 8 + cc * 4 + yy)
            first = 0 if zz < 2 else 1
            one.append((r * 16 + s, to + first))
            two.append((r * 16 + s, to + 1 - first))
    got_one = lax.ppermute(jnp.where(left, upper, lower), ("rec", "seq"), one)
    got_two = lax.ppermute(jnp.where(left, lower, upper), ("rec", "seq"), two)
    even = x % 2 == 0
    all_out = jnp.concatenate(
        [jnp.where(even, got_one, got_two), jnp.where(even, got_two, got_one)], axis=1
    )
    square = jnp.sum(all_in * all_in) + jnp.sum(sum_bc * sum_bc) + jnp.sum(raw_o * raw_o)
    square = jnp.full((8, 128), square)
    square = square + move(square, "c", 1)
    for axis in ("z", "y", "x"):
        square = square + (move(square, axis, 1) + move(square, axis, 3) + move(square, axis, 2))
    entries = DM * 1536 + DM * 256 + 1536 * DM
    factor = jnp.minimum(1.0, 1.0 / jnp.sqrt(square[:1, :1] / entries + 1e-06))
    return d_tok[None], factor * all_in, factor * sum_bc, factor * all_out


def solution(mesh):
    in_specs = (P("rec", "seq", None), P("rec", "seq", None), P("rec", None, "seq"), P(), P(), P())
    out_specs = (
        P("rec", "seq", None),
        P(("rec", "seq"), None),
        P(("rec", "seq"), None),
        P(("rec", "seq"), None),
    )
    return jax.shard_map(body, mesh=mesh, in_specs=in_specs, out_specs=out_specs, check_vma=False)
```

time: 1460 us -> 233 us (0.16); the launches traced: 1430 us -> 231 us
  local copies, waits for them, and re-layouts: 480 us -> 9.22 us
  blocking collectives: 451 us -> 0 us
  other arithmetic: 228 us -> 22.7 us
  matrix products: 131 us -> 7.18 us
  Pallas kernels: 0 us -> 40.2 us
  waiting for transfers between devices: 22.7 us -> 40 us
    unnamed x2 -> x0, blocking collectives: 387 us -> none
    select_n x60 -> x2, other arithmetic: 199 us -> 0.83 us  [the longest x1 0.82 us: body(): got_one = lax.ppermute(jnp.where(left, upper, lower), ('rec', 'seq'), one)]
    dynamic_update_slice x20 -> x0, local copies, waits for them, and re-layouts: 159 us -> none  [ssd_pass(): final, ys = lax.scan(ssd_block, state, blocks)]
    dot_general x56 -> x3, matrix products: 124 us -> 7.18 us  [the longest x1 3.05 us: body(): ci = jnp.einsum('kht,hj->ktj', cirow, spread, precision=best)]
    ppermute x0 -> x66, starting transfers between devices: none -> 108 us  [the longest x64 102 us: move(): return lax.ppermute(value, name, pairs)]
    unnamed x33 -> x0, starting transfers between devices: 96.4 us -> none
    dynamic_slice x68 -> x3, local copies, waits for them, and re-layouts: 87.9 us -> 2.83 us  [the longest x1 1.92 us: body(): wo = lax.dynamic_slice(w_out, (x * HC, 0), (HC, DM))]
    psum x1 -> x0, blocking collectives: 64.1 us -> none  [square_total(): return lax.psum(local, ('rec', 'seq'))]
  transfers between devices with their start and end apart: 37 -> 66, of which waited for: 2 -> 22; matrix products, arithmetic and copies ran while one was open for 62% -> 14% of each run, Pallas kernels for 0% -> 12%
where the time goes in v1:
time: 233 us; the launch traced here: 231 us
  starting transfers between devices  108 us (46%)
  Pallas kernels  40.2 us (17%)
  waiting for transfers between devices  40 us (17%)
  other arithmetic  22.7 us (10%)
  local copies, waits for them, and re-layouts  9.22 us (4%)
  matrix products  7.18 us (3%)
  between operations  3.81 us (2%)
    ppermute x64, starting transfers between devices, move(): return lax.ppermute(value, name, pairs)  102 us
    pallas_call x4, Pallas kernels, call(): pl.pallas_call(kernel, out_shape=[jax.ShapeDtypeStruct(*o) for o in outs]...  40.2 us
    ppermute x64, waiting for transfers between devices, move(): return lax.ppermute(value, name, pairs)  40 us
    ppermute x1, starting transfers between devices, body(): got_one = lax.ppermute(jnp.where(left, upper, lower), ('rec', 'seq'), one)  5.45 us
  transfers between devices with their start and end apart: 66, of which 22 were waited for; matrix products, arithmetic and copies ran while one was open for 14% of the time, Pallas kernels for 12%

profile of v1, /device:TPU:6, one launch (start us, length us, event | category | flops | bytes accessed | tf_op | source)
XLA Modules:
  0.0 231.4 jit_solution(137527147530469052)
XLA Ops:
  0.6 1.2 bitcast_convert_fusion.2
  2.8 2.4 %collective-permute-start.2 = (f32[128,768]{1,0:T(8,128)S(1)}, f32[128,768]{1,0:T(8,128)}, u32[]{:S(2)}, u32[]{:S(2)}) collective-permute-start(f32[128,768]{1,0:T(8,128)S(1)} %get-tuple-element.74.a0), channel_id=1, source_target_pairs={{0,1},{1,2},{2,3},{3,0},{4,5},{5,6},{6,7},{7,4},{8,9},{9,10},{10,1... | collective-permute-start | bytes 1179656 | tf_op jit(solution)/shard_map/ppermute | solution.py:43
  5.2 1.5 collective-permute-start.7
  6.7 1.8 collective-permute-start.8
  9.3 1.8 bitcast_convert_fusion
  11.2 4.0 %collective-permute-done.6 = f32[24,256]{1,0:T(8,128)} collective-permute-done((f32[24,256]{1,0:T(8,128)}, f32[24,256]{1,0:T(8,128)}, u32[]{:S(2)}, u32[]{:S(2)}) %collective-permute-start.6) | collective-permute-done | bytes 24608 | tf_op jit(solution)/shard_map/ppermute | solution.py:43
  15.2 3.2 %collective-permute-start.5 = (f32[128,768]{1,0:T(8,128)S(1)}, f32[128,768]{1,0:T(8,128)}, u32[]{:S(2)}, u32[]{:S(2)}) collective-permute-start(f32[128,768]{1,0:T(8,128)S(1)} %get-tuple-element.73.b0), channel_id=1, source_target_pairs={{0,1},{1,2},{2,3},{3,0},{4,5},{5,6},{6,7},{7,4},{8,9},{9,10},{10,1... | collective-permute-start | bytes 1179656 | tf_op jit(solution)/shard_map/ppermute | solution.py:43
  18.4 3.2 %collective-permute-start.11 = (f32[128,768]{1,0:T(8,128)}, f32[128,768]{1,0:T(8,128)}, u32[]{:S(2)}, u32[]{:S(2)}) collective-permute-start(f32[128,768]{1,0:T(8,128)} %get-tuple-element.72.a0), channel_id=1, source_target_pairs={{0,1},{1,2},{2,3},{3,0},{4,5},{5,6},{6,7},{7,4},{8,9},{9,10},{10,1... | collective-permute-start | bytes 1179656 | tf_op jit(solution)/shard_map/ppermute | solution.py:43
  23.9 1.9 constant_dynamic-slice_fusion.1.w_out
  26.9 1.6 collective-permute-done.1.b1
  29.0 2.8 %collective-permute-start.14 = (f32[128,768]{1,0:T(8,128)S(1)}, f32[128,768]{1,0:T(8,128)S(1)}, u32[]{:S(2)}, u32[]{:S(2)}) collective-permute-start(f32[128,768]{1,0:T(8,128)S(1)} %get-tuple-element.71.b0), channel_id=1, source_target_pairs={{0,1},{1,2},{2,3},{3,0},{4,5},{5,6},{6,7},{7,4},{8,9},{9,10},{10,1... | collective-permute-start | bytes 1179656 | tf_op jit(solution)/shard_map/ppermute | solution.py:43
  31.8 5.2 %collective-permute-done.10.b1 = f32[128,768]{1,0:T(8,128)} collective-permute-done((f32[128,768]{1,0:T(8,128)S(1)}, f32[128,768]{1,0:T(8,128)}, u32[]{:S(2)}, u32[]{:S(2)}) %collective-permute-start.10) | collective-permute-done | bytes 393248 | tf_op jit(solution)/shard_map/ppermute | solution.py:43
  37.0 3.2 %collective-permute-start.12 = (f32[128,768]{1,0:T(8,128)}, f32[128,768]{1,0:T(8,128)S(1)}, u32[]{:S(2)}, u32[]{:S(2)}) collective-permute-start(f32[128,768]{1,0:T(8,128)} %collective-permute-done.11.a3), channel_id=1, source_target_pairs={{0,1},{1,2},{2,3},{3,0},{4,5},{5,6},{6,7},{7,4},{8,9},{9,10},{10,1... | collective-permute-start | bytes 1179656 | tf_op jit(solution)/shard_map/ppermute | solution.py:43
  40.2 4.7 %collective-permute-done.3.a2 = f32[128,768]{1,0:T(8,128)} collective-permute-done((f32[128,768]{1,0:T(8,128)}, f32[128,768]{1,0:T(8,128)}, u32[]{:S(2)}, u32[]{:S(2)}) %collective-permute-start.3) | collective-permute-done | bytes 393248 | tf_op jit(solution)/shard_map/ppermute | solution.py:43
  45.0 3.1 %fusion.32.ci = f32[4,256,384]{2,1,0:T(8,128)} fusion(f32[4,6,256]{2,1,0:T(8,128)S(1)} %get-tuple-element.105.cirow, f32[6,384,1]{1,0,2:T(8,128)S(1)} %reshape.88), kind=kOutput, calls=%fused_computation.107 | convolution fusion | flops 28311552 | bytes 1606656 | tf_op jit(solution)/shard_map/kht,hj->ktj/dot_general | solution.py:295
  48.0 3.0 %fusion.33.ce = f32[4,256,384]{2,1,0:T(8,128)} fusion(f32[4,6,256]{2,1,0:T(8,128)S(1)} %get-tuple-element.104.cerow, f32[6,384,1]{1,0,2:T(8,128)S(1)} %reshape.88), kind=kOutput, calls=%fused_computation.108 | convolution fusion | flops 28311552 | bytes 1606656 | tf_op jit(solution)/shard_map/kht,hj->ktj/dot_general | solution.py:296
  51.1 2.7 %collective-permute-done.4.b2 = f32[128,768]{1,0:T(8,128)S(1)} collective-permute-done((f32[128,768]{1,0:T(8,128)}, f32[128,768]{1,0:T(8,128)S(1)}, u32[]{:S(2)}, u32[]{:S(2)}) %collective-permute-start.4) | collective-permute-done | bytes 393248 | tf_op jit(solution)/shard_map/ppermute | solution.py:43
  54.5 9.1 %shard_map.93 = (bf16[4,256,768]{2,1,0:T(8,128)(2,1)}, bf16[4,256,384]{2,1,0:T(8,128)(2,1)}, bf16[4,256,768]{2,1,0:T(8,128)(2,1)}, bf16[4,256,256]{2,1,0:T(8,128...) custom-call(s32[2]{0:T(128)} %pad_add_fusion.at, f32[128,768]{1,0:T(8,128)} %copy-done.2, ...), custom_call_target="tpu_custom_call" | custom-call | flops 1207959552 | bytes 7274504 | tf_op jit(solution)/shard_map/pallas_call | solution.py:236
  63.7 1.3 collective-permute-start.23
  66.1 8.4 %shard_map.94 = (bf16[4,256,768]{2,1,0:T(8,128)(2,1)}, bf16[4,256,384]{2,1,0:T(8,128)(2,1)}, bf16[4,256,768]{2,1,0:T(8,128)(2,1)}, f32[2,4,128,384]{3,2,1,0:T(8,...) custom-call(s32[2]{0:T(128)} %pad_add_fusion.at, f32[128,768]{1,0:T(8,128)} %get-tuple-element.72.a0, f32[128,768]{1,0:T(8,128)} %copy-done.3, ...), custom_call_target="tpu_custom_call" | custom-call | flops 805306368 | bytes 7405576 | tf_op jit(solution)/shard_map/pallas_call | solution.py:236
  74.5 4.5 %collective-permute-start.18 = (f32[128,384]{1,0:T(8,128)}, f32[128,384]{1,0:T(8,128)S(1)}, u32[]{:S(2)}, u32[]{:S(2)}) collective-permute-start(f32[128,384]{1,0:T(8,128)} %get-tuple-element.36), channel_id=1, source_target_pairs={{0,4},{1,5},{2,6},{3,7},{4,8},{5,9},{6,10},{7,11},{8,12},{9,13},{1... | collective-permute-start | bytes 589832 | tf_op jit(solution)/shard_map/ppermute | solution.py:43
  79.0 3.5 %collective-permute-start.21 = (f32[128,384]{1,0:T(8,128)S(1)}, f32[128,384]{1,0:T(8,128)S(1)}, u32[]{:S(2)}, u32[]{:S(2)}) collective-permute-start(f32[128,384]{1,0:T(8,128)S(1)} %copy-done.14), channel_id=1, source_target_pairs={{0,4},{1,5},{2,6},{3,7},{4,8},{5,9},{6,10},{7,11},{8,12},{9,13},{1... | collective-permute-start | bytes 589832 | tf_op jit(solution)/shard_map/ppermute | solution.py:43
  82.5 1.3 collective-permute-start.15
  84.7 3.1 %collective-permute-start.16 = (f32[8,384]{1,0:T(8,128)S(1)}, f32[8,384]{1,0:T(8,128)S(1)}, u32[]{:S(2)}, u32[]{:S(2)}) collective-permute-start(f32[8,384]{1,0:T(8,128)S(1)} %broadcast_in_dim.25), channel_id=1, source_target_pairs={{0,12},{1,13},{2,14},{3,15},{4,0},{5,1},{6,2},{7,3},{8,4},{9,5},{1... | collective-permute-start | bytes 36872 | tf_op jit(solution)/shard_map/ppermute | solution.py:43
  87.8 2.5 %collective-permute-done.15 = f32[128,384]{1,0:T(8,128)S(1)} collective-permute-done((f32[128,384]{1,0:T(8,128)}, f32[128,384]{1,0:T(8,128)S(1)}, u32[]{:S(2)}, u32[]{:S(2)}) %collective-permute-start.15) | collective-permute-done | bytes 196640 | tf_op jit(solution)/shard_map/ppermute | solution.py:43
  91.4 1.3 collective-permute-start.24
  92.7 1.3 collective-permute-start.17
  94.1 6.1 %collective-permute-start.22 = (f32[128,384]{1,0:T(8,128)S(1)}, f32[128,384]{1,0:T(8,128)S(1)}, u32[]{:S(2)}, u32[]{:S(2)}) collective-permute-start(f32[128,384]{1,0:T(8,128)S(1)} %get-tuple-element.100), channel_id=1, source_target_pairs={{0,8},{1,9},{2,10},{3,11},{4,12},{5,13},{6,14},{7,15},{16,24},{17,... | collective-permute-start | bytes 589832 | tf_op jit(solution)/shard_map/ppermute | solution.py:43
  100.2 1.3 collective-permute-start.20
  103.4 2.1 collective-permute-done.20
  106.2 12.0 %shard_map.95 = (f32[384,384]{1,0:T(8,128)}, f32[384,384]{1,0:T(8,128)}, f32[4,256,384]{2,1,0:T(8,128)}, f32[4,256,128]{2,1,0:T(8,128)}, f32[4,256,128]{2,1,0:T(8,128)}) custom-call(s32[2]{0:T(128)} %pad_add_fusion.at, bf16[4,256,384]{2,1,0:T(8,128)(2,1)} %get-tuple-element.37.xs, bf16[4,256,256]{2,1,0:T(8,128)(2,1)} %get-tuple-element.33.bc, ...), custom_call_target="tpu_custom_call" | custom-call | flops 2214592512 | bytes 10403848 | tf_op jit(solution)/shard_map/pallas_call | solution.py:236
  118.3 10.7 %shard_map.96 = (f32[384,640]{1,0:T(8,128)}, f32[384,640]{1,0:T(8,128)}, f32[256,768]{1,0:T(8,128)}, f32[128,768]{1,0:T(8,128)}, f32[128,768]{1,0:T(8,128)}, /*i...) custom-call(s32[2]{0:T(128)} %pad_add_fusion.at, ...), custom_call_target="tpu_custom_call" | custom-call | flops 2415919104 | bytes 12386312 | tf_op jit(solution)/shard_map/pallas_call | solution.py:236
  134.3 3.9 %collective-permute-start.50 = (f32[4,24,384]{2,1,0:T(8,128)}, f32[4,24,384]{2,1,0:T(8,128)S(1)}, u32[]{:S(2)}, u32[]{:S(2)}) collective-permute-start(f32[4,24,384]{2,1,0:T(8,128)} %get-tuple-element.63), channel_id=1, source_target_pairs={{0,64},{16,80},{32,96},{48,112},{64,0},{80,16},{96,32},{112,48},{1... | collective-permute-start | bytes 442376 | tf_op jit(solution)/shard_map/ppermute | solution.py:43
  138.9 2.0 collective-permute-done.25
  140.9 1.9 collective-permute-start.48
  142.8 2.0 add.345
  145.5 1.8 add.349
  147.3 2.5 %collective-permute-start.28 = (f32[128,768]{1,0:T(8,128)}, f32[128,768]{1,0:T(8,128)}, u32[]{:S(2)}, u32[]{:S(2)}) collective-permute-start(f32[128,768]{1,0:T(8,128)} %get-tuple-element.51), channel_id=1, source_target_pairs={{0,1},{1,2},{2,3},{3,0},{4,5},{5,6},{6,7},{7,4},{8,9},{9,10},{10,1... | collective-permute-start | bytes 1179656 | tf_op jit(solution)/shard_map/ppermute | solution.py:43
  150.9 1.3 add.351
  152.3 3.7 %collective-permute-start.34 = (f32[4,24,256]{2,1,0:T(8,128)S(1)}, f32[4,24,256]{2,1,0:T(8,128)S(1)}, u32[]{:S(2)}, u32[]{:S(2)}) collective-permute-start(f32[4,24,256]{2,1,0:T(8,128)S(1)} %get-tuple-element.69), channel_id=1, source_target_pairs={{0,64},{16,80},{32,96},{48,112},{64,0},{80,16},{96,32},{112,48},{1... | collective-permute-start | bytes 294920 | tf_op jit(solution)/shard_map/ppermute | solution.py:43
  158.1 1.3 collective-permute-done.34
  159.4 4.0 %collective-permute-start.40 = (f32[4,24,384]{2,1,0:T(8,128)S(1)}, f32[4,24,384]{2,1,0:T(8,128)S(1)}, u32[]{:S(2)}, u32[]{:S(2)}) collective-permute-start(f32[4,24,384]{2,1,0:T(8,128)S(1)} %get-tuple-element.66), channel_id=1, source_target_pairs={{0,8},{1,9},{2,10},{3,11},{4,12},{5,13},{6,14},{7,15},{8,0},{9,1},... | collective-permute-start | bytes 442376 | tf_op jit(solution)/shard_map/ppermute | solution.py:43
  163.4 1.9 collective-permute-start.39
  165.4 1.5 collective-permute-done.40
  167.0 4.0 %collective-permute-start.37 = (f32[24,256]{1,0:T(8,128)S(1)}, f32[24,256]{1,0:T(8,128)S(1)}, u32[]{:S(2)}, u32[]{:S(2)}) collective-permute-start(f32[24,256]{1,0:T(8,128)S(1)} %get-tuple-element.82), channel_id=1, source_target_pairs={{0,8},{1,9},{2,10},{3,11},{4,12},{5,13},{6,14},{7,15},{8,0},{9,1},... | collective-permute-start | bytes 73736 | tf_op jit(solution)/shard_map/ppermute | solution.py:43
  171.0 1.7 collective-permute-start.36
  173.1 3.1 %collective-permute-start.43 = (f32[24,384]{1,0:T(8,128)S(1)}, f32[24,384]{1,0:T(8,128)S(1)}, u32[]{:S(2)}, u32[]{:S(2)}) collective-permute-start(f32[24,384]{1,0:T(8,128)S(1)} %get-tuple-element.79), channel_id=1, source_target_pairs={{0,64},{16,80},{32,96},{48,112},{64,0},{80,16},{96,32},{112,48},{1... | collective-permute-start | bytes 110600 | tf_op jit(solution)/shard_map/ppermute | solution.py:43
  178.8 3.0 %collective-permute-start.53 = (f32[24,384]{1,0:T(8,128)S(1)}, f32[24,384]{1,0:T(8,128)}, u32[]{:S(2)}, u32[]{:S(2)}) collective-permute-start(f32[24,384]{1,0:T(8,128)S(1)} %get-tuple-element.76), channel_id=1, source_target_pairs={{0,8},{1,9},{2,10},{3,11},{4,12},{5,13},{6,14},{7,15},{8,0},{9,1},... | collective-permute-start | bytes 110600 | tf_op jit(solution)/shard_map/ppermute | solution.py:43
  181.8 1.1 collective-permute-start.52
  184.5 1.4 collective-permute-done.52
  185.8 1.4 collective-permute-start.45
  187.2 1.3 collective-permute-done.51
  189.5 2.1 multiply_reduce_fusion.1
  192.4 1.2 collective-permute-start.30
  198.6 5.5 %collective-permute-start.64 = (f32[12,384]{1,0:T(8,128)S(1)}, f32[12,384]{1,0:T(8,128)S(1)}, u32[]{:S(2)}, u32[]{:S(2)}) collective-permute-start(f32[12,384]{1,0:T(8,128)S(1)} %get-tuple-element.94), channel_id=1, source_target_pairs={{0,0},{1,32},{2,64},{3,96},{4,2},{5,34},{6,66},{7,98},{8,4},{9,36}... | collective-permute-start | bytes 55304 | tf_op jit(solution)/shard_map/ppermute | solution.py:371
  205.7 2.0 collective-permute-start.55
  207.7 1.8 collective-permute-start.56
  209.5 1.4 fusion.3
  211.5 3.6 %collective-permute-start.60 = (f32[8,128]{1,0:T(8,128)S(1)}, f32[8,128]{1,0:T(8,128)S(1)}, u32[]{:S(2)}, u32[]{:S(2)}) collective-permute-start(f32[8,128]{1,0:T(8,128)S(1)} %add_add_fusion.2), channel_id=1, source_target_pairs={{0,8},{1,9},{2,10},{3,11},{4,12},{5,13},{6,14},{7,15},{8,0},{9,1},... | collective-permute-start | bytes 12296 | tf_op jit(solution)/shard_map/ppermute | solution.py:43
  215.1 3.2 %collective-permute-start.59 = (f32[8,128]{1,0:T(8,128)S(1)}, f32[8,128]{1,0:T(8,128)S(1)}, u32[]{:S(2)}, u32[]{:S(2)}) collective-permute-start(f32[8,128]{1,0:T(8,128)S(1)} %add_add_fusion.2), channel_id=1, source_target_pairs={{0,12},{1,13},{2,14},{3,15},{4,0},{5,1},{6,2},{7,3},{8,4},{9,5},{1... | collective-permute-start | bytes 12296 | tf_op jit(solution)/shard_map/ppermute | solution.py:43
  219.9 1.4 collective-permute-start.63
  221.3 2.2 collective-permute-start.61
  223.5 1.6 collective-permute-done.63
  225.1 3.2 %collective-permute-done.62 = f32[8,128]{1,0:T(8,128)S(1)} collective-permute-done((f32[8,128]{1,0:T(8,128)S(1)}, f32[8,128]{1,0:T(8,128)S(1)}, u32[]{:S(2)}, u32[]{:S(2)}) %collective-permute-start.62) | collective-permute-done | bytes 4128 | tf_op jit(solution)/shard_map/ppermute | solution.py:43
  (187 shorter events, 37.8 us)
Async XLA Ops:
  1.9 16.5 %collective-permute-start = (f32[128,768]{1,0:T(8,128)S(1)}, f32[128,768]{1,0:T(8,128)}, u32[]{:S(2)}, u32[]{:S(2)}) collective-permute-start(f32[128,768]{1,0:T(8,128)S(1)} %get-tuple-element.74.a0), channel_id=1, source_target_pairs={{0,3},{1,0},{2,1},{3,2},{4,7},{5,4},{6,5},{7,6},{8,11},{9,8},{10,9... | collective-permute-start | bytes 1179656 | tf_op jit(solution)/shard_map/ppermute | solution.py:43
  2.8 18.9 %collective-permute-start.2 = (f32[128,768]{1,0:T(8,128)S(1)}, f32[128,768]{1,0:T(8,128)}, u32[]{:S(2)}, u32[]{:S(2)}) collective-permute-start(f32[128,768]{1,0:T(8,128)S(1)} %get-tuple-element.74.a0), channel_id=1, source_target_pairs={{0,1},{1,2},{2,3},{3,0},{4,5},{5,6},{6,7},{7,4},{8,9},{9,10},{10,1... | collective-permute-start | bytes 1179656 | tf_op jit(solution)/shard_map/ppermute | solution.py:43
  5.2 10.0 %collective-permute-start.6 = (f32[24,256]{1,0:T(8,128)}, f32[24,256]{1,0:T(8,128)}, u32[]{:S(2)}, u32[]{:S(2)}) collective-permute-start(f32[24,256]{1,0:T(8,128)} %bitcast.131), channel_id=1, source_target_pairs={{0,3},{1,0},{2,1},{3,2},{4,7},{5,4},{6,5},{7,6},{8,11},{9,8},{10,9... | collective-permute-start | bytes 73736 | tf_op jit(solution)/shard_map/ppermute | solution.py:43
  5.2 10.0 %collective-permute-start.7 = (f32[24,256]{1,0:T(8,128)}, f32[24,256]{1,0:T(8,128)}, u32[]{:S(2)}, u32[]{:S(2)}) collective-permute-start(f32[24,256]{1,0:T(8,128)} %bitcast.132), channel_id=1, source_target_pairs={{0,2},{1,3},{2,0},{3,1},{4,6},{5,7},{6,4},{7,5},{8,10},{9,11},{10,... | collective-permute-start | bytes 73736 | tf_op jit(solution)/shard_map/ppermute | solution.py:43
  6.7 11.8 %collective-permute-start.8 = (f32[24,256]{1,0:T(8,128)}, f32[24,256]{1,0:T(8,128)}, u32[]{:S(2)}, u32[]{:S(2)}) collective-permute-start(f32[24,256]{1,0:T(8,128)} %bitcast.133), channel_id=1, source_target_pairs={{0,1},{1,2},{2,3},{3,0},{4,5},{5,6},{6,7},{7,4},{8,9},{9,10},{10,1... | collective-permute-start | bytes 73736 | tf_op jit(solution)/shard_map/ppermute | solution.py:43
  15.2 13.4 %collective-permute-start.1 = (f32[128,768]{1,0:T(8,128)S(1)}, f32[128,768]{1,0:T(8,128)}, u32[]{:S(2)}, u32[]{:S(2)}) collective-permute-start(f32[128,768]{1,0:T(8,128)S(1)} %get-tuple-element.73.b0), channel_id=1, source_target_pairs={{0,3},{1,0},{2,1},{3,2},{4,7},{5,4},{6,5},{7,6},{8,11},{9,8},{10,9... | collective-permute-start | bytes 1179656 | tf_op jit(solution)/shard_map/ppermute | solution.py:43
  15.2 13.8 %collective-permute-start.5 = (f32[128,768]{1,0:T(8,128)S(1)}, f32[128,768]{1,0:T(8,128)}, u32[]{:S(2)}, u32[]{:S(2)}) collective-permute-start(f32[128,768]{1,0:T(8,128)S(1)} %get-tuple-element.73.b0), channel_id=1, source_target_pairs={{0,1},{1,2},{2,3},{3,0},{4,5},{5,6},{6,7},{7,4},{8,9},{9,10},{10,1... | collective-permute-start | bytes 1179656 | tf_op jit(solution)/shard_map/ppermute | solution.py:43
  18.4 18.5 %collective-permute-start.10 = (f32[128,768]{1,0:T(8,128)S(1)}, f32[128,768]{1,0:T(8,128)}, u32[]{:S(2)}, u32[]{:S(2)}) collective-permute-start(f32[128,768]{1,0:T(8,128)S(1)} %get-tuple-element.71.b0), channel_id=1, source_target_pairs={{0,3},{1,0},{2,1},{3,2},{4,7},{5,4},{6,5},{7,6},{8,11},{9,8},{10,9... | collective-permute-start | bytes 1179656 | tf_op jit(solution)/shard_map/ppermute | solution.py:43
  18.4 18.5 %collective-permute-start.11 = (f32[128,768]{1,0:T(8,128)}, f32[128,768]{1,0:T(8,128)}, u32[]{:S(2)}, u32[]{:S(2)}) collective-permute-start(f32[128,768]{1,0:T(8,128)} %get-tuple-element.72.a0), channel_id=1, source_target_pairs={{0,1},{1,2},{2,3},{3,0},{4,5},{5,6},{6,7},{7,4},{8,9},{9,10},{10,1... | collective-permute-start | bytes 1179656 | tf_op jit(solution)/shard_map/ppermute | solution.py:43
  21.7 23.3 %collective-permute-start.3 = (f32[128,768]{1,0:T(8,128)}, f32[128,768]{1,0:T(8,128)}, u32[]{:S(2)}, u32[]{:S(2)}) collective-permute-start(f32[128,768]{1,0:T(8,128)} %collective-permute-done.2.a3), channel_id=1, source_target_pairs={{0,1},{1,2},{2,3},{3,0},{4,5},{5,6},{6,7},{7,4},{8,9},{9,10},{10,1... | collective-permute-start | bytes 1179656 | tf_op jit(solution)/shard_map/ppermute | solution.py:43
  28.6 36.4 %collective-permute-start.9 = (f32[128,768]{1,0:T(8,128)}, f32[128,768]{1,0:T(8,128)S(1)}, u32[]{:S(2)}, u32[]{:S(2)}) collective-permute-start(f32[128,768]{1,0:T(8,128)} %get-tuple-element.72.a0), channel_id=1, source_target_pairs={{0,3},{1,0},{2,1},{3,2},{4,7},{5,4},{6,5},{7,6},{8,11},{9,8},{10,9... | collective-permute-start | bytes 1179656 | tf_op jit(solution)/shard_map/ppermute | solution.py:43
  29.0 36.0 %collective-permute-start.14 = (f32[128,768]{1,0:T(8,128)S(1)}, f32[128,768]{1,0:T(8,128)S(1)}, u32[]{:S(2)}, u32[]{:S(2)}) collective-permute-start(f32[128,768]{1,0:T(8,128)S(1)} %get-tuple-element.71.b0), channel_id=1, source_target_pairs={{0,1},{1,2},{2,3},{3,0},{4,5},{5,6},{6,7},{7,4},{8,9},{9,10},{10,1... | collective-permute-start | bytes 1179656 | tf_op jit(solution)/shard_map/ppermute | solution.py:43
  37.0 16.7 %collective-permute-start.4 = (f32[128,768]{1,0:T(8,128)}, f32[128,768]{1,0:T(8,128)S(1)}, u32[]{:S(2)}, u32[]{:S(2)}) collective-permute-start(f32[128,768]{1,0:T(8,128)} %collective-permute-done.1.b1), channel_id=1, source_target_pairs={{0,3},{1,0},{2,1},{3,2},{4,7},{5,4},{6,5},{7,6},{8,11},{9,8},{10,9... | collective-permute-start | bytes 1179656 | tf_op jit(solution)/shard_map/ppermute | solution.py:43
  37.0 28.0 %collective-permute-start.12 = (f32[128,768]{1,0:T(8,128)}, f32[128,768]{1,0:T(8,128)S(1)}, u32[]{:S(2)}, u32[]{:S(2)}) collective-permute-start(f32[128,768]{1,0:T(8,128)} %collective-permute-done.11.a3), channel_id=1, source_target_pairs={{0,1},{1,2},{2,3},{3,0},{4,5},{5,6},{6,7},{7,4},{8,9},{9,10},{10,1... | collective-permute-start | bytes 1179656 | tf_op jit(solution)/shard_map/ppermute | solution.py:43
  45.0 20.1 %collective-permute-start.13 = (f32[128,768]{1,0:T(8,128)}, f32[128,768]{1,0:T(8,128)S(1)}, u32[]{:S(2)}, u32[]{:S(2)}) collective-permute-start(f32[128,768]{1,0:T(8,128)} %collective-permute-done.10.b1), channel_id=1, source_target_pairs={{0,3},{1,0},{2,1},{3,2},{4,7},{5,4},{6,5},{7,6},{8,11},{9,8},{10,9... | collective-permute-start | bytes 1179656 | tf_op jit(solution)/shard_map/ppermute | solution.py:43
  63.7 24.1 %collective-permute-start.23 = (f32[128,384]{1,0:T(8,128)}, f32[128,384]{1,0:T(8,128)S(1)}, u32[]{:S(2)}, u32[]{:S(2)}) collective-permute-start(f32[128,384]{1,0:T(8,128)} %get-tuple-element.43), channel_id=1, source_target_pairs={{4,0},{5,1},{6,2},{7,3},{8,4},{9,5},{10,6},{11,7},{12,8},{13,9},{1... | collective-permute-start | bytes 589832 | tf_op jit(solution)/shard_map/ppermute | solution.py:43
  74.5 13.3 %collective-permute-start.18 = (f32[128,384]{1,0:T(8,128)}, f32[128,384]{1,0:T(8,128)S(1)}, u32[]{:S(2)}, u32[]{:S(2)}) collective-permute-start(f32[128,384]{1,0:T(8,128)} %get-tuple-element.36), channel_id=1, source_target_pairs={{0,4},{1,5},{2,6},{3,7},{4,8},{5,9},{6,10},{7,11},{8,12},{9,13},{1... | collective-permute-start | bytes 589832 | tf_op jit(solution)/shard_map/ppermute | solution.py:43
  79.0 8.7 %collective-permute-start.21 = (f32[128,384]{1,0:T(8,128)S(1)}, f32[128,384]{1,0:T(8,128)S(1)}, u32[]{:S(2)}, u32[]{:S(2)}) collective-permute-start(f32[128,384]{1,0:T(8,128)S(1)} %copy-done.14), channel_id=1, source_target_pairs={{0,4},{1,5},{2,6},{3,7},{4,8},{5,9},{6,10},{7,11},{8,12},{9,13},{1... | collective-permute-start | bytes 589832 | tf_op jit(solution)/shard_map/ppermute | solution.py:43
  82.5 7.8 %collective-permute-start.15 = (f32[128,384]{1,0:T(8,128)}, f32[128,384]{1,0:T(8,128)S(1)}, u32[]{:S(2)}, u32[]{:S(2)}) collective-permute-start(f32[128,384]{1,0:T(8,128)} %get-tuple-element.35), channel_id=1, source_target_pairs={{4,0},{5,1},{6,2},{7,3},{8,4},{9,5},{10,6},{11,7},{12,8},{13,9},{1... | collective-permute-start | bytes 589832 | tf_op jit(solution)/shard_map/ppermute | solution.py:43
  84.7 9.3 %collective-permute-start.16 = (f32[8,384]{1,0:T(8,128)S(1)}, f32[8,384]{1,0:T(8,128)S(1)}, u32[]{:S(2)}, u32[]{:S(2)}) collective-permute-start(f32[8,384]{1,0:T(8,128)S(1)} %broadcast_in_dim.25), channel_id=1, source_target_pairs={{0,12},{1,13},{2,14},{3,15},{4,0},{5,1},{6,2},{7,3},{8,4},{9,5},{1... | collective-permute-start | bytes 36872 | tf_op jit(solution)/shard_map/ppermute | solution.py:43
  87.7 6.3 %collective-permute-start.19 = (f32[8,384]{1,0:T(8,128)S(1)}, f32[8,384]{1,0:T(8,128)S(1)}, u32[]{:S(2)}, u32[]{:S(2)}) collective-permute-start(f32[8,384]{1,0:T(8,128)S(1)} %broadcast_in_dim.25), channel_id=1, source_target_pairs={{0,4},{1,5},{2,6},{3,7},{4,8},{5,9},{6,10},{7,11},{8,12},{9,13},{1... | collective-permute-start | bytes 36872 | tf_op jit(solution)/shard_map/ppermute | solution.py:43
  91.4 10.1 %collective-permute-start.24 = (f32[128,384]{1,0:T(8,128)S(1)}, f32[128,384]{1,0:T(8,128)S(1)}, u32[]{:S(2)}, u32[]{:S(2)}) collective-permute-start(f32[128,384]{1,0:T(8,128)S(1)} %get-tuple-element.98), channel_id=1, source_target_pairs={{8,0},{9,1},{10,2},{11,3},{12,4},{13,5},{14,6},{15,7},{24,16},{25,... | collective-permute-start | bytes 589832 | tf_op jit(solution)/shard_map/ppermute | solution.py:43
  92.7 9.9 %collective-permute-start.17 = (f32[128,384]{1,0:T(8,128)S(1)}, f32[128,384]{1,0:T(8,128)S(1)}, u32[]{:S(2)}, u32[]{:S(2)}) collective-permute-start(f32[128,384]{1,0:T(8,128)S(1)} %get-tuple-element.101), channel_id=1, source_target_pairs={{8,0},{9,1},{10,2},{11,3},{12,4},{13,5},{14,6},{15,7},{24,16},{25,... | collective-permute-start | bytes 589832 | tf_op jit(solution)/shard_map/ppermute | solution.py:43
  94.1 9.3 %collective-permute-start.22 = (f32[128,384]{1,0:T(8,128)S(1)}, f32[128,384]{1,0:T(8,128)S(1)}, u32[]{:S(2)}, u32[]{:S(2)}) collective-permute-start(f32[128,384]{1,0:T(8,128)S(1)} %get-tuple-element.100), channel_id=1, source_target_pairs={{0,8},{1,9},{2,10},{3,11},{4,12},{5,13},{6,14},{7,15},{16,24},{17,... | collective-permute-start | bytes 589832 | tf_op jit(solution)/shard_map/ppermute | solution.py:43
  100.2 5.3 %collective-permute-start.20 = (f32[128,384]{1,0:T(8,128)S(1)}, f32[128,384]{1,0:T(8,128)S(1)}, u32[]{:S(2)}, u32[]{:S(2)}) collective-permute-start(f32[128,384]{1,0:T(8,128)S(1)} %get-tuple-element.99), channel_id=1, source_target_pairs={{0,8},{1,9},{2,10},{3,11},{4,12},{5,13},{6,14},{7,15},{16,24},{17,... | collective-permute-start | bytes 589832 | tf_op jit(solution)/shard_map/ppermute | solution.py:43
  118.3 13.2 %collective-permute-start.47 = (f32[384,384]{1,0:T(8,128)}, f32[384,384]{1,0:T(8,128)S(1)}, u32[]{:S(2)}, u32[]{:S(2)}) collective-permute-start(f32[384,384]{1,0:T(8,128)} %get-tuple-element.57), channel_id=1, source_target_pairs={{0,16},{16,0},{32,48},{48,32},{64,80},{80,64},{96,112},{112,96},{1... | collective-permute-start | bytes 1769480 | tf_op jit(solution)/shard_map/ppermute | solution.py:43
  129.0 21.9 %collective-permute-start.31 = (f32[384,640]{1,0:T(8,128)}, f32[384,640]{1,0:T(8,128)}, u32[]{:S(2)}, u32[]{:S(2)}) collective-permute-start(f32[384,640]{1,0:T(8,128)} %get-tuple-element.55), channel_id=1, source_target_pairs={{0,16},{16,0},{32,48},{48,32},{64,80},{80,64},{96,112},{112,96},{1... | collective-permute-start | bytes 2949128 | tf_op jit(solution)/shard_map/ppermute | solution.py:43
  129.5 11.4 %collective-permute-start.25 = (f32[128,768]{1,0:T(8,128)}, f32[128,768]{1,0:T(8,128)}, u32[]{:S(2)}, u32[]{:S(2)}) collective-permute-start(f32[128,768]{1,0:T(8,128)} %get-tuple-element.49), channel_id=1, source_target_pairs={{0,1},{1,2},{2,3},{3,0},{4,5},{5,6},{6,7},{7,4},{8,9},{9,10},{10,1... | collective-permute-start | bytes 1179656 | tf_op jit(solution)/shard_map/ppermute | solution.py:43
  130.5 14.3 %collective-permute-start.29 = (f32[128,768]{1,0:T(8,128)}, f32[128,768]{1,0:T(8,128)}, u32[]{:S(2)}, u32[]{:S(2)}) collective-permute-start(f32[128,768]{1,0:T(8,128)} %get-tuple-element.53), channel_id=1, source_target_pairs={{0,3},{1,0},{2,1},{3,2},{4,7},{5,4},{6,5},{7,6},{8,11},{9,8},{10,9... | collective-permute-start | bytes 1179656 | tf_op jit(solution)/shard_map/ppermute | solution.py:43
  134.3 13.0 %collective-permute-start.50 = (f32[4,24,384]{2,1,0:T(8,128)}, f32[4,24,384]{2,1,0:T(8,128)S(1)}, u32[]{:S(2)}, u32[]{:S(2)}) collective-permute-start(f32[4,24,384]{2,1,0:T(8,128)} %get-tuple-element.63), channel_id=1, source_target_pairs={{0,64},{16,80},{32,96},{48,112},{64,0},{80,16},{96,32},{112,48},{1... | collective-permute-start | bytes 442376 | tf_op jit(solution)/shard_map/ppermute | solution.py:43
  138.2 11.7 %collective-permute-start.49 = (f32[4,24,384]{2,1,0:T(8,128)}, f32[4,24,384]{2,1,0:T(8,128)}, u32[]{:S(2)}, u32[]{:S(2)}) collective-permute-start(f32[4,24,384]{2,1,0:T(8,128)} %get-tuple-element.64), channel_id=1, source_target_pairs={{0,96},{16,112},{32,0},{48,16},{64,32},{80,48},{96,64},{112,80},{1... | collective-permute-start | bytes 442376 | tf_op jit(solution)/shard_map/ppermute | solution.py:43
  140.9 8.9 %collective-permute-start.48 = (f32[4,24,384]{2,1,0:T(8,128)}, f32[4,24,384]{2,1,0:T(8,128)}, u32[]{:S(2)}, u32[]{:S(2)}) collective-permute-start(f32[4,24,384]{2,1,0:T(8,128)} %get-tuple-element.62), channel_id=1, source_target_pairs={{0,32},{16,48},{32,64},{48,80},{64,96},{80,112},{96,0},{112,16},{1... | collective-permute-start | bytes 442376 | tf_op jit(solution)/shard_map/ppermute | solution.py:43
  144.8 59.2 %collective-permute-start.27 = (f32[128,768]{1,0:T(8,128)}, f32[128,768]{1,0:T(8,128)}, u32[]{:S(2)}, u32[]{:S(2)}) collective-permute-start(f32[128,768]{1,0:T(8,128)} %get-tuple-element.50), channel_id=1, source_target_pairs={{0,3},{1,0},{2,1},{3,2},{4,7},{5,4},{6,5},{7,6},{8,11},{9,8},{10,9... | collective-permute-start | bytes 1179656 | tf_op jit(solution)/shard_map/ppermute | solution.py:43
  147.3 57.6 %collective-permute-start.28 = (f32[128,768]{1,0:T(8,128)}, f32[128,768]{1,0:T(8,128)}, u32[]{:S(2)}, u32[]{:S(2)}) collective-permute-start(f32[128,768]{1,0:T(8,128)} %get-tuple-element.51), channel_id=1, source_target_pairs={{0,1},{1,2},{2,3},{3,0},{4,5},{5,6},{6,7},{7,4},{8,9},{9,10},{10,1... | collective-permute-start | bytes 1179656 | tf_op jit(solution)/shard_map/ppermute | solution.py:43
  152.3 7.0 %collective-permute-start.34 = (f32[4,24,256]{2,1,0:T(8,128)S(1)}, f32[4,24,256]{2,1,0:T(8,128)S(1)}, u32[]{:S(2)}, u32[]{:S(2)}) collective-permute-start(f32[4,24,256]{2,1,0:T(8,128)S(1)} %get-tuple-element.69), channel_id=1, source_target_pairs={{0,64},{16,80},{32,96},{48,112},{64,0},{80,16},{96,32},{112,48},{1... | collective-permute-start | bytes 294920 | tf_op jit(solution)/shard_map/ppermute | solution.py:43
  156.0 7.4 %collective-permute-start.33 = (f32[4,24,256]{2,1,0:T(8,128)S(1)}, f32[4,24,256]{2,1,0:T(8,128)S(1)}, u32[]{:S(2)}, u32[]{:S(2)}) collective-permute-start(f32[4,24,256]{2,1,0:T(8,128)S(1)} %get-tuple-element.70), channel_id=1, source_target_pairs={{0,96},{16,112},{32,0},{48,16},{64,32},{80,48},{96,64},{112,80},{1... | collective-permute-start | bytes 294920 | tf_op jit(solution)/shard_map/ppermute | solution.py:43
  157.0 8.3 %collective-permute-start.32 = (f32[4,24,256]{2,1,0:T(8,128)S(1)}, f32[4,24,256]{2,1,0:T(8,128)S(1)}, u32[]{:S(2)}, u32[]{:S(2)}) collective-permute-start(f32[4,24,256]{2,1,0:T(8,128)S(1)} %get-tuple-element.68), channel_id=1, source_target_pairs={{0,32},{16,48},{32,64},{48,80},{64,96},{80,112},{96,0},{112,16},{1... | collective-permute-start | bytes 294920 | tf_op jit(solution)/shard_map/ppermute | solution.py:43
  159.4 7.6 %collective-permute-start.40 = (f32[4,24,384]{2,1,0:T(8,128)S(1)}, f32[4,24,384]{2,1,0:T(8,128)S(1)}, u32[]{:S(2)}, u32[]{:S(2)}) collective-permute-start(f32[4,24,384]{2,1,0:T(8,128)S(1)} %get-tuple-element.66), channel_id=1, source_target_pairs={{0,8},{1,9},{2,10},{3,11},{4,12},{5,13},{6,14},{7,15},{8,0},{9,1},... | collective-permute-start | bytes 442376 | tf_op jit(solution)/shard_map/ppermute | solution.py:43
  163.4 7.6 %collective-permute-start.39 = (f32[4,24,384]{2,1,0:T(8,128)S(1)}, f32[4,24,384]{2,1,0:T(8,128)S(1)}, u32[]{:S(2)}, u32[]{:S(2)}) collective-permute-start(f32[4,24,384]{2,1,0:T(8,128)S(1)} %get-tuple-element.67), channel_id=1, source_target_pairs={{0,12},{1,13},{2,14},{3,15},{4,0},{5,1},{6,2},{7,3},{8,4},{9,5},{1... | collective-permute-start | bytes 442376 | tf_op jit(solution)/shard_map/ppermute | solution.py:43
  165.3 7.3 %collective-permute-start.38 = (f32[4,24,384]{2,1,0:T(8,128)S(1)}, f32[4,24,384]{2,1,0:T(8,128)S(1)}, u32[]{:S(2)}, u32[]{:S(2)}) collective-permute-start(f32[4,24,384]{2,1,0:T(8,128)S(1)} %get-tuple-element.65), channel_id=1, source_target_pairs={{0,4},{1,5},{2,6},{3,7},{4,8},{5,9},{6,10},{7,11},{8,12},{9,13},{1... | collective-permute-start | bytes 442376 | tf_op jit(solution)/shard_map/ppermute | solution.py:43
  167.0 6.1 %collective-permute-start.37 = (f32[24,256]{1,0:T(8,128)S(1)}, f32[24,256]{1,0:T(8,128)S(1)}, u32[]{:S(2)}, u32[]{:S(2)}) collective-permute-start(f32[24,256]{1,0:T(8,128)S(1)} %get-tuple-element.82), channel_id=1, source_target_pairs={{0,8},{1,9},{2,10},{3,11},{4,12},{5,13},{6,14},{7,15},{8,0},{9,1},... | collective-permute-start | bytes 73736 | tf_op jit(solution)/shard_map/ppermute | solution.py:43
  171.0 5.2 %collective-permute-start.36 = (f32[24,256]{1,0:T(8,128)S(1)}, f32[24,256]{1,0:T(8,128)S(1)}, u32[]{:S(2)}, u32[]{:S(2)}) collective-permute-start(f32[24,256]{1,0:T(8,128)S(1)} %get-tuple-element.83), channel_id=1, source_target_pairs={{0,12},{1,13},{2,14},{3,15},{4,0},{5,1},{6,2},{7,3},{8,4},{9,5},{1... | collective-permute-start | bytes 73736 | tf_op jit(solution)/shard_map/ppermute | solution.py:43
  172.6 5.4 %collective-permute-start.35 = (f32[24,256]{1,0:T(8,128)S(1)}, f32[24,256]{1,0:T(8,128)S(1)}, u32[]{:S(2)}, u32[]{:S(2)}) collective-permute-start(f32[24,256]{1,0:T(8,128)S(1)} %get-tuple-element.81), channel_id=1, source_target_pairs={{0,4},{1,5},{2,6},{3,7},{4,8},{5,9},{6,10},{7,11},{8,12},{9,13},{1... | collective-permute-start | bytes 73736 | tf_op jit(solution)/shard_map/ppermute | solution.py:43
  173.1 5.7 %collective-permute-start.43 = (f32[24,384]{1,0:T(8,128)S(1)}, f32[24,384]{1,0:T(8,128)S(1)}, u32[]{:S(2)}, u32[]{:S(2)}) collective-permute-start(f32[24,384]{1,0:T(8,128)S(1)} %get-tuple-element.79), channel_id=1, source_target_pairs={{0,64},{16,80},{32,96},{48,112},{64,0},{80,16},{96,32},{112,48},{1... | collective-permute-start | bytes 110600 | tf_op jit(solution)/shard_map/ppermute | solution.py:43
  176.2 5.6 %collective-permute-start.42 = (f32[24,384]{1,0:T(8,128)S(1)}, f32[24,384]{1,0:T(8,128)S(1)}, u32[]{:S(2)}, u32[]{:S(2)}) collective-permute-start(f32[24,384]{1,0:T(8,128)S(1)} %get-tuple-element.80), channel_id=1, source_target_pairs={{0,96},{16,112},{32,0},{48,16},{64,32},{80,48},{96,64},{112,80},{1... | collective-permute-start | bytes 110600 | tf_op jit(solution)/shard_map/ppermute | solution.py:43
  178.1 5.2 %collective-permute-start.41 = (f32[24,384]{1,0:T(8,128)S(1)}, f32[24,384]{1,0:T(8,128)S(1)}, u32[]{:S(2)}, u32[]{:S(2)}) collective-permute-start(f32[24,384]{1,0:T(8,128)S(1)} %get-tuple-element.78), channel_id=1, source_target_pairs={{0,32},{16,48},{32,64},{48,80},{64,96},{80,112},{96,0},{112,16},{1... | collective-permute-start | bytes 110600 | tf_op jit(solution)/shard_map/ppermute | solution.py:43
  178.8 5.6 %collective-permute-start.53 = (f32[24,384]{1,0:T(8,128)S(1)}, f32[24,384]{1,0:T(8,128)}, u32[]{:S(2)}, u32[]{:S(2)}) collective-permute-start(f32[24,384]{1,0:T(8,128)S(1)} %get-tuple-element.76), channel_id=1, source_target_pairs={{0,8},{1,9},{2,10},{3,11},{4,12},{5,13},{6,14},{7,15},{8,0},{9,1},... | collective-permute-start | bytes 110600 | tf_op jit(solution)/shard_map/ppermute | solution.py:43
  181.8 4.1 %collective-permute-start.52 = (f32[24,384]{1,0:T(8,128)S(1)}, f32[24,384]{1,0:T(8,128)}, u32[]{:S(2)}, u32[]{:S(2)}) collective-permute-start(f32[24,384]{1,0:T(8,128)S(1)} %get-tuple-element.77), channel_id=1, source_target_pairs={{0,12},{1,13},{2,14},{3,15},{4,0},{5,1},{6,2},{7,3},{8,4},{9,5},{1... | collective-permute-start | bytes 110600 | tf_op jit(solution)/shard_map/ppermute | solution.py:43
  183.2 5.3 %collective-permute-start.51 = (f32[24,384]{1,0:T(8,128)S(1)}, f32[24,384]{1,0:T(8,128)}, u32[]{:S(2)}, u32[]{:S(2)}) collective-permute-start(f32[24,384]{1,0:T(8,128)S(1)} %get-tuple-element.75), channel_id=1, source_target_pairs={{0,4},{1,5},{2,6},{3,7},{4,8},{5,9},{6,10},{7,11},{8,12},{9,13},{1... | collective-permute-start | bytes 110600 | tf_op jit(solution)/shard_map/ppermute | solution.py:43
  184.5 7.1 %collective-permute-start.46 = (f32[6,640]{1,0:T(8,128)S(1)}, f32[6,640]{1,0:T(8,128)S(1)}, u32[]{:S(2)}, u32[]{:S(2)}) collective-permute-start(f32[6,640]{1,0:T(8,128)S(1)} %get-tuple-element.89), channel_id=1, source_target_pairs={{0,3},{1,0},{2,1},{3,2},{4,7},{5,4},{6,5},{7,6},{8,11},{9,8},{10,9... | collective-permute-start | bytes 46088 | tf_op jit(solution)/shard_map/ppermute | solution.py:43
  185.8 6.5 %collective-permute-start.45 = (f32[6,640]{1,0:T(8,128)S(1)}, f32[6,640]{1,0:T(8,128)S(1)}, u32[]{:S(2)}, u32[]{:S(2)}) collective-permute-start(f32[6,640]{1,0:T(8,128)S(1)} %get-tuple-element.90), channel_id=1, source_target_pairs={{0,2},{1,3},{2,0},{3,1},{4,6},{5,7},{6,4},{7,5},{8,10},{9,11},{10,... | collective-permute-start | bytes 46088 | tf_op jit(solution)/shard_map/ppermute | solution.py:43
  188.5 5.1 %collective-permute-start.44 = (f32[6,640]{1,0:T(8,128)S(1)}, f32[6,640]{1,0:T(8,128)S(1)}, u32[]{:S(2)}, u32[]{:S(2)}) collective-permute-start(f32[6,640]{1,0:T(8,128)S(1)} %get-tuple-element.91), channel_id=1, source_target_pairs={{0,1},{1,2},{2,3},{3,0},{4,5},{5,6},{6,7},{7,4},{8,9},{9,10},{10,1... | collective-permute-start | bytes 46088 | tf_op jit(solution)/shard_map/ppermute | solution.py:43
  191.6 14.1 %collective-permute-start.26 = (f32[128,768]{1,0:T(8,128)}, f32[128,768]{1,0:T(8,128)S(1)}, u32[]{:S(2)}, u32[]{:S(2)}) collective-permute-start(f32[128,768]{1,0:T(8,128)} %add.345), channel_id=1, source_target_pairs={{0,1},{1,2},{2,3},{3,0},{4,5},{5,6},{6,7},{7,4},{8,9},{9,10},{10,1... | collective-permute-start | bytes 1179656 | tf_op jit(solution)/shard_map/ppermute | solution.py:43
  192.4 15.3 %collective-permute-start.30 = (f32[128,768]{1,0:T(8,128)}, f32[128,768]{1,0:T(8,128)}, u32[]{:S(2)}, u32[]{:S(2)}) collective-permute-start(f32[128,768]{1,0:T(8,128)} %add.349), channel_id=1, source_target_pairs={{0,3},{1,0},{2,1},{3,2},{4,7},{5,4},{6,5},{7,6},{8,11},{9,8},{10,9... | collective-permute-start | bytes 1179656 | tf_op jit(solution)/shard_map/ppermute | solution.py:43
  198.6 24.9 %collective-permute-start.64 = (f32[12,384]{1,0:T(8,128)S(1)}, f32[12,384]{1,0:T(8,128)S(1)}, u32[]{:S(2)}, u32[]{:S(2)}) collective-permute-start(f32[12,384]{1,0:T(8,128)S(1)} %get-tuple-element.94), channel_id=1, source_target_pairs={{0,0},{1,32},{2,64},{3,96},{4,2},{5,34},{6,66},{7,98},{8,4},{9,36}... | collective-permute-start | bytes 55304 | tf_op jit(solution)/shard_map/ppermute | solution.py:371
  204.1 19.5 %collective-permute-start.65 = (f32[12,384]{1,0:T(8,128)S(1)}, f32[12,384]{1,0:T(8,128)S(1)}, u32[]{:S(2)}, u32[]{:S(2)}) collective-permute-start(f32[12,384]{1,0:T(8,128)S(1)} %get-tuple-element.95), channel_id=1, source_target_pairs={{0,1},{1,33},{2,65},{3,97},{4,3},{5,35},{6,67},{7,99},{8,5},{9,37}... | collective-permute-start | bytes 55304 | tf_op jit(solution)/shard_map/ppermute | solution.py:372
  204.9 6.0 %collective-permute-start.57 = (f32[8,128]{1,0:T(8,128)S(1)}, f32[8,128]{1,0:T(8,128)S(1)}, u32[]{:S(2)}, u32[]{:S(2)}) collective-permute-start(f32[8,128]{1,0:T(8,128)S(1)} %broadcast_add_fusion), channel_id=1, source_target_pairs={{0,64},{16,80},{32,96},{48,112},{64,0},{80,16},{96,32},{112,48},{1... | collective-permute-start | bytes 12296 | tf_op jit(solution)/shard_map/ppermute | solution.py:43
  205.7 5.3 %collective-permute-start.55 = (f32[8,128]{1,0:T(8,128)S(1)}, f32[8,128]{1,0:T(8,128)S(1)}, u32[]{:S(2)}, u32[]{:S(2)}) collective-permute-start(f32[8,128]{1,0:T(8,128)S(1)} %broadcast_add_fusion), channel_id=1, source_target_pairs={{0,32},{16,48},{32,64},{48,80},{64,96},{80,112},{96,0},{112,16},{1... | collective-permute-start | bytes 12296 | tf_op jit(solution)/shard_map/ppermute | solution.py:43
  207.7 3.8 %collective-permute-start.56 = (f32[8,128]{1,0:T(8,128)S(1)}, f32[8,128]{1,0:T(8,128)S(1)}, u32[]{:S(2)}, u32[]{:S(2)}) collective-permute-start(f32[8,128]{1,0:T(8,128)S(1)} %broadcast_add_fusion), channel_id=1, source_target_pairs={{0,96},{16,112},{32,0},{48,16},{64,32},{80,48},{96,64},{112,80},{1... | collective-permute-start | bytes 12296 | tf_op jit(solution)/shard_map/ppermute | solution.py:43
  211.5 7.6 %collective-permute-start.60 = (f32[8,128]{1,0:T(8,128)S(1)}, f32[8,128]{1,0:T(8,128)S(1)}, u32[]{:S(2)}, u32[]{:S(2)}) collective-permute-start(f32[8,128]{1,0:T(8,128)S(1)} %add_add_fusion.2), channel_id=1, source_target_pairs={{0,8},{1,9},{2,10},{3,11},{4,12},{5,13},{6,14},{7,15},{8,0},{9,1},... | collective-permute-start | bytes 12296 | tf_op jit(solution)/shard_map/ppermute | solution.py:43
  215.1 4.8 %collective-permute-start.58 = (f32[8,128]{1,0:T(8,128)S(1)}, f32[8,128]{1,0:T(8,128)S(1)}, u32[]{:S(2)}, u32[]{:S(2)}) collective-permute-start(f32[8,128]{1,0:T(8,128)S(1)} %add_add_fusion.2), channel_id=1, source_target_pairs={{0,4},{1,5},{2,6},{3,7},{4,8},{5,9},{6,10},{7,11},{8,12},{9,13},{1... | collective-permute-start | bytes 12296 | tf_op jit(solution)/shard_map/ppermute | solution.py:43
  215.1 4.8 %collective-permute-start.59 = (f32[8,128]{1,0:T(8,128)S(1)}, f32[8,128]{1,0:T(8,128)S(1)}, u32[]{:S(2)}, u32[]{:S(2)}) collective-permute-start(f32[8,128]{1,0:T(8,128)S(1)} %add_add_fusion.2), channel_id=1, source_target_pairs={{0,12},{1,13},{2,14},{3,15},{4,0},{5,1},{6,2},{7,3},{8,4},{9,5},{1... | collective-permute-start | bytes 12296 | tf_op jit(solution)/shard_map/ppermute | solution.py:43
  219.9 5.2 %collective-permute-start.63 = (f32[8,128]{1,0:T(8,128)S(1)}, f32[8,128]{1,0:T(8,128)S(1)}, u32[]{:S(2)}, u32[]{:S(2)}) collective-permute-start(f32[8,128]{1,0:T(8,128)S(1)} %add_add_fusion.1), channel_id=1, source_target_pairs={{0,2},{1,3},{2,0},{3,1},{4,6},{5,7},{6,4},{7,5},{8,10},{9,11},{10,... | collective-permute-start | bytes 12296 | tf_op jit(solution)/shard_map/ppermute | solution.py:43
  223.5 4.8 %collective-permute-start.62 = (f32[8,128]{1,0:T(8,128)S(1)}, f32[8,128]{1,0:T(8,128)S(1)}, u32[]{:S(2)}, u32[]{:S(2)}) collective-permute-start(f32[8,128]{1,0:T(8,128)S(1)} %add_add_fusion.1), channel_id=1, source_target_pairs={{0,3},{1,0},{2,1},{3,2},{4,7},{5,4},{6,5},{7,6},{8,11},{9,8},{10,9... | collective-permute-start | bytes 12296 | tf_op jit(solution)/shard_map/ppermute | solution.py:43
  (28 other events, 350.9 us)

commit v2 on v1

v2 whole, which is shorter than its diff:
```python
import functools

import jax
import jax.numpy as jnp
from jax import lax
from jax.experimental import pallas as pl
from jax.experimental.pallas import tpu as pltpu
from jax.sharding import PartitionSpec as P

F32 = jnp.float32
BF16 = jnp.bfloat16
NX = 4
NY = 4
NZ = 4
SEG = 256
HALF = SEG // 2
DM = 768
NS = 128
NH = 6
HD = 64
HC = NH * HD
ROWS = DM // 2
WIDE = HC + 2 * NS
TALL = NS + 8


def shift(axis, step, wrap=True):
    if axis == "c":
        return "rec", [(r, r ^ 1) for r in range(2 * NZ)]
    count, stride, total, name = {
        "x": (NX, 1, NX * NY, "seq"),
        "y": (NY, NX, NX * NY, "seq"),
        "z": (NZ, 2, 2 * NZ, "rec"),
    }[axis]
    pairs = []
    for i in range(total):
        at = (i // stride) % count
        to = at + step
        if not wrap and not 0 <= to < count:
            continue
        pairs.append((i, i + (to % count - at) * stride))
    return name, pairs


def move(value, axis, step, wrap=True):
    name, pairs = shift(axis, step, wrap)
    return lax.ppermute(value, name, pairs)


def dot(a, b, ca, cb):
    return lax.dot_general(a, b, (((ca,), (cb,)), ((), ())), preferred_element_type=F32)


def place(p, x):
    return lax.rem(p - x + NX, NX)


def vm(n):
    return [pl.BlockSpec(memory_space=pltpu.VMEM)] * n


SMEM = pl.BlockSpec(memory_space=pltpu.SMEM)
PARAMS = pltpu.CompilerParams(vmem_limit_bytes=30 * 2**20)


def send_rows(up, down, log, y, s_p, s_m, s_2):
    s_p[:NS] = jnp.where(y == NY - 1, down, up)
    s_m[:NS] = jnp.where(y == 0, up, down)
    s_2[:NS] = jnp.where(y < 2, up, down)
    log = jnp.broadcast_to(log, (8, HC))
    for s in (s_p, s_m, s_2):
        s[NS:] = log


def from_rows(r_p, r_m, r_2, y):
    def on(yes):
        return jnp.where(yes, 1.0, 0.0).astype(F32)

    l_p, l_m, l_2 = (r[NS : NS + 1, :] for r in (r_p, r_m, r_2))
    v_p, v_m, v_2 = (r[:NS, :] for r in (r_p, r_m, r_2))
    up = v_p * on(y >= 1) + v_2 * (on(y >= 2) * jnp.exp(l_p)) + v_m * (on(y == 3) * jnp.exp(l_p + l_2))
    down = v_m * on(y <= 2) + v_2 * (on(y <= 1) * jnp.exp(l_m)) + v_p * (on(y == 0) * jnp.exp(l_m + l_2))
    return up, down


def row_scan(order, ends, cols, ci, x, pre, which):
    acc = jnp.zeros((NS, HC), F32)
    for p in order:
        k = place(p, x)
        pre[which, k] = acc
        acc = acc * jnp.exp(ci[k, SEG - 1 : SEG, :]) + ends[k, :, cols]
    return acc


def row_log(ci):
    return sum(ci[k, SEG - 1 : SEG, :] for k in range(NX))


FIRST, SECOND = slice(0, HC), slice(HC, 2 * HC)


def tok_kernel(
    at, t0, t1, t2, t3, w_in, w_bc, ci, ce, tokb, xs, xfr, bc, pre, s_p, s_m, s_2, ends
):
    x, y = at[0], at[2]
    for k, t in enumerate((t0, t1, t2, t3)):
        tokb[k] = t[...].astype(BF16)

    def segment(k, _):
        t = tokb[k]
        xv = dot(t, w_in[...], 1, 0).astype(BF16)
        bv = dot(t, w_bc[...], 1, 0).astype(BF16)
        xs[k] = xv
        bc[k] = bv
        xf = xv.astype(F32)
        last = ci[k, SEG - 1 : SEG, :]
        xfr[k, :, :HC] = (xf * jnp.exp(last - ci[k])).astype(BF16)
        xfr[k, :, HC:] = (xf * jnp.exp(ce[k])).astype(BF16)
        ends[k] = dot(bv[:, :NS], xfr[k], 0, 0)
        return 0

    lax.fori_loop(0, NX, segment, 0)
    up = row_scan(range(NX), ends, FIRST, ci, x, pre, 0)
    down = row_scan(reversed(range(NX)), ends, SECOND, ci, x, pre, 1)
    send_rows(up, down, row_log(ci), y, s_p, s_m, s_2)


def cot_part(cots, first, w_out, ci, ce, bc, cotb, dy, dyfr, ends):
    for i, t in enumerate(cots):
        cotb[i] = t[...].astype(BF16)

    def segment(i, _):
        k = first + i
        d = dot(cotb[i], w_out[...], 1, 1)
        dy[i] = d.astype(BF16)
        last = ci[k, SEG - 1 : SEG, :]
        dyfr[i, :, :HC] = (d * jnp.exp(ci[k])).astype(BF16)
        dyfr[i, :, HC:] = (d * jnp.exp(last - ce[k])).astype(BF16)
        ends[k] = dot(bc[k, :, NS:], dyfr[i], 0, 0)
        return 0

    lax.fori_loop(0, len(cots), segment, 0)


def cot_kernel_a(at, c0, c1, w_out, ci, ce, bc, cotb, dy, dyfr, ends_a, ends):
    cot_part((c0, c1), 0, w_out, ci, ce, bc, cotb, dy, dyfr, ends)
    ends_a[...] = ends[:2]


def cot_kernel_b(
    at, c2, c3, w_out, ci, ce, bc, ends_a, cotb, dy, dyfr, pre, s_p, s_m, s_2, ends
):
    x, y = at[0], at[2]
    ends[:2] = ends_a[...]
    cot_part((c2, c3), 2, w_out, ci, ce, bc, cotb, dy, dyfr, ends)
    down = row_scan(reversed(range(NX)), ends, FIRST, ci, x, pre, 0)
    up = row_scan(range(NX), ends, SECOND, ci, x, pre, 1)
    send_rows(up, down, row_log(ci), y, s_p, s_m, s_2)


def enter(pre, which, q, ci, x, order, out, cols):
    log = jnp.zeros((1, HC), F32)
    for p in order:
        k = place(p, x)
        out[k, :, cols] = (pre[which, k] + q * jnp.exp(log)).astype(BF16)
        log = log + ci[k, SEG - 1 : SEG, :]


def inner_kernel(
    at, xs, bc, dy_a, dy_b, dyfr_a, dyfr_b, cotb_a, cotb_b, ci, ce, cirow, cerow, pre, r_p, r_m, r_2,
    keep, send, dxi, dci, dbi, sr, yb, g,
):
    x, core, y_at = at[0], at[1], at[2]
    up, down = from_rows(r_p, r_m, r_2, y_at)
    enter(pre, 0, up, ci, x, range(NX), sr, pl.ds(0, HC))
    enter(pre, 1, down, ci, x, reversed(range(NX)), sr, pl.ds(HC, HC))

    def run(first, dy, dyfr):
        def segment(i, _):
            k = first + i
            b, c = bc[k, :, :NS], bc[k, :, NS:]
            t = lax.broadcasted_iota(jnp.int32, (SEG, SEG), 0)
            s = lax.broadcasted_iota(jnp.int32, (SEG, SEG), 1)
            low, same = t > s, t == s
            scores = dot(c, b, 1, 1)
            scores = jnp.where(same, 2.0 * scores, scores)
            lane = lax.broadcasted_iota(jnp.int32, (SEG, 2 * HD), 1)
            carry = dot(c, sr[k], 1, 0)
            total = jnp.zeros((SEG, SEG), F32)
            for pair in range(NH // 2):
                cols = slice(pair * 2 * HD, (pair + 1) * 2 * HD)
                xp, dp = xs[k, :, cols], dy[i, :, cols]
                ws, xm, dm = [], [], []
                for j in range(2):
                    h = 2 * pair + j
                    at_t = slice(h * HD, h * HD + 1)
                    diff = jnp.where(
                        low,
                        ci[k, :, at_t] - cirow[k, h : h + 1, :],
                        cerow[k, h : h + 1, :] - ce[k, :, at_t],
                    )
                    decay = jnp.exp(diff)
                    mine = (lane < HD) if j == 0 else (lane >= HD)
                    xm.append(jnp.where(mine, xp, jnp.zeros_like(xp)))
                    dm.append(jnp.where(mine, dp, jnp.zeros_like(dp)))
                    ws.append((decay * scores).astype(BF16))
                    total = total + decay * dot(dm[j], xp, 1, 1)
                y = dot(ws[0], xm[0], 1, 0) + dot(ws[1], xm[1], 1, 0)
                last = ci[k, SEG - 1 : SEG, cols]
                y = y + carry[:, cols] * jnp.exp(ci[k, :, cols])
                y = y + carry[:, slice(HC + cols.start, HC + cols.stop)] * jnp.exp(last - ce[k, :, cols])
                yb[pl.ds(k * SEG, SEG), cols] = y.astype(BF16)
                dxi[k, :, cols] = dot(ws[0], dm[0], 0, 0) + dot(ws[1], dm[1], 0, 0)
            total = jnp.where(same, 2.0 * total, total).astype(BF16)
            dci[k] = dot(total, b, 1, 0) + dot(dyfr[i], sr[k], 1, 1)
            dbi[k] = dot(total, c, 0, 0)
            return 0

        lax.fori_loop(0, 2, segment, 0)

    run(0, dy_a, dyfr_a)
    run(2, dy_b, dyfr_b)
    half = 2 * SEG
    raw = dot(yb[:half, :], cotb_a[...].reshape(half, DM), 0, 0)
    raw = raw + dot(yb[half:, :], cotb_b[...].reshape(half, DM), 0, 0)
    for j in range(2):
        for q in range(4):
            z, c = 2 * j + q // 2, q % 2
            g[c, 96 * z : 96 * z + 96, :] = raw[96 * q : 96 * q + 96, HC * j : HC * j + HC]
    keep[...] = g[core]
    send[...] = g[1 - core]


def outer_kernel(
    at, tokb, xfr, bc, ci, ce, pre, r_p, r_m, r_2, dxi, dci, dbi, keep, send, dz, ds, g
):
    x, core, y_at = at[0], at[1], at[2]
    up, down = from_rows(r_p, r_m, r_2, y_at)
    enter(pre, 0, down, ci, x, reversed(range(NX)), ds, pl.ds(0, HC))
    enter(pre, 1, up, ci, x, range(NX), ds, pl.ds(HC, HC))

    def segment(k, _):
        b = bc[k, :, :NS]
        last = ci[k, SEG - 1 : SEG, :]
        back = dot(b, ds[k], 1, 0)
        dx = dxi[k] + back[:, :HC] * jnp.exp(last - ci[k]) + back[:, HC:] * jnp.exp(ce[k])
        dz[k, :, :HC] = dx.astype(BF16)
        dz[k, :, HC : HC + NS] = (dbi[k] + dot(xfr[k], ds[k], 1, 1)).astype(BF16)
        dz[k, :, HC + NS :] = dci[k].astype(BF16)
        return 0

    lax.fori_loop(0, NX, segment, 0)
    raw = dot(tokb[...].reshape(NX * SEG, DM), dz[...].reshape(NX * SEG, WIDE), 0, 0)
    for j in range(2 * NZ * NY):
        z, c, y = j // 8, j // 4 % 2, j % 4
        row = (4 * y + z) * 24
        g[c, row : row + 24, :] = raw[24 * j : 24 * j + 24, :]
    keep[...] = g[core]
    send[...] = g[1 - core]


def tokens_kernel(at, dz, w_in, w_bc, d0, d1, d2a, d2b, d3):
    def tokens_of(k):
        return dot(dz[k, :, :HC], w_in[...], 1, 1) + dot(dz[k, :, HC:], w_bc[...], 1, 1)

    d = tokens_of(2)
    d2a[...] = d[:HALF]
    d2b[...] = d[HALF:]
    d1[...] = tokens_of(1)
    d3[...] = tokens_of(3)
    d0[...] = tokens_of(0)


def pass_kernel(at, d1, d3, r_a, r_b, s1, s3):
    s1[:HALF] = d1[:HALF] + r_a[...]
    s1[HALF:] = d1[HALF:]
    s3[:HALF] = d3[:HALF]
    s3[HALF:] = d3[HALF:] + r_b[...]


def deal_kernel(which, at, *refs):
    terms, outs, total = refs[:-5], refs[-5:-1], refs[-1]
    acc = terms[0][...]
    for term in terms[1:]:
        acc = acc + term[...]
    total[...] = acc.reshape(total.shape)
    for k, out in enumerate(outs):
        out[...] = total[lax.rem(at[which] + k, 4)]


def out_kernel(at, a, b, c, d, one, two, square):
    rows = a[...] + b[...] + c[...] + d[...]
    left = at[3] < 2
    one[...] = jnp.where(left, rows[:12], rows[12:])
    two[...] = jnp.where(left, rows[12:], rows[:12])
    square[...] = jnp.broadcast_to(jnp.sum(rows * rows).reshape(1, 1), (8, 128))


def cut_kernel(at, a, b, c, d, square, p0, p1, p2, p3):
    rows = a[...] + b[...] + c[...] + d[...]
    mine = rows[:, :HC]
    local = jnp.sum(mine * mine).reshape(1, 1) + square[:1, :1]
    for k, out in enumerate((p0, p1, p2, p3)):
        to = lax.rem(at[0] + k, NX)
        part = mine[:6]
        for p in range(1, NX):
            part = jnp.where(to == p, mine[6 * p : 6 * p + 6], part)
        out[:6] = part
        out[6:8] = jnp.zeros((2, HC), F32)
        out[8:32, : 2 * NS] = rows[:, HC:]
        out[8:32, 2 * NS :] = jnp.zeros((24, HC - 2 * NS), F32)
        out[32:] = jnp.broadcast_to(local, (8, HC))


def square_kernel(at, a, b, c, d, square):
    refs = (a, b, c, d)
    bc = sum(r[8:32, : 2 * NS] for r in refs)
    total = sum(r[32:, :128] for r in refs)
    square[...] = total + jnp.sum(bc * bc).reshape(1, 1)


def last_kernel(at, a, b, c, d, one, two, square, all_in, all_bc, all_out, parts):
    x = at[0]
    entries = DM * 1536 + DM * 256 + 1536 * DM
    factor = jnp.minimum(1.0, 1.0 / jnp.sqrt(square[:1, :1] / entries + 1e-06))
    for k, r in enumerate((a, b, c, d)):
        parts[k] = r[...]
    for p in range(NX):
        all_in[:, HC * p : HC * p + HC] = factor * parts[lax.rem(x - p + NX, NX), :6, :]
    rows = sum(r[8:32, : 2 * NS] for r in (a, b, c, d))
    mine = rows[:6]
    for p in range(1, NX):
        mine = jnp.where(x == p, rows[6 * p : 6 * p + 6], mine)
    all_bc[...] = factor * mine
    even = lax.rem(x, 2) == 0
    all_out[:, :HC] = factor * jnp.where(even, one[...], two[...])
    all_out[:, HC:] = factor * jnp.where(even, two[...], one[...])


def call(kernel, outs, scratch, args, flops=0):
    moved = sum(a.size * a.dtype.itemsize for a in args)
    return pl.pallas_call(
        kernel,
        out_shape=[jax.ShapeDtypeStruct(*o) for o in outs],
        in_specs=[SMEM] + vm(len(args) - 1),
        out_specs=vm(len(outs)),
        scratch_shapes=[pltpu.VMEM(*s) for s in scratch],
        compiler_params=PARAMS,
        cost_estimate=pl.CostEstimate(flops=flops, bytes_accessed=moved, transcendentals=0),
    )(*args)


def rows_exchange(s_p, s_m, s_2):
    return [move(s_p, "y", 1), move(s_m, "y", -1), move(s_2, "y", 2)]


def deal(at, which, terms, rows, cols):
    axis = {2: "y", 3: "z"}[which]
    p0, p1, p2, p3 = call(
        functools.partial(deal_kernel, which), [((rows, cols), F32)] * 4, [((4, rows, cols), F32)], [at, *terms]
    )
    return [p0, move(p1, axis, 1), move(p2, axis, 2), move(p3, axis, 3)]


def body(tokens, cotangent, log_decay, w_in, w_bc, w_out):
    seq, rec = lax.axis_index("seq"), lax.axis_index("rec")
    x = seq % NX
    at = jnp.stack([x, rec % 2, seq // NX, rec // 2]).astype(jnp.int32)
    tie = lax.optimization_barrier

    t0, c0 = tokens[0].astype(F32), cotangent[0].astype(F32)
    t3, t1 = move(t0, "x", 1), move(t0, "x", -1)
    la0 = log_decay[0]
    las = jnp.stack([la0, move(la0, "x", -1), move(la0, "x", 2), move(la0, "x", 1)])
    la = lax.dynamic_slice(las, (0, x * NH, 0), (NX, NH, SEG))
    tri = jnp.triu(jnp.ones((SEG, SEG), F32))
    spread = jnp.repeat(jnp.eye(NH, dtype=F32), HD, axis=1)
    best = lax.Precision.HIGHEST
    cirow = jnp.einsum("khs,st->kht", la, tri, precision=best)
    cerow = cirow - la
    ci = jnp.einsum("kht,hj->ktj", cirow, spread, precision=best)
    ce = jnp.einsum("kht,hj->ktj", cerow, spread, precision=best)
    wi = lax.dynamic_slice(w_in, (0, x * HC), (DM, HC))
    wo = lax.dynamic_slice(w_out, (x * HC, 0), (HC, DM))
    t3, ci, ce, cirow, cerow, wi, wo = tie((t3, ci, ce, cirow, cerow, wi, wo))
    t2 = move(t3, "x", 1)
    c0_l, t1 = tie((c0, t1))
    c1 = move(c0_l, "x", -1)
    c0_r, t2 = tie((c0, t2))
    c3 = move(c0_r, "x", 1)
    c2 = move(c1, "x", -1)

    tall = ((TALL, HC), F32)
    edges = ((2, NX, NS, HC), F32)
    ends = ((NX, NS, 2 * HC), F32)
    tokb, xs, xfr, bc, pre_s, *s_rows = call(
        tok_kernel,
        [((NX, SEG, DM), BF16), ((NX, SEG, HC), BF16), ((NX, SEG, 2 * HC), BF16), ((NX, SEG, 2 * NS), BF16),
         edges, tall, tall, tall],
        [ends],
        [at, t0, t1, t2, t3, wi, w_bc, ci, ce],
        2 * 1024 * (DM * (HC + 2 * NS) + NS * 2 * HC),
    )
    q_rows = rows_exchange(*s_rows)
    two = [((2, SEG, DM), BF16), ((2, SEG, HC), BF16), ((2, SEG, 2 * HC), BF16)]
    flops = 1024 * (DM * HC + NS * 2 * HC)
    cotb_a, dy_a, dyfr_a, ends_a = call(
        cot_kernel_a, [*two, ((2, NS, 2 * HC), F32)], [ends], [at, c0, c1, wo, ci, ce, bc], flops
    )
    cotb_b, dy_b, dyfr_b, pre_d, *s_rows = call(
        cot_kernel_b, [*two, edges, tall, tall, tall], [ends], [at, c2, c3, wo, ci, ce, bc, ends_a], flops
    )
    p_rows = rows_exchange(*s_rows)
    keep_o, send_o, dxi, dci, dbi = call(
        inner_kernel,
        [((ROWS, HC), F32), ((ROWS, HC), F32), ((NX, SEG, HC), F32), ((NX, SEG, NS), F32), ((NX, SEG, NS), F32)],
        [((NX, NS, 2 * HC), BF16), ((NX * SEG, HC), BF16), ((2, ROWS, HC), F32)],
        [at, xs, bc, dy_a, dy_b, dyfr_a, dyfr_b, cotb_a, cotb_b, ci, ce, cirow, cerow, pre_s, *q_rows],
        2 * 1024 * (HC * DM + 5 * SEG * HC + 6 * NS * HC),
    )
    terms = deal(at, 3, [keep_o, move(send_o, "c", 1)], 96, HC)
    terms = deal(at, 2, terms, 24, HC)
    one, two_, square_o = call(out_kernel, [((12, HC), F32), ((12, HC), F32), ((8, 128), F32)], [], [at, *terms])
    keep_i, send_i, dz = call(
        outer_kernel,
        [((ROWS, WIDE), F32), ((ROWS, WIDE), F32), ((NX, SEG, WIDE), BF16)],
        [((NX, NS, 2 * HC), BF16), ((2, ROWS, WIDE), F32)],
        [at, tokb, xfr, bc, ci, ce, pre_d, *p_rows, dxi, dci, dbi],
        2 * 1024 * (WIDE * DM + 4 * NS * HC),
    )
    got_i = move(send_i, "c", 1)
    whole, half = ((SEG, DM), F32), ((HALF, DM), F32)
    d0, d1, d2a, d2b, d3 = call(
        tokens_kernel, [whole, whole, half, half, whole], [], [at, dz, wi, w_bc], 2 * 1024 * WIDE * DM
    )
    terms = deal(at, 2, [keep_i, got_i], 96, WIDE)
    r_a, r_b = move(d2a, "x", 1), move(d2b, "x", -1)
    terms = deal(at, 3, terms, 24, WIDE)
    s1, s3 = call(pass_kernel, [whole, whole], [], [at, d1, d3, r_a, r_b])
    m1, m3 = move(s1, "x", 1), move(s3, "x", -1)
    d_tok = (d0 + m1 + m3).astype(BF16)
    p0, p1, p2, p3 = call(cut_kernel, [((40, HC), F32)] * 4, [], [at, *terms, square_o])
    pieces = [p0, move(p1, "x", 1), move(p2, "x", 2), move(p3, "x", 3)]
    pairs = [], []
    for r in range(2 * NZ):
        for s in range(NX * NY):
            zz, cc, yy, xx = r // 2, r % 2, s // NX, s % NX
            to = 32 * xx + 2 * ((zz % 2) * 8 + cc * 4 + yy)
            first = 0 if zz < 2 else 1
            pairs[0].append((r * 16 + s, to + first))
            pairs[1].append((r * 16 + s, to + 1 - first))
    got_one = lax.ppermute(one, ("rec", "seq"), pairs[0])
    got_two = lax.ppermute(two_, ("rec", "seq"), pairs[1])
    (square,) = call(square_kernel, [((8, 128), F32)], [], [at, *pieces])
    for axis in ("y", "z"):
        square = square + (move(square, axis, 1) + move(square, axis, 3) + move(square, axis, 2))
    square = square + move(square, "c", 1)
    all_in, all_bc, all_out = call(
        last_kernel,
        [((6, NX * HC), F32), ((6, 2 * NS), F32), ((12, DM), F32)],
        [((NX, 40, HC), F32)],
        [at, *pieces, got_one, got_two, square],
    )
    return d_tok[None], all_in, all_bc, all_out


def solution(mesh):
    in_specs = (P("rec", "seq", None), P("rec", "seq", None), P("rec", None, "seq"), P(), P(), P())
    out_specs = (
        P("rec", "seq", None),
        P(("rec", "seq"), None),
        P(("rec", "seq"), None),
        P(("rec", "seq"), None),
    )
    return jax.shard_map(body, mesh=mesh, in_specs=in_specs, out_specs=out_specs, check_vma=False)
```

time: 233 us -> 172 us (0.74)
  starting transfers between devices: 108 us -> 72 us
  other arithmetic: 22.7 us -> 4.99 us
  Pallas kernels: 40.2 us -> 30.8 us
  waiting for transfers between devices: 40 us -> 44.8 us
  between operations: 3.81 us -> 0.99 us
    ppermute x64 -> x43, starting transfers between devices: 102 us -> 66 us  [move(): return lax.ppermute(value, name, pairs)]
    add x12 -> x0, other arithmetic: 9.98 us -> none  [the longest x1 1.99 us: body(): from_a = d1a + move(d2a, 'x', 1)]
    pallas_call x4 -> x15, Pallas kernels: 40.2 us -> 30.8 us  [call(): pl.pallas_call(kernel, out_shape=[jax.ShapeDtypeStruct(*o) for o in outs]...]
    reduce_sum x5 -> x0, other arithmetic: 4.16 us -> none  [the longest x1 2.09 us: body(): jnp.sum(raw_o * raw_o)]
    ppermute x2, waiting for transfers between devices: 0.01 us -> 2.82 us  [the longest x1 2.24 us: body(): got_one = lax.ppermute(one, ('rec', 'seq'), pairs[0])]
    unnamed x52 -> x26, local copies, waits for them, and re-layouts: 3.29 us -> 5.86 us
    ppermute x64 -> x43, waiting for transfers between devices: 40 us -> 42 us  [move(): return lax.ppermute(value, name, pairs)]
  transfers between devices with their start and end apart: 66 -> 45, of which waited for: 22 -> 16; matrix products, arithmetic and copies ran while one was open for 14% -> 8% of each run, Pallas kernels for 12% -> 15%
where the time goes in v2:
time: 172 us; the launch traced here: 169 us
  starting transfers between devices  72 us (42%)
  waiting for transfers between devices  44.8 us (26%)
  Pallas kernels  30.8 us (18%)
  local copies, waits for them, and re-layouts  8.52 us (5%)
  matrix products  7.21 us (4%)
  other arithmetic  4.99 us (3%)
    ppermute x43, starting transfers between devices, move(): return lax.ppermute(value, name, pairs)  66 us
    ppermute x43, waiting for transfers between devices, move(): return lax.ppermute(value, name, pairs)  42 us
    pallas_call x15, Pallas kernels, call(): pl.pallas_call(kernel, out_shape=[jax.ShapeDtypeStruct(*o) for o in outs]...  30.8 us
    unnamed x26, local copies, waits for them, and re-layouts  5.86 us
    ppermute x1, starting transfers between devices, body(): got_one = lax.ppermute(one, ('rec', 'seq'), pairs[0])  5.21 us
    convert_element_type x2, other arithmetic, body(): t0, c0 = (tokens[0].astype(F32), cotangent[0].astype(F32))  4.03 us
  transfers between devices with their start and end apart: 45, of which 16 were waited for; matrix products, arithmetic and copies ran while one was open for 8% of the time, Pallas kernels for 15%

profile of v2, /device:TPU:6, one launch (start us, length us, event | category | flops | bytes accessed | tf_op | source)
XLA Modules:
  0.0 169.3 jit_solution(3764172439474597538)
XLA Ops:
  0.6 2.1 %bitcast_convert_fusion.1.t0 = f32[256,768]{1,0:T(8,128)} fusion(bf16[1,256,768]{2,1,0:T(8,128)(2,1)} %param.6), kind=kLoop, calls=%fused_computation.3 | loop fusion | flops 196608 | bytes 1179648 | tf_op jit(solution)/shard_map/convert_element_type | solution.py:371
  2.7 0.8 collective-permute-start
  3.6 2.4 %collective-permute-start.1 = (f32[256,768]{1,0:T(8,128)}, f32[256,768]{1,0:T(8,128)}, u32[]{:S(2)}, u32[]{:S(2)}) collective-permute-start(f32[256,768]{1,0:T(8,128)} %bitcast_convert_fusion.1.t0), channel_id=1, source_target_pairs={{0,1},{1,2},{2,3},{3,0},{4,5},{5,6},{6,7},{7,4},{8,9},{9,10},{10,1... | collective-permute-start | bytes 2359304 | tf_op jit(solution)/shard_map/ppermute | solution.py:47
  6.0 1.5 collective-permute-start.3
  7.4 1.8 %collective-permute-start.4 = (f32[24,256]{1,0:T(8,128)}, f32[24,256]{1,0:T(8,128)}, u32[]{:S(2)}, u32[]{:S(2)}) collective-permute-start(f32[24,256]{1,0:T(8,128)} %bitcast.27), channel_id=1, source_target_pairs={{0,1},{1,2},{2,3},{3,0},{4,5},{5,6},{6,7},{7,4},{8,9},{9,10},{10,1... | collective-permute-start | bytes 73736 | tf_op jit(solution)/shard_map/ppermute | solution.py:47
  9.2 1.9 %bitcast_convert_fusion.c0 = f32[256,768]{1,0:T(8,128)} fusion(bf16[1,256,768]{2,1,0:T(8,128)(2,1)} %param.7), kind=kLoop, calls=%fused_computation.2 | loop fusion | flops 196608 | bytes 1179648 | tf_op jit(solution)/shard_map/convert_element_type | solution.py:371
  11.2 1.1 constant_dynamic-slice_fusion.w_out
  13.8 10.7 %collective-permute-done.2 = f32[24,256]{1,0:T(8,128)} collective-permute-done((f32[24,256]{1,0:T(8,128)}, f32[24,256]{1,0:T(8,128)}, u32[]{:S(2)}, u32[]{:S(2)}) %collective-permute-start.2) | collective-permute-done | bytes 24608 | tf_op jit(solution)/shard_map/ppermute | solution.py:47
  24.6 1.1 fusion.13
  25.7 3.1 %fusion.15.ci = f32[4,256,384]{2,1,0:T(8,128)} fusion(f32[4,6,256]{2,1,0:T(8,128)S(1)} %get-tuple-element.99.cirow, f32[6,384,1]{1,0,2:T(8,128)S(1)} %reshape.21), kind=kOutput, calls=%fused_computation.29 | convolution fusion | flops 28311552 | bytes 1606656 | tf_op jit(solution)/shard_map/kht,hj->ktj/dot_general | solution.py:381
  28.8 3.0 %fusion.16.ce = f32[4,256,384]{2,1,0:T(8,128)} fusion(f32[4,6,256]{2,1,0:T(8,128)S(1)} %get-tuple-element.100.cerow, f32[6,384,1]{1,0,2:T(8,128)S(1)} %reshape.21), kind=kOutput, calls=%fused_computation.30 | convolution fusion | flops 28311552 | bytes 1606656 | tf_op jit(solution)/shard_map/kht,hj->ktj/dot_general | solution.py:382
  31.9 3.0 %collective-permute-start.5 = (f32[256,768]{1,0:T(8,128)}, f32[256,768]{1,0:T(8,128)S(1)}, u32[]{:S(2)}, u32[]{:S(2)}) collective-permute-start(f32[256,768]{1,0:T(8,128)} %collective-permute-done.1.t3), channel_id=1, source_target_pairs={{0,1},{1,2},{2,3},{3,0},{4,5},{5,6},{6,7},{7,4},{8,9},{9,10},{10,1... | collective-permute-start | bytes 2359304 | tf_op jit(solution)/shard_map/ppermute | solution.py:47
  34.9 15.7 %collective-permute-done.5.t2 = f32[256,768]{1,0:T(8,128)S(1)} collective-permute-done((f32[256,768]{1,0:T(8,128)}, f32[256,768]{1,0:T(8,128)S(1)}, u32[]{:S(2)}, u32[]{:S(2)}) %collective-permute-start.5) | collective-permute-done | bytes 786464 | tf_op jit(solution)/shard_map/ppermute | solution.py:47
  50.6 0.9 copy-done.5
  51.4 2.5 %collective-permute-done.6.c1 = f32[256,768]{1,0:T(8,128)} collective-permute-done((f32[256,768]{1,0:T(8,128)}, f32[256,768]{1,0:T(8,128)}, u32[]{:S(2)}, u32[]{:S(2)}) %collective-permute-start.6) | collective-permute-done | bytes 786464 | tf_op jit(solution)/shard_map/ppermute | solution.py:47
  54.0 3.2 %collective-permute-start.8 = (f32[256,768]{1,0:T(8,128)}, f32[256,768]{1,0:T(8,128)}, u32[]{:S(2)}, u32[]{:S(2)}) collective-permute-start(f32[256,768]{1,0:T(8,128)} %bitcast_convert_fusion.c0), channel_id=1, source_target_pairs={{0,1},{1,2},{2,3},{3,0},{4,5},{5,6},{6,7},{7,4},{8,9},{9,10},{10,1... | collective-permute-start | bytes 2359304 | tf_op jit(solution)/shard_map/ppermute | solution.py:47
  57.3 1.4 copy-done.1
  58.7 1.4 copy-done.3
  60.1 1.1 copy-done.6
  61.2 1.0 copy-done.7
  62.2 5.3 %shard_map.93 = (bf16[4,256,768]{2,1,0:T(8,128)(2,1)S(1)}, bf16[4,256,384]{2,1,0:T(8,128)(2,1)S(1)}, bf16[4,256,768]{2,1,0:T(8,128)(2,1)S(1)}, bf16[4,256,256]{2...) custom-call(s32[4]{0:T(128)S(1)} %pad_add_fusion.at, ...), custom_call_target="tpu_custom_call" | custom-call | flops 1207959552 | bytes 7274512 | tf_op jit(solution)/shard_map/pallas_call | solution.py:342
  67.6 1.7 collective-permute-start.12
  69.2 1.7 collective-permute-start.13
  70.9 2.0 %collective-permute-start.14 = (f32[136,384]{1,0:T(8,128)S(1)}, f32[136,384]{1,0:T(8,128)S(1)}, u32[]{:S(2)}, u32[]{:S(2)}) collective-permute-start(f32[136,384]{1,0:T(8,128)S(1)} %get-tuple-element.104), channel_id=1, source_target_pairs={{0,8},{1,9},{2,10},{3,11},{4,12},{5,13},{6,14},{7,15},{8,0},{9,1},... | collective-permute-start | bytes 626696 | tf_op jit(solution)/shard_map/ppermute | solution.py:47
  72.9 2.7 %shard_map.94 = (bf16[2,256,768]{2,1,0:T(8,128)(2,1)S(1)}, bf16[2,256,384]{2,1,0:T(8,128)(2,1)S(1)}, bf16[2,256,768]{2,1,0:T(8,128)(2,1)S(1)}, f32[2,128,768]{2,1,0:T(8,128)S(1)}) custom-call(s32[4]{0:T(128)S(1)} %pad_add_fusion.at, f32[256,768]{1,0:T(8,128)} %bitcast_convert_fusion.c0, f32[256,768]{1,0:T(8,128)} %collective-permute-done.6.c1, ...), custom_call_target="tpu_custom_call" | custom-call | flops 402653184 | bytes 5832720 | tf_op jit(solution)/shard_map/pallas_call | solution.py:342
  75.7 3.0 %shard_map.95 = (bf16[2,256,768]{2,1,0:T(8,128)(2,1)S(1)}, bf16[2,256,384]{2,1,0:T(8,128)(2,1)S(1)}, bf16[2,256,768]{2,1,0:T(8,128)(2,1)S(1)}, f32[2,4,128,384]{...) custom-call(s32[4]{0:T(128)S(1)} %pad_add_fusion.at, ...), custom_call_target="tpu_custom_call" | custom-call | flops 402653184 | bytes 6619152 | tf_op jit(solution)/shard_map/pallas_call | solution.py:342
  79.4 2.6 %collective-permute-start.10 = (f32[136,384]{1,0:T(8,128)S(1)}, f32[136,384]{1,0:T(8,128)S(1)}, u32[]{:S(2)}, u32[]{:S(2)}) collective-permute-start(f32[136,384]{1,0:T(8,128)S(1)} %get-tuple-element.90), channel_id=1, source_target_pairs={{0,12},{1,13},{2,14},{3,15},{4,0},{5,1},{6,2},{7,3},{8,4},{9,5},{1... | collective-permute-start | bytes 626696 | tf_op jit(solution)/shard_map/ppermute | solution.py:47
  82.3 7.5 %shard_map.96 = (f32[384,384]{1,0:T(8,128)S(1)}, f32[384,384]{1,0:T(8,128)S(1)}, f32[4,256,384]{2,1,0:T(8,128)S(1)}, f32[4,256,128]{2,1,0:T(8,128)S(1)}, f32[4,256,128]{2,1,0:T(8,128)S(1)}) custom-call(s32[4]{0:T(128)S(1)} %pad_add_fusion.at, bf16[4,256,384]{2,1,0:T(8,128)(2,1)S(1)} %get-tuple-element.92.xs, bf16[4,256,256]{2,1,0:T(8,128)(2,1)S(1)} %get-tuple-element.83.bc, ...), custom_call_target="tpu_custom_call" | custom-call | flops 2214592512 | bytes 10637328 | tf_op jit(solution)/shard_map/pallas_call | solution.py:342
  89.8 3.9 %shard_map.97 = (f32[384,640]{1,0:T(8,128)S(1)}, f32[384,640]{1,0:T(8,128)S(1)}, bf16[4,256,640]{2,1,0:T(8,128)(2,1)S(1)}) custom-call(s32[4]{0:T(128)S(1)} %pad_add_fusion.at, bf16[4,256,768]{2,1,0:T(8,128)(2,1)S(1)} %get-tuple-element.81.tokb, bf16[4,256,768]{2,1,0:T(8,128)(2,1)S(1)} %get-tuple-element.82.xfr, ...), custom_call_target="tpu_custom_call" | custom-call | flops 1409286144 | bytes 11636752 | tf_op jit(solution)/shard_map/pallas_call | solution.py:342
  94.3 1.9 %shard_map.98 = (f32[256,768]{1,0:T(8,128)S(1)}, f32[256,768]{1,0:T(8,128)S(1)}, f32[128,768]{1,0:T(8,128)S(1)}, f32[128,768]{1,0:T(8,128)S(1)}, f32[256,768]{1,0:T(8,128)S(1)}) custom-call(s32[4]{0:T(128)S(1)} %pad_add_fusion.at, bf16[4,256,640]{2,1,0:T(8,128)(2,1)S(1)} %get-tuple-element.108.dz, bf16[768,384]{1,0:T(8,128)(2,1)S(1)} %constant_dynamic-slice_fusion.1.w_in, ...), custom_call_target="tpu_custom_call" | custom-call | flops 1006632960 | bytes 2293776 | tf_op jit(solution)/shard_map/pallas_call | solution.py:342
  96.3 1.1 collective-permute-start.15
  97.4 1.0 collective-permute-start.16
  99.0 2.0 %collective-permute-start.27 = (f32[96,384]{1,0:T(8,128)S(1)}, f32[96,384]{1,0:T(8,128)S(1)}, u32[]{:S(2)}, u32[]{:S(2)}) collective-permute-start(f32[96,384]{1,0:T(8,128)S(1)} %get-tuple-element.129), channel_id=1, source_target_pairs={{0,32},{16,48},{32,64},{48,80},{64,96},{80,112},{96,0},{112,16},{1... | collective-permute-start | bytes 442376 | tf_op jit(solution)/shard_map/ppermute | solution.py:47
  101.0 3.6 %collective-permute-start.28 = (f32[96,384]{1,0:T(8,128)S(1)}, f32[96,384]{1,0:T(8,128)S(1)}, u32[]{:S(2)}, u32[]{:S(2)}) collective-permute-start(f32[96,384]{1,0:T(8,128)S(1)} %get-tuple-element.130), channel_id=1, source_target_pairs={{0,64},{16,80},{32,96},{48,112},{64,0},{80,16},{96,32},{112,48},{1... | collective-permute-start | bytes 442376 | tf_op jit(solution)/shard_map/ppermute | solution.py:47
  104.6 1.0 collective-permute-start.29
  106.3 1.1 collective-permute-done.15.r_a
  108.0 1.5 collective-permute-done.16.r_b
  109.4 2.5 %collective-permute-start.21 = (f32[96,640]{1,0:T(8,128)S(1)}, f32[96,640]{1,0:T(8,128)S(1)}, u32[]{:S(2)}, u32[]{:S(2)}) collective-permute-start(f32[96,640]{1,0:T(8,128)S(1)} %get-tuple-element.120), channel_id=1, source_target_pairs={{0,8},{1,9},{2,10},{3,11},{4,12},{5,13},{6,14},{7,15},{8,0},{9,1},... | collective-permute-start | bytes 737288 | tf_op jit(solution)/shard_map/ppermute | solution.py:47
  111.9 1.3 collective-permute-start.22
  114.1 3.2 %collective-permute-start.17 = (f32[256,768]{1,0:T(8,128)S(1)}, f32[256,768]{1,0:T(8,128)S(1)}, u32[]{:S(2)}, u32[]{:S(2)}) collective-permute-start(f32[256,768]{1,0:T(8,128)S(1)} %get-tuple-element.114), channel_id=1, source_target_pairs={{0,1},{1,2},{2,3},{3,0},{4,5},{5,6},{6,7},{7,4},{8,9},{9,10},{10,1... | collective-permute-start | bytes 2359304 | tf_op jit(solution)/shard_map/ppermute | solution.py:47
  117.9 3.0 %collective-permute-start.30 = (f32[24,384]{1,0:T(8,128)S(1)}, f32[24,384]{1,0:T(8,128)S(1)}, u32[]{:S(2)}, u32[]{:S(2)}) collective-permute-start(f32[24,384]{1,0:T(8,128)S(1)} %get-tuple-element.133), channel_id=1, source_target_pairs={{0,4},{1,5},{2,6},{3,7},{4,8},{5,9},{6,10},{7,11},{8,12},{9,13},{1... | collective-permute-start | bytes 110600 | tf_op jit(solution)/shard_map/ppermute | solution.py:47
  121.7 1.8 %collective-permute-start.31 = (f32[24,384]{1,0:T(8,128)S(1)}, f32[24,384]{1,0:T(8,128)S(1)}, u32[]{:S(2)}, u32[]{:S(2)}) collective-permute-start(f32[24,384]{1,0:T(8,128)S(1)} %get-tuple-element.134), channel_id=1, source_target_pairs={{0,8},{1,9},{2,10},{3,11},{4,12},{5,13},{6,14},{7,15},{8,0},{9,1},... | collective-permute-start | bytes 110600 | tf_op jit(solution)/shard_map/ppermute | solution.py:47
  123.4 2.6 %collective-permute-start.32 = (f32[24,384]{1,0:T(8,128)S(1)}, f32[24,384]{1,0:T(8,128)S(1)}, u32[]{:S(2)}, u32[]{:S(2)}) collective-permute-start(f32[24,384]{1,0:T(8,128)S(1)} %get-tuple-element.135), channel_id=1, source_target_pairs={{0,12},{1,13},{2,14},{3,15},{4,0},{5,1},{6,2},{7,3},{8,4},{9,5},{1... | collective-permute-start | bytes 110600 | tf_op jit(solution)/shard_map/ppermute | solution.py:47
  126.7 2.0 %collective-permute-start.23 = (f32[24,640]{1,0:T(8,128)S(1)}, f32[24,640]{1,0:T(8,128)S(1)}, u32[]{:S(2)}, u32[]{:S(2)}) collective-permute-start(f32[24,640]{1,0:T(8,128)S(1)} %get-tuple-element.123), channel_id=1, source_target_pairs={{0,32},{16,48},{32,64},{48,80},{64,96},{80,112},{96,0},{112,16},{1... | collective-permute-start | bytes 184328 | tf_op jit(solution)/shard_map/ppermute | solution.py:47
  128.7 3.6 %collective-permute-start.24 = (f32[24,640]{1,0:T(8,128)S(1)}, f32[24,640]{1,0:T(8,128)S(1)}, u32[]{:S(2)}, u32[]{:S(2)}) collective-permute-start(f32[24,640]{1,0:T(8,128)S(1)} %get-tuple-element.124), channel_id=1, source_target_pairs={{0,64},{16,80},{32,96},{48,112},{64,0},{80,16},{96,32},{112,48},{1... | collective-permute-start | bytes 184328 | tf_op jit(solution)/shard_map/ppermute | solution.py:47
  132.2 1.0 collective-permute-start.25
  134.0 1.1 collective-permute-done.24.c
  135.1 1.4 collective-permute-done.25.d
  137.2 1.9 %collective-permute-start.33 = (f32[40,384]{1,0:T(8,128)S(1)}, f32[40,384]{1,0:T(8,128)S(1)}, u32[]{:S(2)}, u32[]{:S(2)}) collective-permute-start(f32[40,384]{1,0:T(8,128)S(1)} %get-tuple-element.138), channel_id=1, source_target_pairs={{0,1},{1,2},{2,3},{3,0},{4,5},{5,6},{6,7},{7,4},{8,9},{9,10},{10,1... | collective-permute-start | bytes 184328 | tf_op jit(solution)/shard_map/ppermute | solution.py:47
  139.1 0.9 collective-permute-start.35
  140.0 1.5 collective-permute-done.33.b
  141.5 3.4 %collective-permute-done.34.c = f32[40,384]{1,0:T(8,128)S(1)} collective-permute-done((f32[40,384]{1,0:T(8,128)S(1)}, f32[40,384]{1,0:T(8,128)S(1)}, u32[]{:S(2)}, u32[]{:S(2)}) %collective-permute-start.34) | collective-permute-done | bytes 61472 | tf_op jit(solution)/shard_map/ppermute | solution.py:47
  145.8 1.0 collective-permute-start.40
  146.8 1.1 collective-permute-start.38
  148.0 2.1 %collective-permute-start.39 = (f32[8,128]{1,0:T(8,128)S(1)}, f32[8,128]{1,0:T(8,128)S(1)}, u32[]{:S(2)}, u32[]{:S(2)}) collective-permute-start(f32[8,128]{1,0:T(8,128)S(1)} %shard_map.106), channel_id=1, source_target_pairs={{0,12},{1,13},{2,14},{3,15},{4,0},{5,1},{6,2},{7,3},{8,4},{9,5},{1... | collective-permute-start | bytes 12296 | tf_op jit(solution)/shard_map/ppermute | solution.py:47
  150.1 1.0 collective-permute-done.40
  151.7 1.6 collective-permute-start.43
  153.2 2.2 %collective-permute-start.41 = (f32[8,128]{1,0:T(8,128)S(1)}, f32[8,128]{1,0:T(8,128)S(1)}, u32[]{:S(2)}, u32[]{:S(2)}) collective-permute-start(f32[8,128]{1,0:T(8,128)S(1)} %add_add_fusion.1), channel_id=1, source_target_pairs={{0,32},{16,48},{32,64},{48,80},{64,96},{80,112},{96,0},{112,16},{1... | collective-permute-start | bytes 12296 | tf_op jit(solution)/shard_map/ppermute | solution.py:47
  155.5 1.0 collective-permute-start.42
  156.9 5.2 %collective-permute-start.36 = (f32[12,384]{1,0:T(8,128)S(1)}, f32[12,384]{1,0:T(8,128)S(1)}, u32[]{:S(2)}, u32[]{:S(2)}) collective-permute-start(f32[12,384]{1,0:T(8,128)S(1)} %get-tuple-element.141), channel_id=1, source_target_pairs={{0,0},{1,32},{2,64},{3,96},{4,2},{5,34},{6,66},{7,98},{8,4},{9,36}... | collective-permute-start | bytes 55304 | tf_op jit(solution)/shard_map/ppermute | solution.py:452
  162.8 1.6 collective-permute-start.44
  164.4 0.9 fusion
  165.3 2.2 %collective-permute-done.36.one = f32[12,384]{1,0:T(8,128)S(1)} collective-permute-done((f32[12,384]{1,0:T(8,128)S(1)}, f32[12,384]{1,0:T(8,128)S(1)}, u32[]{:S(2)}, u32[]{:S(2)}) %collective-permute-start.36) | collective-permute-done | bytes 18464 | tf_op jit(solution)/shard_map/ppermute | solution.py:452
  168.1 1.2 shard_map.107
  (83 shorter events, 12.7 us)
Async XLA Ops:
  0.6 10.5 %copy-start = (bf16[768,1536]{1,0:T(8,128)(2,1)S(1)}, bf16[768,1536]{1,0:T(8,128)(2,1)}, u32[]{:S(2)}) copy-start(bf16[768,1536]{1,0:T(8,128)(2,1)} %param.9) | copy-start | bytes 7077892
  2.7 32.2 %collective-permute-start = (f32[256,768]{1,0:T(8,128)}, f32[256,768]{1,0:T(8,128)}, u32[]{:S(2)}, u32[]{:S(2)}) collective-permute-start(f32[256,768]{1,0:T(8,128)} %bitcast_convert_fusion.1.t0), channel_id=1, source_target_pairs={{0,3},{1,0},{2,1},{3,2},{4,7},{5,4},{6,5},{7,6},{8,11},{9,8},{10,9... | collective-permute-start | bytes 2359304 | tf_op jit(solution)/shard_map/ppermute | solution.py:47
  3.6 28.3 %collective-permute-start.1 = (f32[256,768]{1,0:T(8,128)}, f32[256,768]{1,0:T(8,128)}, u32[]{:S(2)}, u32[]{:S(2)}) collective-permute-start(f32[256,768]{1,0:T(8,128)} %bitcast_convert_fusion.1.t0), channel_id=1, source_target_pairs={{0,1},{1,2},{2,3},{3,0},{4,5},{5,6},{6,7},{7,4},{8,9},{9,10},{10,1... | collective-permute-start | bytes 2359304 | tf_op jit(solution)/shard_map/ppermute | solution.py:47
  6.0 18.6 %collective-permute-start.2 = (f32[24,256]{1,0:T(8,128)}, f32[24,256]{1,0:T(8,128)}, u32[]{:S(2)}, u32[]{:S(2)}) collective-permute-start(f32[24,256]{1,0:T(8,128)} %bitcast.25), channel_id=1, source_target_pairs={{0,3},{1,0},{2,1},{3,2},{4,7},{5,4},{6,5},{7,6},{8,11},{9,8},{10,9... | collective-permute-start | bytes 73736 | tf_op jit(solution)/shard_map/ppermute | solution.py:47
  6.0 18.6 %collective-permute-start.3 = (f32[24,256]{1,0:T(8,128)}, f32[24,256]{1,0:T(8,128)}, u32[]{:S(2)}, u32[]{:S(2)}) collective-permute-start(f32[24,256]{1,0:T(8,128)} %bitcast.26), channel_id=1, source_target_pairs={{0,2},{1,3},{2,0},{3,1},{4,6},{5,7},{6,4},{7,5},{8,10},{9,11},{10,... | collective-permute-start | bytes 73736 | tf_op jit(solution)/shard_map/ppermute | solution.py:47
  7.4 17.2 %collective-permute-start.4 = (f32[24,256]{1,0:T(8,128)}, f32[24,256]{1,0:T(8,128)}, u32[]{:S(2)}, u32[]{:S(2)}) collective-permute-start(f32[24,256]{1,0:T(8,128)} %bitcast.27), channel_id=1, source_target_pairs={{0,1},{1,2},{2,3},{3,0},{4,5},{5,6},{6,7},{7,4},{8,9},{9,10},{10,1... | collective-permute-start | bytes 73736 | tf_op jit(solution)/shard_map/ppermute | solution.py:47
  25.7 6.2 %copy-start.9 = (f32[4,6,256]{2,1,0:T(8,128)}, f32[4,6,256]{2,1,0:T(8,128)S(1)}, u32[]{:S(2)}) copy-start(f32[4,6,256]{2,1,0:T(8,128)S(1)} %get-tuple-element.100.cerow) | copy-start | bytes 73732
  25.7 6.1 %copy-start.11 = (f32[4,6,256]{2,1,0:T(8,128)}, f32[4,6,256]{2,1,0:T(8,128)S(1)}, u32[]{:S(2)}) copy-start(f32[4,6,256]{2,1,0:T(8,128)S(1)} %get-tuple-element.99.cirow) | copy-start | bytes 73732
  31.9 18.7 %collective-permute-start.5 = (f32[256,768]{1,0:T(8,128)}, f32[256,768]{1,0:T(8,128)S(1)}, u32[]{:S(2)}, u32[]{:S(2)}) collective-permute-start(f32[256,768]{1,0:T(8,128)} %collective-permute-done.1.t3), channel_id=1, source_target_pairs={{0,1},{1,2},{2,3},{3,0},{4,5},{5,6},{6,7},{7,4},{8,9},{9,10},{10,1... | collective-permute-start | bytes 2359304 | tf_op jit(solution)/shard_map/ppermute | solution.py:47
  34.9 19.1 %collective-permute-start.6 = (f32[256,768]{1,0:T(8,128)}, f32[256,768]{1,0:T(8,128)}, u32[]{:S(2)}, u32[]{:S(2)}) collective-permute-start(f32[256,768]{1,0:T(8,128)} %bitcast_convert_fusion.c0), channel_id=1, source_target_pairs={{0,3},{1,0},{2,1},{3,2},{4,7},{5,4},{6,5},{7,6},{8,11},{9,8},{10,9... | collective-permute-start | bytes 2359304 | tf_op jit(solution)/shard_map/ppermute | solution.py:47
  50.6 0.9 copy-start.5
  54.0 21.7 %collective-permute-start.7 = (f32[256,768]{1,0:T(8,128)}, f32[256,768]{1,0:T(8,128)}, u32[]{:S(2)}, u32[]{:S(2)}) collective-permute-start(f32[256,768]{1,0:T(8,128)} %collective-permute-done.6.c1), channel_id=1, source_target_pairs={{0,3},{1,0},{2,1},{3,2},{4,7},{5,4},{6,5},{7,6},{8,11},{9,8},{10,9... | collective-permute-start | bytes 2359304 | tf_op jit(solution)/shard_map/ppermute | solution.py:47
  54.0 21.7 %collective-permute-start.8 = (f32[256,768]{1,0:T(8,128)}, f32[256,768]{1,0:T(8,128)}, u32[]{:S(2)}, u32[]{:S(2)}) collective-permute-start(f32[256,768]{1,0:T(8,128)} %bitcast_convert_fusion.c0), channel_id=1, source_target_pairs={{0,1},{1,2},{2,3},{3,0},{4,5},{5,6},{6,7},{7,4},{8,9},{9,10},{10,1... | collective-permute-start | bytes 2359304 | tf_op jit(solution)/shard_map/ppermute | solution.py:47
  57.3 1.4 copy-start.1
  58.7 1.4 copy-start.3
  60.1 1.1 copy-start.6
  61.2 1.0 copy-start.7
  62.2 10.6 %copy-start.2 = (f32[4,256,384]{2,1,0:T(8,128)S(1)}, f32[4,256,384]{2,1,0:T(8,128)}, u32[]{:S(2)}) copy-start(f32[4,256,384]{2,1,0:T(8,128)} %fusion.15.ci) | copy-start | bytes 4718596
  62.2 10.6 %copy-start.4 = (f32[4,256,384]{2,1,0:T(8,128)S(1)}, f32[4,256,384]{2,1,0:T(8,128)}, u32[]{:S(2)}) copy-start(f32[4,256,384]{2,1,0:T(8,128)} %fusion.16.ce) | copy-start | bytes 4718596
  67.6 14.4 %collective-permute-start.12 = (f32[136,384]{1,0:T(8,128)S(1)}, f32[136,384]{1,0:T(8,128)S(1)}, u32[]{:S(2)}, u32[]{:S(2)}) collective-permute-start(f32[136,384]{1,0:T(8,128)S(1)} %get-tuple-element.102), channel_id=1, source_target_pairs={{0,4},{1,5},{2,6},{3,7},{4,8},{5,9},{6,10},{7,11},{8,12},{9,13},{1... | collective-permute-start | bytes 626696 | tf_op jit(solution)/shard_map/ppermute | solution.py:47
  69.2 13.1 %collective-permute-start.13 = (f32[136,384]{1,0:T(8,128)S(1)}, f32[136,384]{1,0:T(8,128)S(1)}, u32[]{:S(2)}, u32[]{:S(2)}) collective-permute-start(f32[136,384]{1,0:T(8,128)S(1)} %get-tuple-element.103), channel_id=1, source_target_pairs={{0,12},{1,13},{2,14},{3,15},{4,0},{5,1},{6,2},{7,3},{8,4},{9,5},{1... | collective-permute-start | bytes 626696 | tf_op jit(solution)/shard_map/ppermute | solution.py:47
  70.9 11.4 %collective-permute-start.14 = (f32[136,384]{1,0:T(8,128)S(1)}, f32[136,384]{1,0:T(8,128)S(1)}, u32[]{:S(2)}, u32[]{:S(2)}) collective-permute-start(f32[136,384]{1,0:T(8,128)S(1)} %get-tuple-element.104), channel_id=1, source_target_pairs={{0,8},{1,9},{2,10},{3,11},{4,12},{5,13},{6,14},{7,15},{8,0},{9,1},... | collective-permute-start | bytes 626696 | tf_op jit(solution)/shard_map/ppermute | solution.py:47
  75.6 6.6 %copy-start.10 = (f32[4,6,256]{2,1,0:T(8,128)S(1)}, f32[4,6,256]{2,1,0:T(8,128)}, u32[]{:S(2)}) copy-start(f32[4,6,256]{2,1,0:T(8,128)} %copy-done.9) | copy-start | bytes 73732
  75.7 6.6 %copy-start.12 = (f32[4,6,256]{2,1,0:T(8,128)S(1)}, f32[4,6,256]{2,1,0:T(8,128)}, u32[]{:S(2)}) copy-start(f32[4,6,256]{2,1,0:T(8,128)} %copy-done.11) | copy-start | bytes 73732
  78.6 11.1 %collective-permute-start.9 = (f32[136,384]{1,0:T(8,128)S(1)}, f32[136,384]{1,0:T(8,128)S(1)}, u32[]{:S(2)}, u32[]{:S(2)}) collective-permute-start(f32[136,384]{1,0:T(8,128)S(1)} %get-tuple-element.89), channel_id=1, source_target_pairs={{0,4},{1,5},{2,6},{3,7},{4,8},{5,9},{6,10},{7,11},{8,12},{9,13},{1... | collective-permute-start | bytes 626696 | tf_op jit(solution)/shard_map/ppermute | solution.py:47
  79.4 10.4 %collective-permute-start.10 = (f32[136,384]{1,0:T(8,128)S(1)}, f32[136,384]{1,0:T(8,128)S(1)}, u32[]{:S(2)}, u32[]{:S(2)}) collective-permute-start(f32[136,384]{1,0:T(8,128)S(1)} %get-tuple-element.90), channel_id=1, source_target_pairs={{0,12},{1,13},{2,14},{3,15},{4,0},{5,1},{6,2},{7,3},{8,4},{9,5},{1... | collective-permute-start | bytes 626696 | tf_op jit(solution)/shard_map/ppermute | solution.py:47
  81.9 7.8 %collective-permute-start.11 = (f32[136,384]{1,0:T(8,128)S(1)}, f32[136,384]{1,0:T(8,128)S(1)}, u32[]{:S(2)}, u32[]{:S(2)}) collective-permute-start(f32[136,384]{1,0:T(8,128)S(1)} %get-tuple-element.91), channel_id=1, source_target_pairs={{0,8},{1,9},{2,10},{3,11},{4,12},{5,13},{6,14},{7,15},{8,0},{9,1},... | collective-permute-start | bytes 626696 | tf_op jit(solution)/shard_map/ppermute | solution.py:47
  89.8 4.5 %copy-start.8 = (bf16[768,256]{1,0:T(8,128)(2,1)S(1)}, bf16[768,256]{1,0:T(8,128)(2,1)}, u32[]{:S(2)}) copy-start(bf16[768,256]{1,0:T(8,128)(2,1)} %w_bc.3) | copy-start | bytes 1179652
  93.7 10.9 %collective-permute-start.19 = (f32[384,640]{1,0:T(8,128)S(1)}, f32[384,640]{1,0:T(8,128)S(1)}, u32[]{:S(2)}, u32[]{:S(2)}) collective-permute-start(f32[384,640]{1,0:T(8,128)S(1)} %get-tuple-element.117), channel_id=1, source_target_pairs={{0,16},{16,0},{32,48},{48,32},{64,80},{80,64},{96,112},{112,96},{1... | collective-permute-start | bytes 2949128 | tf_op jit(solution)/shard_map/ppermute | solution.py:47
  93.8 4.5 %collective-permute-start.26 = (f32[384,384]{1,0:T(8,128)S(1)}, f32[384,384]{1,0:T(8,128)S(1)}, u32[]{:S(2)}, u32[]{:S(2)}) collective-permute-start(f32[384,384]{1,0:T(8,128)S(1)} %get-tuple-element.127), channel_id=1, source_target_pairs={{0,16},{16,0},{32,48},{48,32},{64,80},{80,64},{96,112},{112,96},{1... | collective-permute-start | bytes 1769480 | tf_op jit(solution)/shard_map/ppermute | solution.py:47
  96.3 11.2 %collective-permute-start.15 = (f32[128,768]{1,0:T(8,128)S(1)}, f32[128,768]{1,0:T(8,128)S(1)}, u32[]{:S(2)}, u32[]{:S(2)}) collective-permute-start(f32[128,768]{1,0:T(8,128)S(1)} %get-tuple-element.112), channel_id=1, source_target_pairs={{0,1},{1,2},{2,3},{3,0},{4,5},{5,6},{6,7},{7,4},{8,9},{9,10},{10,1... | collective-permute-start | bytes 1179656 | tf_op jit(solution)/shard_map/ppermute | solution.py:47
  97.4 12.0 %collective-permute-start.16 = (f32[128,768]{1,0:T(8,128)S(1)}, f32[128,768]{1,0:T(8,128)S(1)}, u32[]{:S(2)}, u32[]{:S(2)}) collective-permute-start(f32[128,768]{1,0:T(8,128)S(1)} %get-tuple-element.113), channel_id=1, source_target_pairs={{0,3},{1,0},{2,1},{3,2},{4,7},{5,4},{6,5},{7,6},{8,11},{9,8},{10,9... | collective-permute-start | bytes 1179656 | tf_op jit(solution)/shard_map/ppermute | solution.py:47
  99.0 12.9 %collective-permute-start.27 = (f32[96,384]{1,0:T(8,128)S(1)}, f32[96,384]{1,0:T(8,128)S(1)}, u32[]{:S(2)}, u32[]{:S(2)}) collective-permute-start(f32[96,384]{1,0:T(8,128)S(1)} %get-tuple-element.129), channel_id=1, source_target_pairs={{0,32},{16,48},{32,64},{48,80},{64,96},{80,112},{96,0},{112,16},{1... | collective-permute-start | bytes 442376 | tf_op jit(solution)/shard_map/ppermute | solution.py:47
  101.0 13.0 %collective-permute-start.28 = (f32[96,384]{1,0:T(8,128)S(1)}, f32[96,384]{1,0:T(8,128)S(1)}, u32[]{:S(2)}, u32[]{:S(2)}) collective-permute-start(f32[96,384]{1,0:T(8,128)S(1)} %get-tuple-element.130), channel_id=1, source_target_pairs={{0,64},{16,80},{32,96},{48,112},{64,0},{80,16},{96,32},{112,48},{1... | collective-permute-start | bytes 442376 | tf_op jit(solution)/shard_map/ppermute | solution.py:47
  104.6 9.5 %collective-permute-start.29 = (f32[96,384]{1,0:T(8,128)S(1)}, f32[96,384]{1,0:T(8,128)S(1)}, u32[]{:S(2)}, u32[]{:S(2)}) collective-permute-start(f32[96,384]{1,0:T(8,128)S(1)} %get-tuple-element.131), channel_id=1, source_target_pairs={{0,96},{16,112},{32,0},{48,16},{64,32},{80,48},{96,64},{112,80},{1... | collective-permute-start | bytes 442376 | tf_op jit(solution)/shard_map/ppermute | solution.py:47
  107.4 10.4 %collective-permute-start.20 = (f32[96,640]{1,0:T(8,128)S(1)}, f32[96,640]{1,0:T(8,128)S(1)}, u32[]{:S(2)}, u32[]{:S(2)}) collective-permute-start(f32[96,640]{1,0:T(8,128)S(1)} %get-tuple-element.119), channel_id=1, source_target_pairs={{0,4},{1,5},{2,6},{3,7},{4,8},{5,9},{6,10},{7,11},{8,12},{9,13},{1... | collective-permute-start | bytes 737288 | tf_op jit(solution)/shard_map/ppermute | solution.py:47
  109.4 12.2 %collective-permute-start.21 = (f32[96,640]{1,0:T(8,128)S(1)}, f32[96,640]{1,0:T(8,128)S(1)}, u32[]{:S(2)}, u32[]{:S(2)}) collective-permute-start(f32[96,640]{1,0:T(8,128)S(1)} %get-tuple-element.120), channel_id=1, source_target_pairs={{0,8},{1,9},{2,10},{3,11},{4,12},{5,13},{6,14},{7,15},{8,0},{9,1},... | collective-permute-start | bytes 737288 | tf_op jit(solution)/shard_map/ppermute | solution.py:47
  111.9 11.5 %collective-permute-start.22 = (f32[96,640]{1,0:T(8,128)S(1)}, f32[96,640]{1,0:T(8,128)S(1)}, u32[]{:S(2)}, u32[]{:S(2)}) collective-permute-start(f32[96,640]{1,0:T(8,128)S(1)} %get-tuple-element.121), channel_id=1, source_target_pairs={{0,12},{1,13},{2,14},{3,15},{4,0},{5,1},{6,2},{7,3},{8,4},{9,5},{1... | collective-permute-start | bytes 737288 | tf_op jit(solution)/shard_map/ppermute | solution.py:47
  114.0 50.4 %collective-permute-start.18 = (f32[256,768]{1,0:T(8,128)S(1)}, f32[256,768]{1,0:T(8,128)S(1)}, u32[]{:S(2)}, u32[]{:S(2)}) collective-permute-start(f32[256,768]{1,0:T(8,128)S(1)} %get-tuple-element.115), channel_id=1, source_target_pairs={{0,3},{1,0},{2,1},{3,2},{4,7},{5,4},{6,5},{7,6},{8,11},{9,8},{10,9... | collective-permute-start | bytes 2359304 | tf_op jit(solution)/shard_map/ppermute | solution.py:47
  114.1 50.3 %collective-permute-start.17 = (f32[256,768]{1,0:T(8,128)S(1)}, f32[256,768]{1,0:T(8,128)S(1)}, u32[]{:S(2)}, u32[]{:S(2)}) collective-permute-start(f32[256,768]{1,0:T(8,128)S(1)} %get-tuple-element.114), channel_id=1, source_target_pairs={{0,1},{1,2},{2,3},{3,0},{4,5},{5,6},{6,7},{7,4},{8,9},{9,10},{10,1... | collective-permute-start | bytes 2359304 | tf_op jit(solution)/shard_map/ppermute | solution.py:47
  117.9 8.8 %collective-permute-start.30 = (f32[24,384]{1,0:T(8,128)S(1)}, f32[24,384]{1,0:T(8,128)S(1)}, u32[]{:S(2)}, u32[]{:S(2)}) collective-permute-start(f32[24,384]{1,0:T(8,128)S(1)} %get-tuple-element.133), channel_id=1, source_target_pairs={{0,4},{1,5},{2,6},{3,7},{4,8},{5,9},{6,10},{7,11},{8,12},{9,13},{1... | collective-permute-start | bytes 110600 | tf_op jit(solution)/shard_map/ppermute | solution.py:47
  121.7 7.0 %collective-permute-start.31 = (f32[24,384]{1,0:T(8,128)S(1)}, f32[24,384]{1,0:T(8,128)S(1)}, u32[]{:S(2)}, u32[]{:S(2)}) collective-permute-start(f32[24,384]{1,0:T(8,128)S(1)} %get-tuple-element.134), channel_id=1, source_target_pairs={{0,8},{1,9},{2,10},{3,11},{4,12},{5,13},{6,14},{7,15},{8,0},{9,1},... | collective-permute-start | bytes 110600 | tf_op jit(solution)/shard_map/ppermute | solution.py:47
  123.4 8.8 %collective-permute-start.32 = (f32[24,384]{1,0:T(8,128)S(1)}, f32[24,384]{1,0:T(8,128)S(1)}, u32[]{:S(2)}, u32[]{:S(2)}) collective-permute-start(f32[24,384]{1,0:T(8,128)S(1)} %get-tuple-element.135), channel_id=1, source_target_pairs={{0,12},{1,13},{2,14},{3,15},{4,0},{5,1},{6,2},{7,3},{8,4},{9,5},{1... | collective-permute-start | bytes 110600 | tf_op jit(solution)/shard_map/ppermute | solution.py:47
  126.7 7.3 %collective-permute-start.23 = (f32[24,640]{1,0:T(8,128)S(1)}, f32[24,640]{1,0:T(8,128)S(1)}, u32[]{:S(2)}, u32[]{:S(2)}) collective-permute-start(f32[24,640]{1,0:T(8,128)S(1)} %get-tuple-element.123), channel_id=1, source_target_pairs={{0,32},{16,48},{32,64},{48,80},{64,96},{80,112},{96,0},{112,16},{1... | collective-permute-start | bytes 184328 | tf_op jit(solution)/shard_map/ppermute | solution.py:47
  128.7 6.4 %collective-permute-start.24 = (f32[24,640]{1,0:T(8,128)S(1)}, f32[24,640]{1,0:T(8,128)S(1)}, u32[]{:S(2)}, u32[]{:S(2)}) collective-permute-start(f32[24,640]{1,0:T(8,128)S(1)} %get-tuple-element.124), channel_id=1, source_target_pairs={{0,64},{16,80},{32,96},{48,112},{64,0},{80,16},{96,32},{112,48},{1... | collective-permute-start | bytes 184328 | tf_op jit(solution)/shard_map/ppermute | solution.py:47
  132.2 4.2 %collective-permute-start.25 = (f32[24,640]{1,0:T(8,128)S(1)}, f32[24,640]{1,0:T(8,128)S(1)}, u32[]{:S(2)}, u32[]{:S(2)}) collective-permute-start(f32[24,640]{1,0:T(8,128)S(1)} %get-tuple-element.125), channel_id=1, source_target_pairs={{0,96},{16,112},{32,0},{48,16},{64,32},{80,48},{96,64},{112,80},{1... | collective-permute-start | bytes 184328 | tf_op jit(solution)/shard_map/ppermute | solution.py:47
  137.2 4.3 %collective-permute-start.33 = (f32[40,384]{1,0:T(8,128)S(1)}, f32[40,384]{1,0:T(8,128)S(1)}, u32[]{:S(2)}, u32[]{:S(2)}) collective-permute-start(f32[40,384]{1,0:T(8,128)S(1)} %get-tuple-element.138), channel_id=1, source_target_pairs={{0,1},{1,2},{2,3},{3,0},{4,5},{5,6},{6,7},{7,4},{8,9},{9,10},{10,1... | collective-permute-start | bytes 184328 | tf_op jit(solution)/shard_map/ppermute | solution.py:47
  139.1 5.8 %collective-permute-start.34 = (f32[40,384]{1,0:T(8,128)S(1)}, f32[40,384]{1,0:T(8,128)S(1)}, u32[]{:S(2)}, u32[]{:S(2)}) collective-permute-start(f32[40,384]{1,0:T(8,128)S(1)} %get-tuple-element.139), channel_id=1, source_target_pairs={{0,2},{1,3},{2,0},{3,1},{4,6},{5,7},{6,4},{7,5},{8,10},{9,11},{10,... | collective-permute-start | bytes 184328 | tf_op jit(solution)/shard_map/ppermute | solution.py:47
  139.1 6.1 %collective-permute-start.35 = (f32[40,384]{1,0:T(8,128)S(1)}, f32[40,384]{1,0:T(8,128)S(1)}, u32[]{:S(2)}, u32[]{:S(2)}) collective-permute-start(f32[40,384]{1,0:T(8,128)S(1)} %get-tuple-element.140), channel_id=1, source_target_pairs={{0,3},{1,0},{2,1},{3,2},{4,7},{5,4},{6,5},{7,6},{8,11},{9,8},{10,9... | collective-permute-start | bytes 184328 | tf_op jit(solution)/shard_map/ppermute | solution.py:47
  145.8 5.2 %collective-permute-start.40 = (f32[8,128]{1,0:T(8,128)S(1)}, f32[8,128]{1,0:T(8,128)S(1)}, u32[]{:S(2)}, u32[]{:S(2)}) collective-permute-start(f32[8,128]{1,0:T(8,128)S(1)} %shard_map.106), channel_id=1, source_target_pairs={{0,8},{1,9},{2,10},{3,11},{4,12},{5,13},{6,14},{7,15},{8,0},{9,1},... | collective-permute-start | bytes 12296 | tf_op jit(solution)/shard_map/ppermute | solution.py:47
  146.8 4.8 %collective-permute-start.38 = (f32[8,128]{1,0:T(8,128)S(1)}, f32[8,128]{1,0:T(8,128)S(1)}, u32[]{:S(2)}, u32[]{:S(2)}) collective-permute-start(f32[8,128]{1,0:T(8,128)S(1)} %shard_map.106), channel_id=1, source_target_pairs={{0,4},{1,5},{2,6},{3,7},{4,8},{5,9},{6,10},{7,11},{8,12},{9,13},{1... | collective-permute-start | bytes 12296 | tf_op jit(solution)/shard_map/ppermute | solution.py:47
  148.0 3.7 %collective-permute-start.39 = (f32[8,128]{1,0:T(8,128)S(1)}, f32[8,128]{1,0:T(8,128)S(1)}, u32[]{:S(2)}, u32[]{:S(2)}) collective-permute-start(f32[8,128]{1,0:T(8,128)S(1)} %shard_map.106), channel_id=1, source_target_pairs={{0,12},{1,13},{2,14},{3,15},{4,0},{5,1},{6,2},{7,3},{8,4},{9,5},{1... | collective-permute-start | bytes 12296 | tf_op jit(solution)/shard_map/ppermute | solution.py:47
  151.7 5.2 %collective-permute-start.43 = (f32[8,128]{1,0:T(8,128)S(1)}, f32[8,128]{1,0:T(8,128)S(1)}, u32[]{:S(2)}, u32[]{:S(2)}) collective-permute-start(f32[8,128]{1,0:T(8,128)S(1)} %add_add_fusion.1), channel_id=1, source_target_pairs={{0,64},{16,80},{32,96},{48,112},{64,0},{80,16},{96,32},{112,48},{1... | collective-permute-start | bytes 12296 | tf_op jit(solution)/shard_map/ppermute | solution.py:47
  153.2 8.8 %collective-permute-start.41 = (f32[8,128]{1,0:T(8,128)S(1)}, f32[8,128]{1,0:T(8,128)S(1)}, u32[]{:S(2)}, u32[]{:S(2)}) collective-permute-start(f32[8,128]{1,0:T(8,128)S(1)} %add_add_fusion.1), channel_id=1, source_target_pairs={{0,32},{16,48},{32,64},{48,80},{64,96},{80,112},{96,0},{112,16},{1... | collective-permute-start | bytes 12296 | tf_op jit(solution)/shard_map/ppermute | solution.py:47
  155.5 7.4 %collective-permute-start.42 = (f32[8,128]{1,0:T(8,128)S(1)}, f32[8,128]{1,0:T(8,128)S(1)}, u32[]{:S(2)}, u32[]{:S(2)}) collective-permute-start(f32[8,128]{1,0:T(8,128)S(1)} %add_add_fusion.1), channel_id=1, source_target_pairs={{0,96},{16,112},{32,0},{48,16},{64,32},{80,48},{96,64},{112,80},{1... | collective-permute-start | bytes 12296 | tf_op jit(solution)/shard_map/ppermute | solution.py:47
  156.9 10.7 %collective-permute-start.36 = (f32[12,384]{1,0:T(8,128)S(1)}, f32[12,384]{1,0:T(8,128)S(1)}, u32[]{:S(2)}, u32[]{:S(2)}) collective-permute-start(f32[12,384]{1,0:T(8,128)S(1)} %get-tuple-element.141), channel_id=1, source_target_pairs={{0,0},{1,32},{2,64},{3,96},{4,2},{5,34},{6,66},{7,98},{8,4},{9,36}... | collective-permute-start | bytes 55304 | tf_op jit(solution)/shard_map/ppermute | solution.py:452
  162.1 6.0 %collective-permute-start.37 = (f32[12,384]{1,0:T(8,128)S(1)}, f32[12,384]{1,0:T(8,128)S(1)}, u32[]{:S(2)}, u32[]{:S(2)}) collective-permute-start(f32[12,384]{1,0:T(8,128)S(1)} %get-tuple-element.142), channel_id=1, source_target_pairs={{0,1},{1,33},{2,65},{3,97},{4,3},{5,35},{6,67},{7,99},{8,5},{9,37}... | collective-permute-start | bytes 55304 | tf_op jit(solution)/shard_map/ppermute | solution.py:453
  162.8 2.4 %collective-permute-start.44 = (f32[8,128]{1,0:T(8,128)S(1)}, f32[8,128]{1,0:T(8,128)S(1)}, u32[]{:S(2)}, u32[]{:S(2)}) collective-permute-start(f32[8,128]{1,0:T(8,128)S(1)} %add_add_fusion), channel_id=1, source_target_pairs={{0,16},{16,0},{32,48},{48,32},{64,80},{80,64},{96,112},{112,96},{1... | collective-permute-start | bytes 12296 | tf_op jit(solution)/shard_map/ppermute | solution.py:47

commit v3 on v2

--- a/solution.py
+++ b/solution.py
@@ -21,6 +21,7 @@
 HC = NH * HD
 ROWS = DM // 2
 WIDE = HC + 2 * NS
+ALL = WIDE + HC
 TALL = NS + 8
 
 
@@ -51,6 +52,12 @@
     return lax.dot_general(a, b, (((ca,), (cb,)), ((), ())), preferred_element_type=F32)
 
 
+def exact(a, b, ca, cb):
+    return lax.dot_general(
+        a, b, (((ca,), (cb,)), ((), ())), precision=lax.Precision.HIGHEST, preferred_element_type=F32
+    )
+
+
 def place(p, x):
     return lax.rem(p - x + NX, NX)
 
@@ -99,12 +106,45 @@
 FIRST, SECOND = slice(0, HC), slice(HC, 2 * HC)
 
 
+def pack_kernel(tok, cot, log, out, cot_out):
+    cot_out[...] = cot[...].astype(F32)
+    out[:SEG] = tok[...].astype(F32)
+    for part in range(3):
+        out[SEG:, SEG * part : SEG * part + SEG] = log[8 * part : 8 * part + 8]
+
+
+def decays(x, toks, cirow, cerow, ci, ce, la):
+    s = lax.broadcasted_iota(jnp.int32, (SEG, SEG), 0)
+    t = lax.broadcasted_iota(jnp.int32, (SEG, SEG), 1)
+    tri = jnp.where(s <= t, 1.0, 0.0).astype(F32)
+    head = lax.broadcasted_iota(jnp.int32, (8, HC), 0) * HD
+    lane = lax.broadcasted_iota(jnp.int32, (8, HC), 1)
+    spread = jnp.where((lane >= head) & (lane < head + HD), 1.0, 0.0).astype(F32)
+    la[...] = jnp.zeros((8, SEG), F32)
+    for k, tok in enumerate(toks):
+        for j in range(NH):
+            mine = jnp.zeros((1, SEG), F32)
+            for p in range(NX):
+                row, part = (NH * p + j) % 8, (NH * p + j) // 8
+                its = tok[SEG + row : SEG + row + 1, SEG * part : SEG * part + SEG]
+                mine = jnp.where(x == p, its, mine)
+            la[j : j + 1] = mine
+        through = exact(la[...], tri, 1, 0)
+        before = through - la[...]
+        cirow[k] = through
+        cerow[k] = before
+        ci[k] = exact(through, spread, 0, 0)
+        ce[k] = exact(before, spread, 0, 0)
+
+
 def tok_kernel(
-    at, t0, t1, t2, t3, w_in, w_bc, ci, ce, tokb, xs, xfr, bc, pre, s_p, s_m, s_2, ends
+    at, t0, t1, t2, t3, w_in, w_bc,
+    cirow, cerow, ci, ce, tokb, xs, xfr, bc, pre, s_p, s_m, s_2, ends, la,
 ):
     x, y = at[0], at[2]
+    decays(x, (t0, t1, t2, t3), cirow, cerow, ci, ce, la)
     for k, t in enumerate((t0, t1, t2, t3)):
-        tokb[k] = t[...].astype(BF16)
+        tokb[k] = t[:SEG].astype(BF16)
 
     def segment(k, _):
         t = tokb[k]
@@ -166,11 +206,15 @@
         log = log + ci[k, SEG - 1 : SEG, :]
 
 
+def blocks():
+    return [(j, j // 4 % 2, (4 * (j % 4) + j // 8) * 24) for j in range(2 * NZ * NY)]
+
+
 def inner_kernel(
     at, xs, bc, dy_a, dy_b, dyfr_a, dyfr_b, cotb_a, cotb_b, ci, ce, cirow, cerow, pre, r_p, r_m, r_2,
-    keep, send, dxi, dci, dbi, sr, yb, g,
+    g, dxi, dci, dbi, sr, yb,
 ):
-    x, core, y_at = at[0], at[1], at[2]
+    x, y_at = at[0], at[2]
     up, down = from_rows(r_p, r_m, r_2, y_at)
     enter(pre, 0, up, ci, x, range(NX), sr, pl.ds(0, HC))
     enter(pre, 1, down, ci, x, reversed(range(NX)), sr, pl.ds(HC, HC))
@@ -223,16 +267,13 @@
     half = 2 * SEG
     raw = dot(yb[:half, :], cotb_a[...].reshape(half, DM), 0, 0)
     raw = raw + dot(yb[half:, :], cotb_b[...].reshape(half, DM), 0, 0)
-    for j in range(2):
-        for q in range(4):
-            z, c = 2 * j + q // 2, q % 2
-            g[c, 96 * z : 96 * z + 96, :] = raw[96 * q : 96 * q + 96, HC * j : HC * j + HC]
-    keep[...] = g[core]
-    send[...] = g[1 - core]
+    for j, c, row in blocks():
+        g[c, row : row + 12, :] = raw[12 * j : 12 * j + 12, :HC]
+        g[c, row + 12 : row + 24, :] = raw[12 * j : 12 * j + 12, HC:]
 
 
 def outer_kernel(
-    at, tokb, xfr, bc, ci, ce, pre, r_p, r_m, r_2, dxi, dci, dbi, keep, send, dz, ds, g
+    at, tokb, xfr, bc, ci, ce, pre, r_p, r_m, r_2, dxi, dci, dbi, g_out, keep, send, dz, ds, g
 ):
     x, core, y_at = at[0], at[1], at[2]
     up, down = from_rows(r_p, r_m, r_2, y_at)
@@ -251,12 +292,11 @@
 
     lax.fori_loop(0, NX, segment, 0)
     raw = dot(tokb[...].reshape(NX * SEG, DM), dz[...].reshape(NX * SEG, WIDE), 0, 0)
-    for j in range(2 * NZ * NY):
-        z, c, y = j // 8, j // 4 % 2, j % 4
-        row = (4 * y + z) * 24
+    for j, c, row in blocks():
         g[c, row : row + 24, :] = raw[24 * j : 24 * j + 24, :]
-    keep[...] = g[core]
-    send[...] = g[1 - core]
+    for out, c in ((keep, core), (send, 1 - core)):
+        out[:, :WIDE] = g[c]
+        out[:, WIDE:] = g_out[c]
 
 
 def tokens_kernel(at, dz, w_in, w_bc, d0, d1, d2a, d2b, d3):
@@ -288,18 +328,11 @@
         out[...] = total[lax.rem(at[which] + k, 4)]
 
 
-def out_kernel(at, a, b, c, d, one, two, square):
+def cut_kernel(at, a, b, c, d, p0, p1, p2, p3, rows_out):
     rows = a[...] + b[...] + c[...] + d[...]
-    left = at[3] < 2
-    one[...] = jnp.where(left, rows[:12], rows[12:])
-    two[...] = jnp.where(left, rows[12:], rows[:12])
-    square[...] = jnp.broadcast_to(jnp.sum(rows * rows).reshape(1, 1), (8, 128))
-
-
-def cut_kernel(at, a, b, c, d, square, p0, p1, p2, p3):
-    rows = a[...] + b[...] + c[...] + d[...]
-    mine = rows[:, :HC]
-    local = jnp.sum(mine * mine).reshape(1, 1) + square[:1, :1]
+    mine, of_out = rows[:, :HC], rows[:, WIDE:]
+    rows_out[...] = of_out
+    local = (jnp.sum(mine * mine) + jnp.sum(of_out * of_out)).reshape(1, 1)
     for k, out in enumerate((p0, p1, p2, p3)):
         to = lax.rem(at[0] + k, NX)
         part = mine[:6]
@@ -307,7 +340,7 @@
             part = jnp.where(to == p, mine[6 * p : 6 * p + 6], part)
         out[:6] = part
         out[6:8] = jnp.zeros((2, HC), F32)
-        out[8:32, : 2 * NS] = rows[:, HC:]
+        out[8:32, : 2 * NS] = rows[:, HC:WIDE]
         out[8:32, 2 * NS :] = jnp.zeros((24, HC - 2 * NS), F32)
         out[32:] = jnp.broadcast_to(local, (8, HC))
 
@@ -319,7 +352,7 @@
     square[...] = total + jnp.sum(bc * bc).reshape(1, 1)
 
 
-def last_kernel(at, a, b, c, d, one, two, square, all_in, all_bc, all_out, parts):
+def last_kernel(at, a, b, c, d, rows_out, square, all_in, all_bc, all_out, parts):
     x = at[0]
     entries = DM * 1536 + DM * 256 + 1536 * DM
     factor = jnp.minimum(1.0, 1.0 / jnp.sqrt(square[:1, :1] / entries + 1e-06))
@@ -332,9 +365,8 @@
     for p in range(1, NX):
         mine = jnp.where(x == p, rows[6 * p : 6 * p + 6], mine)
     all_bc[...] = factor * mine
-    even = lax.rem(x, 2) == 0
-    all_out[:, :HC] = factor * jnp.where(even, one[...], two[...])
-    all_out[:, HC:] = factor * jnp.where(even, two[...], one[...])
+    all_out[:, :HC] = factor * rows_out[:12]
+    all_out[:, HC:] = factor * rows_out[12:]
 
 
 def call(kernel, outs, scratch, args, flops=0):
@@ -368,21 +400,16 @@
     at = jnp.stack([x, rec % 2, seq // NX, rec // 2]).astype(jnp.int32)
     tie = lax.optimization_barrier
 
-    t0, c0 = tokens[0].astype(F32), cotangent[0].astype(F32)
+    t0, c0 = pl.pallas_call(
+        pack_kernel,
+        out_shape=[jax.ShapeDtypeStruct((SEG + 8, DM), F32), jax.ShapeDtypeStruct((SEG, DM), F32)],
+        in_specs=vm(3),
+        out_specs=vm(2),
+        compiler_params=PARAMS,
+    )(tokens[0], cotangent[0], log_decay[0])
     t3, t1 = move(t0, "x", 1), move(t0, "x", -1)
-    la0 = log_decay[0]
-    las = jnp.stack([la0, move(la0, "x", -1), move(la0, "x", 2), move(la0, "x", 1)])
-    la = lax.dynamic_slice(las, (0, x * NH, 0), (NX, NH, SEG))
-    tri = jnp.triu(jnp.ones((SEG, SEG), F32))
-    spread = jnp.repeat(jnp.eye(NH, dtype=F32), HD, axis=1)
-    best = lax.Precision.HIGHEST
-    cirow = jnp.einsum("khs,st->kht", la, tri, precision=best)
-    cerow = cirow - la
-    ci = jnp.einsum("kht,hj->ktj", cirow, spread, precision=best)
-    ce = jnp.einsum("kht,hj->ktj", cerow, spread, precision=best)
     wi = lax.dynamic_slice(w_in, (0, x * HC), (DM, HC))
     wo = lax.dynamic_slice(w_out, (x * HC, 0), (HC, DM))
-    t3, ci, ce, cirow, cerow, wi, wo = tie((t3, ci, ce, cirow, cerow, wi, wo))
     t2 = move(t3, "x", 1)
     c0_l, t1 = tie((c0, t1))
     c1 = move(c0_l, "x", -1)
@@ -393,12 +420,13 @@
     tall = ((TALL, HC), F32)
     edges = ((2, NX, NS, HC), F32)
     ends = ((NX, NS, 2 * HC), F32)
-    tokb, xs, xfr, bc, pre_s, *s_rows = call(
+    cirow, cerow, ci, ce, tokb, xs, xfr, bc, pre_s, *s_rows = call(
         tok_kernel,
-        [((NX, SEG, DM), BF16), ((NX, SEG, HC), BF16), ((NX, SEG, 2 * HC), BF16), ((NX, SEG, 2 * NS), BF16),
+        [((NX, 8, SEG), F32), ((NX, 8, SEG), F32), ((NX, SEG, HC), F32), ((NX, SEG, HC), F32),
+         ((NX, SEG, DM), BF16), ((NX, SEG, HC), BF16), ((NX, SEG, 2 * HC), BF16), ((NX, SEG, 2 * NS), BF16),
          edges, tall, tall, tall],
-        [ends],
-        [at, t0, t1, t2, t3, wi, w_bc, ci, ce],
+        [ends, ((8, SEG), F32)],
+        [at, t0, t1, t2, t3, wi, w_bc],
         2 * 1024 * (DM * (HC + 2 * NS) + NS * 2 * HC),
     )
     q_rows = rows_exchange(*s_rows)
@@ -411,46 +439,38 @@
         cot_kernel_b, [*two, edges, tall, tall, tall], [ends], [at, c2, c3, wo, ci, ce, bc, ends_a], flops
     )
     p_rows = rows_exchange(*s_rows)
-    keep_o, send_o, dxi, dci, dbi = call(
+    g_out, dxi, dci, dbi = call(
         inner_kernel,
-        [((ROWS, HC), F32), ((ROWS, HC), F32), ((NX, SEG, HC), F32), ((NX, SEG, NS), F32), ((NX, SEG, NS), F32)],
-        [((NX, NS, 2 * HC), BF16), ((NX * SEG, HC), BF16), ((2, ROWS, HC), F32)],
+        [((2, ROWS, HC), F32), ((NX, SEG, HC), F32), ((NX, SEG, NS), F32), ((NX, SEG, NS), F32)],
+        [((NX, NS, 2 * HC), BF16), ((NX * SEG, HC), BF16)],
         [at, xs, bc, dy_a, dy_b, dyfr_a, dyfr_b, cotb_a, cotb_b, ci, ce, cirow, cerow, pre_s, *q_rows],
         2 * 1024 * (HC * DM + 5 * SEG * HC + 6 * NS * HC),
     )
-    terms = deal(at, 3, [keep_o, move(send_o, "c", 1)], 96, HC)
-    terms = deal(at, 2, terms, 24, HC)
-    one, two_, square_o = call(out_kernel, [((12, HC), F32), ((12, HC), F32), ((8, 128), F32)], [], [at, *terms])
-    keep_i, send_i, dz = call(
+    keep, send, dz = call(
         outer_kernel,
-        [((ROWS, WIDE), F32), ((ROWS, WIDE), F32), ((NX, SEG, WIDE), BF16)],
+        [((ROWS, ALL), F32), ((ROWS, ALL), F32), ((NX, SEG, WIDE), BF16)],
         [((NX, NS, 2 * HC), BF16), ((2, ROWS, WIDE), F32)],
-        [at, tokb, xfr, bc, ci, ce, pre_d, *p_rows, dxi, dci, dbi],
+        [at, tokb, xfr, bc, ci, ce, pre_d, *p_rows, dxi, dci, dbi, g_out],
         2 * 1024 * (WIDE * DM + 4 * NS * HC),
     )
-    got_i = move(send_i, "c", 1)
+    got = move(send, "c", 1)
     whole, half = ((SEG, DM), F32), ((HALF, DM), F32)
     d0, d1, d2a, d2b, d3 = call(
         tokens_kernel, [whole, whole, half, half, whole], [], [at, dz, wi, w_bc], 2 * 1024 * WIDE * DM
     )
-    terms = deal(at, 2, [keep_i, got_i], 96, WIDE)
+    terms = deal(at, 2, [keep, got], 96, ALL)
     r_a, r_b = move(d2a, "x", 1), move(d2b, "x", -1)
-    terms = deal(at, 3, terms, 24, WIDE)
     s1, s3 = call(pass_kernel, [whole, whole], [], [at, d1, d3, r_a, r_b])
     m1, m3 = move(s1, "x", 1), move(s3, "x", -1)
     d_tok = (d0 + m1 + m3).astype(BF16)
-    p0, p1, p2, p3 = call(cut_kernel, [((40, HC), F32)] * 4, [], [at, *terms, square_o])
+    terms = deal(at, 3, terms, 24, ALL)
+    p0, p1, p2, p3, rows_out = call(
+        cut_kernel, [((40, HC), F32)] * 4 + [((24, HC), F32)], [], [at, *terms]
+    )
     pieces = [p0, move(p1, "x", 1), move(p2, "x", 2), move(p3, "x", 3)]
-    pairs = [], []
-    for r in range(2 * NZ):
-        for s in range(NX * NY):
-            zz, cc, yy, xx = r // 2, r % 2, s // NX, s % NX
-            to = 32 * xx + 2 * ((zz % 2) * 8 + cc * 4 + yy)
-            first = 0 if zz < 2 else 1
-            pairs[0].append((r * 16 + s, to + first))
-            pairs[1].append((r * 16 + s, to + 1 - first))
-    got_one = lax.ppermute(one, ("rec", "seq"), pairs[0])
-    got_two = lax.ppermute(two_, ("rec", "seq"), pairs[1])
+    lanes = NX * NY
+    pairs = [(r * lanes + i, 2 * NZ * NY * (i % NX) + r * NY + i // NX) for r in range(2 * NZ) for i in range(lanes)]
+    rows_out = lax.ppermute(rows_out, ("rec", "seq"), pairs)
     (square,) = call(square_kernel, [((8, 128), F32)], [], [at, *pieces])
     for axis in ("y", "z"):
         square = square + (move(square, axis, 1) + move(square, axis, 3) + move(square, axis, 2))
@@ -459,7 +479,7 @@
         last_kernel,
         [((6, NX * HC), F32), ((6, 2 * NS), F32), ((12, DM), F32)],
         [((NX, 40, HC), F32)],
-        [at, *pieces, got_one, got_two, square],
+        [at, *pieces, rows_out, square],
     )
     return d_tok[None], all_in, all_bc, all_out
 

time: 172 us -> 162 us (0.942); the launches traced: 169 us -> 162 us
  starting transfers between devices: 72 us -> 53.5 us
  waiting for transfers between devices: 44.8 us -> 62.2 us
  matrix products: 7.21 us -> 0 us
  other arithmetic: 4.99 us -> 0.95 us
  local copies, waits for them, and re-layouts: 8.52 us -> 12.2 us
    ppermute x43 -> x33, starting transfers between devices: 66 us -> 49 us  [move(): return lax.ppermute(value, name, pairs)]
    ppermute x43 -> x33, waiting for transfers between devices: 42 us -> 58.2 us  [move(): return lax.ppermute(value, name, pairs)]
    dot_general x3 -> x0, matrix products: 7.21 us -> none  [the longest x1 3.09 us: body(): ci = jnp.einsum('kht,hj->ktj', cirow, spread, precision=best)]
    unnamed x26, local copies, waits for them, and re-layouts: 5.86 us -> 11 us
    convert_element_type x3 -> x0, other arithmetic: 4.04 us -> none  [the longest x2 4.03 us: body(): t0, c0 = (tokens[0].astype(F32), cotangent[0].astype(F32))]
    ppermute x2 -> x1, starting transfers between devices: 5.94 us -> 4.51 us  [body(): rows_out = lax.ppermute(rows_out, ('rec', 'seq'), pairs)]
    ppermute x2 -> x1, waiting for transfers between devices: 2.82 us -> 4.04 us  [body(): rows_out = lax.ppermute(rows_out, ('rec', 'seq'), pairs)]
    pallas_call x15 -> x12, Pallas kernels: 30.8 us -> 31.8 us  [call(): pl.pallas_call(kernel, out_shape=[jax.ShapeDtypeStruct(*o) for o in outs]...]
  transfers between devices with their start and end apart: 45 -> 34, of which waited for: 16 -> 16; matrix products, arithmetic and copies ran while one was open for 8% -> 1% of each run, Pallas kernels for 15% -> 16%
where the time goes in v3:
time: 162 us
  waiting for transfers between devices  62.2 us (38%)
  starting transfers between devices  53.5 us (33%)
  Pallas kernels  31.9 us (20%)
  local copies, waits for them, and re-layouts  12.2 us (8%)
    ppermute x33, waiting for transfers between devices, move(): return lax.ppermute(value, name, pairs)  58.2 us
    ppermute x33, starting transfers between devices, move(): return lax.ppermute(value, name, pairs)  49 us
    pallas_call x12, Pallas kernels, call(): pl.pallas_call(kernel, out_shape=[jax.ShapeDtypeStruct(*o) for o in outs]...  31.8 us
    unnamed x26, local copies, waits for them, and re-layouts  11 us
    ppermute x1, starting transfers between devices, body(): rows_out = lax.ppermute(rows_out, ('rec', 'seq'), pairs)  4.51 us
    ppermute x1, waiting for transfers between devices, body(): rows_out = lax.ppermute(rows_out, ('rec', 'seq'), pairs)  4.04 us
  transfers between devices with their start and end apart: 34, of which 16 were waited for; matrix products, arithmetic and copies ran while one was open for 1% of the time, Pallas kernels for 16%

profile of v3, /device:TPU:6, one launch (start us, length us, event | category | flops | bytes accessed | tf_op | source)
XLA Modules:
  0.0 161.6 jit_solution(14472440964788958795)
XLA Ops:
  0.7 1.1 copy-done.1
  1.8 1.0 copy-done.2
  2.8 0.7 copy-done.3
  4.1 1.6 %collective-permute-start = (f32[264,768]{1,0:T(8,128)S(1)}, f32[264,768]{1,0:T(8,128)S(1)}, u32[]{:S(2)}, u32[]{:S(2)}) collective-permute-start(f32[264,768]{1,0:T(8,128)S(1)} %get-tuple-element.63.t0), channel_id=1, source_target_pairs={{0,3},{1,0},{2,1},{3,2},{4,7},{5,4},{6,5},{7,6},{8,11},{9,8},{10,9... | collective-permute-start | bytes 2433032 | tf_op jit(solution)/shard_map/ppermute | solution.py:48
  5.7 0.9 copy-done.4
  6.6 16.9 %collective-permute-done.1.t3 = f32[264,768]{1,0:T(8,128)S(1)} collective-permute-done((f32[264,768]{1,0:T(8,128)S(1)}, f32[264,768]{1,0:T(8,128)S(1)}, u32[]{:S(2)}, u32[]{:S(2)}) %collective-permute-start.1) | collective-permute-done | bytes 811040 | tf_op jit(solution)/shard_map/ppermute | solution.py:48
  23.5 1.5 collective-permute-start.2
  25.0 0.9 copy-done.6
  25.9 0.9 copy-done.8
  26.8 0.5 collective-permute-start.3
  27.3 18.8 %collective-permute-done.3.c1 = f32[256,768]{1,0:T(8,128)} collective-permute-done((f32[256,768]{1,0:T(8,128)S(1)}, f32[256,768]{1,0:T(8,128)}, u32[]{:S(2)}, u32[]{:S(2)}) %collective-permute-start.3) | collective-permute-done | bytes 786464 | tf_op jit(solution)/shard_map/ppermute | solution.py:48
  46.1 0.9 copy-done.10
  47.0 3.2 %collective-permute-start.5 = (f32[256,768]{1,0:T(8,128)S(1)}, f32[256,768]{1,0:T(8,128)}, u32[]{:S(2)}, u32[]{:S(2)}) collective-permute-start(f32[256,768]{1,0:T(8,128)S(1)} %get-tuple-element.73.c0), channel_id=1, source_target_pairs={{0,1},{1,2},{2,3},{3,0},{4,5},{5,6},{6,7},{7,4},{8,9},{9,10},{10,1... | collective-permute-start | bytes 2359304 | tf_op jit(solution)/shard_map/ppermute | solution.py:48
  50.4 1.1 copy-done.5
  51.6 1.1 copy-done.7
  52.7 1.1 copy-done.9
  53.9 1.1 copy-done.11
  55.0 8.0 %shard_map.94 = (f32[4,8,256]{2,1,0:T(8,128)S(1)}, f32[4,8,256]{2,1,0:T(8,128)S(1)}, f32[4,256,384]{2,1,0:T(8,128)S(1)}, f32[4,256,384]{2,1,0:T(8,128)S(1)}, bf1...) custom-call(s32[4]{0:T(128)S(1)} %pad_add_fusion.at, ...), custom_call_target="tpu_custom_call" | custom-call | flops 1207959552 | bytes 4227088 | tf_op jit(solution)/shard_map/pallas_call | solution.py:374
  63.1 2.0 %collective-permute-start.9 = (f32[136,384]{1,0:T(8,128)S(1)}, f32[136,384]{1,0:T(8,128)S(1)}, u32[]{:S(2)}, u32[]{:S(2)}) collective-permute-start(f32[136,384]{1,0:T(8,128)S(1)} %get-tuple-element.89), channel_id=1, source_target_pairs={{0,4},{1,5},{2,6},{3,7},{4,8},{5,9},{6,10},{7,11},{8,12},{9,13},{1... | collective-permute-start | bytes 626696 | tf_op jit(solution)/shard_map/ppermute | solution.py:48
  65.0 1.5 collective-permute-start.10
  66.5 2.1 %collective-permute-start.11 = (f32[136,384]{1,0:T(8,128)S(1)}, f32[136,384]{1,0:T(8,128)S(1)}, u32[]{:S(2)}, u32[]{:S(2)}) collective-permute-start(f32[136,384]{1,0:T(8,128)S(1)} %get-tuple-element.91), channel_id=1, source_target_pairs={{0,8},{1,9},{2,10},{3,11},{4,12},{5,13},{6,14},{7,15},{8,0},{9,1},... | collective-permute-start | bytes 626696 | tf_op jit(solution)/shard_map/ppermute | solution.py:48
  68.7 1.1 constant_dynamic-slice_fusion.w_out
  69.8 2.5 %shard_map.95 = (bf16[2,256,768]{2,1,0:T(8,128)(2,1)S(1)}, bf16[2,256,384]{2,1,0:T(8,128)(2,1)S(1)}, bf16[2,256,768]{2,1,0:T(8,128)(2,1)S(1)}, f32[2,128,768]{2,1,0:T(8,128)S(1)}) custom-call(s32[4]{0:T(128)S(1)} %pad_add_fusion.at, f32[256,768]{1,0:T(8,128)S(1)} %get-tuple-element.73.c0, f32[256,768]{1,0:T(8,128)} %collective-permute-done.3.c1, ...), custom_call_target="tpu_custom_call" | custom-call | flops 402653184 | bytes 5832720 | tf_op jit(solution)/shard_map/pallas_call | solution.py:374
  72.3 3.0 %shard_map.96 = (bf16[2,256,768]{2,1,0:T(8,128)(2,1)S(1)}, bf16[2,256,384]{2,1,0:T(8,128)(2,1)S(1)}, bf16[2,256,768]{2,1,0:T(8,128)(2,1)S(1)}, f32[2,4,128,384]{...) custom-call(s32[4]{0:T(128)S(1)} %pad_add_fusion.at, ...), custom_call_target="tpu_custom_call" | custom-call | flops 402653184 | bytes 6619152 | tf_op jit(solution)/shard_map/pallas_call | solution.py:374
  75.3 0.7 collective-permute-start.6
  76.0 2.6 %collective-permute-start.7 = (f32[136,384]{1,0:T(8,128)S(1)}, f32[136,384]{1,0:T(8,128)S(1)}, u32[]{:S(2)}, u32[]{:S(2)}) collective-permute-start(f32[136,384]{1,0:T(8,128)S(1)} %get-tuple-element.77), channel_id=1, source_target_pairs={{0,12},{1,13},{2,14},{3,15},{4,0},{5,1},{6,2},{7,3},{8,4},{9,5},{1... | collective-permute-start | bytes 626696 | tf_op jit(solution)/shard_map/ppermute | solution.py:48
  78.8 7.5 %shard_map.97 = (f32[2,384,384]{2,1,0:T(8,128)S(1)}, f32[4,256,384]{2,1,0:T(8,128)S(1)}, f32[4,256,128]{2,1,0:T(8,128)S(1)}, f32[4,256,128]{2,1,0:T(8,128)S(1)}) custom-call(s32[4]{0:T(128)S(1)} %pad_add_fusion.at, bf16[4,256,384]{2,1,0:T(8,128)(2,1)S(1)} %get-tuple-element.79.xs, bf16[4,256,256]{2,1,0:T(8,128)(2,1)S(1)} %get-tuple-element.69.bc, ...), custom_call_target="tpu_custom_call" | custom-call | flops 2214592512 | bytes 10653712 | tf_op jit(solution)/shard_map/pallas_call | solution.py:374
  86.4 4.0 %shard_map.98 = (f32[384,1024]{1,0:T(8,128)S(1)}, f32[384,1024]{1,0:T(8,128)S(1)}, bf16[4,256,640]{2,1,0:T(8,128)(2,1)S(1)}) custom-call(s32[4]{0:T(128)S(1)} %pad_add_fusion.at, bf16[4,256,768]{2,1,0:T(8,128)(2,1)S(1)} %get-tuple-element.67.tokb, bf16[4,256,768]{2,1,0:T(8,128)(2,1)S(1)} %get-tuple-element.68.xfr, ...), custom_call_target="tpu_custom_call" | custom-call | flops 1409286144 | bytes 12816400 | tf_op jit(solution)/shard_map/pallas_call | solution.py:374
  90.5 2.0 %shard_map.99 = (f32[256,768]{1,0:T(8,128)S(1)}, f32[256,768]{1,0:T(8,128)S(1)}, f32[128,768]{1,0:T(8,128)S(1)}, f32[128,768]{1,0:T(8,128)S(1)}, f32[256,768]{1,0:T(8,128)S(1)}) custom-call(s32[4]{0:T(128)S(1)} %pad_add_fusion.at, bf16[4,256,640]{2,1,0:T(8,128)(2,1)S(1)} %get-tuple-element.96.dz, bf16[768,384]{1,0:T(8,128)(2,1)S(1)} %constant_dynamic-slice_fusion.1.w_in, ...), custom_call_target="tpu_custom_call" | custom-call | flops 1006632960 | bytes 2293776 | tf_op jit(solution)/shard_map/pallas_call | solution.py:374
  92.5 2.0 %collective-permute-start.13 = (f32[128,768]{1,0:T(8,128)S(1)}, f32[128,768]{1,0:T(8,128)S(1)}, u32[]{:S(2)}, u32[]{:S(2)}) collective-permute-start(f32[128,768]{1,0:T(8,128)S(1)} %get-tuple-element.101), channel_id=1, source_target_pairs={{0,3},{1,0},{2,1},{3,2},{4,7},{5,4},{6,5},{7,6},{8,11},{9,8},{10,9... | collective-permute-start | bytes 1179656 | tf_op jit(solution)/shard_map/ppermute | solution.py:48
  94.6 0.8 shard_map.101
  95.4 0.7 collective-permute-start.17
  96.1 2.7 %collective-permute-start.18 = (f32[96,1024]{1,0:T(8,128)S(1)}, f32[96,1024]{1,0:T(8,128)S(1)}, u32[]{:S(2)}, u32[]{:S(2)}) collective-permute-start(f32[96,1024]{1,0:T(8,128)S(1)} %get-tuple-element.108), channel_id=1, source_target_pairs={{0,8},{1,9},{2,10},{3,11},{4,12},{5,13},{6,14},{7,15},{8,0},{9,1},... | collective-permute-start | bytes 1179656 | tf_op jit(solution)/shard_map/ppermute | solution.py:48
  98.8 2.5 %collective-permute-start.19 = (f32[96,1024]{1,0:T(8,128)S(1)}, f32[96,1024]{1,0:T(8,128)S(1)}, u32[]{:S(2)}, u32[]{:S(2)}) collective-permute-start(f32[96,1024]{1,0:T(8,128)S(1)} %get-tuple-element.109), channel_id=1, source_target_pairs={{0,12},{1,13},{2,14},{3,15},{4,0},{5,1},{6,2},{7,3},{8,4},{9,5},{1... | collective-permute-start | bytes 1179656 | tf_op jit(solution)/shard_map/ppermute | solution.py:48
  101.4 2.6 %collective-permute-done.12.r_a = f32[128,768]{1,0:T(8,128)S(1)} collective-permute-done((f32[128,768]{1,0:T(8,128)S(1)}, f32[128,768]{1,0:T(8,128)S(1)}, u32[]{:S(2)}, u32[]{:S(2)}) %collective-permute-start.12) | collective-permute-done | bytes 393248 | tf_op jit(solution)/shard_map/ppermute | solution.py:48
  104.0 1.3 collective-permute-done.13.r_b
  105.3 0.7 shard_map.100
  106.0 0.5 collective-permute-start.15
  106.5 2.8 %collective-permute-start.14 = (f32[256,768]{1,0:T(8,128)S(1)}, f32[256,768]{1,0:T(8,128)S(1)}, u32[]{:S(2)}, u32[]{:S(2)}) collective-permute-start(f32[256,768]{1,0:T(8,128)S(1)} %get-tuple-element.102), channel_id=1, source_target_pairs={{0,1},{1,2},{2,3},{3,0},{4,5},{5,6},{6,7},{7,4},{8,9},{9,10},{10,1... | collective-permute-start | bytes 2359304 | tf_op jit(solution)/shard_map/ppermute | solution.py:48
  109.3 7.1 %collective-permute-done.18.refs_2_ = f32[96,1024]{1,0:T(8,128)S(1)} collective-permute-done((f32[96,1024]{1,0:T(8,128)S(1)}, f32[96,1024]{1,0:T(8,128)S(1)}, u32[]{:S(2)}, u32[]{:S(2)}) %collective-permute-start.18) | collective-permute-done | bytes 393248 | tf_op jit(solution)/shard_map/ppermute | solution.py:48
  116.6 0.7 shard_map.102
  117.3 2.1 %collective-permute-start.20 = (f32[24,1024]{1,0:T(8,128)S(1)}, f32[24,1024]{1,0:T(8,128)S(1)}, u32[]{:S(2)}, u32[]{:S(2)}) collective-permute-start(f32[24,1024]{1,0:T(8,128)S(1)} %get-tuple-element.111), channel_id=1, source_target_pairs={{0,32},{16,48},{32,64},{48,80},{64,96},{80,112},{96,0},{112,16},{1... | collective-permute-start | bytes 294920 | tf_op jit(solution)/shard_map/ppermute | solution.py:48
  119.5 3.6 %collective-permute-start.21 = (f32[24,1024]{1,0:T(8,128)S(1)}, f32[24,1024]{1,0:T(8,128)S(1)}, u32[]{:S(2)}, u32[]{:S(2)}) collective-permute-start(f32[24,1024]{1,0:T(8,128)S(1)} %get-tuple-element.112), channel_id=1, source_target_pairs={{0,64},{16,80},{32,96},{48,112},{64,0},{80,16},{96,32},{112,48},{1... | collective-permute-start | bytes 294920 | tf_op jit(solution)/shard_map/ppermute | solution.py:48
  123.0 1.0 collective-permute-start.22
  124.0 1.2 collective-permute-done.20.b
  125.2 1.6 collective-permute-done.21.c
  126.8 0.8 collective-permute-done.22.d
  127.7 0.7 shard_map.103
  128.4 1.6 %collective-permute-start.23 = (f32[40,384]{1,0:T(8,128)S(1)}, f32[40,384]{1,0:T(8,128)S(1)}, u32[]{:S(2)}, u32[]{:S(2)}) collective-permute-start(f32[40,384]{1,0:T(8,128)S(1)} %get-tuple-element.115), channel_id=1, source_target_pairs={{0,1},{1,2},{2,3},{3,0},{4,5},{5,6},{6,7},{7,4},{8,9},{9,10},{10,1... | collective-permute-start | bytes 184328 | tf_op jit(solution)/shard_map/ppermute | solution.py:48
  130.0 0.8 collective-permute-start.24
  130.9 1.7 %collective-permute-done.23.b = f32[40,384]{1,0:T(8,128)S(1)} collective-permute-done((f32[40,384]{1,0:T(8,128)S(1)}, f32[40,384]{1,0:T(8,128)S(1)}, u32[]{:S(2)}, u32[]{:S(2)}) %collective-permute-start.23) | collective-permute-done | bytes 61472 | tf_op jit(solution)/shard_map/ppermute | solution.py:48
  132.6 3.1 %collective-permute-done.24.c = f32[40,384]{1,0:T(8,128)S(1)} collective-permute-done((f32[40,384]{1,0:T(8,128)S(1)}, f32[40,384]{1,0:T(8,128)S(1)}, u32[]{:S(2)}, u32[]{:S(2)}) %collective-permute-start.24) | collective-permute-done | bytes 61472 | tf_op jit(solution)/shard_map/ppermute | solution.py:48
  135.7 0.6 collective-permute-done.25.d
  136.4 0.7 shard_map.104
  137.1 3.5 %collective-permute-start.29 = (f32[8,128]{1,0:T(8,128)S(1)}, f32[8,128]{1,0:T(8,128)S(1)}, u32[]{:S(2)}, u32[]{:S(2)}) collective-permute-start(f32[8,128]{1,0:T(8,128)S(1)} %shard_map.104), channel_id=1, source_target_pairs={{0,8},{1,9},{2,10},{3,11},{4,12},{5,13},{6,14},{7,15},{8,0},{9,1},... | collective-permute-start | bytes 12296 | tf_op jit(solution)/shard_map/ppermute | solution.py:48
  141.0 2.7 %collective-permute-start.28 = (f32[8,128]{1,0:T(8,128)S(1)}, f32[8,128]{1,0:T(8,128)S(1)}, u32[]{:S(2)}, u32[]{:S(2)}) collective-permute-start(f32[8,128]{1,0:T(8,128)S(1)} %shard_map.104), channel_id=1, source_target_pairs={{0,12},{1,13},{2,14},{3,15},{4,0},{5,1},{6,2},{7,3},{8,4},{9,5},{1... | collective-permute-start | bytes 12296 | tf_op jit(solution)/shard_map/ppermute | solution.py:48
  143.8 1.6 collective-permute-done.27
  145.4 1.6 %collective-permute-start.32 = (f32[8,128]{1,0:T(8,128)S(1)}, f32[8,128]{1,0:T(8,128)S(1)}, u32[]{:S(2)}, u32[]{:S(2)}) collective-permute-start(f32[8,128]{1,0:T(8,128)S(1)} %add_add_fusion.1), channel_id=1, source_target_pairs={{0,64},{16,80},{32,96},{48,112},{64,0},{80,16},{96,32},{112,48},{1... | collective-permute-start | bytes 12296 | tf_op jit(solution)/shard_map/ppermute | solution.py:48
  147.0 1.5 collective-permute-start.30
  148.5 1.7 %collective-permute-start.31 = (f32[8,128]{1,0:T(8,128)S(1)}, f32[8,128]{1,0:T(8,128)S(1)}, u32[]{:S(2)}, u32[]{:S(2)}) collective-permute-start(f32[8,128]{1,0:T(8,128)S(1)} %add_add_fusion.1), channel_id=1, source_target_pairs={{0,96},{16,112},{32,0},{48,16},{64,32},{80,48},{96,64},{112,80},{1... | collective-permute-start | bytes 12296 | tf_op jit(solution)/shard_map/ppermute | solution.py:48
  150.6 4.5 %collective-permute-start.26 = (f32[24,384]{1,0:T(8,128)S(1)}, f32[24,384]{1,0:T(8,128)S(1)}, u32[]{:S(2)}, u32[]{:S(2)}) collective-permute-start(f32[24,384]{1,0:T(8,128)S(1)} %get-tuple-element.118), channel_id=1, source_target_pairs={{0,0},{1,32},{2,64},{3,96},{4,1},{5,33},{6,65},{7,97},{8,2},{9,34}... | collective-permute-start | bytes 110600 | tf_op jit(solution)/shard_map/ppermute | solution.py:473
  155.2 0.9 fusion
  156.4 4.0 %collective-permute-done.26.rows_out = f32[24,384]{1,0:T(8,128)S(1)} collective-permute-done((f32[24,384]{1,0:T(8,128)S(1)}, f32[24,384]{1,0:T(8,128)S(1)}, u32[]{:S(2)}, u32[]{:S(2)}) %collective-permute-start.26) | collective-permute-done | bytes 36896 | tf_op jit(solution)/shard_map/ppermute | solution.py:473
  160.4 1.2 shard_map.105
  (50 shorter events, 2.7 us)
Async XLA Ops:
  0.6 49.7 %copy-start = (bf16[768,1536]{1,0:T(8,128)(2,1)S(1)}, bf16[768,1536]{1,0:T(8,128)(2,1)}, u32[]{:S(2)}) copy-start(bf16[768,1536]{1,0:T(8,128)(2,1)} %param.9) | copy-start | bytes 7077892
  0.6 1.1 copy-start.1
  1.8 1.0 copy-start.2
  2.8 0.7 copy-start.3
  3.5 46.9 %copy-start.12 = (bf16[768,256]{1,0:T(8,128)(2,1)S(1)}, bf16[768,256]{1,0:T(8,128)(2,1)}, u32[]{:S(2)}) copy-start(bf16[768,256]{1,0:T(8,128)(2,1)} %w_bc.3) | copy-start | bytes 1179652
  3.6 19.9 %collective-permute-start.1 = (f32[264,768]{1,0:T(8,128)S(1)}, f32[264,768]{1,0:T(8,128)S(1)}, u32[]{:S(2)}, u32[]{:S(2)}) collective-permute-start(f32[264,768]{1,0:T(8,128)S(1)} %get-tuple-element.63.t0), channel_id=1, source_target_pairs={{0,1},{1,2},{2,3},{3,0},{4,5},{5,6},{6,7},{7,4},{8,9},{9,10},{10,1... | collective-permute-start | bytes 2433032 | tf_op jit(solution)/shard_map/ppermute | solution.py:48
  4.1 21.8 %collective-permute-start = (f32[264,768]{1,0:T(8,128)S(1)}, f32[264,768]{1,0:T(8,128)S(1)}, u32[]{:S(2)}, u32[]{:S(2)}) collective-permute-start(f32[264,768]{1,0:T(8,128)S(1)} %get-tuple-element.63.t0), channel_id=1, source_target_pairs={{0,3},{1,0},{2,1},{3,2},{4,7},{5,4},{6,5},{7,6},{8,11},{9,8},{10,9... | collective-permute-start | bytes 2433032 | tf_op jit(solution)/shard_map/ppermute | solution.py:48
  5.7 0.9 copy-start.4
  23.5 22.6 %collective-permute-start.2 = (f32[264,768]{1,0:T(8,128)S(1)}, f32[264,768]{1,0:T(8,128)S(1)}, u32[]{:S(2)}, u32[]{:S(2)}) collective-permute-start(f32[264,768]{1,0:T(8,128)S(1)} %collective-permute-done.1.t3), channel_id=1, source_target_pairs={{0,1},{1,2},{2,3},{3,0},{4,5},{5,6},{6,7},{7,4},{8,9},{9,10},{10,1... | collective-permute-start | bytes 2433032 | tf_op jit(solution)/shard_map/ppermute | solution.py:48
  25.0 0.9 copy-start.6
  25.9 0.9 copy-start.8
  26.8 19.3 %collective-permute-start.3 = (f32[256,768]{1,0:T(8,128)S(1)}, f32[256,768]{1,0:T(8,128)}, u32[]{:S(2)}, u32[]{:S(2)}) collective-permute-start(f32[256,768]{1,0:T(8,128)S(1)} %get-tuple-element.73.c0), channel_id=1, source_target_pairs={{0,3},{1,0},{2,1},{3,2},{4,7},{5,4},{6,5},{7,6},{8,11},{9,8},{10,9... | collective-permute-start | bytes 2359304 | tf_op jit(solution)/shard_map/ppermute | solution.py:48
  46.1 26.2 %collective-permute-start.4 = (f32[256,768]{1,0:T(8,128)}, f32[256,768]{1,0:T(8,128)}, u32[]{:S(2)}, u32[]{:S(2)}) collective-permute-start(f32[256,768]{1,0:T(8,128)} %collective-permute-done.3.c1), channel_id=1, source_target_pairs={{0,3},{1,0},{2,1},{3,2},{4,7},{5,4},{6,5},{7,6},{8,11},{9,8},{10,9... | collective-permute-start | bytes 2359304 | tf_op jit(solution)/shard_map/ppermute | solution.py:48
  46.1 0.9 copy-start.10
  47.0 25.2 %collective-permute-start.5 = (f32[256,768]{1,0:T(8,128)S(1)}, f32[256,768]{1,0:T(8,128)}, u32[]{:S(2)}, u32[]{:S(2)}) collective-permute-start(f32[256,768]{1,0:T(8,128)S(1)} %get-tuple-element.73.c0), channel_id=1, source_target_pairs={{0,1},{1,2},{2,3},{3,0},{4,5},{5,6},{6,7},{7,4},{8,9},{9,10},{10,1... | collective-permute-start | bytes 2359304 | tf_op jit(solution)/shard_map/ppermute | solution.py:48
  50.4 1.1 copy-start.5
  51.6 1.1 copy-start.7
  52.7 1.1 copy-start.9
  53.9 1.1 copy-start.11
  63.1 15.5 %collective-permute-start.9 = (f32[136,384]{1,0:T(8,128)S(1)}, f32[136,384]{1,0:T(8,128)S(1)}, u32[]{:S(2)}, u32[]{:S(2)}) collective-permute-start(f32[136,384]{1,0:T(8,128)S(1)} %get-tuple-element.89), channel_id=1, source_target_pairs={{0,4},{1,5},{2,6},{3,7},{4,8},{5,9},{6,10},{7,11},{8,12},{9,13},{1... | collective-permute-start | bytes 626696 | tf_op jit(solution)/shard_map/ppermute | solution.py:48
  65.0 13.8 %collective-permute-start.10 = (f32[136,384]{1,0:T(8,128)S(1)}, f32[136,384]{1,0:T(8,128)S(1)}, u32[]{:S(2)}, u32[]{:S(2)}) collective-permute-start(f32[136,384]{1,0:T(8,128)S(1)} %get-tuple-element.90), channel_id=1, source_target_pairs={{0,12},{1,13},{2,14},{3,15},{4,0},{5,1},{6,2},{7,3},{8,4},{9,5},{1... | collective-permute-start | bytes 626696 | tf_op jit(solution)/shard_map/ppermute | solution.py:48
  66.5 12.3 %collective-permute-start.11 = (f32[136,384]{1,0:T(8,128)S(1)}, f32[136,384]{1,0:T(8,128)S(1)}, u32[]{:S(2)}, u32[]{:S(2)}) collective-permute-start(f32[136,384]{1,0:T(8,128)S(1)} %get-tuple-element.91), channel_id=1, source_target_pairs={{0,8},{1,9},{2,10},{3,11},{4,12},{5,13},{6,14},{7,15},{8,0},{9,1},... | collective-permute-start | bytes 626696 | tf_op jit(solution)/shard_map/ppermute | solution.py:48
  75.3 11.1 %collective-permute-start.6 = (f32[136,384]{1,0:T(8,128)S(1)}, f32[136,384]{1,0:T(8,128)S(1)}, u32[]{:S(2)}, u32[]{:S(2)}) collective-permute-start(f32[136,384]{1,0:T(8,128)S(1)} %get-tuple-element.76), channel_id=1, source_target_pairs={{0,4},{1,5},{2,6},{3,7},{4,8},{5,9},{6,10},{7,11},{8,12},{9,13},{1... | collective-permute-start | bytes 626696 | tf_op jit(solution)/shard_map/ppermute | solution.py:48
  76.0 10.3 %collective-permute-start.7 = (f32[136,384]{1,0:T(8,128)S(1)}, f32[136,384]{1,0:T(8,128)S(1)}, u32[]{:S(2)}, u32[]{:S(2)}) collective-permute-start(f32[136,384]{1,0:T(8,128)S(1)} %get-tuple-element.77), channel_id=1, source_target_pairs={{0,12},{1,13},{2,14},{3,15},{4,0},{5,1},{6,2},{7,3},{8,4},{9,5},{1... | collective-permute-start | bytes 626696 | tf_op jit(solution)/shard_map/ppermute | solution.py:48
  78.6 7.8 %collective-permute-start.8 = (f32[136,384]{1,0:T(8,128)S(1)}, f32[136,384]{1,0:T(8,128)S(1)}, u32[]{:S(2)}, u32[]{:S(2)}) collective-permute-start(f32[136,384]{1,0:T(8,128)S(1)} %get-tuple-element.78), channel_id=1, source_target_pairs={{0,8},{1,9},{2,10},{3,11},{4,12},{5,13},{6,14},{7,15},{8,0},{9,1},... | collective-permute-start | bytes 626696 | tf_op jit(solution)/shard_map/ppermute | solution.py:48
  90.4 4.2 %collective-permute-start.16 = (f32[384,1024]{1,0:T(8,128)S(1)}, f32[384,1024]{1,0:T(8,128)S(1)}, u32[]{:S(2)}, u32[]{:S(2)}) collective-permute-start(f32[384,1024]{1,0:T(8,128)S(1)} %get-tuple-element.105), channel_id=1, source_target_pairs={{0,16},{16,0},{32,48},{48,32},{64,80},{80,64},{96,112},{112,96},{1... | collective-permute-start | bytes 4718600 | tf_op jit(solution)/shard_map/ppermute | solution.py:48
  92.5 11.6 %collective-permute-start.12 = (f32[128,768]{1,0:T(8,128)S(1)}, f32[128,768]{1,0:T(8,128)S(1)}, u32[]{:S(2)}, u32[]{:S(2)}) collective-permute-start(f32[128,768]{1,0:T(8,128)S(1)} %get-tuple-element.100), channel_id=1, source_target_pairs={{0,1},{1,2},{2,3},{3,0},{4,5},{5,6},{6,7},{7,4},{8,9},{9,10},{10,1... | collective-permute-start | bytes 1179656 | tf_op jit(solution)/shard_map/ppermute | solution.py:48
  92.5 12.8 %collective-permute-start.13 = (f32[128,768]{1,0:T(8,128)S(1)}, f32[128,768]{1,0:T(8,128)S(1)}, u32[]{:S(2)}, u32[]{:S(2)}) collective-permute-start(f32[128,768]{1,0:T(8,128)S(1)} %get-tuple-element.101), channel_id=1, source_target_pairs={{0,3},{1,0},{2,1},{3,2},{4,7},{5,4},{6,5},{7,6},{8,11},{9,8},{10,9... | collective-permute-start | bytes 1179656 | tf_op jit(solution)/shard_map/ppermute | solution.py:48
  95.4 14.0 %collective-permute-start.17 = (f32[96,1024]{1,0:T(8,128)S(1)}, f32[96,1024]{1,0:T(8,128)S(1)}, u32[]{:S(2)}, u32[]{:S(2)}) collective-permute-start(f32[96,1024]{1,0:T(8,128)S(1)} %get-tuple-element.107), channel_id=1, source_target_pairs={{0,4},{1,5},{2,6},{3,7},{4,8},{5,9},{6,10},{7,11},{8,12},{9,13},{1... | collective-permute-start | bytes 1179656 | tf_op jit(solution)/shard_map/ppermute | solution.py:48
  96.1 20.3 %collective-permute-start.18 = (f32[96,1024]{1,0:T(8,128)S(1)}, f32[96,1024]{1,0:T(8,128)S(1)}, u32[]{:S(2)}, u32[]{:S(2)}) collective-permute-start(f32[96,1024]{1,0:T(8,128)S(1)} %get-tuple-element.108), channel_id=1, source_target_pairs={{0,8},{1,9},{2,10},{3,11},{4,12},{5,13},{6,14},{7,15},{8,0},{9,1},... | collective-permute-start | bytes 1179656 | tf_op jit(solution)/shard_map/ppermute | solution.py:48
  98.8 17.8 %collective-permute-start.19 = (f32[96,1024]{1,0:T(8,128)S(1)}, f32[96,1024]{1,0:T(8,128)S(1)}, u32[]{:S(2)}, u32[]{:S(2)}) collective-permute-start(f32[96,1024]{1,0:T(8,128)S(1)} %get-tuple-element.109), channel_id=1, source_target_pairs={{0,12},{1,13},{2,14},{3,15},{4,0},{5,1},{6,2},{7,3},{8,4},{9,5},{1... | collective-permute-start | bytes 1179656 | tf_op jit(solution)/shard_map/ppermute | solution.py:48
  106.0 49.2 %collective-permute-start.15 = (f32[256,768]{1,0:T(8,128)S(1)}, f32[256,768]{1,0:T(8,128)S(1)}, u32[]{:S(2)}, u32[]{:S(2)}) collective-permute-start(f32[256,768]{1,0:T(8,128)S(1)} %get-tuple-element.103), channel_id=1, source_target_pairs={{0,3},{1,0},{2,1},{3,2},{4,7},{5,4},{6,5},{7,6},{8,11},{9,8},{10,9... | collective-permute-start | bytes 2359304 | tf_op jit(solution)/shard_map/ppermute | solution.py:48
  106.5 48.7 %collective-permute-start.14 = (f32[256,768]{1,0:T(8,128)S(1)}, f32[256,768]{1,0:T(8,128)S(1)}, u32[]{:S(2)}, u32[]{:S(2)}) collective-permute-start(f32[256,768]{1,0:T(8,128)S(1)} %get-tuple-element.102), channel_id=1, source_target_pairs={{0,1},{1,2},{2,3},{3,0},{4,5},{5,6},{6,7},{7,4},{8,9},{9,10},{10,1... | collective-permute-start | bytes 2359304 | tf_op jit(solution)/shard_map/ppermute | solution.py:48
  117.3 7.9 %collective-permute-start.20 = (f32[24,1024]{1,0:T(8,128)S(1)}, f32[24,1024]{1,0:T(8,128)S(1)}, u32[]{:S(2)}, u32[]{:S(2)}) collective-permute-start(f32[24,1024]{1,0:T(8,128)S(1)} %get-tuple-element.111), channel_id=1, source_target_pairs={{0,32},{16,48},{32,64},{48,80},{64,96},{80,112},{96,0},{112,16},{1... | collective-permute-start | bytes 294920 | tf_op jit(solution)/shard_map/ppermute | solution.py:48
  119.5 7.4 %collective-permute-start.21 = (f32[24,1024]{1,0:T(8,128)S(1)}, f32[24,1024]{1,0:T(8,128)S(1)}, u32[]{:S(2)}, u32[]{:S(2)}) collective-permute-start(f32[24,1024]{1,0:T(8,128)S(1)} %get-tuple-element.112), channel_id=1, source_target_pairs={{0,64},{16,80},{32,96},{48,112},{64,0},{80,16},{96,32},{112,48},{1... | collective-permute-start | bytes 294920 | tf_op jit(solution)/shard_map/ppermute | solution.py:48
  123.0 4.6 %collective-permute-start.22 = (f32[24,1024]{1,0:T(8,128)S(1)}, f32[24,1024]{1,0:T(8,128)S(1)}, u32[]{:S(2)}, u32[]{:S(2)}) collective-permute-start(f32[24,1024]{1,0:T(8,128)S(1)} %get-tuple-element.113), channel_id=1, source_target_pairs={{0,96},{16,112},{32,0},{48,16},{64,32},{80,48},{96,64},{112,80},{1... | collective-permute-start | bytes 294920 | tf_op jit(solution)/shard_map/ppermute | solution.py:48
  128.4 4.3 %collective-permute-start.23 = (f32[40,384]{1,0:T(8,128)S(1)}, f32[40,384]{1,0:T(8,128)S(1)}, u32[]{:S(2)}, u32[]{:S(2)}) collective-permute-start(f32[40,384]{1,0:T(8,128)S(1)} %get-tuple-element.115), channel_id=1, source_target_pairs={{0,1},{1,2},{2,3},{3,0},{4,5},{5,6},{6,7},{7,4},{8,9},{9,10},{10,1... | collective-permute-start | bytes 184328 | tf_op jit(solution)/shard_map/ppermute | solution.py:48
  130.0 5.7 %collective-permute-start.24 = (f32[40,384]{1,0:T(8,128)S(1)}, f32[40,384]{1,0:T(8,128)S(1)}, u32[]{:S(2)}, u32[]{:S(2)}) collective-permute-start(f32[40,384]{1,0:T(8,128)S(1)} %get-tuple-element.116), channel_id=1, source_target_pairs={{0,2},{1,3},{2,0},{3,1},{4,6},{5,7},{6,4},{7,5},{8,10},{9,11},{10,... | collective-permute-start | bytes 184328 | tf_op jit(solution)/shard_map/ppermute | solution.py:48
  130.8 5.6 %collective-permute-start.25 = (f32[40,384]{1,0:T(8,128)S(1)}, f32[40,384]{1,0:T(8,128)S(1)}, u32[]{:S(2)}, u32[]{:S(2)}) collective-permute-start(f32[40,384]{1,0:T(8,128)S(1)} %get-tuple-element.117), channel_id=1, source_target_pairs={{0,3},{1,0},{2,1},{3,2},{4,7},{5,4},{6,5},{7,6},{8,11},{9,8},{10,9... | collective-permute-start | bytes 184328 | tf_op jit(solution)/shard_map/ppermute | solution.py:48
  137.1 6.7 %collective-permute-start.29 = (f32[8,128]{1,0:T(8,128)S(1)}, f32[8,128]{1,0:T(8,128)S(1)}, u32[]{:S(2)}, u32[]{:S(2)}) collective-permute-start(f32[8,128]{1,0:T(8,128)S(1)} %shard_map.104), channel_id=1, source_target_pairs={{0,8},{1,9},{2,10},{3,11},{4,12},{5,13},{6,14},{7,15},{8,0},{9,1},... | collective-permute-start | bytes 12296 | tf_op jit(solution)/shard_map/ppermute | solution.py:48
  140.5 4.8 %collective-permute-start.27 = (f32[8,128]{1,0:T(8,128)S(1)}, f32[8,128]{1,0:T(8,128)S(1)}, u32[]{:S(2)}, u32[]{:S(2)}) collective-permute-start(f32[8,128]{1,0:T(8,128)S(1)} %shard_map.104), channel_id=1, source_target_pairs={{0,4},{1,5},{2,6},{3,7},{4,8},{5,9},{6,10},{7,11},{8,12},{9,13},{1... | collective-permute-start | bytes 12296 | tf_op jit(solution)/shard_map/ppermute | solution.py:48
  141.0 4.3 %collective-permute-start.28 = (f32[8,128]{1,0:T(8,128)S(1)}, f32[8,128]{1,0:T(8,128)S(1)}, u32[]{:S(2)}, u32[]{:S(2)}) collective-permute-start(f32[8,128]{1,0:T(8,128)S(1)} %shard_map.104), channel_id=1, source_target_pairs={{0,12},{1,13},{2,14},{3,15},{4,0},{5,1},{6,2},{7,3},{8,4},{9,5},{1... | collective-permute-start | bytes 12296 | tf_op jit(solution)/shard_map/ppermute | solution.py:48
  145.4 5.2 %collective-permute-start.32 = (f32[8,128]{1,0:T(8,128)S(1)}, f32[8,128]{1,0:T(8,128)S(1)}, u32[]{:S(2)}, u32[]{:S(2)}) collective-permute-start(f32[8,128]{1,0:T(8,128)S(1)} %add_add_fusion.1), channel_id=1, source_target_pairs={{0,64},{16,80},{32,96},{48,112},{64,0},{80,16},{96,32},{112,48},{1... | collective-permute-start | bytes 12296 | tf_op jit(solution)/shard_map/ppermute | solution.py:48
  147.0 8.1 %collective-permute-start.30 = (f32[8,128]{1,0:T(8,128)S(1)}, f32[8,128]{1,0:T(8,128)S(1)}, u32[]{:S(2)}, u32[]{:S(2)}) collective-permute-start(f32[8,128]{1,0:T(8,128)S(1)} %add_add_fusion.1), channel_id=1, source_target_pairs={{0,32},{16,48},{32,64},{48,80},{64,96},{80,112},{96,0},{112,16},{1... | collective-permute-start | bytes 12296 | tf_op jit(solution)/shard_map/ppermute | solution.py:48
  148.5 6.6 %collective-permute-start.31 = (f32[8,128]{1,0:T(8,128)S(1)}, f32[8,128]{1,0:T(8,128)S(1)}, u32[]{:S(2)}, u32[]{:S(2)}) collective-permute-start(f32[8,128]{1,0:T(8,128)S(1)} %add_add_fusion.1), channel_id=1, source_target_pairs={{0,96},{16,112},{32,0},{48,16},{64,32},{80,48},{96,64},{112,80},{1... | collective-permute-start | bytes 12296 | tf_op jit(solution)/shard_map/ppermute | solution.py:48
  150.6 9.8 %collective-permute-start.26 = (f32[24,384]{1,0:T(8,128)S(1)}, f32[24,384]{1,0:T(8,128)S(1)}, u32[]{:S(2)}, u32[]{:S(2)}) collective-permute-start(f32[24,384]{1,0:T(8,128)S(1)} %get-tuple-element.118), channel_id=1, source_target_pairs={{0,0},{1,32},{2,64},{3,96},{4,1},{5,33},{6,65},{7,97},{8,2},{9,34}... | collective-permute-start | bytes 110600 | tf_op jit(solution)/shard_map/ppermute | solution.py:473
  155.1 1.2 collective-permute-start.33

commit v4 on v3

--- a/solution.py
+++ b/solution.py
@@ -59,7 +59,8 @@
 
 
 def place(p, x):
-    return lax.rem(p - x + NX, NX)
+    k = lax.rem(p - x + NX, NX)
+    return k ^ (k >> 1)
 
 
 def vm(n):
@@ -67,7 +68,7 @@
 
 
 SMEM = pl.BlockSpec(memory_space=pltpu.SMEM)
-PARAMS = pltpu.CompilerParams(vmem_limit_bytes=30 * 2**20)
+PARAMS = pltpu.CompilerParams(vmem_limit_bytes=20 * 2**20)
 
 
 def send_rows(up, down, log, y, s_p, s_m, s_2):
@@ -106,14 +107,13 @@
 FIRST, SECOND = slice(0, HC), slice(HC, 2 * HC)
 
 
-def pack_kernel(tok, cot, log, out, cot_out):
-    cot_out[...] = cot[...].astype(F32)
+def pack_kernel(tok, log, out):
     out[:SEG] = tok[...].astype(F32)
     for part in range(3):
         out[SEG:, SEG * part : SEG * part + SEG] = log[8 * part : 8 * part + 8]
 
 
-def decays(x, toks, cirow, cerow, ci, ce, la):
+def decays(x, toks, first, cirow, cerow, ci, ce, la):
     s = lax.broadcasted_iota(jnp.int32, (SEG, SEG), 0)
     t = lax.broadcasted_iota(jnp.int32, (SEG, SEG), 1)
     tri = jnp.where(s <= t, 1.0, 0.0).astype(F32)
@@ -121,7 +121,7 @@
     lane = lax.broadcasted_iota(jnp.int32, (8, HC), 1)
     spread = jnp.where((lane >= head) & (lane < head + HD), 1.0, 0.0).astype(F32)
     la[...] = jnp.zeros((8, SEG), F32)
-    for k, tok in enumerate(toks):
+    for k, tok in enumerate(toks, first):
         for j in range(NH):
             mine = jnp.zeros((1, SEG), F32)
             for p in range(NX):
@@ -137,16 +137,13 @@
         ce[k] = exact(before, spread, 0, 0)
 
 
-def tok_kernel(
-    at, t0, t1, t2, t3, w_in, w_bc,
-    cirow, cerow, ci, ce, tokb, xs, xfr, bc, pre, s_p, s_m, s_2, ends, la,
-):
-    x, y = at[0], at[2]
-    decays(x, (t0, t1, t2, t3), cirow, cerow, ci, ce, la)
-    for k, t in enumerate((t0, t1, t2, t3)):
+def tok_part(at, toks, first, w_in, w_bc, cirow, cerow, ci, ce, tokb, xs, xfr, bc, ends, la):
+    decays(at[0], toks, first, cirow, cerow, ci, ce, la)
+    for k, t in enumerate(toks, first):
         tokb[k] = t[:SEG].astype(BF16)
 
-    def segment(k, _):
+    def segment(i, _):
+        k = first + i
         t = tokb[k]
         xv = dot(t, w_in[...], 1, 0).astype(BF16)
         bv = dot(t, w_bc[...], 1, 0).astype(BF16)
@@ -159,7 +156,20 @@
         ends[k] = dot(bv[:, :NS], xfr[k], 0, 0)
         return 0
 
-    lax.fori_loop(0, NX, segment, 0)
+    lax.fori_loop(0, len(toks), segment, 0)
+
+
+def tok_kernel_a(at, t0, t1, t3, w_in, w_bc, *refs):
+    tok_part(at, (t0, t1, t3), 0, w_in, w_bc, *refs)
+
+
+def tok_kernel_b(at, t2, w_in, w_bc, *refs):
+    given, full, (pre, s_p, s_m, s_2, ends, la) = refs[:9], refs[9:17], refs[17:]
+    full = (*full, ends)
+    for a, b in zip(given, full, strict=True):
+        b[: NX - 1] = a[...]
+    tok_part(at, (t2,), NX - 1, w_in, w_bc, *full, la)
+    x, y, ci = at[0], at[2], full[2]
     up = row_scan(range(NX), ends, FIRST, ci, x, pre, 0)
     down = row_scan(reversed(range(NX)), ends, SECOND, ci, x, pre, 1)
     send_rows(up, down, row_log(ci), y, s_p, s_m, s_2)
@@ -303,11 +313,11 @@
     def tokens_of(k):
         return dot(dz[k, :, :HC], w_in[...], 1, 1) + dot(dz[k, :, HC:], w_bc[...], 1, 1)
 
-    d = tokens_of(2)
+    d = tokens_of(3)
     d2a[...] = d[:HALF]
     d2b[...] = d[HALF:]
     d1[...] = tokens_of(1)
-    d3[...] = tokens_of(3)
+    d3[...] = tokens_of(2)
     d0[...] = tokens_of(0)
 
 
@@ -400,43 +410,52 @@
     at = jnp.stack([x, rec % 2, seq // NX, rec // 2]).astype(jnp.int32)
     tie = lax.optimization_barrier
 
-    t0, c0 = pl.pallas_call(
+    (t0,) = pl.pallas_call(
         pack_kernel,
-        out_shape=[jax.ShapeDtypeStruct((SEG + 8, DM), F32), jax.ShapeDtypeStruct((SEG, DM), F32)],
-        in_specs=vm(3),
-        out_specs=vm(2),
+        out_shape=[jax.ShapeDtypeStruct((SEG + 8, DM), F32)],
+        in_specs=vm(2),
+        out_specs=vm(1),
         compiler_params=PARAMS,
-    )(tokens[0], cotangent[0], log_decay[0])
-    t3, t1 = move(t0, "x", 1), move(t0, "x", -1)
+    )(tokens[0], log_decay[0])
+    c0 = cotangent[0].astype(F32)
     wi = lax.dynamic_slice(w_in, (0, x * HC), (DM, HC))
     wo = lax.dynamic_slice(w_out, (x * HC, 0), (HC, DM))
+    t3, t1 = move(t0, "x", 1), move(t0, "x", -1)
+    t3, t1, c0 = tie((t3, t1, c0))
     t2 = move(t3, "x", 1)
-    c0_l, t1 = tie((c0, t1))
-    c1 = move(c0_l, "x", -1)
-    c0_r, t2 = tie((c0, t2))
-    c3 = move(c0_r, "x", 1)
-    c2 = move(c1, "x", -1)
+    c1 = move(c0, "x", -1)
+    t1, wi, wo = tie((t1, wi, wo))
 
     tall = ((TALL, HC), F32)
     edges = ((2, NX, NS, HC), F32)
-    ends = ((NX, NS, 2 * HC), F32)
+
+    def of_tokens(n):
+        return [
+            ((n, 8, SEG), F32), ((n, 8, SEG), F32), ((n, SEG, HC), F32), ((n, SEG, HC), F32),
+            ((n, SEG, DM), BF16), ((n, SEG, HC), BF16), ((n, SEG, 2 * HC), BF16), ((n, SEG, 2 * NS), BF16),
+        ]
+
+    def ends(n):
+        return ((n, NS, 2 * HC), F32)
+
+    flops = 2 * SEG * (DM * (HC + 2 * NS) + NS * 2 * HC)
+    row = ((8, SEG), F32)
+    three = call(
+        tok_kernel_a, [*of_tokens(3), ends(3)], [row], [at, t0, t1, t3, wi, w_bc], 3 * flops
+    )
+    c0_r, t2, c1, *three = tie((c0, t2, c1, *three))
+    c3, c2 = move(c0_r, "x", 1), move(c1, "x", -1)
     cirow, cerow, ci, ce, tokb, xs, xfr, bc, pre_s, *s_rows = call(
-        tok_kernel,
-        [((NX, 8, SEG), F32), ((NX, 8, SEG), F32), ((NX, SEG, HC), F32), ((NX, SEG, HC), F32),
-         ((NX, SEG, DM), BF16), ((NX, SEG, HC), BF16), ((NX, SEG, 2 * HC), BF16), ((NX, SEG, 2 * NS), BF16),
-         edges, tall, tall, tall],
-        [ends, ((8, SEG), F32)],
-        [at, t0, t1, t2, t3, wi, w_bc],
-        2 * 1024 * (DM * (HC + 2 * NS) + NS * 2 * HC),
+        tok_kernel_b, [*of_tokens(4), edges, tall, tall, tall], [ends(4), row], [at, t2, wi, w_bc, *three], flops
     )
     q_rows = rows_exchange(*s_rows)
     two = [((2, SEG, DM), BF16), ((2, SEG, HC), BF16), ((2, SEG, 2 * HC), BF16)]
     flops = 1024 * (DM * HC + NS * 2 * HC)
     cotb_a, dy_a, dyfr_a, ends_a = call(
-        cot_kernel_a, [*two, ((2, NS, 2 * HC), F32)], [ends], [at, c0, c1, wo, ci, ce, bc], flops
+        cot_kernel_a, [*two, ends(2)], [ends(4)], [at, c0, c1, wo, ci, ce, bc], flops
     )
     cotb_b, dy_b, dyfr_b, pre_d, *s_rows = call(
-        cot_kernel_b, [*two, edges, tall, tall, tall], [ends], [at, c2, c3, wo, ci, ce, bc, ends_a], flops
+        cot_kernel_b, [*two, edges, tall, tall, tall], [ends(4)], [at, c3, c2, wo, ci, ce, bc, ends_a], flops
     )
     p_rows = rows_exchange(*s_rows)
     g_out, dxi, dci, dbi = call(

time: 162 us -> 154 us (0.951)
  local copies, waits for them, and re-layouts: 12.2 us -> 4.14 us
  starting transfers between devices: 53.5 us -> 50.8 us
  other arithmetic: 0.95 us -> 2.88 us
    unnamed x26 -> x12, local copies, waits for them, and re-layouts: 11 us -> 2.89 us
    ppermute x33, starting transfers between devices: 49 us -> 46.7 us  [move(): return lax.ppermute(value, name, pairs)]
    convert_element_type x0 -> x1, other arithmetic: none -> 1.93 us  [body(): c0 = cotangent[0].astype(F32)]
    pallas_call x12 -> x13, Pallas kernels: 31.8 us -> 33 us  [call(): pl.pallas_call(kernel, out_shape=[jax.ShapeDtypeStruct(*o) for o in outs]...]
  transfers between devices with their start and end apart: 34 -> 34, of which waited for: 16 -> 20; matrix products, arithmetic and copies ran while one was open for 1% -> 3% of each run, Pallas kernels for 16% -> 18%
where the time goes in v4:
time: 154 us; the launch traced here: 153 us
  waiting for transfers between devices  61.3 us (40%)
  starting transfers between devices  50.8 us (33%)
  Pallas kernels  33.1 us (21%)
  local copies, waits for them, and re-layouts  4.14 us (3%)
  other arithmetic  2.88 us (2%)
    ppermute x33, waiting for transfers between devices, move(): return lax.ppermute(value, name, pairs)  57.3 us
    ppermute x33, starting transfers between devices, move(): return lax.ppermute(value, name, pairs)  46.7 us
    pallas_call x13, Pallas kernels, call(): pl.pallas_call(kernel, out_shape=[jax.ShapeDtypeStruct(*o) for o in outs]...  33 us
    ppermute x1, starting transfers between devices, body(): rows_out = lax.ppermute(rows_out, ('rec', 'seq'), pairs)  4.1 us
    ppermute x1, waiting for transfers between devices, body(): rows_out = lax.ppermute(rows_out, ('rec', 'seq'), pairs)  4.07 us
  transfers between devices with their start and end apart: 34, of which 20 were waited for; matrix products, arithmetic and copies ran while one was open for 3% of the time, Pallas kernels for 18%

profile of v4, /device:TPU:6, one launch (start us, length us, event | category | flops | bytes accessed | tf_op | source)
XLA Modules:
  0.0 153.1 jit_solution(18361751204429035412)
XLA Ops:
  0.7 1.1 copy-done.4
  1.8 0.7 copy-done.5
  3.1 1.6 %collective-permute-start.1 = (f32[264,768]{1,0:T(8,128)S(1)}, f32[264,768]{1,0:T(8,128)S(1)}, u32[]{:S(2)}, u32[]{:S(2)}) collective-permute-start(f32[264,768]{1,0:T(8,128)S(1)} %shard_map.93.t0), channel_id=1, source_target_pairs={{0,3},{1,0},{2,1},{3,2},{4,7},{5,4},{6,5},{7,6},{8,11},{9,8},{10,9... | collective-permute-start | bytes 2433032 | tf_op jit(solution)/shard_map/ppermute | solution.py:48
  4.7 1.9 %bitcast_convert_fusion.c0 = f32[256,768]{1,0:T(8,128)} fusion(bf16[1,256,768]{2,1,0:T(8,128)(2,1)} %param.7), kind=kLoop, calls=%fused_computation.2 | loop fusion | flops 196608 | bytes 1179648 | tf_op jit(solution)/shard_map/convert_element_type | solution.py:420
  6.6 16.0 %collective-permute-done.t3 = f32[264,768]{1,0:T(8,128)} collective-permute-done((f32[264,768]{1,0:T(8,128)S(1)}, f32[264,768]{1,0:T(8,128)}, u32[]{:S(2)}, u32[]{:S(2)}) %collective-permute-start) | collective-permute-done | bytes 811040 | tf_op jit(solution)/shard_map/ppermute | solution.py:48
  22.6 1.2 collective-permute-done.1.t1
  23.8 0.9 copy-done.2
  25.1 1.6 %collective-permute-start.3 = (f32[256,768]{1,0:T(8,128)}, f32[256,768]{1,0:T(8,128)}, u32[]{:S(2)}, u32[]{:S(2)}) collective-permute-start(f32[256,768]{1,0:T(8,128)} %bitcast_convert_fusion.c0), channel_id=1, source_target_pairs={{0,3},{1,0},{2,1},{3,2},{4,7},{5,4},{6,5},{7,6},{8,11},{9,8},{10,9... | collective-permute-start | bytes 2359304 | tf_op jit(solution)/shard_map/ppermute | solution.py:48
  26.8 1.2 constant_dynamic-slice_fusion.w_out
  28.1 6.6 %shard_map.94 = (f32[3,8,256]{2,1,0:T(8,128)S(1)}, f32[3,8,256]{2,1,0:T(8,128)S(1)}, f32[3,256,384]{2,1,0:T(8,128)S(1)}, f32[3,256,384]{2,1,0:T(8,128)S(1)}, bf1...) custom-call(s32[4]{0:T(128)S(1)} %pad_add_fusion.at, ...), custom_call_target="tpu_custom_call" | custom-call | flops 905969664 | bytes 3416080 | tf_op jit(solution)/shard_map/pallas_call | solution.py:384
  34.8 9.7 %collective-permute-done.3.c1 = f32[256,768]{1,0:T(8,128)} collective-permute-done((f32[256,768]{1,0:T(8,128)}, f32[256,768]{1,0:T(8,128)}, u32[]{:S(2)}, u32[]{:S(2)}) %collective-permute-start.3) | collective-permute-done | bytes 786464 | tf_op jit(solution)/shard_map/ppermute | solution.py:48
  44.5 0.8 collective-permute-start.4
  45.3 1.2 collective-permute-start.5
  46.5 3.5 %shard_map.95 = (f32[4,8,256]{2,1,0:T(8,128)S(1)}, f32[4,8,256]{2,1,0:T(8,128)S(1)}, f32[4,256,384]{2,1,0:T(8,128)S(1)}, f32[4,256,384]{2,1,0:T(8,128)S(1)}, bf1...) custom-call(s32[4]{0:T(128)S(1)} %pad_add_fusion.at, ...), custom_call_target="tpu_custom_call" | custom-call | flops 301989888 | bytes 8724496 | tf_op jit(solution)/shard_map/pallas_call | solution.py:384
  50.0 2.0 %collective-permute-start.9 = (f32[136,384]{1,0:T(8,128)S(1)}, f32[136,384]{1,0:T(8,128)S(1)}, u32[]{:S(2)}, u32[]{:S(2)}) collective-permute-start(f32[136,384]{1,0:T(8,128)S(1)} %get-tuple-element.131), channel_id=1, source_target_pairs={{0,4},{1,5},{2,6},{3,7},{4,8},{5,9},{6,10},{7,11},{8,12},{9,13},{1... | collective-permute-start | bytes 626696 | tf_op jit(solution)/shard_map/ppermute | solution.py:48
  52.0 1.5 collective-permute-start.10
  53.5 2.1 %collective-permute-start.11 = (f32[136,384]{1,0:T(8,128)S(1)}, f32[136,384]{1,0:T(8,128)S(1)}, u32[]{:S(2)}, u32[]{:S(2)}) collective-permute-start(f32[136,384]{1,0:T(8,128)S(1)} %get-tuple-element.133), channel_id=1, source_target_pairs={{0,8},{1,9},{2,10},{3,11},{4,12},{5,13},{6,14},{7,15},{8,0},{9,1},... | collective-permute-start | bytes 626696 | tf_op jit(solution)/shard_map/ppermute | solution.py:48
  55.6 2.7 %shard_map.96 = (bf16[2,256,768]{2,1,0:T(8,128)(2,1)S(1)}, bf16[2,256,384]{2,1,0:T(8,128)(2,1)S(1)}, bf16[2,256,768]{2,1,0:T(8,128)(2,1)S(1)}, f32[2,128,768]{2,1,0:T(8,128)S(1)}) custom-call(s32[4]{0:T(128)S(1)} %pad_add_fusion.at, f32[256,768]{1,0:T(8,128)} %bitcast_convert_fusion.c0, f32[256,768]{1,0:T(8,128)} %collective-permute-done.3.c1, ...), custom_call_target="tpu_custom_call" | custom-call | flops 402653184 | bytes 5832720 | tf_op jit(solution)/shard_map/pallas_call | solution.py:384
  58.4 3.3 %collective-permute-done.4.c2 = f32[256,768]{1,0:T(8,128)S(1)} collective-permute-done((f32[256,768]{1,0:T(8,128)}, f32[256,768]{1,0:T(8,128)S(1)}, u32[]{:S(2)}, u32[]{:S(2)}) %collective-permute-start.4) | collective-permute-done | bytes 786464 | tf_op jit(solution)/shard_map/ppermute | solution.py:48
  61.7 2.0 %collective-permute-done.5.c3 = f32[256,768]{1,0:T(8,128)S(1)} collective-permute-done((f32[256,768]{1,0:T(8,128)}, f32[256,768]{1,0:T(8,128)S(1)}, u32[]{:S(2)}, u32[]{:S(2)}) %collective-permute-start.5) | collective-permute-done | bytes 786464 | tf_op jit(solution)/shard_map/ppermute | solution.py:48
  63.7 2.1 %shard_map.97 = (bf16[2,256,768]{2,1,0:T(8,128)(2,1)S(1)}, bf16[2,256,384]{2,1,0:T(8,128)(2,1)S(1)}, bf16[2,256,768]{2,1,0:T(8,128)(2,1)S(1)}, f32[2,4,128,384]{...) custom-call(s32[4]{0:T(128)S(1)} %pad_add_fusion.at, ...), custom_call_target="tpu_custom_call" | custom-call | flops 402653184 | bytes 6619152 | tf_op jit(solution)/shard_map/pallas_call | solution.py:384
  65.9 2.2 %collective-permute-start.6 = (f32[136,384]{1,0:T(8,128)S(1)}, f32[136,384]{1,0:T(8,128)S(1)}, u32[]{:S(2)}, u32[]{:S(2)}) collective-permute-start(f32[136,384]{1,0:T(8,128)S(1)} %get-tuple-element.118), channel_id=1, source_target_pairs={{0,4},{1,5},{2,6},{3,7},{4,8},{5,9},{6,10},{7,11},{8,12},{9,13},{1... | collective-permute-start | bytes 626696 | tf_op jit(solution)/shard_map/ppermute | solution.py:48
  68.0 1.5 collective-permute-start.7
  69.6 2.1 %collective-permute-start.8 = (f32[136,384]{1,0:T(8,128)S(1)}, f32[136,384]{1,0:T(8,128)S(1)}, u32[]{:S(2)}, u32[]{:S(2)}) collective-permute-start(f32[136,384]{1,0:T(8,128)S(1)} %get-tuple-element.120), channel_id=1, source_target_pairs={{0,8},{1,9},{2,10},{3,11},{4,12},{5,13},{6,14},{7,15},{8,0},{9,1},... | collective-permute-start | bytes 626696 | tf_op jit(solution)/shard_map/ppermute | solution.py:48
  71.7 7.4 %shard_map.98 = (f32[2,384,384]{2,1,0:T(8,128)S(1)}, f32[4,256,384]{2,1,0:T(8,128)S(1)}, f32[4,256,128]{2,1,0:T(8,128)S(1)}, f32[4,256,128]{2,1,0:T(8,128)S(1)}) custom-call(s32[4]{0:T(128)S(1)} %pad_add_fusion.at, bf16[4,256,384]{2,1,0:T(8,128)(2,1)S(1)} %get-tuple-element.121.xs, bf16[4,256,256]{2,1,0:T(8,128)(2,1)S(1)} %get-tuple-element.110.bc, ...), custom_call_target="tpu_custom_call" | custom-call | flops 2214592512 | bytes 10653712 | tf_op jit(solution)/shard_map/pallas_call | solution.py:384
  79.1 4.0 %shard_map.99 = (f32[384,1024]{1,0:T(8,128)S(1)}, f32[384,1024]{1,0:T(8,128)S(1)}, bf16[4,256,640]{2,1,0:T(8,128)(2,1)S(1)}) custom-call(s32[4]{0:T(128)S(1)} %pad_add_fusion.at, bf16[4,256,768]{2,1,0:T(8,128)(2,1)S(1)} %get-tuple-element.108.tokb, bf16[4,256,768]{2,1,0:T(8,128)(2,1)S(1)} %get-tuple-element.109.xfr, ...), custom_call_target="tpu_custom_call" | custom-call | flops 1409286144 | bytes 12816400 | tf_op jit(solution)/shard_map/pallas_call | solution.py:384
  83.2 2.0 %shard_map.100 = (f32[256,768]{1,0:T(8,128)S(1)}, f32[256,768]{1,0:T(8,128)S(1)}, f32[128,768]{1,0:T(8,128)S(1)}, f32[128,768]{1,0:T(8,128)S(1)}, f32[256,768]{1,0:T(8,128)S(1)}) custom-call(s32[4]{0:T(128)S(1)} %pad_add_fusion.at, bf16[4,256,640]{2,1,0:T(8,128)(2,1)S(1)} %get-tuple-element.138.dz, bf16[768,384]{1,0:T(8,128)(2,1)S(1)} %constant_dynamic-slice_fusion.1.w_in, ...), custom_call_target="tpu_custom_call" | custom-call | flops 1006632960 | bytes 2293776 | tf_op jit(solution)/shard_map/pallas_call | solution.py:384
  85.5 1.7 %collective-permute-start.13 = (f32[128,768]{1,0:T(8,128)S(1)}, f32[128,768]{1,0:T(8,128)S(1)}, u32[]{:S(2)}, u32[]{:S(2)}) collective-permute-start(f32[128,768]{1,0:T(8,128)S(1)} %get-tuple-element.143), channel_id=1, source_target_pairs={{0,3},{1,0},{2,1},{3,2},{4,7},{5,4},{6,5},{7,6},{8,11},{9,8},{10,9... | collective-permute-start | bytes 1179656 | tf_op jit(solution)/shard_map/ppermute | solution.py:48
  87.3 0.8 shard_map.102
  88.1 0.8 collective-permute-start.17
  88.8 1.8 %collective-permute-start.18 = (f32[96,1024]{1,0:T(8,128)S(1)}, f32[96,1024]{1,0:T(8,128)S(1)}, u32[]{:S(2)}, u32[]{:S(2)}) collective-permute-start(f32[96,1024]{1,0:T(8,128)S(1)} %get-tuple-element.150), channel_id=1, source_target_pairs={{0,8},{1,9},{2,10},{3,11},{4,12},{5,13},{6,14},{7,15},{8,0},{9,1},... | collective-permute-start | bytes 1179656 | tf_op jit(solution)/shard_map/ppermute | solution.py:48
  90.7 1.5 collective-permute-start.19
  92.2 4.6 %collective-permute-done.12.r_a = f32[128,768]{1,0:T(8,128)S(1)} collective-permute-done((f32[128,768]{1,0:T(8,128)S(1)}, f32[128,768]{1,0:T(8,128)S(1)}, u32[]{:S(2)}, u32[]{:S(2)}) %collective-permute-start.12) | collective-permute-done | bytes 393248 | tf_op jit(solution)/shard_map/ppermute | solution.py:48
  96.7 1.3 collective-permute-done.13.r_b
  98.0 0.7 shard_map.101
  99.2 2.8 %collective-permute-start.14 = (f32[256,768]{1,0:T(8,128)S(1)}, f32[256,768]{1,0:T(8,128)S(1)}, u32[]{:S(2)}, u32[]{:S(2)}) collective-permute-start(f32[256,768]{1,0:T(8,128)S(1)} %get-tuple-element.144), channel_id=1, source_target_pairs={{0,1},{1,2},{2,3},{3,0},{4,5},{5,6},{6,7},{7,4},{8,9},{9,10},{10,1... | collective-permute-start | bytes 2359304 | tf_op jit(solution)/shard_map/ppermute | solution.py:48
  102.0 6.7 %collective-permute-done.17.refs_1_ = f32[96,1024]{1,0:T(8,128)S(1)} collective-permute-done((f32[96,1024]{1,0:T(8,128)S(1)}, f32[96,1024]{1,0:T(8,128)S(1)}, u32[]{:S(2)}, u32[]{:S(2)}) %collective-permute-start.17) | collective-permute-done | bytes 393248 | tf_op jit(solution)/shard_map/ppermute | solution.py:48
  108.7 0.6 collective-permute-done.19.refs_3_
  109.3 0.7 shard_map.103
  110.0 2.0 %collective-permute-start.20 = (f32[24,1024]{1,0:T(8,128)S(1)}, f32[24,1024]{1,0:T(8,128)S(1)}, u32[]{:S(2)}, u32[]{:S(2)}) collective-permute-start(f32[24,1024]{1,0:T(8,128)S(1)} %get-tuple-element.153), channel_id=1, source_target_pairs={{0,32},{16,48},{32,64},{48,80},{64,96},{80,112},{96,0},{112,16},{1... | collective-permute-start | bytes 294920 | tf_op jit(solution)/shard_map/ppermute | solution.py:48
  112.0 3.6 %collective-permute-start.21 = (f32[24,1024]{1,0:T(8,128)S(1)}, f32[24,1024]{1,0:T(8,128)S(1)}, u32[]{:S(2)}, u32[]{:S(2)}) collective-permute-start(f32[24,1024]{1,0:T(8,128)S(1)} %get-tuple-element.154), channel_id=1, source_target_pairs={{0,64},{16,80},{32,96},{48,112},{64,0},{80,16},{96,32},{112,48},{1... | collective-permute-start | bytes 294920 | tf_op jit(solution)/shard_map/ppermute | solution.py:48
  115.6 1.0 collective-permute-start.22
  116.6 1.2 collective-permute-done.20.b
  117.8 1.6 %collective-permute-done.21.c = f32[24,1024]{1,0:T(8,128)S(1)} collective-permute-done((f32[24,1024]{1,0:T(8,128)S(1)}, f32[24,1024]{1,0:T(8,128)S(1)}, u32[]{:S(2)}, u32[]{:S(2)}) %collective-permute-start.21) | collective-permute-done | bytes 98336 | tf_op jit(solution)/shard_map/ppermute | solution.py:48
  119.4 0.8 collective-permute-done.22.d
  120.2 0.7 shard_map.104
  120.9 1.6 %collective-permute-start.23 = (f32[40,384]{1,0:T(8,128)S(1)}, f32[40,384]{1,0:T(8,128)S(1)}, u32[]{:S(2)}, u32[]{:S(2)}) collective-permute-start(f32[40,384]{1,0:T(8,128)S(1)} %get-tuple-element.157), channel_id=1, source_target_pairs={{0,1},{1,2},{2,3},{3,0},{4,5},{5,6},{6,7},{7,4},{8,9},{9,10},{10,1... | collective-permute-start | bytes 184328 | tf_op jit(solution)/shard_map/ppermute | solution.py:48
  122.6 0.8 collective-permute-start.24
  123.5 1.7 %collective-permute-done.23.b = f32[40,384]{1,0:T(8,128)S(1)} collective-permute-done((f32[40,384]{1,0:T(8,128)S(1)}, f32[40,384]{1,0:T(8,128)S(1)}, u32[]{:S(2)}, u32[]{:S(2)}) %collective-permute-start.23) | collective-permute-done | bytes 61472 | tf_op jit(solution)/shard_map/ppermute | solution.py:48
  125.2 3.1 %collective-permute-done.24.c = f32[40,384]{1,0:T(8,128)S(1)} collective-permute-done((f32[40,384]{1,0:T(8,128)S(1)}, f32[40,384]{1,0:T(8,128)S(1)}, u32[]{:S(2)}, u32[]{:S(2)}) %collective-permute-start.24) | collective-permute-done | bytes 61472 | tf_op jit(solution)/shard_map/ppermute | solution.py:48
  128.3 0.6 collective-permute-done.25.d
  128.9 0.7 shard_map.105
  129.6 1.6 %collective-permute-start.29 = (f32[8,128]{1,0:T(8,128)S(1)}, f32[8,128]{1,0:T(8,128)S(1)}, u32[]{:S(2)}, u32[]{:S(2)}) collective-permute-start(f32[8,128]{1,0:T(8,128)S(1)} %shard_map.105), channel_id=1, source_target_pairs={{0,8},{1,9},{2,10},{3,11},{4,12},{5,13},{6,14},{7,15},{8,0},{9,1},... | collective-permute-start | bytes 12296 | tf_op jit(solution)/shard_map/ppermute | solution.py:48
  131.2 2.1 %collective-permute-start.27 = (f32[8,128]{1,0:T(8,128)S(1)}, f32[8,128]{1,0:T(8,128)S(1)}, u32[]{:S(2)}, u32[]{:S(2)}) collective-permute-start(f32[8,128]{1,0:T(8,128)S(1)} %shard_map.105), channel_id=1, source_target_pairs={{0,4},{1,5},{2,6},{3,7},{4,8},{5,9},{6,10},{7,11},{8,12},{9,13},{1... | collective-permute-start | bytes 12296 | tf_op jit(solution)/shard_map/ppermute | solution.py:48
  133.4 1.1 collective-permute-start.28
  134.8 1.2 collective-permute-done.27
  136.0 0.9 collective-permute-done.28
  137.0 2.2 %collective-permute-start.32 = (f32[8,128]{1,0:T(8,128)S(1)}, f32[8,128]{1,0:T(8,128)S(1)}, u32[]{:S(2)}, u32[]{:S(2)}) collective-permute-start(f32[8,128]{1,0:T(8,128)S(1)} %add_add_fusion.1), channel_id=1, source_target_pairs={{0,64},{16,80},{32,96},{48,112},{64,0},{80,16},{96,32},{112,48},{1... | collective-permute-start | bytes 12296 | tf_op jit(solution)/shard_map/ppermute | solution.py:48
  139.2 0.8 collective-permute-start.30
  140.0 2.5 %collective-permute-start.31 = (f32[8,128]{1,0:T(8,128)S(1)}, f32[8,128]{1,0:T(8,128)S(1)}, u32[]{:S(2)}, u32[]{:S(2)}) collective-permute-start(f32[8,128]{1,0:T(8,128)S(1)} %add_add_fusion.1), channel_id=1, source_target_pairs={{0,96},{16,112},{32,0},{48,16},{64,32},{80,48},{96,64},{112,80},{1... | collective-permute-start | bytes 12296 | tf_op jit(solution)/shard_map/ppermute | solution.py:48
  142.4 4.1 %collective-permute-start.26 = (f32[24,384]{1,0:T(8,128)S(1)}, f32[24,384]{1,0:T(8,128)S(1)}, u32[]{:S(2)}, u32[]{:S(2)}) collective-permute-start(f32[24,384]{1,0:T(8,128)S(1)} %get-tuple-element.160), channel_id=1, source_target_pairs={{0,0},{1,32},{2,64},{3,96},{4,1},{5,33},{6,65},{7,97},{8,2},{9,34}... | collective-permute-start | bytes 110600 | tf_op jit(solution)/shard_map/ppermute | solution.py:492
  146.7 0.9 fusion
  147.8 4.1 %collective-permute-done.26.rows_out = f32[24,384]{1,0:T(8,128)S(1)} collective-permute-done((f32[24,384]{1,0:T(8,128)S(1)}, f32[24,384]{1,0:T(8,128)S(1)}, u32[]{:S(2)}, u32[]{:S(2)}) %collective-permute-start.26) | collective-permute-done | bytes 36896 | tf_op jit(solution)/shard_map/ppermute | solution.py:492
  151.9 1.2 shard_map.106
  (38 shorter events, 3.0 us)
Async XLA Ops:
  0.6 26.2 %copy-start = (bf16[768,1536]{1,0:T(8,128)(2,1)S(1)}, bf16[768,1536]{1,0:T(8,128)(2,1)}, u32[]{:S(2)}) copy-start(bf16[768,1536]{1,0:T(8,128)(2,1)} %param.9) | copy-start | bytes 7077892
  0.6 1.1 copy-start.4
  1.8 0.7 copy-start.5
  2.6 20.0 %collective-permute-start = (f32[264,768]{1,0:T(8,128)S(1)}, f32[264,768]{1,0:T(8,128)}, u32[]{:S(2)}, u32[]{:S(2)}) collective-permute-start(f32[264,768]{1,0:T(8,128)S(1)} %shard_map.93.t0), channel_id=1, source_target_pairs={{0,1},{1,2},{2,3},{3,0},{4,5},{5,6},{6,7},{7,4},{8,9},{9,10},{10,1... | collective-permute-start | bytes 2433032 | tf_op jit(solution)/shard_map/ppermute | solution.py:48
  3.1 20.7 %collective-permute-start.1 = (f32[264,768]{1,0:T(8,128)S(1)}, f32[264,768]{1,0:T(8,128)S(1)}, u32[]{:S(2)}, u32[]{:S(2)}) collective-permute-start(f32[264,768]{1,0:T(8,128)S(1)} %shard_map.93.t0), channel_id=1, source_target_pairs={{0,3},{1,0},{2,1},{3,2},{4,7},{5,4},{6,5},{7,6},{8,11},{9,8},{10,9... | collective-permute-start | bytes 2433032 | tf_op jit(solution)/shard_map/ppermute | solution.py:48
  23.8 0.9 copy-start.2
  24.7 19.8 %collective-permute-start.2 = (f32[264,768]{1,0:T(8,128)}, f32[264,768]{1,0:T(8,128)}, u32[]{:S(2)}, u32[]{:S(2)}) collective-permute-start(f32[264,768]{1,0:T(8,128)} %collective-permute-done.t3), channel_id=1, source_target_pairs={{0,1},{1,2},{2,3},{3,0},{4,5},{5,6},{6,7},{7,4},{8,9},{9,10},{10,1... | collective-permute-start | bytes 2433032 | tf_op jit(solution)/shard_map/ppermute | solution.py:48
  25.1 19.4 %collective-permute-start.3 = (f32[256,768]{1,0:T(8,128)}, f32[256,768]{1,0:T(8,128)}, u32[]{:S(2)}, u32[]{:S(2)}) collective-permute-start(f32[256,768]{1,0:T(8,128)} %bitcast_convert_fusion.c0), channel_id=1, source_target_pairs={{0,3},{1,0},{2,1},{3,2},{4,7},{5,4},{6,5},{7,6},{8,11},{9,8},{10,9... | collective-permute-start | bytes 2359304 | tf_op jit(solution)/shard_map/ppermute | solution.py:48
  26.7 1.3 copy-start.1
  26.7 1.4 copy-start.3
  44.5 17.2 %collective-permute-start.4 = (f32[256,768]{1,0:T(8,128)}, f32[256,768]{1,0:T(8,128)S(1)}, u32[]{:S(2)}, u32[]{:S(2)}) collective-permute-start(f32[256,768]{1,0:T(8,128)} %bitcast_convert_fusion.c0), channel_id=1, source_target_pairs={{0,1},{1,2},{2,3},{3,0},{4,5},{5,6},{6,7},{7,4},{8,9},{9,10},{10,1... | collective-permute-start | bytes 2359304 | tf_op jit(solution)/shard_map/ppermute | solution.py:48
  45.3 18.4 %collective-permute-start.5 = (f32[256,768]{1,0:T(8,128)}, f32[256,768]{1,0:T(8,128)S(1)}, u32[]{:S(2)}, u32[]{:S(2)}) collective-permute-start(f32[256,768]{1,0:T(8,128)} %collective-permute-done.3.c1), channel_id=1, source_target_pairs={{0,3},{1,0},{2,1},{3,2},{4,7},{5,4},{6,5},{7,6},{8,11},{9,8},{10,9... | collective-permute-start | bytes 2359304 | tf_op jit(solution)/shard_map/ppermute | solution.py:48
  50.0 19.5 %collective-permute-start.9 = (f32[136,384]{1,0:T(8,128)S(1)}, f32[136,384]{1,0:T(8,128)S(1)}, u32[]{:S(2)}, u32[]{:S(2)}) collective-permute-start(f32[136,384]{1,0:T(8,128)S(1)} %get-tuple-element.131), channel_id=1, source_target_pairs={{0,4},{1,5},{2,6},{3,7},{4,8},{5,9},{6,10},{7,11},{8,12},{9,13},{1... | collective-permute-start | bytes 626696 | tf_op jit(solution)/shard_map/ppermute | solution.py:48
  52.0 19.7 %collective-permute-start.10 = (f32[136,384]{1,0:T(8,128)S(1)}, f32[136,384]{1,0:T(8,128)S(1)}, u32[]{:S(2)}, u32[]{:S(2)}) collective-permute-start(f32[136,384]{1,0:T(8,128)S(1)} %get-tuple-element.132), channel_id=1, source_target_pairs={{0,12},{1,13},{2,14},{3,15},{4,0},{5,1},{6,2},{7,3},{8,4},{9,5},{1... | collective-permute-start | bytes 626696 | tf_op jit(solution)/shard_map/ppermute | solution.py:48
  53.5 18.2 %collective-permute-start.11 = (f32[136,384]{1,0:T(8,128)S(1)}, f32[136,384]{1,0:T(8,128)S(1)}, u32[]{:S(2)}, u32[]{:S(2)}) collective-permute-start(f32[136,384]{1,0:T(8,128)S(1)} %get-tuple-element.133), channel_id=1, source_target_pairs={{0,8},{1,9},{2,10},{3,11},{4,12},{5,13},{6,14},{7,15},{8,0},{9,1},... | collective-permute-start | bytes 626696 | tf_op jit(solution)/shard_map/ppermute | solution.py:48
  65.9 13.2 %collective-permute-start.6 = (f32[136,384]{1,0:T(8,128)S(1)}, f32[136,384]{1,0:T(8,128)S(1)}, u32[]{:S(2)}, u32[]{:S(2)}) collective-permute-start(f32[136,384]{1,0:T(8,128)S(1)} %get-tuple-element.118), channel_id=1, source_target_pairs={{0,4},{1,5},{2,6},{3,7},{4,8},{5,9},{6,10},{7,11},{8,12},{9,13},{1... | collective-permute-start | bytes 626696 | tf_op jit(solution)/shard_map/ppermute | solution.py:48
  68.0 11.1 %collective-permute-start.7 = (f32[136,384]{1,0:T(8,128)S(1)}, f32[136,384]{1,0:T(8,128)S(1)}, u32[]{:S(2)}, u32[]{:S(2)}) collective-permute-start(f32[136,384]{1,0:T(8,128)S(1)} %get-tuple-element.119), channel_id=1, source_target_pairs={{0,12},{1,13},{2,14},{3,15},{4,0},{5,1},{6,2},{7,3},{8,4},{9,5},{1... | collective-permute-start | bytes 626696 | tf_op jit(solution)/shard_map/ppermute | solution.py:48
  69.6 9.5 %collective-permute-start.8 = (f32[136,384]{1,0:T(8,128)S(1)}, f32[136,384]{1,0:T(8,128)S(1)}, u32[]{:S(2)}, u32[]{:S(2)}) collective-permute-start(f32[136,384]{1,0:T(8,128)S(1)} %get-tuple-element.120), channel_id=1, source_target_pairs={{0,8},{1,9},{2,10},{3,11},{4,12},{5,13},{6,14},{7,15},{8,0},{9,1},... | collective-permute-start | bytes 626696 | tf_op jit(solution)/shard_map/ppermute | solution.py:48
  83.1 4.2 %collective-permute-start.16 = (f32[384,1024]{1,0:T(8,128)S(1)}, f32[384,1024]{1,0:T(8,128)S(1)}, u32[]{:S(2)}, u32[]{:S(2)}) collective-permute-start(f32[384,1024]{1,0:T(8,128)S(1)} %get-tuple-element.147), channel_id=1, source_target_pairs={{0,16},{16,0},{32,48},{48,32},{64,80},{80,64},{96,112},{112,96},{1... | collective-permute-start | bytes 4718600 | tf_op jit(solution)/shard_map/ppermute | solution.py:48
  85.2 11.6 %collective-permute-start.12 = (f32[128,768]{1,0:T(8,128)S(1)}, f32[128,768]{1,0:T(8,128)S(1)}, u32[]{:S(2)}, u32[]{:S(2)}) collective-permute-start(f32[128,768]{1,0:T(8,128)S(1)} %get-tuple-element.142), channel_id=1, source_target_pairs={{0,1},{1,2},{2,3},{3,0},{4,5},{5,6},{6,7},{7,4},{8,9},{9,10},{10,1... | collective-permute-start | bytes 1179656 | tf_op jit(solution)/shard_map/ppermute | solution.py:48
  85.5 12.5 %collective-permute-start.13 = (f32[128,768]{1,0:T(8,128)S(1)}, f32[128,768]{1,0:T(8,128)S(1)}, u32[]{:S(2)}, u32[]{:S(2)}) collective-permute-start(f32[128,768]{1,0:T(8,128)S(1)} %get-tuple-element.143), channel_id=1, source_target_pairs={{0,3},{1,0},{2,1},{3,2},{4,7},{5,4},{6,5},{7,6},{8,11},{9,8},{10,9... | collective-permute-start | bytes 1179656 | tf_op jit(solution)/shard_map/ppermute | solution.py:48
  88.1 20.7 %collective-permute-start.17 = (f32[96,1024]{1,0:T(8,128)S(1)}, f32[96,1024]{1,0:T(8,128)S(1)}, u32[]{:S(2)}, u32[]{:S(2)}) collective-permute-start(f32[96,1024]{1,0:T(8,128)S(1)} %get-tuple-element.149), channel_id=1, source_target_pairs={{0,4},{1,5},{2,6},{3,7},{4,8},{5,9},{6,10},{7,11},{8,12},{9,13},{1... | collective-permute-start | bytes 1179656 | tf_op jit(solution)/shard_map/ppermute | solution.py:48
  88.8 19.9 %collective-permute-start.18 = (f32[96,1024]{1,0:T(8,128)S(1)}, f32[96,1024]{1,0:T(8,128)S(1)}, u32[]{:S(2)}, u32[]{:S(2)}) collective-permute-start(f32[96,1024]{1,0:T(8,128)S(1)} %get-tuple-element.150), channel_id=1, source_target_pairs={{0,8},{1,9},{2,10},{3,11},{4,12},{5,13},{6,14},{7,15},{8,0},{9,1},... | collective-permute-start | bytes 1179656 | tf_op jit(solution)/shard_map/ppermute | solution.py:48
  90.7 18.7 %collective-permute-start.19 = (f32[96,1024]{1,0:T(8,128)S(1)}, f32[96,1024]{1,0:T(8,128)S(1)}, u32[]{:S(2)}, u32[]{:S(2)}) collective-permute-start(f32[96,1024]{1,0:T(8,128)S(1)} %get-tuple-element.151), channel_id=1, source_target_pairs={{0,12},{1,13},{2,14},{3,15},{4,0},{5,1},{6,2},{7,3},{8,4},{9,5},{1... | collective-permute-start | bytes 1179656 | tf_op jit(solution)/shard_map/ppermute | solution.py:48
  98.7 48.0 %collective-permute-start.15 = (f32[256,768]{1,0:T(8,128)S(1)}, f32[256,768]{1,0:T(8,128)S(1)}, u32[]{:S(2)}, u32[]{:S(2)}) collective-permute-start(f32[256,768]{1,0:T(8,128)S(1)} %get-tuple-element.145), channel_id=1, source_target_pairs={{0,3},{1,0},{2,1},{3,2},{4,7},{5,4},{6,5},{7,6},{8,11},{9,8},{10,9... | collective-permute-start | bytes 2359304 | tf_op jit(solution)/shard_map/ppermute | solution.py:48
  99.2 47.5 %collective-permute-start.14 = (f32[256,768]{1,0:T(8,128)S(1)}, f32[256,768]{1,0:T(8,128)S(1)}, u32[]{:S(2)}, u32[]{:S(2)}) collective-permute-start(f32[256,768]{1,0:T(8,128)S(1)} %get-tuple-element.144), channel_id=1, source_target_pairs={{0,1},{1,2},{2,3},{3,0},{4,5},{5,6},{6,7},{7,4},{8,9},{9,10},{10,1... | collective-permute-start | bytes 2359304 | tf_op jit(solution)/shard_map/ppermute | solution.py:48
  110.0 7.8 %collective-permute-start.20 = (f32[24,1024]{1,0:T(8,128)S(1)}, f32[24,1024]{1,0:T(8,128)S(1)}, u32[]{:S(2)}, u32[]{:S(2)}) collective-permute-start(f32[24,1024]{1,0:T(8,128)S(1)} %get-tuple-element.153), channel_id=1, source_target_pairs={{0,32},{16,48},{32,64},{48,80},{64,96},{80,112},{96,0},{112,16},{1... | collective-permute-start | bytes 294920 | tf_op jit(solution)/shard_map/ppermute | solution.py:48
  112.0 7.4 %collective-permute-start.21 = (f32[24,1024]{1,0:T(8,128)S(1)}, f32[24,1024]{1,0:T(8,128)S(1)}, u32[]{:S(2)}, u32[]{:S(2)}) collective-permute-start(f32[24,1024]{1,0:T(8,128)S(1)} %get-tuple-element.154), channel_id=1, source_target_pairs={{0,64},{16,80},{32,96},{48,112},{64,0},{80,16},{96,32},{112,48},{1... | collective-permute-start | bytes 294920 | tf_op jit(solution)/shard_map/ppermute | solution.py:48
  115.6 4.6 %collective-permute-start.22 = (f32[24,1024]{1,0:T(8,128)S(1)}, f32[24,1024]{1,0:T(8,128)S(1)}, u32[]{:S(2)}, u32[]{:S(2)}) collective-permute-start(f32[24,1024]{1,0:T(8,128)S(1)} %get-tuple-element.155), channel_id=1, source_target_pairs={{0,96},{16,112},{32,0},{48,16},{64,32},{80,48},{96,64},{112,80},{1... | collective-permute-start | bytes 294920 | tf_op jit(solution)/shard_map/ppermute | solution.py:48
  120.9 4.3 %collective-permute-start.23 = (f32[40,384]{1,0:T(8,128)S(1)}, f32[40,384]{1,0:T(8,128)S(1)}, u32[]{:S(2)}, u32[]{:S(2)}) collective-permute-start(f32[40,384]{1,0:T(8,128)S(1)} %get-tuple-element.157), channel_id=1, source_target_pairs={{0,1},{1,2},{2,3},{3,0},{4,5},{5,6},{6,7},{7,4},{8,9},{9,10},{10,1... | collective-permute-start | bytes 184328 | tf_op jit(solution)/shard_map/ppermute | solution.py:48
  122.6 5.7 %collective-permute-start.24 = (f32[40,384]{1,0:T(8,128)S(1)}, f32[40,384]{1,0:T(8,128)S(1)}, u32[]{:S(2)}, u32[]{:S(2)}) collective-permute-start(f32[40,384]{1,0:T(8,128)S(1)} %get-tuple-element.158), channel_id=1, source_target_pairs={{0,2},{1,3},{2,0},{3,1},{4,6},{5,7},{6,4},{7,5},{8,10},{9,11},{10,... | collective-permute-start | bytes 184328 | tf_op jit(solution)/shard_map/ppermute | solution.py:48
  123.3 5.6 %collective-permute-start.25 = (f32[40,384]{1,0:T(8,128)S(1)}, f32[40,384]{1,0:T(8,128)S(1)}, u32[]{:S(2)}, u32[]{:S(2)}) collective-permute-start(f32[40,384]{1,0:T(8,128)S(1)} %get-tuple-element.159), channel_id=1, source_target_pairs={{0,3},{1,0},{2,1},{3,2},{4,7},{5,4},{6,5},{7,6},{8,11},{9,8},{10,9... | collective-permute-start | bytes 184328 | tf_op jit(solution)/shard_map/ppermute | solution.py:48
  129.6 5.2 %collective-permute-start.29 = (f32[8,128]{1,0:T(8,128)S(1)}, f32[8,128]{1,0:T(8,128)S(1)}, u32[]{:S(2)}, u32[]{:S(2)}) collective-permute-start(f32[8,128]{1,0:T(8,128)S(1)} %shard_map.105), channel_id=1, source_target_pairs={{0,8},{1,9},{2,10},{3,11},{4,12},{5,13},{6,14},{7,15},{8,0},{9,1},... | collective-permute-start | bytes 12296 | tf_op jit(solution)/shard_map/ppermute | solution.py:48
  131.2 4.8 %collective-permute-start.27 = (f32[8,128]{1,0:T(8,128)S(1)}, f32[8,128]{1,0:T(8,128)S(1)}, u32[]{:S(2)}, u32[]{:S(2)}) collective-permute-start(f32[8,128]{1,0:T(8,128)S(1)} %shard_map.105), channel_id=1, source_target_pairs={{0,4},{1,5},{2,6},{3,7},{4,8},{5,9},{6,10},{7,11},{8,12},{9,13},{1... | collective-permute-start | bytes 12296 | tf_op jit(solution)/shard_map/ppermute | solution.py:48
  133.4 3.6 %collective-permute-start.28 = (f32[8,128]{1,0:T(8,128)S(1)}, f32[8,128]{1,0:T(8,128)S(1)}, u32[]{:S(2)}, u32[]{:S(2)}) collective-permute-start(f32[8,128]{1,0:T(8,128)S(1)} %shard_map.105), channel_id=1, source_target_pairs={{0,12},{1,13},{2,14},{3,15},{4,0},{5,1},{6,2},{7,3},{8,4},{9,5},{1... | collective-permute-start | bytes 12296 | tf_op jit(solution)/shard_map/ppermute | solution.py:48
  137.0 5.5 %collective-permute-start.32 = (f32[8,128]{1,0:T(8,128)S(1)}, f32[8,128]{1,0:T(8,128)S(1)}, u32[]{:S(2)}, u32[]{:S(2)}) collective-permute-start(f32[8,128]{1,0:T(8,128)S(1)} %add_add_fusion.1), channel_id=1, source_target_pairs={{0,64},{16,80},{32,96},{48,112},{64,0},{80,16},{96,32},{112,48},{1... | collective-permute-start | bytes 12296 | tf_op jit(solution)/shard_map/ppermute | solution.py:48
  139.2 7.3 %collective-permute-start.30 = (f32[8,128]{1,0:T(8,128)S(1)}, f32[8,128]{1,0:T(8,128)S(1)}, u32[]{:S(2)}, u32[]{:S(2)}) collective-permute-start(f32[8,128]{1,0:T(8,128)S(1)} %add_add_fusion.1), channel_id=1, source_target_pairs={{0,32},{16,48},{32,64},{48,80},{64,96},{80,112},{96,0},{112,16},{1... | collective-permute-start | bytes 12296 | tf_op jit(solution)/shard_map/ppermute | solution.py:48
  140.0 6.6 %collective-permute-start.31 = (f32[8,128]{1,0:T(8,128)S(1)}, f32[8,128]{1,0:T(8,128)S(1)}, u32[]{:S(2)}, u32[]{:S(2)}) collective-permute-start(f32[8,128]{1,0:T(8,128)S(1)} %add_add_fusion.1), channel_id=1, source_target_pairs={{0,96},{16,112},{32,0},{48,16},{64,32},{80,48},{96,64},{112,80},{1... | collective-permute-start | bytes 12296 | tf_op jit(solution)/shard_map/ppermute | solution.py:48
  142.4 9.5 %collective-permute-start.26 = (f32[24,384]{1,0:T(8,128)S(1)}, f32[24,384]{1,0:T(8,128)S(1)}, u32[]{:S(2)}, u32[]{:S(2)}) collective-permute-start(f32[24,384]{1,0:T(8,128)S(1)} %get-tuple-element.160), channel_id=1, source_target_pairs={{0,0},{1,32},{2,64},{3,96},{4,1},{5,33},{6,65},{7,97},{8,2},{9,34}... | collective-permute-start | bytes 110600 | tf_op jit(solution)/shard_map/ppermute | solution.py:492
  146.6 1.2 collective-permute-start.33

commit v5 on v4

--- a/solution.py
+++ b/solution.py
@@ -113,7 +113,7 @@
         out[SEG:, SEG * part : SEG * part + SEG] = log[8 * part : 8 * part + 8]
 
 
-def decays(x, toks, first, cirow, cerow, ci, ce, la):
+def decays(x, toks, own, first, cirow, cerow, ci, ce, la):
     s = lax.broadcasted_iota(jnp.int32, (SEG, SEG), 0)
     t = lax.broadcasted_iota(jnp.int32, (SEG, SEG), 1)
     tri = jnp.where(s <= t, 1.0, 0.0).astype(F32)
@@ -125,8 +125,12 @@
         for j in range(NH):
             mine = jnp.zeros((1, SEG), F32)
             for p in range(NX):
-                row, part = (NH * p + j) % 8, (NH * p + j) // 8
-                its = tok[SEG + row : SEG + row + 1, SEG * part : SEG * part + SEG]
+                h = NH * p + j
+                if tok.shape[0] > SEG:
+                    row, part = SEG + h % 8, h // 8
+                    its = tok[row : row + 1, SEG * part : SEG * part + SEG]
+                else:
+                    its = own[h : h + 1]
                 mine = jnp.where(x == p, its, mine)
             la[j : j + 1] = mine
         through = exact(la[...], tri, 1, 0)
@@ -137,8 +141,8 @@
         ce[k] = exact(before, spread, 0, 0)
 
 
-def tok_part(at, toks, first, w_in, w_bc, cirow, cerow, ci, ce, tokb, xs, xfr, bc, ends, la):
-    decays(at[0], toks, first, cirow, cerow, ci, ce, la)
+def tok_part(at, toks, own, first, w_in, w_bc, cirow, cerow, ci, ce, tokb, xs, xfr, bc, ends, la):
+    decays(at[0], toks, own, first, cirow, cerow, ci, ce, la)
     for k, t in enumerate(toks, first):
         tokb[k] = t[:SEG].astype(BF16)
 
@@ -159,8 +163,8 @@
     lax.fori_loop(0, len(toks), segment, 0)
 
 
-def tok_kernel_a(at, t0, t1, t3, w_in, w_bc, *refs):
-    tok_part(at, (t0, t1, t3), 0, w_in, w_bc, *refs)
+def tok_kernel_a(at, t0, own, t1, t3, w_in, w_bc, *refs):
+    tok_part(at, (t0, t1, t3), own, 0, w_in, w_bc, *refs)
 
 
 def tok_kernel_b(at, t2, w_in, w_bc, *refs):
@@ -168,11 +172,44 @@
     full = (*full, ends)
     for a, b in zip(given, full, strict=True):
         b[: NX - 1] = a[...]
-    tok_part(at, (t2,), NX - 1, w_in, w_bc, *full, la)
+    tok_part(at, (t2,), None, NX - 1, w_in, w_bc, *full, la)
     x, y, ci = at[0], at[2], full[2]
     up = row_scan(range(NX), ends, FIRST, ci, x, pre, 0)
     down = row_scan(reversed(range(NX)), ends, SECOND, ci, x, pre, 1)
     send_rows(up, down, row_log(ci), y, s_p, s_m, s_2)
+
+
+def decay_kernel(first, count, at, cirow, cerow, ci, ce, xs, bc, mat, mat_t, y):
+    def segment(i, _):
+        k = first + i
+        b, c = bc[k, :, :NS], bc[k, :, NS:]
+        t = lax.broadcasted_iota(jnp.int32, (SEG, SEG), 0)
+        s = lax.broadcasted_iota(jnp.int32, (SEG, SEG), 1)
+        low, same = t > s, t == s
+        scores = dot(c, b, 1, 1)
+        lane = lax.broadcasted_iota(jnp.int32, (SEG, 2 * HD), 1)
+        for pair in range(NH // 2):
+            cols = slice(pair * 2 * HD, (pair + 1) * 2 * HD)
+            xp = xs[k, :, cols]
+            rows = jnp.zeros((SEG, 2 * HD), F32)
+            for j in range(2):
+                h = 2 * pair + j
+                at_t = slice(h * HD, h * HD + 1)
+                diff = jnp.where(
+                    low,
+                    ci[k, :, at_t] - cirow[k, h : h + 1, :],
+                    cerow[k, h : h + 1, :] - ce[k, :, at_t],
+                )
+                decay = jnp.where(same, 2.0, jnp.exp(diff))
+                mat[i, h] = decay.astype(BF16)
+                w = (decay * scores).astype(BF16)
+                mat_t[i, h] = w.T
+                xm = jnp.where((lane < HD) if j == 0 else (lane >= HD), xp, jnp.zeros_like(xp))
+                rows = rows + dot(w, xm, 1, 0)
+            y[i, :, cols] = rows
+        return 0
+
+    lax.fori_loop(0, count, segment, 0)
 
 
 def cot_part(cots, first, w_out, ci, ce, bc, cotb, dy, dyfr, ends):
@@ -221,7 +258,8 @@
 
 
 def inner_kernel(
-    at, xs, bc, dy_a, dy_b, dyfr_a, dyfr_b, cotb_a, cotb_b, ci, ce, cirow, cerow, pre, r_p, r_m, r_2,
+    at, xs, bc, dy_a, dy_b, dyfr_a, dyfr_b, cotb_a, cotb_b, ci, ce, pre, r_p, r_m, r_2,
+    mat_a, mat_t_a, y_a, mat_b, mat_t_b, y_b,
     g, dxi, dci, dbi, sr, yb,
 ):
     x, y_at = at[0], at[2]
@@ -229,51 +267,37 @@
     enter(pre, 0, up, ci, x, range(NX), sr, pl.ds(0, HC))
     enter(pre, 1, down, ci, x, reversed(range(NX)), sr, pl.ds(HC, HC))
 
-    def run(first, dy, dyfr):
-        def segment(i, _):
-            k = first + i
+    def run(first, count, mat, mat_t, y_in, m0, dy, dyfr, d0):
+        def segment(n, _):
+            k, m, i = first + n, m0 + n, d0 + n
             b, c = bc[k, :, :NS], bc[k, :, NS:]
-            t = lax.broadcasted_iota(jnp.int32, (SEG, SEG), 0)
-            s = lax.broadcasted_iota(jnp.int32, (SEG, SEG), 1)
-            low, same = t > s, t == s
-            scores = dot(c, b, 1, 1)
-            scores = jnp.where(same, 2.0 * scores, scores)
             lane = lax.broadcasted_iota(jnp.int32, (SEG, 2 * HD), 1)
             carry = dot(c, sr[k], 1, 0)
             total = jnp.zeros((SEG, SEG), F32)
             for pair in range(NH // 2):
                 cols = slice(pair * 2 * HD, (pair + 1) * 2 * HD)
                 xp, dp = xs[k, :, cols], dy[i, :, cols]
-                ws, xm, dm = [], [], []
+                dx = jnp.zeros((SEG, 2 * HD), F32)
                 for j in range(2):
                     h = 2 * pair + j
-                    at_t = slice(h * HD, h * HD + 1)
-                    diff = jnp.where(
-                        low,
-                        ci[k, :, at_t] - cirow[k, h : h + 1, :],
-                        cerow[k, h : h + 1, :] - ce[k, :, at_t],
-                    )
-                    decay = jnp.exp(diff)
-                    mine = (lane < HD) if j == 0 else (lane >= HD)
-                    xm.append(jnp.where(mine, xp, jnp.zeros_like(xp)))
-                    dm.append(jnp.where(mine, dp, jnp.zeros_like(dp)))
-                    ws.append((decay * scores).astype(BF16))
-                    total = total + decay * dot(dm[j], xp, 1, 1)
-                y = dot(ws[0], xm[0], 1, 0) + dot(ws[1], xm[1], 1, 0)
+                    dm = jnp.where((lane < HD) if j == 0 else (lane >= HD), dp, jnp.zeros_like(dp))
+                    total = total + mat[m, h].astype(F32) * dot(dm, xp, 1, 1)
+                    dx = dx + dot(mat_t[m, h], dm, 1, 0)
                 last = ci[k, SEG - 1 : SEG, cols]
-                y = y + carry[:, cols] * jnp.exp(ci[k, :, cols])
+                y = y_in[m, :, cols] + carry[:, cols] * jnp.exp(ci[k, :, cols])
                 y = y + carry[:, slice(HC + cols.start, HC + cols.stop)] * jnp.exp(last - ce[k, :, cols])
                 yb[pl.ds(k * SEG, SEG), cols] = y.astype(BF16)
-                dxi[k, :, cols] = dot(ws[0], dm[0], 0, 0) + dot(ws[1], dm[1], 0, 0)
-            total = jnp.where(same, 2.0 * total, total).astype(BF16)
+                dxi[k, :, cols] = dx
+            total = total.astype(BF16)
             dci[k] = dot(total, b, 1, 0) + dot(dyfr[i], sr[k], 1, 1)
             dbi[k] = dot(total, c, 0, 0)
             return 0
 
-        lax.fori_loop(0, 2, segment, 0)
-
-    run(0, dy_a, dyfr_a)
-    run(2, dy_b, dyfr_b)
+        lax.fori_loop(0, count, segment, 0)
+
+    run(0, 2, mat_a, mat_t_a, y_a, 0, dy_a, dyfr_a, 0)
+    run(2, 1, mat_a, mat_t_a, y_a, 2, dy_b, dyfr_b, 0)
+    run(3, 1, mat_b, mat_t_b, y_b, 0, dy_b, dyfr_b, 1)
     half = 2 * SEG
     raw = dot(yb[:half, :], cotb_a[...].reshape(half, DM), 0, 0)
     raw = raw + dot(yb[half:, :], cotb_b[...].reshape(half, DM), 0, 0)
@@ -393,7 +417,8 @@
 
 
 def rows_exchange(s_p, s_m, s_2):
-    return [move(s_p, "y", 1), move(s_m, "y", -1), move(s_2, "y", 2)]
+    r_2 = move(s_2, "y", 2)
+    return [move(s_p, "y", 1), move(s_m, "y", -1), r_2]
 
 
 def deal(at, which, terms, rows, cols):
@@ -401,7 +426,8 @@
     p0, p1, p2, p3 = call(
         functools.partial(deal_kernel, which), [((rows, cols), F32)] * 4, [((4, rows, cols), F32)], [at, *terms]
     )
-    return [p0, move(p1, axis, 1), move(p2, axis, 2), move(p3, axis, 3)]
+    r_2 = move(p2, axis, 2)
+    return [p0, move(p1, axis, 1), r_2, move(p3, axis, 3)]
 
 
 def body(tokens, cotangent, log_decay, w_in, w_bc, w_out):
@@ -421,9 +447,10 @@
     wi = lax.dynamic_slice(w_in, (0, x * HC), (DM, HC))
     wo = lax.dynamic_slice(w_out, (x * HC, 0), (HC, DM))
     t3, t1 = move(t0, "x", 1), move(t0, "x", -1)
-    t3, t1, c0 = tie((t3, t1, c0))
+    t3, c0 = tie((t3, c0))
     t2 = move(t3, "x", 1)
-    c1 = move(c0, "x", -1)
+    c0_l, t1 = tie((c0, t1))
+    c1 = move(c0_l, "x", -1)
     t1, wi, wo = tie((t1, wi, wo))
 
     tall = ((TALL, HC), F32)
@@ -441,9 +468,17 @@
     flops = 2 * SEG * (DM * (HC + 2 * NS) + NS * 2 * HC)
     row = ((8, SEG), F32)
     three = call(
-        tok_kernel_a, [*of_tokens(3), ends(3)], [row], [at, t0, t1, t3, wi, w_bc], 3 * flops
-    )
-    c0_r, t2, c1, *three = tie((c0, t2, c1, *three))
+        tok_kernel_a, [*of_tokens(3), ends(3)], [row], [at, tokens[0], log_decay[0], t1, t3, wi, w_bc], 3 * flops
+    )
+    def mats(n):
+        return [((n, NH, SEG, SEG), BF16), ((n, NH, SEG, SEG), BF16), ((n, SEG, HC), F32)]
+
+    within = 2 * SEG * SEG * 2 * HC
+    mats_a = call(
+        functools.partial(decay_kernel, 0, 3), mats(3), [], [at, *three[:4], three[5], three[7]], 3 * within
+    )
+    c0_r, t2, c1, *both = tie((c0, t2, c1, *three, *mats_a))
+    three, mats_a = both[:9], both[9:]
     c3, c2 = move(c0_r, "x", 1), move(c1, "x", -1)
     cirow, cerow, ci, ce, tokb, xs, xfr, bc, pre_s, *s_rows = call(
         tok_kernel_b, [*of_tokens(4), edges, tall, tall, tall], [ends(4), row], [at, t2, wi, w_bc, *three], flops
@@ -452,8 +487,10 @@
     two = [((2, SEG, DM), BF16), ((2, SEG, HC), BF16), ((2, SEG, 2 * HC), BF16)]
     flops = 1024 * (DM * HC + NS * 2 * HC)
     cotb_a, dy_a, dyfr_a, ends_a = call(
-        cot_kernel_a, [*two, ends(2)], [ends(4)], [at, c0, c1, wo, ci, ce, bc], flops
-    )
+        cot_kernel_a, [*two, ends(2)], [ends(4)], [at, cotangent[0], c1, wo, ci, ce, bc], flops
+    )
+    mats_b = call(functools.partial(decay_kernel, 3, 1), mats(1), [], [at, cirow, cerow, ci, ce, xs, bc], within)
+    c3, c2, ends_a, *mats_b = tie((c3, c2, ends_a, *mats_b))
     cotb_b, dy_b, dyfr_b, pre_d, *s_rows = call(
         cot_kernel_b, [*two, edges, tall, tall, tall], [ends(4)], [at, c3, c2, wo, ci, ce, bc, ends_a], flops
     )
@@ -462,7 +499,7 @@
         inner_kernel,
         [((2, ROWS, HC), F32), ((NX, SEG, HC), F32), ((NX, SEG, NS), F32), ((NX, SEG, NS), F32)],
         [((NX, NS, 2 * HC), BF16), ((NX * SEG, HC), BF16)],
-        [at, xs, bc, dy_a, dy_b, dyfr_a, dyfr_b, cotb_a, cotb_b, ci, ce, cirow, cerow, pre_s, *q_rows],
+        [at, xs, bc, dy_a, dy_b, dyfr_a, dyfr_b, cotb_a, cotb_b, ci, ce, pre_s, *q_rows, *mats_a, *mats_b],
         2 * 1024 * (HC * DM + 5 * SEG * HC + 6 * NS * HC),
     )
     keep, send, dz = call(
@@ -473,11 +510,11 @@
         2 * 1024 * (WIDE * DM + 4 * NS * HC),
     )
     got = move(send, "c", 1)
+    terms = deal(at, 2, [keep, got], 96, ALL)
     whole, half = ((SEG, DM), F32), ((HALF, DM), F32)
     d0, d1, d2a, d2b, d3 = call(
         tokens_kernel, [whole, whole, half, half, whole], [], [at, dz, wi, w_bc], 2 * 1024 * WIDE * DM
     )
-    terms = deal(at, 2, [keep, got], 96, ALL)
     r_a, r_b = move(d2a, "x", 1), move(d2b, "x", -1)
     s1, s3 = call(pass_kernel, [whole, whole], [], [at, d1, d3, r_a, r_b])
     m1, m3 = move(s1, "x", 1), move(s3, "x", -1)

time: 154 us -> 151 us (0.981)
  waiting for transfers between devices: 61.3 us -> 56.6 us
  Pallas kernels: 33.1 us -> 34.9 us
    ppermute x33, waiting for transfers between devices: 57.3 us -> 52.4 us  [move(): return lax.ppermute(value, name, pairs)]
    pallas_call x13 -> x15, Pallas kernels: 33 us -> 34.9 us  [call(): pl.pallas_call(kernel, out_shape=[jax.ShapeDtypeStruct(*o) for o in outs]...]
  transfers between devices with their start and end apart: 34 -> 34, of which waited for: 20 -> 20; matrix products, arithmetic and copies ran while one was open for 3% -> 3% of each run, Pallas kernels for 18% -> 20%
where the time goes in v5:
time: 151 us
  waiting for transfers between devices  56.6 us (37%)
  starting transfers between devices  51.3 us (34%)
  Pallas kernels  34.9 us (23%)
  local copies, waits for them, and re-layouts  4.25 us (3%)
  other arithmetic  2.91 us (2%)
    ppermute x33, waiting for transfers between devices, move(): return lax.ppermute(value, name, pairs)  52.4 us
    ppermute x33, starting transfers between devices, move(): return lax.ppermute(value, name, pairs)  47.4 us
    pallas_call x15, Pallas kernels, call(): pl.pallas_call(kernel, out_shape=[jax.ShapeDtypeStruct(*o) for o in outs]...  34.9 us
    ppermute x1, waiting for transfers between devices, body(): rows_out = lax.ppermute(rows_out, ('rec', 'seq'), pairs)  4.28 us
    ppermute x1, starting transfers between devices, body(): rows_out = lax.ppermute(rows_out, ('rec', 'seq'), pairs)  3.89 us
  transfers between devices with their start and end apart: 34, of which 20 were waited for; matrix products, arithmetic and copies ran while one was open for 3% of the time, Pallas kernels for 20%

profile of v5, /device:TPU:6, one launch (start us, length us, event | category | flops | bytes accessed | tf_op | source)
XLA Modules:
  0.0 150.9 jit_solution(1970861225726914940)
XLA Ops:
  0.7 1.1 copy-done.4
  1.8 0.7 copy-done.6
  3.1 1.6 %collective-permute-start.2 = (f32[264,768]{1,0:T(8,128)S(1)}, f32[264,768]{1,0:T(8,128)S(1)}, u32[]{:S(2)}, u32[]{:S(2)}) collective-permute-start(f32[264,768]{1,0:T(8,128)S(1)} %shard_map.93), channel_id=1, source_target_pairs={{0,3},{1,0},{2,1},{3,2},{4,7},{5,4},{6,5},{7,6},{8,11},{9,8},{10,9... | collective-permute-start | bytes 2433032 | tf_op jit(solution)/shard_map/ppermute | solution.py:48
  4.7 1.9 %bitcast_convert_fusion = f32[256,768]{1,0:T(8,128)} fusion(bf16[1,256,768]{2,1,0:T(8,128)(2,1)} %param.7), kind=kLoop, calls=%fused_computation.7 | loop fusion | flops 196608 | bytes 1179648 | tf_op jit(solution)/shard_map/convert_element_type | solution.py:446
  6.6 16.0 %collective-permute-done.t3 = f32[264,768]{1,0:T(8,128)} collective-permute-done((f32[264,768]{1,0:T(8,128)S(1)}, f32[264,768]{1,0:T(8,128)}, u32[]{:S(2)}, u32[]{:S(2)}) %collective-permute-start) | collective-permute-done | bytes 811040 | tf_op jit(solution)/shard_map/ppermute | solution.py:48
  22.6 1.5 collective-permute-start.1
  24.1 0.9 copy-done.8
  25.7 1.2 constant_dynamic-slice_fusion.w_out
  27.1 6.6 %shard_map.94 = (f32[3,8,256]{2,1,0:T(8,128)S(1)}, f32[3,8,256]{2,1,0:T(8,128)S(1)}, f32[3,256,384]{2,1,0:T(8,128)S(1)}, f32[3,256,384]{2,1,0:T(8,128)S(1)}, bf1...) custom-call(s32[4]{0:T(128)S(1)} %pad_add_fusion.at, ...), custom_call_target="tpu_custom_call" | custom-call | flops 905969664 | bytes 3022864 | tf_op jit(solution)/shard_map/pallas_call | solution.py:408
  33.7 3.5 %shard_map.95 = (bf16[3,6,256,256]{3,2,1,0:T(8,128)(2,1)S(1)}, bf16[3,6,256,256]{3,2,1,0:T(8,128)(2,1)S(1)}, f32[3,256,384]{2,1,0:T(8,128)S(1)}) custom-call(s32[4]{0:T(128)S(1)} %pad_add_fusion.at, f32[3,8,256]{2,1,0:T(8,128)S(1)} %get-tuple-element.119.cirow.refs_0_, f32[3,8,256]{2,1,0:T(8,128)S(1)} %get-tuple-element.120.cerow.refs_1_, ...), custom_call_target="tpu_custom_call" | custom-call | flops 301989888 | bytes 3391504 | tf_op jit(solution)/shard_map/pallas_call | solution.py:408
  37.2 7.3 %collective-permute-done.3.c1 = f32[256,768]{1,0:T(8,128)} collective-permute-done((f32[256,768]{1,0:T(8,128)}, f32[256,768]{1,0:T(8,128)}, u32[]{:S(2)}, u32[]{:S(2)}) %collective-permute-start.3) | collective-permute-done | bytes 786464 | tf_op jit(solution)/shard_map/ppermute | solution.py:48
  44.5 2.0 %collective-permute-start.5 = (f32[256,768]{1,0:T(8,128)}, f32[256,768]{1,0:T(8,128)S(1)}, u32[]{:S(2)}, u32[]{:S(2)}) collective-permute-start(f32[256,768]{1,0:T(8,128)} %collective-permute-done.3.c1), channel_id=1, source_target_pairs={{0,3},{1,0},{2,1},{3,2},{4,7},{5,4},{6,5},{7,6},{8,11},{9,8},{10,9... | collective-permute-start | bytes 2359304 | tf_op jit(solution)/shard_map/ppermute | solution.py:48
  46.6 2.9 %shard_map.96 = (f32[4,8,256]{2,1,0:T(8,128)S(1)}, f32[4,8,256]{2,1,0:T(8,128)S(1)}, f32[4,256,384]{2,1,0:T(8,128)S(1)}, f32[4,256,384]{2,1,0:T(8,128)S(1)}, bf1...) custom-call(s32[4]{0:T(128)S(1)} %pad_add_fusion.at, ...), custom_call_target="tpu_custom_call" | custom-call | flops 301989888 | bytes 8724496 | tf_op jit(solution)/shard_map/pallas_call | solution.py:408
  49.5 2.0 %collective-permute-start.9 = (f32[136,384]{1,0:T(8,128)S(1)}, f32[136,384]{1,0:T(8,128)S(1)}, u32[]{:S(2)}, u32[]{:S(2)}) collective-permute-start(f32[136,384]{1,0:T(8,128)S(1)} %get-tuple-element.157), channel_id=1, source_target_pairs={{0,4},{1,5},{2,6},{3,7},{4,8},{5,9},{6,10},{7,11},{8,12},{9,13},{1... | collective-permute-start | bytes 626696 | tf_op jit(solution)/shard_map/ppermute | solution.py:48
  51.4 1.5 %collective-permute-start.10 = (f32[136,384]{1,0:T(8,128)S(1)}, f32[136,384]{1,0:T(8,128)S(1)}, u32[]{:S(2)}, u32[]{:S(2)}) collective-permute-start(f32[136,384]{1,0:T(8,128)S(1)} %get-tuple-element.158), channel_id=1, source_target_pairs={{0,12},{1,13},{2,14},{3,15},{4,0},{5,1},{6,2},{7,3},{8,4},{9,5},{1... | collective-permute-start | bytes 626696 | tf_op jit(solution)/shard_map/ppermute | solution.py:48
  52.9 2.1 %collective-permute-start.11 = (f32[136,384]{1,0:T(8,128)S(1)}, f32[136,384]{1,0:T(8,128)S(1)}, u32[]{:S(2)}, u32[]{:S(2)}) collective-permute-start(f32[136,384]{1,0:T(8,128)S(1)} %get-tuple-element.159), channel_id=1, source_target_pairs={{0,8},{1,9},{2,10},{3,11},{4,12},{5,13},{6,14},{7,15},{8,0},{9,1},... | collective-permute-start | bytes 626696 | tf_op jit(solution)/shard_map/ppermute | solution.py:48
  55.1 1.5 %shard_map.98 = (bf16[1,6,256,256]{3,2,1,0:T(8,128)(2,1)S(1)}, bf16[1,6,256,256]{3,2,1,0:T(8,128)(2,1)S(1)}, f32[1,256,384]{2,1,0:T(8,128)S(1)}) custom-call(s32[4]{0:T(128)S(1)} %pad_add_fusion.at, f32[4,8,256]{2,1,0:T(8,128)S(1)} %get-tuple-element.137.cirow, f32[4,8,256]{2,1,0:T(8,128)S(1)} %get-tuple-element.138.cerow, ...), custom_call_target="tpu_custom_call" | custom-call | flops 100663296 | bytes 4522000 | tf_op jit(solution)/shard_map/pallas_call | solution.py:408
  56.6 2.5 %shard_map.97 = (bf16[2,256,768]{2,1,0:T(8,128)(2,1)S(1)}, bf16[2,256,384]{2,1,0:T(8,128)(2,1)S(1)}, bf16[2,256,768]{2,1,0:T(8,128)(2,1)S(1)}, f32[2,128,768]{2,1,0:T(8,128)S(1)}) custom-call(s32[4]{0:T(128)S(1)} %pad_add_fusion.at, bf16[256,768]{1,0:T(8,128)(2,1)S(1)} %bitcast.10, f32[256,768]{1,0:T(8,128)} %collective-permute-done.3.c1, ...), custom_call_target="tpu_custom_call" | custom-call | flops 402653184 | bytes 5439504 | tf_op jit(solution)/shard_map/pallas_call | solution.py:408
  59.1 2.7 %collective-permute-done.4.c2 = f32[256,768]{1,0:T(8,128)S(1)} collective-permute-done((f32[256,768]{1,0:T(8,128)}, f32[256,768]{1,0:T(8,128)S(1)}, u32[]{:S(2)}, u32[]{:S(2)}) %collective-permute-start.4) | collective-permute-done | bytes 786464 | tf_op jit(solution)/shard_map/ppermute | solution.py:48
  61.8 1.2 collective-permute-done.5.c3
  63.0 2.1 %shard_map.99 = (bf16[2,256,768]{2,1,0:T(8,128)(2,1)S(1)}, bf16[2,256,384]{2,1,0:T(8,128)(2,1)S(1)}, bf16[2,256,768]{2,1,0:T(8,128)(2,1)S(1)}, f32[2,4,128,384]{...) custom-call(s32[4]{0:T(128)S(1)} %pad_add_fusion.at, ...), custom_call_target="tpu_custom_call" | custom-call | flops 402653184 | bytes 6619152 | tf_op jit(solution)/shard_map/pallas_call | solution.py:408
  65.2 2.1 %collective-permute-start.6 = (f32[136,384]{1,0:T(8,128)S(1)}, f32[136,384]{1,0:T(8,128)S(1)}, u32[]{:S(2)}, u32[]{:S(2)}) collective-permute-start(f32[136,384]{1,0:T(8,128)S(1)} %get-tuple-element.147), channel_id=1, source_target_pairs={{0,4},{1,5},{2,6},{3,7},{4,8},{5,9},{6,10},{7,11},{8,12},{9,13},{1... | collective-permute-start | bytes 626696 | tf_op jit(solution)/shard_map/ppermute | solution.py:48
  67.3 1.7 %collective-permute-start.7 = (f32[136,384]{1,0:T(8,128)S(1)}, f32[136,384]{1,0:T(8,128)S(1)}, u32[]{:S(2)}, u32[]{:S(2)}) collective-permute-start(f32[136,384]{1,0:T(8,128)S(1)} %get-tuple-element.148), channel_id=1, source_target_pairs={{0,12},{1,13},{2,14},{3,15},{4,0},{5,1},{6,2},{7,3},{8,4},{9,5},{1... | collective-permute-start | bytes 626696 | tf_op jit(solution)/shard_map/ppermute | solution.py:48
  69.0 1.9 %collective-permute-start.8 = (f32[136,384]{1,0:T(8,128)S(1)}, f32[136,384]{1,0:T(8,128)S(1)}, u32[]{:S(2)}, u32[]{:S(2)}) collective-permute-start(f32[136,384]{1,0:T(8,128)S(1)} %get-tuple-element.149), channel_id=1, source_target_pairs={{0,8},{1,9},{2,10},{3,11},{4,12},{5,13},{6,14},{7,15},{8,0},{9,1},... | collective-permute-start | bytes 626696 | tf_op jit(solution)/shard_map/ppermute | solution.py:48
  70.9 5.1 %shard_map.100 = (f32[2,384,384]{2,1,0:T(8,128)S(1)}, f32[4,256,384]{2,1,0:T(8,128)S(1)}, f32[4,256,128]{2,1,0:T(8,128)S(1)}, f32[4,256,128]{2,1,0:T(8,128)S(1)}) custom-call(s32[4]{0:T(128)S(1)} %pad_add_fusion.at, bf16[4,256,384]{2,1,0:T(8,128)(2,1)S(1)} %get-tuple-element.139.xs, bf16[4,256,256]{2,1,0:T(8,128)(2,1)S(1)} %get-tuple-element.130.bc, ...), custom_call_target="tpu_custom_call" | custom-call | flops 2214592512 | bytes 18452496 | tf_op jit(solution)/shard_map/pallas_call | solution.py:408
  76.5 4.0 %shard_map.101 = (f32[384,1024]{1,0:T(8,128)S(1)}, f32[384,1024]{1,0:T(8,128)S(1)}, bf16[4,256,640]{2,1,0:T(8,128)(2,1)S(1)}) custom-call(s32[4]{0:T(128)S(1)} %pad_add_fusion.at, bf16[4,256,768]{2,1,0:T(8,128)(2,1)S(1)} %get-tuple-element.128.tokb, bf16[4,256,768]{2,1,0:T(8,128)(2,1)S(1)} %get-tuple-element.129.xfr, ...), custom_call_target="tpu_custom_call" | custom-call | flops 1409286144 | bytes 12816400 | tf_op jit(solution)/shard_map/pallas_call | solution.py:408
  80.6 1.9 %shard_map.102 = (f32[256,768]{1,0:T(8,128)S(1)}, f32[256,768]{1,0:T(8,128)S(1)}, f32[128,768]{1,0:T(8,128)S(1)}, f32[128,768]{1,0:T(8,128)S(1)}, f32[256,768]{1,0:T(8,128)S(1)}) custom-call(s32[4]{0:T(128)S(1)} %pad_add_fusion.at, bf16[4,256,640]{2,1,0:T(8,128)(2,1)S(1)} %get-tuple-element.170.dz, bf16[768,384]{1,0:T(8,128)(2,1)S(1)} %constant_dynamic-slice_fusion.1.w_in, ...), custom_call_target="tpu_custom_call" | custom-call | flops 1006632960 | bytes 2293776 | tf_op jit(solution)/shard_map/pallas_call | solution.py:408
  82.5 0.6 collective-permute-start.12
  83.2 1.5 collective-permute-start.13
  84.6 0.8 shard_map.104
  85.4 1.2 collective-permute-start.17
  86.7 2.4 %collective-permute-start.18 = (f32[96,1024]{1,0:T(8,128)S(1)}, f32[96,1024]{1,0:T(8,128)S(1)}, u32[]{:S(2)}, u32[]{:S(2)}) collective-permute-start(f32[96,1024]{1,0:T(8,128)S(1)} %get-tuple-element.182), channel_id=1, source_target_pairs={{0,8},{1,9},{2,10},{3,11},{4,12},{5,13},{6,14},{7,15},{8,0},{9,1},... | collective-permute-start | bytes 1179656 | tf_op jit(solution)/shard_map/ppermute | solution.py:48
  89.0 0.8 collective-permute-start.19
  89.8 4.3 %collective-permute-done.12.r_a = f32[128,768]{1,0:T(8,128)S(1)} collective-permute-done((f32[128,768]{1,0:T(8,128)S(1)}, f32[128,768]{1,0:T(8,128)S(1)}, u32[]{:S(2)}, u32[]{:S(2)}) %collective-permute-start.12) | collective-permute-done | bytes 393248 | tf_op jit(solution)/shard_map/ppermute | solution.py:48
  94.1 1.5 collective-permute-done.13.r_b
  95.6 0.7 shard_map.103
  96.6 3.0 %collective-permute-start.14 = (f32[256,768]{1,0:T(8,128)S(1)}, f32[256,768]{1,0:T(8,128)S(1)}, u32[]{:S(2)}, u32[]{:S(2)}) collective-permute-start(f32[256,768]{1,0:T(8,128)S(1)} %get-tuple-element.176), channel_id=1, source_target_pairs={{0,1},{1,2},{2,3},{3,0},{4,5},{5,6},{6,7},{7,4},{8,9},{9,10},{10,1... | collective-permute-start | bytes 2359304 | tf_op jit(solution)/shard_map/ppermute | solution.py:48
  99.6 6.8 %collective-permute-done.18.refs_2_ = f32[96,1024]{1,0:T(8,128)S(1)} collective-permute-done((f32[96,1024]{1,0:T(8,128)S(1)}, f32[96,1024]{1,0:T(8,128)S(1)}, u32[]{:S(2)}, u32[]{:S(2)}) %collective-permute-start.18) | collective-permute-done | bytes 393248 | tf_op jit(solution)/shard_map/ppermute | solution.py:48
  106.7 0.7 shard_map.105
  107.4 2.0 %collective-permute-start.20 = (f32[24,1024]{1,0:T(8,128)S(1)}, f32[24,1024]{1,0:T(8,128)S(1)}, u32[]{:S(2)}, u32[]{:S(2)}) collective-permute-start(f32[24,1024]{1,0:T(8,128)S(1)} %get-tuple-element.185), channel_id=1, source_target_pairs={{0,32},{16,48},{32,64},{48,80},{64,96},{80,112},{96,0},{112,16},{1... | collective-permute-start | bytes 294920 | tf_op jit(solution)/shard_map/ppermute | solution.py:48
  109.4 3.6 %collective-permute-start.21 = (f32[24,1024]{1,0:T(8,128)S(1)}, f32[24,1024]{1,0:T(8,128)S(1)}, u32[]{:S(2)}, u32[]{:S(2)}) collective-permute-start(f32[24,1024]{1,0:T(8,128)S(1)} %get-tuple-element.186), channel_id=1, source_target_pairs={{0,64},{16,80},{32,96},{48,112},{64,0},{80,16},{96,32},{112,48},{1... | collective-permute-start | bytes 294920 | tf_op jit(solution)/shard_map/ppermute | solution.py:48
  113.0 1.0 collective-permute-start.22
  114.0 1.2 collective-permute-done.20.b
  115.2 1.6 %collective-permute-done.21.c = f32[24,1024]{1,0:T(8,128)S(1)} collective-permute-done((f32[24,1024]{1,0:T(8,128)S(1)}, f32[24,1024]{1,0:T(8,128)S(1)}, u32[]{:S(2)}, u32[]{:S(2)}) %collective-permute-start.21) | collective-permute-done | bytes 98336 | tf_op jit(solution)/shard_map/ppermute | solution.py:48
  116.8 0.8 collective-permute-done.22.d
  117.6 0.7 shard_map.106
  118.3 1.8 %collective-permute-start.23 = (f32[40,384]{1,0:T(8,128)S(1)}, f32[40,384]{1,0:T(8,128)S(1)}, u32[]{:S(2)}, u32[]{:S(2)}) collective-permute-start(f32[40,384]{1,0:T(8,128)S(1)} %get-tuple-element.189), channel_id=1, source_target_pairs={{0,1},{1,2},{2,3},{3,0},{4,5},{5,6},{6,7},{7,4},{8,9},{9,10},{10,1... | collective-permute-start | bytes 184328 | tf_op jit(solution)/shard_map/ppermute | solution.py:48
  120.1 0.6 collective-permute-start.24
  121.1 1.5 collective-permute-done.23.b
  122.6 3.3 %collective-permute-done.24.c = f32[40,384]{1,0:T(8,128)S(1)} collective-permute-done((f32[40,384]{1,0:T(8,128)S(1)}, f32[40,384]{1,0:T(8,128)S(1)}, u32[]{:S(2)}, u32[]{:S(2)}) %collective-permute-start.24) | collective-permute-done | bytes 61472 | tf_op jit(solution)/shard_map/ppermute | solution.py:48
  125.9 0.6 collective-permute-done.25.d
  126.5 0.7 shard_map.107
  127.2 1.9 %collective-permute-start.29 = (f32[8,128]{1,0:T(8,128)S(1)}, f32[8,128]{1,0:T(8,128)S(1)}, u32[]{:S(2)}, u32[]{:S(2)}) collective-permute-start(f32[8,128]{1,0:T(8,128)S(1)} %shard_map.107), channel_id=1, source_target_pairs={{0,8},{1,9},{2,10},{3,11},{4,12},{5,13},{6,14},{7,15},{8,0},{9,1},... | collective-permute-start | bytes 12296 | tf_op jit(solution)/shard_map/ppermute | solution.py:48
  129.1 2.1 %collective-permute-start.27 = (f32[8,128]{1,0:T(8,128)S(1)}, f32[8,128]{1,0:T(8,128)S(1)}, u32[]{:S(2)}, u32[]{:S(2)}) collective-permute-start(f32[8,128]{1,0:T(8,128)S(1)} %shard_map.107), channel_id=1, source_target_pairs={{0,4},{1,5},{2,6},{3,7},{4,8},{5,9},{6,10},{7,11},{8,12},{9,13},{1... | collective-permute-start | bytes 12296 | tf_op jit(solution)/shard_map/ppermute | solution.py:48
  131.2 1.1 collective-permute-start.28
  132.6 1.3 collective-permute-done.27
  133.9 0.9 collective-permute-done.28
  134.8 2.2 %collective-permute-start.32 = (f32[8,128]{1,0:T(8,128)S(1)}, f32[8,128]{1,0:T(8,128)S(1)}, u32[]{:S(2)}, u32[]{:S(2)}) collective-permute-start(f32[8,128]{1,0:T(8,128)S(1)} %add_add_fusion.1), channel_id=1, source_target_pairs={{0,64},{16,80},{32,96},{48,112},{64,0},{80,16},{96,32},{112,48},{1... | collective-permute-start | bytes 12296 | tf_op jit(solution)/shard_map/ppermute | solution.py:48
  137.0 0.8 collective-permute-start.30
  137.8 2.5 %collective-permute-start.31 = (f32[8,128]{1,0:T(8,128)S(1)}, f32[8,128]{1,0:T(8,128)S(1)}, u32[]{:S(2)}, u32[]{:S(2)}) collective-permute-start(f32[8,128]{1,0:T(8,128)S(1)} %add_add_fusion.1), channel_id=1, source_target_pairs={{0,96},{16,112},{32,0},{48,16},{64,32},{80,48},{96,64},{112,80},{1... | collective-permute-start | bytes 12296 | tf_op jit(solution)/shard_map/ppermute | solution.py:48
  140.3 3.9 %collective-permute-start.26 = (f32[24,384]{1,0:T(8,128)S(1)}, f32[24,384]{1,0:T(8,128)S(1)}, u32[]{:S(2)}, u32[]{:S(2)}) collective-permute-start(f32[24,384]{1,0:T(8,128)S(1)} %get-tuple-element.192), channel_id=1, source_target_pairs={{0,0},{1,32},{2,64},{3,96},{4,1},{5,33},{6,65},{7,97},{8,2},{9,34}... | collective-permute-start | bytes 110600 | tf_op jit(solution)/shard_map/ppermute | solution.py:529
  144.3 0.9 fusion
  145.4 4.3 %collective-permute-done.26.rows_out = f32[24,384]{1,0:T(8,128)S(1)} collective-permute-done((f32[24,384]{1,0:T(8,128)S(1)}, f32[24,384]{1,0:T(8,128)S(1)}, u32[]{:S(2)}, u32[]{:S(2)}) %collective-permute-start.26) | collective-permute-done | bytes 36896 | tf_op jit(solution)/shard_map/ppermute | solution.py:529
  149.7 1.2 shard_map.108
  (48 shorter events, 3.7 us)
Async XLA Ops:
  0.6 25.0 %copy-start = (bf16[768,1536]{1,0:T(8,128)(2,1)S(1)}, bf16[768,1536]{1,0:T(8,128)(2,1)}, u32[]{:S(2)}) copy-start(bf16[768,1536]{1,0:T(8,128)(2,1)} %param.9) | copy-start | bytes 7077892
  0.6 1.1 copy-start.4
  1.8 0.7 copy-start.6
  2.6 24.3 %copy-start.7 = (f32[1,24,256]{2,1,0:T(8,128)S(1)}, f32[1,24,256]{2,1,0:T(8,128)}, u32[]{:S(2)}) copy-start(f32[1,24,256]{2,1,0:T(8,128)} %param.8) | copy-start | bytes 73732
  2.6 20.0 %collective-permute-start = (f32[264,768]{1,0:T(8,128)S(1)}, f32[264,768]{1,0:T(8,128)}, u32[]{:S(2)}, u32[]{:S(2)}) collective-permute-start(f32[264,768]{1,0:T(8,128)S(1)} %shard_map.93), channel_id=1, source_target_pairs={{0,1},{1,2},{2,3},{3,0},{4,5},{5,6},{6,7},{7,4},{8,9},{9,10},{10,1... | collective-permute-start | bytes 2433032 | tf_op jit(solution)/shard_map/ppermute | solution.py:48
  3.1 21.0 %collective-permute-start.2 = (f32[264,768]{1,0:T(8,128)S(1)}, f32[264,768]{1,0:T(8,128)S(1)}, u32[]{:S(2)}, u32[]{:S(2)}) collective-permute-start(f32[264,768]{1,0:T(8,128)S(1)} %shard_map.93), channel_id=1, source_target_pairs={{0,3},{1,0},{2,1},{3,2},{4,7},{5,4},{6,5},{7,6},{8,11},{9,8},{10,9... | collective-permute-start | bytes 2433032 | tf_op jit(solution)/shard_map/ppermute | solution.py:48
  22.6 21.9 %collective-permute-start.1 = (f32[264,768]{1,0:T(8,128)}, f32[264,768]{1,0:T(8,128)S(1)}, u32[]{:S(2)}, u32[]{:S(2)}) collective-permute-start(f32[264,768]{1,0:T(8,128)} %collective-permute-done.t3), channel_id=1, source_target_pairs={{0,1},{1,2},{2,3},{3,0},{4,5},{5,6},{6,7},{7,4},{8,9},{9,10},{10,1... | collective-permute-start | bytes 2433032 | tf_op jit(solution)/shard_map/ppermute | solution.py:48
  24.1 0.9 copy-start.8
  25.0 19.5 %collective-permute-start.3 = (f32[256,768]{1,0:T(8,128)}, f32[256,768]{1,0:T(8,128)}, u32[]{:S(2)}, u32[]{:S(2)}) collective-permute-start(f32[256,768]{1,0:T(8,128)} %bitcast_convert_fusion), channel_id=1, source_target_pairs={{0,3},{1,0},{2,1},{3,2},{4,7},{5,4},{6,5},{7,6},{8,11},{9,8},{10,9... | collective-permute-start | bytes 2359304 | tf_op jit(solution)/shard_map/ppermute | solution.py:48
  25.5 1.4 copy-start.3
  25.5 1.4 copy-start.5
  25.5 1.6 %copy-start.9 = (f32[264,768]{1,0:T(8,128)S(1)}, f32[264,768]{1,0:T(8,128)}, u32[]{:S(2)}) copy-start(f32[264,768]{1,0:T(8,128)} %copy-done.8) | copy-start | bytes 2433028
  44.5 17.3 %collective-permute-start.4 = (f32[256,768]{1,0:T(8,128)}, f32[256,768]{1,0:T(8,128)S(1)}, u32[]{:S(2)}, u32[]{:S(2)}) collective-permute-start(f32[256,768]{1,0:T(8,128)} %bitcast_convert_fusion), channel_id=1, source_target_pairs={{0,1},{1,2},{2,3},{3,0},{4,5},{5,6},{6,7},{7,4},{8,9},{9,10},{10,1... | collective-permute-start | bytes 2359304 | tf_op jit(solution)/shard_map/ppermute | solution.py:48
  44.5 18.5 %collective-permute-start.5 = (f32[256,768]{1,0:T(8,128)}, f32[256,768]{1,0:T(8,128)S(1)}, u32[]{:S(2)}, u32[]{:S(2)}) collective-permute-start(f32[256,768]{1,0:T(8,128)} %collective-permute-done.3.c1), channel_id=1, source_target_pairs={{0,3},{1,0},{2,1},{3,2},{4,7},{5,4},{6,5},{7,6},{8,11},{9,8},{10,9... | collective-permute-start | bytes 2359304 | tf_op jit(solution)/shard_map/ppermute | solution.py:48
  49.5 19.5 %collective-permute-start.9 = (f32[136,384]{1,0:T(8,128)S(1)}, f32[136,384]{1,0:T(8,128)S(1)}, u32[]{:S(2)}, u32[]{:S(2)}) collective-permute-start(f32[136,384]{1,0:T(8,128)S(1)} %get-tuple-element.157), channel_id=1, source_target_pairs={{0,4},{1,5},{2,6},{3,7},{4,8},{5,9},{6,10},{7,11},{8,12},{9,13},{1... | collective-permute-start | bytes 626696 | tf_op jit(solution)/shard_map/ppermute | solution.py:48
  51.4 19.5 %collective-permute-start.10 = (f32[136,384]{1,0:T(8,128)S(1)}, f32[136,384]{1,0:T(8,128)S(1)}, u32[]{:S(2)}, u32[]{:S(2)}) collective-permute-start(f32[136,384]{1,0:T(8,128)S(1)} %get-tuple-element.158), channel_id=1, source_target_pairs={{0,12},{1,13},{2,14},{3,15},{4,0},{5,1},{6,2},{7,3},{8,4},{9,5},{1... | collective-permute-start | bytes 626696 | tf_op jit(solution)/shard_map/ppermute | solution.py:48
  52.9 18.0 %collective-permute-start.11 = (f32[136,384]{1,0:T(8,128)S(1)}, f32[136,384]{1,0:T(8,128)S(1)}, u32[]{:S(2)}, u32[]{:S(2)}) collective-permute-start(f32[136,384]{1,0:T(8,128)S(1)} %get-tuple-element.159), channel_id=1, source_target_pairs={{0,8},{1,9},{2,10},{3,11},{4,12},{5,13},{6,14},{7,15},{8,0},{9,1},... | collective-permute-start | bytes 626696 | tf_op jit(solution)/shard_map/ppermute | solution.py:48
  55.1 1.5 %copy-start.2 = (bf16[1,256,768]{2,1,0:T(8,128)(2,1)S(1)}, bf16[1,256,768]{2,1,0:T(8,128)(2,1)}, u32[]{:S(2)}) copy-start(bf16[1,256,768]{2,1,0:T(8,128)(2,1)} %param.7) | copy-start | bytes 1179652
  65.2 10.8 %collective-permute-start.6 = (f32[136,384]{1,0:T(8,128)S(1)}, f32[136,384]{1,0:T(8,128)S(1)}, u32[]{:S(2)}, u32[]{:S(2)}) collective-permute-start(f32[136,384]{1,0:T(8,128)S(1)} %get-tuple-element.147), channel_id=1, source_target_pairs={{0,4},{1,5},{2,6},{3,7},{4,8},{5,9},{6,10},{7,11},{8,12},{9,13},{1... | collective-permute-start | bytes 626696 | tf_op jit(solution)/shard_map/ppermute | solution.py:48
  67.3 8.8 %collective-permute-start.7 = (f32[136,384]{1,0:T(8,128)S(1)}, f32[136,384]{1,0:T(8,128)S(1)}, u32[]{:S(2)}, u32[]{:S(2)}) collective-permute-start(f32[136,384]{1,0:T(8,128)S(1)} %get-tuple-element.148), channel_id=1, source_target_pairs={{0,12},{1,13},{2,14},{3,15},{4,0},{5,1},{6,2},{7,3},{8,4},{9,5},{1... | collective-permute-start | bytes 626696 | tf_op jit(solution)/shard_map/ppermute | solution.py:48
  69.0 7.6 %collective-permute-start.8 = (f32[136,384]{1,0:T(8,128)S(1)}, f32[136,384]{1,0:T(8,128)S(1)}, u32[]{:S(2)}, u32[]{:S(2)}) collective-permute-start(f32[136,384]{1,0:T(8,128)S(1)} %get-tuple-element.149), channel_id=1, source_target_pairs={{0,8},{1,9},{2,10},{3,11},{4,12},{5,13},{6,14},{7,15},{8,0},{9,1},... | collective-permute-start | bytes 626696 | tf_op jit(solution)/shard_map/ppermute | solution.py:48
  80.5 4.1 %collective-permute-start.16 = (f32[384,1024]{1,0:T(8,128)S(1)}, f32[384,1024]{1,0:T(8,128)S(1)}, u32[]{:S(2)}, u32[]{:S(2)}) collective-permute-start(f32[384,1024]{1,0:T(8,128)S(1)} %get-tuple-element.179), channel_id=1, source_target_pairs={{0,16},{16,0},{32,48},{48,32},{64,80},{80,64},{96,112},{112,96},{1... | collective-permute-start | bytes 4718600 | tf_op jit(solution)/shard_map/ppermute | solution.py:48
  82.5 11.6 %collective-permute-start.12 = (f32[128,768]{1,0:T(8,128)S(1)}, f32[128,768]{1,0:T(8,128)S(1)}, u32[]{:S(2)}, u32[]{:S(2)}) collective-permute-start(f32[128,768]{1,0:T(8,128)S(1)} %get-tuple-element.174), channel_id=1, source_target_pairs={{0,1},{1,2},{2,3},{3,0},{4,5},{5,6},{6,7},{7,4},{8,9},{9,10},{10,1... | collective-permute-start | bytes 1179656 | tf_op jit(solution)/shard_map/ppermute | solution.py:48
  83.2 12.4 %collective-permute-start.13 = (f32[128,768]{1,0:T(8,128)S(1)}, f32[128,768]{1,0:T(8,128)S(1)}, u32[]{:S(2)}, u32[]{:S(2)}) collective-permute-start(f32[128,768]{1,0:T(8,128)S(1)} %get-tuple-element.175), channel_id=1, source_target_pairs={{0,3},{1,0},{2,1},{3,2},{4,7},{5,4},{6,5},{7,6},{8,11},{9,8},{10,9... | collective-permute-start | bytes 1179656 | tf_op jit(solution)/shard_map/ppermute | solution.py:48
  85.4 14.2 %collective-permute-start.17 = (f32[96,1024]{1,0:T(8,128)S(1)}, f32[96,1024]{1,0:T(8,128)S(1)}, u32[]{:S(2)}, u32[]{:S(2)}) collective-permute-start(f32[96,1024]{1,0:T(8,128)S(1)} %get-tuple-element.181), channel_id=1, source_target_pairs={{0,4},{1,5},{2,6},{3,7},{4,8},{5,9},{6,10},{7,11},{8,12},{9,13},{1... | collective-permute-start | bytes 1179656 | tf_op jit(solution)/shard_map/ppermute | solution.py:48
  86.7 19.7 %collective-permute-start.18 = (f32[96,1024]{1,0:T(8,128)S(1)}, f32[96,1024]{1,0:T(8,128)S(1)}, u32[]{:S(2)}, u32[]{:S(2)}) collective-permute-start(f32[96,1024]{1,0:T(8,128)S(1)} %get-tuple-element.182), channel_id=1, source_target_pairs={{0,8},{1,9},{2,10},{3,11},{4,12},{5,13},{6,14},{7,15},{8,0},{9,1},... | collective-permute-start | bytes 1179656 | tf_op jit(solution)/shard_map/ppermute | solution.py:48
  89.0 17.7 %collective-permute-start.19 = (f32[96,1024]{1,0:T(8,128)S(1)}, f32[96,1024]{1,0:T(8,128)S(1)}, u32[]{:S(2)}, u32[]{:S(2)}) collective-permute-start(f32[96,1024]{1,0:T(8,128)S(1)} %get-tuple-element.183), channel_id=1, source_target_pairs={{0,12},{1,13},{2,14},{3,15},{4,0},{5,1},{6,2},{7,3},{8,4},{9,5},{1... | collective-permute-start | bytes 1179656 | tf_op jit(solution)/shard_map/ppermute | solution.py:48
  96.3 48.0 %collective-permute-start.15 = (f32[256,768]{1,0:T(8,128)S(1)}, f32[256,768]{1,0:T(8,128)S(1)}, u32[]{:S(2)}, u32[]{:S(2)}) collective-permute-start(f32[256,768]{1,0:T(8,128)S(1)} %get-tuple-element.177), channel_id=1, source_target_pairs={{0,3},{1,0},{2,1},{3,2},{4,7},{5,4},{6,5},{7,6},{8,11},{9,8},{10,9... | collective-permute-start | bytes 2359304 | tf_op jit(solution)/shard_map/ppermute | solution.py:48
  96.6 47.7 %collective-permute-start.14 = (f32[256,768]{1,0:T(8,128)S(1)}, f32[256,768]{1,0:T(8,128)S(1)}, u32[]{:S(2)}, u32[]{:S(2)}) collective-permute-start(f32[256,768]{1,0:T(8,128)S(1)} %get-tuple-element.176), channel_id=1, source_target_pairs={{0,1},{1,2},{2,3},{3,0},{4,5},{5,6},{6,7},{7,4},{8,9},{9,10},{10,1... | collective-permute-start | bytes 2359304 | tf_op jit(solution)/shard_map/ppermute | solution.py:48
  107.4 7.8 %collective-permute-start.20 = (f32[24,1024]{1,0:T(8,128)S(1)}, f32[24,1024]{1,0:T(8,128)S(1)}, u32[]{:S(2)}, u32[]{:S(2)}) collective-permute-start(f32[24,1024]{1,0:T(8,128)S(1)} %get-tuple-element.185), channel_id=1, source_target_pairs={{0,32},{16,48},{32,64},{48,80},{64,96},{80,112},{96,0},{112,16},{1... | collective-permute-start | bytes 294920 | tf_op jit(solution)/shard_map/ppermute | solution.py:48
  109.4 7.4 %collective-permute-start.21 = (f32[24,1024]{1,0:T(8,128)S(1)}, f32[24,1024]{1,0:T(8,128)S(1)}, u32[]{:S(2)}, u32[]{:S(2)}) collective-permute-start(f32[24,1024]{1,0:T(8,128)S(1)} %get-tuple-element.186), channel_id=1, source_target_pairs={{0,64},{16,80},{32,96},{48,112},{64,0},{80,16},{96,32},{112,48},{1... | collective-permute-start | bytes 294920 | tf_op jit(solution)/shard_map/ppermute | solution.py:48
  113.0 4.6 %collective-permute-start.22 = (f32[24,1024]{1,0:T(8,128)S(1)}, f32[24,1024]{1,0:T(8,128)S(1)}, u32[]{:S(2)}, u32[]{:S(2)}) collective-permute-start(f32[24,1024]{1,0:T(8,128)S(1)} %get-tuple-element.187), channel_id=1, source_target_pairs={{0,96},{16,112},{32,0},{48,16},{64,32},{80,48},{96,64},{112,80},{1... | collective-permute-start | bytes 294920 | tf_op jit(solution)/shard_map/ppermute | solution.py:48
  118.3 4.3 %collective-permute-start.23 = (f32[40,384]{1,0:T(8,128)S(1)}, f32[40,384]{1,0:T(8,128)S(1)}, u32[]{:S(2)}, u32[]{:S(2)}) collective-permute-start(f32[40,384]{1,0:T(8,128)S(1)} %get-tuple-element.189), channel_id=1, source_target_pairs={{0,1},{1,2},{2,3},{3,0},{4,5},{5,6},{6,7},{7,4},{8,9},{9,10},{10,1... | collective-permute-start | bytes 184328 | tf_op jit(solution)/shard_map/ppermute | solution.py:48
  120.1 5.8 %collective-permute-start.24 = (f32[40,384]{1,0:T(8,128)S(1)}, f32[40,384]{1,0:T(8,128)S(1)}, u32[]{:S(2)}, u32[]{:S(2)}) collective-permute-start(f32[40,384]{1,0:T(8,128)S(1)} %get-tuple-element.190), channel_id=1, source_target_pairs={{0,2},{1,3},{2,0},{3,1},{4,6},{5,7},{6,4},{7,5},{8,10},{9,11},{10,... | collective-permute-start | bytes 184328 | tf_op jit(solution)/shard_map/ppermute | solution.py:48
  120.7 5.8 %collective-permute-start.25 = (f32[40,384]{1,0:T(8,128)S(1)}, f32[40,384]{1,0:T(8,128)S(1)}, u32[]{:S(2)}, u32[]{:S(2)}) collective-permute-start(f32[40,384]{1,0:T(8,128)S(1)} %get-tuple-element.191), channel_id=1, source_target_pairs={{0,3},{1,0},{2,1},{3,2},{4,7},{5,4},{6,5},{7,6},{8,11},{9,8},{10,9... | collective-permute-start | bytes 184328 | tf_op jit(solution)/shard_map/ppermute | solution.py:48
  126.5 24.4 %copy-start.1 = (bf16[768,1536]{1,0:T(8,128)(2,1)S(1)}, bf16[768,1536]{1,0:T(8,128)(2,1)}, u32[]{:S(2)}) copy-start(bf16[768,1536]{1,0:T(8,128)(2,1)} %param.9) | copy-start | bytes 7077892
  127.2 5.4 %collective-permute-start.29 = (f32[8,128]{1,0:T(8,128)S(1)}, f32[8,128]{1,0:T(8,128)S(1)}, u32[]{:S(2)}, u32[]{:S(2)}) collective-permute-start(f32[8,128]{1,0:T(8,128)S(1)} %shard_map.107), channel_id=1, source_target_pairs={{0,8},{1,9},{2,10},{3,11},{4,12},{5,13},{6,14},{7,15},{8,0},{9,1},... | collective-permute-start | bytes 12296 | tf_op jit(solution)/shard_map/ppermute | solution.py:48
  129.1 4.8 %collective-permute-start.27 = (f32[8,128]{1,0:T(8,128)S(1)}, f32[8,128]{1,0:T(8,128)S(1)}, u32[]{:S(2)}, u32[]{:S(2)}) collective-permute-start(f32[8,128]{1,0:T(8,128)S(1)} %shard_map.107), channel_id=1, source_target_pairs={{0,4},{1,5},{2,6},{3,7},{4,8},{5,9},{6,10},{7,11},{8,12},{9,13},{1... | collective-permute-start | bytes 12296 | tf_op jit(solution)/shard_map/ppermute | solution.py:48
  131.2 3.6 %collective-permute-start.28 = (f32[8,128]{1,0:T(8,128)S(1)}, f32[8,128]{1,0:T(8,128)S(1)}, u32[]{:S(2)}, u32[]{:S(2)}) collective-permute-start(f32[8,128]{1,0:T(8,128)S(1)} %shard_map.107), channel_id=1, source_target_pairs={{0,12},{1,13},{2,14},{3,15},{4,0},{5,1},{6,2},{7,3},{8,4},{9,5},{1... | collective-permute-start | bytes 12296 | tf_op jit(solution)/shard_map/ppermute | solution.py:48
  134.8 5.5 %collective-permute-start.32 = (f32[8,128]{1,0:T(8,128)S(1)}, f32[8,128]{1,0:T(8,128)S(1)}, u32[]{:S(2)}, u32[]{:S(2)}) collective-permute-start(f32[8,128]{1,0:T(8,128)S(1)} %add_add_fusion.1), channel_id=1, source_target_pairs={{0,64},{16,80},{32,96},{48,112},{64,0},{80,16},{96,32},{112,48},{1... | collective-permute-start | bytes 12296 | tf_op jit(solution)/shard_map/ppermute | solution.py:48
  137.0 7.1 %collective-permute-start.30 = (f32[8,128]{1,0:T(8,128)S(1)}, f32[8,128]{1,0:T(8,128)S(1)}, u32[]{:S(2)}, u32[]{:S(2)}) collective-permute-start(f32[8,128]{1,0:T(8,128)S(1)} %add_add_fusion.1), channel_id=1, source_target_pairs={{0,32},{16,48},{32,64},{48,80},{64,96},{80,112},{96,0},{112,16},{1... | collective-permute-start | bytes 12296 | tf_op jit(solution)/shard_map/ppermute | solution.py:48
  137.8 6.4 %collective-permute-start.31 = (f32[8,128]{1,0:T(8,128)S(1)}, f32[8,128]{1,0:T(8,128)S(1)}, u32[]{:S(2)}, u32[]{:S(2)}) collective-permute-start(f32[8,128]{1,0:T(8,128)S(1)} %add_add_fusion.1), channel_id=1, source_target_pairs={{0,96},{16,112},{32,0},{48,16},{64,32},{80,48},{96,64},{112,80},{1... | collective-permute-start | bytes 12296 | tf_op jit(solution)/shard_map/ppermute | solution.py:48
  140.3 9.5 %collective-permute-start.26 = (f32[24,384]{1,0:T(8,128)S(1)}, f32[24,384]{1,0:T(8,128)S(1)}, u32[]{:S(2)}, u32[]{:S(2)}) collective-permute-start(f32[24,384]{1,0:T(8,128)S(1)} %get-tuple-element.192), channel_id=1, source_target_pairs={{0,0},{1,32},{2,64},{3,96},{4,1},{5,33},{6,65},{7,97},{8,2},{9,34}... | collective-permute-start | bytes 110600 | tf_op jit(solution)/shard_map/ppermute | solution.py:529
  144.2 1.2 collective-permute-start.33

commit v6 on v5

--- a/solution.py
+++ b/solution.py
@@ -449,8 +449,8 @@
     t3, t1 = move(t0, "x", 1), move(t0, "x", -1)
     t3, c0 = tie((t3, c0))
     t2 = move(t3, "x", 1)
-    c0_l, t1 = tie((c0, t1))
-    c1 = move(c0_l, "x", -1)
+    c0, t1 = tie((c0, t1))
+    c1, c3 = move(c0, "x", -1), move(c0, "x", 1)
     t1, wi, wo = tie((t1, wi, wo))
 
     tall = ((TALL, HC), F32)
@@ -477,9 +477,9 @@
     mats_a = call(
         functools.partial(decay_kernel, 0, 3), mats(3), [], [at, *three[:4], three[5], three[7]], 3 * within
     )
-    c0_r, t2, c1, *both = tie((c0, t2, c1, *three, *mats_a))
+    t2, c1, *both = tie((t2, c1, *three, *mats_a))
     three, mats_a = both[:9], both[9:]
-    c3, c2 = move(c0_r, "x", 1), move(c1, "x", -1)
+    c2 = move(c1, "x", -1)
     cirow, cerow, ci, ce, tokb, xs, xfr, bc, pre_s, *s_rows = call(
         tok_kernel_b, [*of_tokens(4), edges, tall, tall, tall], [ends(4), row], [at, t2, wi, w_bc, *three], flops
     )

time: 151 us -> 151 us (level)
  no operation moved by 1% of the time
where the time goes in v6:
time: 151 us
  waiting for transfers between devices  55.8 us (37%)
  starting transfers between devices  52.2 us (35%)
  Pallas kernels  35 us (23%)
  local copies, waits for them, and re-layouts  4.08 us (3%)
  other arithmetic  2.91 us (2%)
    ppermute x33, waiting for transfers between devices, move(): return lax.ppermute(value, name, pairs)  51.7 us
    ppermute x33, starting transfers between devices, move(): return lax.ppermute(value, name, pairs)  48.1 us
    pallas_call x15, Pallas kernels, call(): pl.pallas_call(kernel, out_shape=[jax.ShapeDtypeStruct(*o) for o in outs]...  34.9 us
    ppermute x1, waiting for transfers between devices, body(): rows_out = lax.ppermute(rows_out, ('rec', 'seq'), pairs)  4.09 us
    ppermute x1, starting transfers between devices, body(): rows_out = lax.ppermute(rows_out, ('rec', 'seq'), pairs)  4.08 us
  transfers between devices with their start and end apart: 34, of which 20 were waited for; matrix products, arithmetic and copies ran while one was open for 3% of the time, Pallas kernels for 20%

profile of v6, /device:TPU:6, one launch (start us, length us, event | category | flops | bytes accessed | tf_op | source)
XLA Modules:
  0.0 150.8 jit_solution(17656810337808360441)
XLA Ops:
  0.7 1.1 copy-done.4
  1.8 0.7 copy-done.6
  3.1 1.6 %collective-permute-start.2 = (f32[264,768]{1,0:T(8,128)S(1)}, f32[264,768]{1,0:T(8,128)S(1)}, u32[]{:S(2)}, u32[]{:S(2)}) collective-permute-start(f32[264,768]{1,0:T(8,128)S(1)} %shard_map.93), channel_id=1, source_target_pairs={{0,3},{1,0},{2,1},{3,2},{4,7},{5,4},{6,5},{7,6},{8,11},{9,8},{10,9... | collective-permute-start | bytes 2433032 | tf_op jit(solution)/shard_map/ppermute | solution.py:48
  4.7 1.9 %bitcast_convert_fusion = f32[256,768]{1,0:T(8,128)} fusion(bf16[1,256,768]{2,1,0:T(8,128)(2,1)} %param.7), kind=kLoop, calls=%fused_computation.7 | loop fusion | flops 196608 | bytes 1179648 | tf_op jit(solution)/shard_map/convert_element_type | solution.py:446
  6.6 16.0 %collective-permute-done.t3 = f32[264,768]{1,0:T(8,128)} collective-permute-done((f32[264,768]{1,0:T(8,128)S(1)}, f32[264,768]{1,0:T(8,128)}, u32[]{:S(2)}, u32[]{:S(2)}) %collective-permute-start) | collective-permute-done | bytes 811040 | tf_op jit(solution)/shard_map/ppermute | solution.py:48
  22.6 1.5 collective-permute-start.1
  24.1 0.9 copy-done.8
  25.0 0.5 collective-permute-start.3
  25.7 1.2 constant_dynamic-slice_fusion.w_out
  26.9 2.8 %collective-permute-start.4 = (f32[256,768]{1,0:T(8,128)}, f32[256,768]{1,0:T(8,128)S(1)}, u32[]{:S(2)}, u32[]{:S(2)}) collective-permute-start(f32[256,768]{1,0:T(8,128)} %bitcast_convert_fusion), channel_id=1, source_target_pairs={{0,1},{1,2},{2,3},{3,0},{4,5},{5,6},{6,7},{7,4},{8,9},{9,10},{10,1... | collective-permute-start | bytes 2359304 | tf_op jit(solution)/shard_map/ppermute | solution.py:48
  29.7 6.6 %shard_map.94 = (f32[3,8,256]{2,1,0:T(8,128)S(1)}, f32[3,8,256]{2,1,0:T(8,128)S(1)}, f32[3,256,384]{2,1,0:T(8,128)S(1)}, f32[3,256,384]{2,1,0:T(8,128)S(1)}, bf1...) custom-call(s32[4]{0:T(128)S(1)} %pad_add_fusion.at, ...), custom_call_target="tpu_custom_call" | custom-call | flops 905969664 | bytes 3022864 | tf_op jit(solution)/shard_map/pallas_call | solution.py:408
  36.3 3.5 %shard_map.95 = (bf16[3,6,256,256]{3,2,1,0:T(8,128)(2,1)S(1)}, bf16[3,6,256,256]{3,2,1,0:T(8,128)(2,1)S(1)}, f32[3,256,384]{2,1,0:T(8,128)S(1)}) custom-call(s32[4]{0:T(128)S(1)} %pad_add_fusion.at, f32[3,8,256]{2,1,0:T(8,128)S(1)} %get-tuple-element.118.cirow.refs_0_, f32[3,8,256]{2,1,0:T(8,128)S(1)} %get-tuple-element.119.cerow.refs_1_, ...), custom_call_target="tpu_custom_call" | custom-call | flops 301989888 | bytes 3391504 | tf_op jit(solution)/shard_map/pallas_call | solution.py:408
  39.8 4.7 %collective-permute-done.3.c1 = f32[256,768]{1,0:T(8,128)} collective-permute-done((f32[256,768]{1,0:T(8,128)}, f32[256,768]{1,0:T(8,128)}, u32[]{:S(2)}, u32[]{:S(2)}) %collective-permute-start.3) | collective-permute-done | bytes 786464 | tf_op jit(solution)/shard_map/ppermute | solution.py:48
  44.6 2.9 %shard_map.96 = (f32[4,8,256]{2,1,0:T(8,128)S(1)}, f32[4,8,256]{2,1,0:T(8,128)S(1)}, f32[4,256,384]{2,1,0:T(8,128)S(1)}, f32[4,256,384]{2,1,0:T(8,128)S(1)}, bf1...) custom-call(s32[4]{0:T(128)S(1)} %pad_add_fusion.at, ...), custom_call_target="tpu_custom_call" | custom-call | flops 301989888 | bytes 8724496 | tf_op jit(solution)/shard_map/pallas_call | solution.py:408
  47.5 1.9 %collective-permute-start.9 = (f32[136,384]{1,0:T(8,128)S(1)}, f32[136,384]{1,0:T(8,128)S(1)}, u32[]{:S(2)}, u32[]{:S(2)}) collective-permute-start(f32[136,384]{1,0:T(8,128)S(1)} %get-tuple-element.155), channel_id=1, source_target_pairs={{0,4},{1,5},{2,6},{3,7},{4,8},{5,9},{6,10},{7,11},{8,12},{9,13},{1... | collective-permute-start | bytes 626696 | tf_op jit(solution)/shard_map/ppermute | solution.py:48
  49.4 1.5 %collective-permute-start.10 = (f32[136,384]{1,0:T(8,128)S(1)}, f32[136,384]{1,0:T(8,128)S(1)}, u32[]{:S(2)}, u32[]{:S(2)}) collective-permute-start(f32[136,384]{1,0:T(8,128)S(1)} %get-tuple-element.156), channel_id=1, source_target_pairs={{0,12},{1,13},{2,14},{3,15},{4,0},{5,1},{6,2},{7,3},{8,4},{9,5},{1... | collective-permute-start | bytes 626696 | tf_op jit(solution)/shard_map/ppermute | solution.py:48
  50.9 2.1 %collective-permute-start.11 = (f32[136,384]{1,0:T(8,128)S(1)}, f32[136,384]{1,0:T(8,128)S(1)}, u32[]{:S(2)}, u32[]{:S(2)}) collective-permute-start(f32[136,384]{1,0:T(8,128)S(1)} %get-tuple-element.157), channel_id=1, source_target_pairs={{0,8},{1,9},{2,10},{3,11},{4,12},{5,13},{6,14},{7,15},{8,0},{9,1},... | collective-permute-start | bytes 626696 | tf_op jit(solution)/shard_map/ppermute | solution.py:48
  53.0 1.5 %shard_map.98 = (bf16[1,6,256,256]{3,2,1,0:T(8,128)(2,1)S(1)}, bf16[1,6,256,256]{3,2,1,0:T(8,128)(2,1)S(1)}, f32[1,256,384]{2,1,0:T(8,128)S(1)}) custom-call(s32[4]{0:T(128)S(1)} %pad_add_fusion.at, f32[4,8,256]{2,1,0:T(8,128)S(1)} %get-tuple-element.135.cirow, f32[4,8,256]{2,1,0:T(8,128)S(1)} %get-tuple-element.136.cerow, ...), custom_call_target="tpu_custom_call" | custom-call | flops 100663296 | bytes 4522000 | tf_op jit(solution)/shard_map/pallas_call | solution.py:408
  54.6 2.5 %shard_map.97 = (bf16[2,256,768]{2,1,0:T(8,128)(2,1)S(1)}, bf16[2,256,384]{2,1,0:T(8,128)(2,1)S(1)}, bf16[2,256,768]{2,1,0:T(8,128)(2,1)S(1)}, f32[2,128,768]{2,1,0:T(8,128)S(1)}) custom-call(s32[4]{0:T(128)S(1)} %pad_add_fusion.at, bf16[256,768]{1,0:T(8,128)(2,1)S(1)} %bitcast.10, f32[256,768]{1,0:T(8,128)} %collective-permute-done.3.c1, ...), custom_call_target="tpu_custom_call" | custom-call | flops 402653184 | bytes 5439504 | tf_op jit(solution)/shard_map/pallas_call | solution.py:408
  57.1 1.5 collective-permute-done.4.c2
  58.6 4.4 %collective-permute-done.5.c3 = f32[256,768]{1,0:T(8,128)S(1)} collective-permute-done((f32[256,768]{1,0:T(8,128)}, f32[256,768]{1,0:T(8,128)S(1)}, u32[]{:S(2)}, u32[]{:S(2)}) %collective-permute-start.5) | collective-permute-done | bytes 786464 | tf_op jit(solution)/shard_map/ppermute | solution.py:48
  63.0 2.1 %shard_map.99 = (bf16[2,256,768]{2,1,0:T(8,128)(2,1)S(1)}, bf16[2,256,384]{2,1,0:T(8,128)(2,1)S(1)}, bf16[2,256,768]{2,1,0:T(8,128)(2,1)S(1)}, f32[2,4,128,384]{...) custom-call(s32[4]{0:T(128)S(1)} %pad_add_fusion.at, ...), custom_call_target="tpu_custom_call" | custom-call | flops 402653184 | bytes 6619152 | tf_op jit(solution)/shard_map/pallas_call | solution.py:408
  65.2 2.1 %collective-permute-start.6 = (f32[136,384]{1,0:T(8,128)S(1)}, f32[136,384]{1,0:T(8,128)S(1)}, u32[]{:S(2)}, u32[]{:S(2)}) collective-permute-start(f32[136,384]{1,0:T(8,128)S(1)} %get-tuple-element.145), channel_id=1, source_target_pairs={{0,4},{1,5},{2,6},{3,7},{4,8},{5,9},{6,10},{7,11},{8,12},{9,13},{1... | collective-permute-start | bytes 626696 | tf_op jit(solution)/shard_map/ppermute | solution.py:48
  67.3 1.7 %collective-permute-start.7 = (f32[136,384]{1,0:T(8,128)S(1)}, f32[136,384]{1,0:T(8,128)S(1)}, u32[]{:S(2)}, u32[]{:S(2)}) collective-permute-start(f32[136,384]{1,0:T(8,128)S(1)} %get-tuple-element.146), channel_id=1, source_target_pairs={{0,12},{1,13},{2,14},{3,15},{4,0},{5,1},{6,2},{7,3},{8,4},{9,5},{1... | collective-permute-start | bytes 626696 | tf_op jit(solution)/shard_map/ppermute | solution.py:48
  69.0 1.9 %collective-permute-start.8 = (f32[136,384]{1,0:T(8,128)S(1)}, f32[136,384]{1,0:T(8,128)S(1)}, u32[]{:S(2)}, u32[]{:S(2)}) collective-permute-start(f32[136,384]{1,0:T(8,128)S(1)} %get-tuple-element.147), channel_id=1, source_target_pairs={{0,8},{1,9},{2,10},{3,11},{4,12},{5,13},{6,14},{7,15},{8,0},{9,1},... | collective-permute-start | bytes 626696 | tf_op jit(solution)/shard_map/ppermute | solution.py:48
  70.9 5.1 %shard_map.100 = (f32[2,384,384]{2,1,0:T(8,128)S(1)}, f32[4,256,384]{2,1,0:T(8,128)S(1)}, f32[4,256,128]{2,1,0:T(8,128)S(1)}, f32[4,256,128]{2,1,0:T(8,128)S(1)}) custom-call(s32[4]{0:T(128)S(1)} %pad_add_fusion.at, bf16[4,256,384]{2,1,0:T(8,128)(2,1)S(1)} %get-tuple-element.137.xs, bf16[4,256,256]{2,1,0:T(8,128)(2,1)S(1)} %get-tuple-element.129.bc, ...), custom_call_target="tpu_custom_call" | custom-call | flops 2214592512 | bytes 18452496 | tf_op jit(solution)/shard_map/pallas_call | solution.py:408
  76.5 4.0 %shard_map.101 = (f32[384,1024]{1,0:T(8,128)S(1)}, f32[384,1024]{1,0:T(8,128)S(1)}, bf16[4,256,640]{2,1,0:T(8,128)(2,1)S(1)}) custom-call(s32[4]{0:T(128)S(1)} %pad_add_fusion.at, bf16[4,256,768]{2,1,0:T(8,128)(2,1)S(1)} %get-tuple-element.127.tokb, bf16[4,256,768]{2,1,0:T(8,128)(2,1)S(1)} %get-tuple-element.128.xfr, ...), custom_call_target="tpu_custom_call" | custom-call | flops 1409286144 | bytes 12816400 | tf_op jit(solution)/shard_map/pallas_call | solution.py:408
  80.6 1.9 %shard_map.102 = (f32[256,768]{1,0:T(8,128)S(1)}, f32[256,768]{1,0:T(8,128)S(1)}, f32[128,768]{1,0:T(8,128)S(1)}, f32[128,768]{1,0:T(8,128)S(1)}, f32[256,768]{1,0:T(8,128)S(1)}) custom-call(s32[4]{0:T(128)S(1)} %pad_add_fusion.at, bf16[4,256,640]{2,1,0:T(8,128)(2,1)S(1)} %get-tuple-element.168.dz, bf16[768,384]{1,0:T(8,128)(2,1)S(1)} %constant_dynamic-slice_fusion.1.w_in, ...), custom_call_target="tpu_custom_call" | custom-call | flops 1006632960 | bytes 2293776 | tf_op jit(solution)/shard_map/pallas_call | solution.py:408
  82.6 2.0 %collective-permute-start.13 = (f32[128,768]{1,0:T(8,128)S(1)}, f32[128,768]{1,0:T(8,128)S(1)}, u32[]{:S(2)}, u32[]{:S(2)}) collective-permute-start(f32[128,768]{1,0:T(8,128)S(1)} %get-tuple-element.173), channel_id=1, source_target_pairs={{0,3},{1,0},{2,1},{3,2},{4,7},{5,4},{6,5},{7,6},{8,11},{9,8},{10,9... | collective-permute-start | bytes 1179656 | tf_op jit(solution)/shard_map/ppermute | solution.py:48
  84.6 0.8 shard_map.104
  85.5 1.2 collective-permute-start.17
  86.7 2.4 %collective-permute-start.18 = (f32[96,1024]{1,0:T(8,128)S(1)}, f32[96,1024]{1,0:T(8,128)S(1)}, u32[]{:S(2)}, u32[]{:S(2)}) collective-permute-start(f32[96,1024]{1,0:T(8,128)S(1)} %get-tuple-element.180), channel_id=1, source_target_pairs={{0,8},{1,9},{2,10},{3,11},{4,12},{5,13},{6,14},{7,15},{8,0},{9,1},... | collective-permute-start | bytes 1179656 | tf_op jit(solution)/shard_map/ppermute | solution.py:48
  89.0 0.8 collective-permute-start.19
  89.8 4.3 %collective-permute-done.12.r_a = f32[128,768]{1,0:T(8,128)S(1)} collective-permute-done((f32[128,768]{1,0:T(8,128)S(1)}, f32[128,768]{1,0:T(8,128)S(1)}, u32[]{:S(2)}, u32[]{:S(2)}) %collective-permute-start.12) | collective-permute-done | bytes 393248 | tf_op jit(solution)/shard_map/ppermute | solution.py:48
  94.1 1.3 collective-permute-done.13.r_b
  95.4 0.7 shard_map.103
  96.6 2.8 %collective-permute-start.14 = (f32[256,768]{1,0:T(8,128)S(1)}, f32[256,768]{1,0:T(8,128)S(1)}, u32[]{:S(2)}, u32[]{:S(2)}) collective-permute-start(f32[256,768]{1,0:T(8,128)S(1)} %get-tuple-element.174), channel_id=1, source_target_pairs={{0,1},{1,2},{2,3},{3,0},{4,5},{5,6},{6,7},{7,4},{8,9},{9,10},{10,1... | collective-permute-start | bytes 2359304 | tf_op jit(solution)/shard_map/ppermute | solution.py:48
  99.4 7.0 %collective-permute-done.18.refs_2_ = f32[96,1024]{1,0:T(8,128)S(1)} collective-permute-done((f32[96,1024]{1,0:T(8,128)S(1)}, f32[96,1024]{1,0:T(8,128)S(1)}, u32[]{:S(2)}, u32[]{:S(2)}) %collective-permute-start.18) | collective-permute-done | bytes 393248 | tf_op jit(solution)/shard_map/ppermute | solution.py:48
  106.7 0.7 shard_map.105
  107.4 2.0 %collective-permute-start.20 = (f32[24,1024]{1,0:T(8,128)S(1)}, f32[24,1024]{1,0:T(8,128)S(1)}, u32[]{:S(2)}, u32[]{:S(2)}) collective-permute-start(f32[24,1024]{1,0:T(8,128)S(1)} %get-tuple-element.183), channel_id=1, source_target_pairs={{0,32},{16,48},{32,64},{48,80},{64,96},{80,112},{96,0},{112,16},{1... | collective-permute-start | bytes 294920 | tf_op jit(solution)/shard_map/ppermute | solution.py:48
  109.4 3.6 %collective-permute-start.21 = (f32[24,1024]{1,0:T(8,128)S(1)}, f32[24,1024]{1,0:T(8,128)S(1)}, u32[]{:S(2)}, u32[]{:S(2)}) collective-permute-start(f32[24,1024]{1,0:T(8,128)S(1)} %get-tuple-element.184), channel_id=1, source_target_pairs={{0,64},{16,80},{32,96},{48,112},{64,0},{80,16},{96,32},{112,48},{1... | collective-permute-start | bytes 294920 | tf_op jit(solution)/shard_map/ppermute | solution.py:48
  113.0 1.0 collective-permute-start.22
  114.0 1.2 collective-permute-done.20.b
  115.2 1.6 %collective-permute-done.21.c = f32[24,1024]{1,0:T(8,128)S(1)} collective-permute-done((f32[24,1024]{1,0:T(8,128)S(1)}, f32[24,1024]{1,0:T(8,128)S(1)}, u32[]{:S(2)}, u32[]{:S(2)}) %collective-permute-start.21) | collective-permute-done | bytes 98336 | tf_op jit(solution)/shard_map/ppermute | solution.py:48
  116.8 0.8 collective-permute-done.22.d
  117.6 0.7 shard_map.106
  118.3 1.6 %collective-permute-start.23 = (f32[40,384]{1,0:T(8,128)S(1)}, f32[40,384]{1,0:T(8,128)S(1)}, u32[]{:S(2)}, u32[]{:S(2)}) collective-permute-start(f32[40,384]{1,0:T(8,128)S(1)} %get-tuple-element.187), channel_id=1, source_target_pairs={{0,1},{1,2},{2,3},{3,0},{4,5},{5,6},{6,7},{7,4},{8,9},{9,10},{10,1... | collective-permute-start | bytes 184328 | tf_op jit(solution)/shard_map/ppermute | solution.py:48
  119.9 0.8 collective-permute-start.24
  120.9 1.7 %collective-permute-done.23.b = f32[40,384]{1,0:T(8,128)S(1)} collective-permute-done((f32[40,384]{1,0:T(8,128)S(1)}, f32[40,384]{1,0:T(8,128)S(1)}, u32[]{:S(2)}, u32[]{:S(2)}) %collective-permute-start.23) | collective-permute-done | bytes 61472 | tf_op jit(solution)/shard_map/ppermute | solution.py:48
  122.6 3.1 %collective-permute-done.24.c = f32[40,384]{1,0:T(8,128)S(1)} collective-permute-done((f32[40,384]{1,0:T(8,128)S(1)}, f32[40,384]{1,0:T(8,128)S(1)}, u32[]{:S(2)}, u32[]{:S(2)}) %collective-permute-start.24) | collective-permute-done | bytes 61472 | tf_op jit(solution)/shard_map/ppermute | solution.py:48
  125.7 0.6 collective-permute-done.25.d
  126.3 0.7 shard_map.107
  127.0 2.0 %collective-permute-start.29 = (f32[8,128]{1,0:T(8,128)S(1)}, f32[8,128]{1,0:T(8,128)S(1)}, u32[]{:S(2)}, u32[]{:S(2)}) collective-permute-start(f32[8,128]{1,0:T(8,128)S(1)} %shard_map.107), channel_id=1, source_target_pairs={{0,8},{1,9},{2,10},{3,11},{4,12},{5,13},{6,14},{7,15},{8,0},{9,1},... | collective-permute-start | bytes 12296 | tf_op jit(solution)/shard_map/ppermute | solution.py:48
  129.0 2.0 %collective-permute-start.27 = (f32[8,128]{1,0:T(8,128)S(1)}, f32[8,128]{1,0:T(8,128)S(1)}, u32[]{:S(2)}, u32[]{:S(2)}) collective-permute-start(f32[8,128]{1,0:T(8,128)S(1)} %shard_map.107), channel_id=1, source_target_pairs={{0,4},{1,5},{2,6},{3,7},{4,8},{5,9},{6,10},{7,11},{8,12},{9,13},{1... | collective-permute-start | bytes 12296 | tf_op jit(solution)/shard_map/ppermute | solution.py:48
  131.0 1.3 collective-permute-start.28
  132.4 1.4 collective-permute-done.27
  133.8 0.8 collective-permute-done.28
  134.6 2.2 %collective-permute-start.32 = (f32[8,128]{1,0:T(8,128)S(1)}, f32[8,128]{1,0:T(8,128)S(1)}, u32[]{:S(2)}, u32[]{:S(2)}) collective-permute-start(f32[8,128]{1,0:T(8,128)S(1)} %add_add_fusion.1), channel_id=1, source_target_pairs={{0,64},{16,80},{32,96},{48,112},{64,0},{80,16},{96,32},{112,48},{1... | collective-permute-start | bytes 12296 | tf_op jit(solution)/shard_map/ppermute | solution.py:48
  136.8 0.8 collective-permute-start.30
  137.6 2.5 %collective-permute-start.31 = (f32[8,128]{1,0:T(8,128)S(1)}, f32[8,128]{1,0:T(8,128)S(1)}, u32[]{:S(2)}, u32[]{:S(2)}) collective-permute-start(f32[8,128]{1,0:T(8,128)S(1)} %add_add_fusion.1), channel_id=1, source_target_pairs={{0,96},{16,112},{32,0},{48,16},{64,32},{80,48},{96,64},{112,80},{1... | collective-permute-start | bytes 12296 | tf_op jit(solution)/shard_map/ppermute | solution.py:48
  140.1 4.1 %collective-permute-start.26 = (f32[24,384]{1,0:T(8,128)S(1)}, f32[24,384]{1,0:T(8,128)S(1)}, u32[]{:S(2)}, u32[]{:S(2)}) collective-permute-start(f32[24,384]{1,0:T(8,128)S(1)} %get-tuple-element.190), channel_id=1, source_target_pairs={{0,0},{1,32},{2,64},{3,96},{4,1},{5,33},{6,65},{7,97},{8,2},{9,34}... | collective-permute-start | bytes 110600 | tf_op jit(solution)/shard_map/ppermute | solution.py:529
  144.3 0.9 fusion
  145.4 4.1 %collective-permute-done.26.rows_out = f32[24,384]{1,0:T(8,128)S(1)} collective-permute-done((f32[24,384]{1,0:T(8,128)S(1)}, f32[24,384]{1,0:T(8,128)S(1)}, u32[]{:S(2)}, u32[]{:S(2)}) %collective-permute-start.26) | collective-permute-done | bytes 36896 | tf_op jit(solution)/shard_map/ppermute | solution.py:529
  149.5 1.2 shard_map.108
  (48 shorter events, 3.1 us)
Async XLA Ops:
  0.6 25.0 %copy-start = (bf16[768,1536]{1,0:T(8,128)(2,1)S(1)}, bf16[768,1536]{1,0:T(8,128)(2,1)}, u32[]{:S(2)}) copy-start(bf16[768,1536]{1,0:T(8,128)(2,1)} %param.9) | copy-start | bytes 7077892
  0.6 1.1 copy-start.4
  1.8 0.7 copy-start.6
  2.6 27.1 %copy-start.7 = (f32[1,24,256]{2,1,0:T(8,128)S(1)}, f32[1,24,256]{2,1,0:T(8,128)}, u32[]{:S(2)}) copy-start(f32[1,24,256]{2,1,0:T(8,128)} %param.8) | copy-start | bytes 73732
  2.6 20.0 %collective-permute-start = (f32[264,768]{1,0:T(8,128)S(1)}, f32[264,768]{1,0:T(8,128)}, u32[]{:S(2)}, u32[]{:S(2)}) collective-permute-start(f32[264,768]{1,0:T(8,128)S(1)} %shard_map.93), channel_id=1, source_target_pairs={{0,1},{1,2},{2,3},{3,0},{4,5},{5,6},{6,7},{7,4},{8,9},{9,10},{10,1... | collective-permute-start | bytes 2433032 | tf_op jit(solution)/shard_map/ppermute | solution.py:48
  3.1 21.0 %collective-permute-start.2 = (f32[264,768]{1,0:T(8,128)S(1)}, f32[264,768]{1,0:T(8,128)S(1)}, u32[]{:S(2)}, u32[]{:S(2)}) collective-permute-start(f32[264,768]{1,0:T(8,128)S(1)} %shard_map.93), channel_id=1, source_target_pairs={{0,3},{1,0},{2,1},{3,2},{4,7},{5,4},{6,5},{7,6},{8,11},{9,8},{10,9... | collective-permute-start | bytes 2433032 | tf_op jit(solution)/shard_map/ppermute | solution.py:48
  22.6 21.9 %collective-permute-start.1 = (f32[264,768]{1,0:T(8,128)}, f32[264,768]{1,0:T(8,128)S(1)}, u32[]{:S(2)}, u32[]{:S(2)}) collective-permute-start(f32[264,768]{1,0:T(8,128)} %collective-permute-done.t3), channel_id=1, source_target_pairs={{0,1},{1,2},{2,3},{3,0},{4,5},{5,6},{6,7},{7,4},{8,9},{9,10},{10,1... | collective-permute-start | bytes 2433032 | tf_op jit(solution)/shard_map/ppermute | solution.py:48
  24.1 0.9 copy-start.8
  25.0 19.5 %collective-permute-start.3 = (f32[256,768]{1,0:T(8,128)}, f32[256,768]{1,0:T(8,128)}, u32[]{:S(2)}, u32[]{:S(2)}) collective-permute-start(f32[256,768]{1,0:T(8,128)} %bitcast_convert_fusion), channel_id=1, source_target_pairs={{0,3},{1,0},{2,1},{3,2},{4,7},{5,4},{6,5},{7,6},{8,11},{9,8},{10,9... | collective-permute-start | bytes 2359304 | tf_op jit(solution)/shard_map/ppermute | solution.py:48
  25.5 4.1 %copy-start.3 = (bf16[768,256]{1,0:T(8,128)(2,1)S(1)}, bf16[768,256]{1,0:T(8,128)(2,1)}, u32[]{:S(2)}) copy-start(bf16[768,256]{1,0:T(8,128)(2,1)} %w_bc.5) | copy-start | bytes 1179652
  25.5 4.1 %copy-start.5 = (bf16[1,256,768]{2,1,0:T(8,128)(2,1)S(1)}, bf16[1,256,768]{2,1,0:T(8,128)(2,1)}, u32[]{:S(2)}) copy-start(bf16[1,256,768]{2,1,0:T(8,128)(2,1)} %param.6) | copy-start | bytes 1179652
  25.5 4.1 %copy-start.9 = (f32[264,768]{1,0:T(8,128)S(1)}, f32[264,768]{1,0:T(8,128)}, u32[]{:S(2)}) copy-start(f32[264,768]{1,0:T(8,128)} %copy-done.8) | copy-start | bytes 2433028
  26.9 31.7 %collective-permute-start.4 = (f32[256,768]{1,0:T(8,128)}, f32[256,768]{1,0:T(8,128)S(1)}, u32[]{:S(2)}, u32[]{:S(2)}) collective-permute-start(f32[256,768]{1,0:T(8,128)} %bitcast_convert_fusion), channel_id=1, source_target_pairs={{0,1},{1,2},{2,3},{3,0},{4,5},{5,6},{6,7},{7,4},{8,9},{9,10},{10,1... | collective-permute-start | bytes 2359304 | tf_op jit(solution)/shard_map/ppermute | solution.py:48
  44.5 18.5 %collective-permute-start.5 = (f32[256,768]{1,0:T(8,128)}, f32[256,768]{1,0:T(8,128)S(1)}, u32[]{:S(2)}, u32[]{:S(2)}) collective-permute-start(f32[256,768]{1,0:T(8,128)} %collective-permute-done.3.c1), channel_id=1, source_target_pairs={{0,3},{1,0},{2,1},{3,2},{4,7},{5,4},{6,5},{7,6},{8,11},{9,8},{10,9... | collective-permute-start | bytes 2359304 | tf_op jit(solution)/shard_map/ppermute | solution.py:48
  47.5 21.4 %collective-permute-start.9 = (f32[136,384]{1,0:T(8,128)S(1)}, f32[136,384]{1,0:T(8,128)S(1)}, u32[]{:S(2)}, u32[]{:S(2)}) collective-permute-start(f32[136,384]{1,0:T(8,128)S(1)} %get-tuple-element.155), channel_id=1, source_target_pairs={{0,4},{1,5},{2,6},{3,7},{4,8},{5,9},{6,10},{7,11},{8,12},{9,13},{1... | collective-permute-start | bytes 626696 | tf_op jit(solution)/shard_map/ppermute | solution.py:48
  49.4 21.5 %collective-permute-start.10 = (f32[136,384]{1,0:T(8,128)S(1)}, f32[136,384]{1,0:T(8,128)S(1)}, u32[]{:S(2)}, u32[]{:S(2)}) collective-permute-start(f32[136,384]{1,0:T(8,128)S(1)} %get-tuple-element.156), channel_id=1, source_target_pairs={{0,12},{1,13},{2,14},{3,15},{4,0},{5,1},{6,2},{7,3},{8,4},{9,5},{1... | collective-permute-start | bytes 626696 | tf_op jit(solution)/shard_map/ppermute | solution.py:48
  50.9 20.0 %collective-permute-start.11 = (f32[136,384]{1,0:T(8,128)S(1)}, f32[136,384]{1,0:T(8,128)S(1)}, u32[]{:S(2)}, u32[]{:S(2)}) collective-permute-start(f32[136,384]{1,0:T(8,128)S(1)} %get-tuple-element.157), channel_id=1, source_target_pairs={{0,8},{1,9},{2,10},{3,11},{4,12},{5,13},{6,14},{7,15},{8,0},{9,1},... | collective-permute-start | bytes 626696 | tf_op jit(solution)/shard_map/ppermute | solution.py:48
  53.0 1.5 %copy-start.2 = (bf16[1,256,768]{2,1,0:T(8,128)(2,1)S(1)}, bf16[1,256,768]{2,1,0:T(8,128)(2,1)}, u32[]{:S(2)}) copy-start(bf16[1,256,768]{2,1,0:T(8,128)(2,1)} %param.7) | copy-start | bytes 1179652
  65.2 10.8 %collective-permute-start.6 = (f32[136,384]{1,0:T(8,128)S(1)}, f32[136,384]{1,0:T(8,128)S(1)}, u32[]{:S(2)}, u32[]{:S(2)}) collective-permute-start(f32[136,384]{1,0:T(8,128)S(1)} %get-tuple-element.145), channel_id=1, source_target_pairs={{0,4},{1,5},{2,6},{3,7},{4,8},{5,9},{6,10},{7,11},{8,12},{9,13},{1... | collective-permute-start | bytes 626696 | tf_op jit(solution)/shard_map/ppermute | solution.py:48
  67.3 8.8 %collective-permute-start.7 = (f32[136,384]{1,0:T(8,128)S(1)}, f32[136,384]{1,0:T(8,128)S(1)}, u32[]{:S(2)}, u32[]{:S(2)}) collective-permute-start(f32[136,384]{1,0:T(8,128)S(1)} %get-tuple-element.146), channel_id=1, source_target_pairs={{0,12},{1,13},{2,14},{3,15},{4,0},{5,1},{6,2},{7,3},{8,4},{9,5},{1... | collective-permute-start | bytes 626696 | tf_op jit(solution)/shard_map/ppermute | solution.py:48
  69.0 7.6 %collective-permute-start.8 = (f32[136,384]{1,0:T(8,128)S(1)}, f32[136,384]{1,0:T(8,128)S(1)}, u32[]{:S(2)}, u32[]{:S(2)}) collective-permute-start(f32[136,384]{1,0:T(8,128)S(1)} %get-tuple-element.147), channel_id=1, source_target_pairs={{0,8},{1,9},{2,10},{3,11},{4,12},{5,13},{6,14},{7,15},{8,0},{9,1},... | collective-permute-start | bytes 626696 | tf_op jit(solution)/shard_map/ppermute | solution.py:48
  80.5 4.1 %collective-permute-start.16 = (f32[384,1024]{1,0:T(8,128)S(1)}, f32[384,1024]{1,0:T(8,128)S(1)}, u32[]{:S(2)}, u32[]{:S(2)}) collective-permute-start(f32[384,1024]{1,0:T(8,128)S(1)} %get-tuple-element.177), channel_id=1, source_target_pairs={{0,16},{16,0},{32,48},{48,32},{64,80},{80,64},{96,112},{112,96},{1... | collective-permute-start | bytes 4718600 | tf_op jit(solution)/shard_map/ppermute | solution.py:48
  82.5 11.6 %collective-permute-start.12 = (f32[128,768]{1,0:T(8,128)S(1)}, f32[128,768]{1,0:T(8,128)S(1)}, u32[]{:S(2)}, u32[]{:S(2)}) collective-permute-start(f32[128,768]{1,0:T(8,128)S(1)} %get-tuple-element.172), channel_id=1, source_target_pairs={{0,1},{1,2},{2,3},{3,0},{4,5},{5,6},{6,7},{7,4},{8,9},{9,10},{10,1... | collective-permute-start | bytes 1179656 | tf_op jit(solution)/shard_map/ppermute | solution.py:48
  82.6 12.8 %collective-permute-start.13 = (f32[128,768]{1,0:T(8,128)S(1)}, f32[128,768]{1,0:T(8,128)S(1)}, u32[]{:S(2)}, u32[]{:S(2)}) collective-permute-start(f32[128,768]{1,0:T(8,128)S(1)} %get-tuple-element.173), channel_id=1, source_target_pairs={{0,3},{1,0},{2,1},{3,2},{4,7},{5,4},{6,5},{7,6},{8,11},{9,8},{10,9... | collective-permute-start | bytes 1179656 | tf_op jit(solution)/shard_map/ppermute | solution.py:48
  85.5 14.0 %collective-permute-start.17 = (f32[96,1024]{1,0:T(8,128)S(1)}, f32[96,1024]{1,0:T(8,128)S(1)}, u32[]{:S(2)}, u32[]{:S(2)}) collective-permute-start(f32[96,1024]{1,0:T(8,128)S(1)} %get-tuple-element.179), channel_id=1, source_target_pairs={{0,4},{1,5},{2,6},{3,7},{4,8},{5,9},{6,10},{7,11},{8,12},{9,13},{1... | collective-permute-start | bytes 1179656 | tf_op jit(solution)/shard_map/ppermute | solution.py:48
  86.7 19.7 %collective-permute-start.18 = (f32[96,1024]{1,0:T(8,128)S(1)}, f32[96,1024]{1,0:T(8,128)S(1)}, u32[]{:S(2)}, u32[]{:S(2)}) collective-permute-start(f32[96,1024]{1,0:T(8,128)S(1)} %get-tuple-element.180), channel_id=1, source_target_pairs={{0,8},{1,9},{2,10},{3,11},{4,12},{5,13},{6,14},{7,15},{8,0},{9,1},... | collective-permute-start | bytes 1179656 | tf_op jit(solution)/shard_map/ppermute | solution.py:48
  89.0 17.7 %collective-permute-start.19 = (f32[96,1024]{1,0:T(8,128)S(1)}, f32[96,1024]{1,0:T(8,128)S(1)}, u32[]{:S(2)}, u32[]{:S(2)}) collective-permute-start(f32[96,1024]{1,0:T(8,128)S(1)} %get-tuple-element.181), channel_id=1, source_target_pairs={{0,12},{1,13},{2,14},{3,15},{4,0},{5,1},{6,2},{7,3},{8,4},{9,5},{1... | collective-permute-start | bytes 1179656 | tf_op jit(solution)/shard_map/ppermute | solution.py:48
  96.1 48.2 %collective-permute-start.15 = (f32[256,768]{1,0:T(8,128)S(1)}, f32[256,768]{1,0:T(8,128)S(1)}, u32[]{:S(2)}, u32[]{:S(2)}) collective-permute-start(f32[256,768]{1,0:T(8,128)S(1)} %get-tuple-element.175), channel_id=1, source_target_pairs={{0,3},{1,0},{2,1},{3,2},{4,7},{5,4},{6,5},{7,6},{8,11},{9,8},{10,9... | collective-permute-start | bytes 2359304 | tf_op jit(solution)/shard_map/ppermute | solution.py:48
  96.6 47.7 %collective-permute-start.14 = (f32[256,768]{1,0:T(8,128)S(1)}, f32[256,768]{1,0:T(8,128)S(1)}, u32[]{:S(2)}, u32[]{:S(2)}) collective-permute-start(f32[256,768]{1,0:T(8,128)S(1)} %get-tuple-element.174), channel_id=1, source_target_pairs={{0,1},{1,2},{2,3},{3,0},{4,5},{5,6},{6,7},{7,4},{8,9},{9,10},{10,1... | collective-permute-start | bytes 2359304 | tf_op jit(solution)/shard_map/ppermute | solution.py:48
  107.4 7.7 %collective-permute-start.20 = (f32[24,1024]{1,0:T(8,128)S(1)}, f32[24,1024]{1,0:T(8,128)S(1)}, u32[]{:S(2)}, u32[]{:S(2)}) collective-permute-start(f32[24,1024]{1,0:T(8,128)S(1)} %get-tuple-element.183), channel_id=1, source_target_pairs={{0,32},{16,48},{32,64},{48,80},{64,96},{80,112},{96,0},{112,16},{1... | collective-permute-start | bytes 294920 | tf_op jit(solution)/shard_map/ppermute | solution.py:48
  109.4 7.4 %collective-permute-start.21 = (f32[24,1024]{1,0:T(8,128)S(1)}, f32[24,1024]{1,0:T(8,128)S(1)}, u32[]{:S(2)}, u32[]{:S(2)}) collective-permute-start(f32[24,1024]{1,0:T(8,128)S(1)} %get-tuple-element.184), channel_id=1, source_target_pairs={{0,64},{16,80},{32,96},{48,112},{64,0},{80,16},{96,32},{112,48},{1... | collective-permute-start | bytes 294920 | tf_op jit(solution)/shard_map/ppermute | solution.py:48
  113.0 4.6 %collective-permute-start.22 = (f32[24,1024]{1,0:T(8,128)S(1)}, f32[24,1024]{1,0:T(8,128)S(1)}, u32[]{:S(2)}, u32[]{:S(2)}) collective-permute-start(f32[24,1024]{1,0:T(8,128)S(1)} %get-tuple-element.185), channel_id=1, source_target_pairs={{0,96},{16,112},{32,0},{48,16},{64,32},{80,48},{96,64},{112,80},{1... | collective-permute-start | bytes 294920 | tf_op jit(solution)/shard_map/ppermute | solution.py:48
  118.3 4.3 %collective-permute-start.23 = (f32[40,384]{1,0:T(8,128)S(1)}, f32[40,384]{1,0:T(8,128)S(1)}, u32[]{:S(2)}, u32[]{:S(2)}) collective-permute-start(f32[40,384]{1,0:T(8,128)S(1)} %get-tuple-element.187), channel_id=1, source_target_pairs={{0,1},{1,2},{2,3},{3,0},{4,5},{5,6},{6,7},{7,4},{8,9},{9,10},{10,1... | collective-permute-start | bytes 184328 | tf_op jit(solution)/shard_map/ppermute | solution.py:48
  119.9 5.7 %collective-permute-start.24 = (f32[40,384]{1,0:T(8,128)S(1)}, f32[40,384]{1,0:T(8,128)S(1)}, u32[]{:S(2)}, u32[]{:S(2)}) collective-permute-start(f32[40,384]{1,0:T(8,128)S(1)} %get-tuple-element.188), channel_id=1, source_target_pairs={{0,2},{1,3},{2,0},{3,1},{4,6},{5,7},{6,4},{7,5},{8,10},{9,11},{10,... | collective-permute-start | bytes 184328 | tf_op jit(solution)/shard_map/ppermute | solution.py:48
  120.7 5.6 %collective-permute-start.25 = (f32[40,384]{1,0:T(8,128)S(1)}, f32[40,384]{1,0:T(8,128)S(1)}, u32[]{:S(2)}, u32[]{:S(2)}) collective-permute-start(f32[40,384]{1,0:T(8,128)S(1)} %get-tuple-element.189), channel_id=1, source_target_pairs={{0,3},{1,0},{2,1},{3,2},{4,7},{5,4},{6,5},{7,6},{8,11},{9,8},{10,9... | collective-permute-start | bytes 184328 | tf_op jit(solution)/shard_map/ppermute | solution.py:48
  126.3 24.4 %copy-start.1 = (bf16[768,1536]{1,0:T(8,128)(2,1)S(1)}, bf16[768,1536]{1,0:T(8,128)(2,1)}, u32[]{:S(2)}) copy-start(bf16[768,1536]{1,0:T(8,128)(2,1)} %param.9) | copy-start | bytes 7077892
  127.0 5.4 %collective-permute-start.29 = (f32[8,128]{1,0:T(8,128)S(1)}, f32[8,128]{1,0:T(8,128)S(1)}, u32[]{:S(2)}, u32[]{:S(2)}) collective-permute-start(f32[8,128]{1,0:T(8,128)S(1)} %shard_map.107), channel_id=1, source_target_pairs={{0,8},{1,9},{2,10},{3,11},{4,12},{5,13},{6,14},{7,15},{8,0},{9,1},... | collective-permute-start | bytes 12296 | tf_op jit(solution)/shard_map/ppermute | solution.py:48
  129.0 4.8 %collective-permute-start.27 = (f32[8,128]{1,0:T(8,128)S(1)}, f32[8,128]{1,0:T(8,128)S(1)}, u32[]{:S(2)}, u32[]{:S(2)}) collective-permute-start(f32[8,128]{1,0:T(8,128)S(1)} %shard_map.107), channel_id=1, source_target_pairs={{0,4},{1,5},{2,6},{3,7},{4,8},{5,9},{6,10},{7,11},{8,12},{9,13},{1... | collective-permute-start | bytes 12296 | tf_op jit(solution)/shard_map/ppermute | solution.py:48
  131.0 3.6 %collective-permute-start.28 = (f32[8,128]{1,0:T(8,128)S(1)}, f32[8,128]{1,0:T(8,128)S(1)}, u32[]{:S(2)}, u32[]{:S(2)}) collective-permute-start(f32[8,128]{1,0:T(8,128)S(1)} %shard_map.107), channel_id=1, source_target_pairs={{0,12},{1,13},{2,14},{3,15},{4,0},{5,1},{6,2},{7,3},{8,4},{9,5},{1... | collective-permute-start | bytes 12296 | tf_op jit(solution)/shard_map/ppermute | solution.py:48
  134.6 5.5 %collective-permute-start.32 = (f32[8,128]{1,0:T(8,128)S(1)}, f32[8,128]{1,0:T(8,128)S(1)}, u32[]{:S(2)}, u32[]{:S(2)}) collective-permute-start(f32[8,128]{1,0:T(8,128)S(1)} %add_add_fusion.1), channel_id=1, source_target_pairs={{0,64},{16,80},{32,96},{48,112},{64,0},{80,16},{96,32},{112,48},{1... | collective-permute-start | bytes 12296 | tf_op jit(solution)/shard_map/ppermute | solution.py:48
  136.8 7.3 %collective-permute-start.30 = (f32[8,128]{1,0:T(8,128)S(1)}, f32[8,128]{1,0:T(8,128)S(1)}, u32[]{:S(2)}, u32[]{:S(2)}) collective-permute-start(f32[8,128]{1,0:T(8,128)S(1)} %add_add_fusion.1), channel_id=1, source_target_pairs={{0,32},{16,48},{32,64},{48,80},{64,96},{80,112},{96,0},{112,16},{1... | collective-permute-start | bytes 12296 | tf_op jit(solution)/shard_map/ppermute | solution.py:48
  137.6 6.6 %collective-permute-start.31 = (f32[8,128]{1,0:T(8,128)S(1)}, f32[8,128]{1,0:T(8,128)S(1)}, u32[]{:S(2)}, u32[]{:S(2)}) collective-permute-start(f32[8,128]{1,0:T(8,128)S(1)} %add_add_fusion.1), channel_id=1, source_target_pairs={{0,96},{16,112},{32,0},{48,16},{64,32},{80,48},{96,64},{112,80},{1... | collective-permute-start | bytes 12296 | tf_op jit(solution)/shard_map/ppermute | solution.py:48
  140.1 9.5 %collective-permute-start.26 = (f32[24,384]{1,0:T(8,128)S(1)}, f32[24,384]{1,0:T(8,128)S(1)}, u32[]{:S(2)}, u32[]{:S(2)}) collective-permute-start(f32[24,384]{1,0:T(8,128)S(1)} %get-tuple-element.190), channel_id=1, source_target_pairs={{0,0},{1,32},{2,64},{3,96},{4,1},{5,33},{6,65},{7,97},{8,2},{9,34}... | collective-permute-start | bytes 110600 | tf_op jit(solution)/shard_map/ppermute | solution.py:529
  144.2 1.2 collective-permute-start.33

commit v7 on v6

--- a/solution.py
+++ b/solution.py
@@ -13,7 +13,6 @@
 NY = 4
 NZ = 4
 SEG = 256
-HALF = SEG // 2
 DM = 768
 NS = 128
 NH = 6
@@ -325,31 +324,28 @@
         return 0
 
     lax.fori_loop(0, NX, segment, 0)
-    raw = dot(tokb[...].reshape(NX * SEG, DM), dz[...].reshape(NX * SEG, WIDE), 0, 0)
-    for j, c, row in blocks():
-        g[c, row : row + 24, :] = raw[24 * j : 24 * j + 24, :]
+    g[...] = dot(tokb[...].reshape(NX * SEG, DM), dz[...].reshape(NX * SEG, WIDE), 0, 0)
     for out, c in ((keep, core), (send, 1 - core)):
-        out[:, :WIDE] = g[c]
+        for z in range(NZ):
+            for y in range(NY):
+                first = pl.multiple_of(24 * (8 * z + y) + 96 * c, 8)
+                row = (4 * y + z) * 24
+                out[row : row + 24, :WIDE] = g[pl.ds(first, 24), :]
         out[:, WIDE:] = g_out[c]
 
 
-def tokens_kernel(at, dz, w_in, w_bc, d0, d1, d2a, d2b, d3):
+def tokens_kernel(at, dz, w_in, w_bc, d0, d1, d2, d3):
     def tokens_of(k):
         return dot(dz[k, :, :HC], w_in[...], 1, 1) + dot(dz[k, :, HC:], w_bc[...], 1, 1)
 
-    d = tokens_of(3)
-    d2a[...] = d[:HALF]
-    d2b[...] = d[HALF:]
+    d2[...] = tokens_of(3)
     d1[...] = tokens_of(1)
     d3[...] = tokens_of(2)
     d0[...] = tokens_of(0)
 
 
-def pass_kernel(at, d1, d3, r_a, r_b, s1, s3):
-    s1[:HALF] = d1[:HALF] + r_a[...]
-    s1[HALF:] = d1[HALF:]
-    s3[:HALF] = d3[:HALF]
-    s3[HALF:] = d3[HALF:] + r_b[...]
+def pass_kernel(at, a, b, out):
+    out[...] = a[...] + b[...]
 
 
 def deal_kernel(which, at, *refs):
@@ -505,19 +501,17 @@
     keep, send, dz = call(
         outer_kernel,
         [((ROWS, ALL), F32), ((ROWS, ALL), F32), ((NX, SEG, WIDE), BF16)],
-        [((NX, NS, 2 * HC), BF16), ((2, ROWS, WIDE), F32)],
+        [((NX, NS, 2 * HC), BF16), ((DM, WIDE), F32)],
         [at, tokb, xfr, bc, ci, ce, pre_d, *p_rows, dxi, dci, dbi, g_out],
         2 * 1024 * (WIDE * DM + 4 * NS * HC),
     )
     got = move(send, "c", 1)
     terms = deal(at, 2, [keep, got], 96, ALL)
-    whole, half = ((SEG, DM), F32), ((HALF, DM), F32)
-    d0, d1, d2a, d2b, d3 = call(
-        tokens_kernel, [whole, whole, half, half, whole], [], [at, dz, wi, w_bc], 2 * 1024 * WIDE * DM
-    )
-    r_a, r_b = move(d2a, "x", 1), move(d2b, "x", -1)
-    s1, s3 = call(pass_kernel, [whole, whole], [], [at, d1, d3, r_a, r_b])
-    m1, m3 = move(s1, "x", 1), move(s3, "x", -1)
+    whole = ((SEG, DM), F32)
+    d0, d1, d2, d3 = call(tokens_kernel, [whole] * 4, [], [at, dz, wi, w_bc], 2 * 1024 * WIDE * DM)
+    far, d3 = tie((move(d2, "x", 1), d3))
+    (s1,) = call(pass_kernel, [whole], [], [at, d1, far])
+    m1, m3 = move(s1, "x", 1), move(d3, "x", -1)
     d_tok = (d0 + m1 + m3).astype(BF16)
     terms = deal(at, 3, terms, 24, ALL)
     p0, p1, p2, p3, rows_out = call(

time: 151 us -> 154 us (1.020); the launches traced: 151 us -> 151 us
    ppermute x1, starting transfers between devices: 4.08 us -> 7.02 us  [body(): rows_out = lax.ppermute(rows_out, ('rec', 'seq'), pairs)]
    ppermute x1, waiting for transfers between devices: 4.09 us -> 1.76 us  [body(): rows_out = lax.ppermute(rows_out, ('rec', 'seq'), pairs)]
    ppermute x33 -> x32, waiting for transfers between devices: 51.7 us -> 53.5 us  [move(): return lax.ppermute(value, name, pairs)]
    ppermute x33 -> x32, starting transfers between devices: 48.1 us -> 46.3 us  [move(): return lax.ppermute(value, name, pairs)]
  transfers between devices with their start and end apart: 34 -> 33, of which waited for: 20 -> 17; matrix products, arithmetic and copies ran while one was open for 3% -> 3% of each run, Pallas kernels for 20% -> 20%
where the time goes in v7:
time: 154 us; the launch traced here: 151 us
  waiting for transfers between devices  55.3 us (36%)
  starting transfers between devices  53.4 us (35%)
  Pallas kernels  34.9 us (23%)
  local copies, waits for them, and re-layouts  4.07 us (3%)
  other arithmetic  2.88 us (2%)
    ppermute x32, waiting for transfers between devices, move(): return lax.ppermute(value, name, pairs)  53.5 us
    ppermute x32, starting transfers between devices, move(): return lax.ppermute(value, name, pairs)  46.3 us
    pallas_call x15, Pallas kernels, call(): pl.pallas_call(kernel, out_shape=[jax.ShapeDtypeStruct(*o) for o in outs]...  34.8 us
    ppermute x1, starting transfers between devices, body(): rows_out = lax.ppermute(rows_out, ('rec', 'seq'), pairs)  7.02 us
  transfers between devices with their start and end apart: 33, of which 17 were waited for; matrix products, arithmetic and copies ran while one was open for 3% of the time, Pallas kernels for 20%

profile of v7, /device:TPU:6, one launch (start us, length us, event | category | flops | bytes accessed | tf_op | source)
XLA Modules:
  0.0 151.3 jit_solution(16680042090848060020)
XLA Ops:
  0.7 1.1 copy-done.3
  1.8 0.7 copy-done.5
  2.6 0.5 collective-permute-start
  3.1 1.6 %collective-permute-start.2 = (f32[264,768]{1,0:T(8,128)S(1)}, f32[264,768]{1,0:T(8,128)S(1)}, u32[]{:S(2)}, u32[]{:S(2)}) collective-permute-start(f32[264,768]{1,0:T(8,128)S(1)} %shard_map.93), channel_id=1, source_target_pairs={{0,3},{1,0},{2,1},{3,2},{4,7},{5,4},{6,5},{7,6},{8,11},{9,8},{10,9... | collective-permute-start | bytes 2433032 | tf_op jit(solution)/shard_map/ppermute | solution.py:47
  4.7 1.9 %bitcast_convert_fusion = f32[256,768]{1,0:T(8,128)} fusion(bf16[1,256,768]{2,1,0:T(8,128)(2,1)} %param.7), kind=kLoop, calls=%fused_computation.7 | loop fusion | flops 196608 | bytes 1179648 | tf_op jit(solution)/shard_map/convert_element_type | solution.py:442
  6.6 16.0 %collective-permute-done.t3 = f32[264,768]{1,0:T(8,128)} collective-permute-done((f32[264,768]{1,0:T(8,128)S(1)}, f32[264,768]{1,0:T(8,128)}, u32[]{:S(2)}, u32[]{:S(2)}) %collective-permute-start) | collective-permute-done | bytes 811040 | tf_op jit(solution)/shard_map/ppermute | solution.py:47
  22.6 1.5 collective-permute-start.1
  24.1 0.9 copy-done.7
  25.0 0.5 collective-permute-start.3
  25.7 1.2 constant_dynamic-slice_fusion.w_out
  26.9 2.8 %collective-permute-start.4 = (f32[256,768]{1,0:T(8,128)}, f32[256,768]{1,0:T(8,128)S(1)}, u32[]{:S(2)}, u32[]{:S(2)}) collective-permute-start(f32[256,768]{1,0:T(8,128)} %bitcast_convert_fusion), channel_id=1, source_target_pairs={{0,1},{1,2},{2,3},{3,0},{4,5},{5,6},{6,7},{7,4},{8,9},{9,10},{10,1... | collective-permute-start | bytes 2359304 | tf_op jit(solution)/shard_map/ppermute | solution.py:47
  29.7 6.6 %shard_map.94 = (f32[3,8,256]{2,1,0:T(8,128)S(1)}, f32[3,8,256]{2,1,0:T(8,128)S(1)}, f32[3,256,384]{2,1,0:T(8,128)S(1)}, f32[3,256,384]{2,1,0:T(8,128)S(1)}, bf1...) custom-call(s32[4]{0:T(128)S(1)} %pad_add_fusion.at, ...), custom_call_target="tpu_custom_call" | custom-call | flops 905969664 | bytes 3022864 | tf_op jit(solution)/shard_map/pallas_call | solution.py:404
  36.3 3.5 %shard_map.95 = (bf16[3,6,256,256]{3,2,1,0:T(8,128)(2,1)S(1)}, bf16[3,6,256,256]{3,2,1,0:T(8,128)(2,1)S(1)}, f32[3,256,384]{2,1,0:T(8,128)S(1)}) custom-call(s32[4]{0:T(128)S(1)} %pad_add_fusion.at, f32[3,8,256]{2,1,0:T(8,128)S(1)} %get-tuple-element.117.cirow.refs_0_, f32[3,8,256]{2,1,0:T(8,128)S(1)} %get-tuple-element.118.cerow.refs_1_, ...), custom_call_target="tpu_custom_call" | custom-call | flops 301989888 | bytes 3391504 | tf_op jit(solution)/shard_map/pallas_call | solution.py:404
  39.8 4.7 %collective-permute-done.3.c1 = f32[256,768]{1,0:T(8,128)} collective-permute-done((f32[256,768]{1,0:T(8,128)}, f32[256,768]{1,0:T(8,128)}, u32[]{:S(2)}, u32[]{:S(2)}) %collective-permute-start.3) | collective-permute-done | bytes 786464 | tf_op jit(solution)/shard_map/ppermute | solution.py:47
  44.6 2.9 %shard_map.96 = (f32[4,8,256]{2,1,0:T(8,128)S(1)}, f32[4,8,256]{2,1,0:T(8,128)S(1)}, f32[4,256,384]{2,1,0:T(8,128)S(1)}, f32[4,256,384]{2,1,0:T(8,128)S(1)}, bf1...) custom-call(s32[4]{0:T(128)S(1)} %pad_add_fusion.at, ...), custom_call_target="tpu_custom_call" | custom-call | flops 301989888 | bytes 8724496 | tf_op jit(solution)/shard_map/pallas_call | solution.py:404
  47.5 1.9 %collective-permute-start.9 = (f32[136,384]{1,0:T(8,128)S(1)}, f32[136,384]{1,0:T(8,128)S(1)}, u32[]{:S(2)}, u32[]{:S(2)}) collective-permute-start(f32[136,384]{1,0:T(8,128)S(1)} %get-tuple-element.154), channel_id=1, source_target_pairs={{0,4},{1,5},{2,6},{3,7},{4,8},{5,9},{6,10},{7,11},{8,12},{9,13},{1... | collective-permute-start | bytes 626696 | tf_op jit(solution)/shard_map/ppermute | solution.py:47
  49.4 1.5 %collective-permute-start.10 = (f32[136,384]{1,0:T(8,128)S(1)}, f32[136,384]{1,0:T(8,128)S(1)}, u32[]{:S(2)}, u32[]{:S(2)}) collective-permute-start(f32[136,384]{1,0:T(8,128)S(1)} %get-tuple-element.155), channel_id=1, source_target_pairs={{0,12},{1,13},{2,14},{3,15},{4,0},{5,1},{6,2},{7,3},{8,4},{9,5},{1... | collective-permute-start | bytes 626696 | tf_op jit(solution)/shard_map/ppermute | solution.py:47
  50.9 2.1 %collective-permute-start.11 = (f32[136,384]{1,0:T(8,128)S(1)}, f32[136,384]{1,0:T(8,128)S(1)}, u32[]{:S(2)}, u32[]{:S(2)}) collective-permute-start(f32[136,384]{1,0:T(8,128)S(1)} %get-tuple-element.156), channel_id=1, source_target_pairs={{0,8},{1,9},{2,10},{3,11},{4,12},{5,13},{6,14},{7,15},{8,0},{9,1},... | collective-permute-start | bytes 626696 | tf_op jit(solution)/shard_map/ppermute | solution.py:47
  53.0 1.5 %shard_map.98 = (bf16[1,6,256,256]{3,2,1,0:T(8,128)(2,1)S(1)}, bf16[1,6,256,256]{3,2,1,0:T(8,128)(2,1)S(1)}, f32[1,256,384]{2,1,0:T(8,128)S(1)}) custom-call(s32[4]{0:T(128)S(1)} %pad_add_fusion.at, f32[4,8,256]{2,1,0:T(8,128)S(1)} %get-tuple-element.134.cirow, f32[4,8,256]{2,1,0:T(8,128)S(1)} %get-tuple-element.135.cerow, ...), custom_call_target="tpu_custom_call" | custom-call | flops 100663296 | bytes 4522000 | tf_op jit(solution)/shard_map/pallas_call | solution.py:404
  54.6 2.5 %shard_map.97 = (bf16[2,256,768]{2,1,0:T(8,128)(2,1)S(1)}, bf16[2,256,384]{2,1,0:T(8,128)(2,1)S(1)}, bf16[2,256,768]{2,1,0:T(8,128)(2,1)S(1)}, f32[2,128,768]{2,1,0:T(8,128)S(1)}) custom-call(s32[4]{0:T(128)S(1)} %pad_add_fusion.at, bf16[256,768]{1,0:T(8,128)(2,1)S(1)} %bitcast.10, f32[256,768]{1,0:T(8,128)} %collective-permute-done.3.c1, ...), custom_call_target="tpu_custom_call" | custom-call | flops 402653184 | bytes 5439504 | tf_op jit(solution)/shard_map/pallas_call | solution.py:404
  57.1 1.5 collective-permute-done.4.c2
  58.6 4.4 %collective-permute-done.5.c3 = f32[256,768]{1,0:T(8,128)S(1)} collective-permute-done((f32[256,768]{1,0:T(8,128)}, f32[256,768]{1,0:T(8,128)S(1)}, u32[]{:S(2)}, u32[]{:S(2)}) %collective-permute-start.5) | collective-permute-done | bytes 786464 | tf_op jit(solution)/shard_map/ppermute | solution.py:47
  63.0 2.1 %shard_map.99 = (bf16[2,256,768]{2,1,0:T(8,128)(2,1)S(1)}, bf16[2,256,384]{2,1,0:T(8,128)(2,1)S(1)}, bf16[2,256,768]{2,1,0:T(8,128)(2,1)S(1)}, f32[2,4,128,384]{...) custom-call(s32[4]{0:T(128)S(1)} %pad_add_fusion.at, ...), custom_call_target="tpu_custom_call" | custom-call | flops 402653184 | bytes 6619152 | tf_op jit(solution)/shard_map/pallas_call | solution.py:404
  65.1 2.1 %collective-permute-start.6 = (f32[136,384]{1,0:T(8,128)S(1)}, f32[136,384]{1,0:T(8,128)S(1)}, u32[]{:S(2)}, u32[]{:S(2)}) collective-permute-start(f32[136,384]{1,0:T(8,128)S(1)} %get-tuple-element.144), channel_id=1, source_target_pairs={{0,4},{1,5},{2,6},{3,7},{4,8},{5,9},{6,10},{7,11},{8,12},{9,13},{1... | collective-permute-start | bytes 626696 | tf_op jit(solution)/shard_map/ppermute | solution.py:47
  67.2 1.7 %collective-permute-start.7 = (f32[136,384]{1,0:T(8,128)S(1)}, f32[136,384]{1,0:T(8,128)S(1)}, u32[]{:S(2)}, u32[]{:S(2)}) collective-permute-start(f32[136,384]{1,0:T(8,128)S(1)} %get-tuple-element.145), channel_id=1, source_target_pairs={{0,12},{1,13},{2,14},{3,15},{4,0},{5,1},{6,2},{7,3},{8,4},{9,5},{1... | collective-permute-start | bytes 626696 | tf_op jit(solution)/shard_map/ppermute | solution.py:47
  69.0 1.9 %collective-permute-start.8 = (f32[136,384]{1,0:T(8,128)S(1)}, f32[136,384]{1,0:T(8,128)S(1)}, u32[]{:S(2)}, u32[]{:S(2)}) collective-permute-start(f32[136,384]{1,0:T(8,128)S(1)} %get-tuple-element.146), channel_id=1, source_target_pairs={{0,8},{1,9},{2,10},{3,11},{4,12},{5,13},{6,14},{7,15},{8,0},{9,1},... | collective-permute-start | bytes 626696 | tf_op jit(solution)/shard_map/ppermute | solution.py:47
  70.9 5.1 %shard_map.100 = (f32[2,384,384]{2,1,0:T(8,128)S(1)}, f32[4,256,384]{2,1,0:T(8,128)S(1)}, f32[4,256,128]{2,1,0:T(8,128)S(1)}, f32[4,256,128]{2,1,0:T(8,128)S(1)}) custom-call(s32[4]{0:T(128)S(1)} %pad_add_fusion.at, bf16[4,256,384]{2,1,0:T(8,128)(2,1)S(1)} %get-tuple-element.136.xs, bf16[4,256,256]{2,1,0:T(8,128)(2,1)S(1)} %get-tuple-element.128.bc, ...), custom_call_target="tpu_custom_call" | custom-call | flops 2214592512 | bytes 18452496 | tf_op jit(solution)/shard_map/pallas_call | solution.py:404
  76.0 0.5 collective-permute-done.8.r_2
  76.5 4.0 %shard_map.101 = (f32[384,1024]{1,0:T(8,128)S(1)}, f32[384,1024]{1,0:T(8,128)S(1)}, bf16[4,256,640]{2,1,0:T(8,128)(2,1)S(1)}) custom-call(s32[4]{0:T(128)S(1)} %pad_add_fusion.at, bf16[4,256,768]{2,1,0:T(8,128)(2,1)S(1)} %get-tuple-element.126.tokb, bf16[4,256,768]{2,1,0:T(8,128)(2,1)S(1)} %get-tuple-element.127.xfr, ...), custom_call_target="tpu_custom_call" | custom-call | flops 1409286144 | bytes 12816400 | tf_op jit(solution)/shard_map/pallas_call | solution.py:404
  80.6 2.0 %shard_map.102 = (f32[256,768]{1,0:T(8,128)S(1)}, f32[256,768]{1,0:T(8,128)S(1)}, f32[256,768]{1,0:T(8,128)S(1)}, f32[256,768]{1,0:T(8,128)S(1)}) custom-call(s32[4]{0:T(128)S(1)} %pad_add_fusion.at, bf16[4,256,640]{2,1,0:T(8,128)(2,1)S(1)} %get-tuple-element.167.dz, bf16[768,384]{1,0:T(8,128)(2,1)S(1)} %constant_dynamic-slice_fusion.1.w_in, ...), custom_call_target="tpu_custom_call" | custom-call | flops 1006632960 | bytes 2293776 | tf_op jit(solution)/shard_map/pallas_call | solution.py:404
  82.6 1.4 collective-permute-done.15.refs_1_
  84.0 0.8 shard_map.104
  84.8 1.2 collective-permute-start.16
  86.0 2.4 %collective-permute-start.17 = (f32[96,1024]{1,0:T(8,128)S(1)}, f32[96,1024]{1,0:T(8,128)S(1)}, u32[]{:S(2)}, u32[]{:S(2)}) collective-permute-start(f32[96,1024]{1,0:T(8,128)S(1)} %get-tuple-element.178), channel_id=1, source_target_pairs={{0,8},{1,9},{2,10},{3,11},{4,12},{5,13},{6,14},{7,15},{8,0},{9,1},... | collective-permute-start | bytes 1179656 | tf_op jit(solution)/shard_map/ppermute | solution.py:47
  88.3 0.8 collective-permute-start.18
  89.2 13.4 %collective-permute-done.12.b = f32[256,768]{1,0:T(8,128)S(1)} collective-permute-done((f32[256,768]{1,0:T(8,128)S(1)}, f32[256,768]{1,0:T(8,128)S(1)}, u32[]{:S(2)}, u32[]{:S(2)}) %collective-permute-start.12) | collective-permute-done | bytes 786464 | tf_op jit(solution)/shard_map/ppermute | solution.py:47
  102.5 0.6 shard_map.103
  103.2 3.3 %collective-permute-start.13 = (f32[256,768]{1,0:T(8,128)S(1)}, f32[256,768]{1,0:T(8,128)S(1)}, u32[]{:S(2)}, u32[]{:S(2)}) collective-permute-start(f32[256,768]{1,0:T(8,128)S(1)} %shard_map.103), channel_id=1, source_target_pairs={{0,1},{1,2},{2,3},{3,0},{4,5},{5,6},{6,7},{7,4},{8,9},{9,10},{10,1... | collective-permute-start | bytes 2359304 | tf_op jit(solution)/shard_map/ppermute | solution.py:47
  106.5 0.7 shard_map.105
  107.2 2.0 %collective-permute-start.19 = (f32[24,1024]{1,0:T(8,128)S(1)}, f32[24,1024]{1,0:T(8,128)S(1)}, u32[]{:S(2)}, u32[]{:S(2)}) collective-permute-start(f32[24,1024]{1,0:T(8,128)S(1)} %get-tuple-element.181), channel_id=1, source_target_pairs={{0,32},{16,48},{32,64},{48,80},{64,96},{80,112},{96,0},{112,16},{1... | collective-permute-start | bytes 294920 | tf_op jit(solution)/shard_map/ppermute | solution.py:47
  109.2 3.6 %collective-permute-start.20 = (f32[24,1024]{1,0:T(8,128)S(1)}, f32[24,1024]{1,0:T(8,128)S(1)}, u32[]{:S(2)}, u32[]{:S(2)}) collective-permute-start(f32[24,1024]{1,0:T(8,128)S(1)} %get-tuple-element.182), channel_id=1, source_target_pairs={{0,64},{16,80},{32,96},{48,112},{64,0},{80,16},{96,32},{112,48},{1... | collective-permute-start | bytes 294920 | tf_op jit(solution)/shard_map/ppermute | solution.py:47
  112.7 1.0 collective-permute-start.21
  113.8 1.2 collective-permute-done.19.b
  114.9 1.7 %collective-permute-done.20.c = f32[24,1024]{1,0:T(8,128)S(1)} collective-permute-done((f32[24,1024]{1,0:T(8,128)S(1)}, f32[24,1024]{1,0:T(8,128)S(1)}, u32[]{:S(2)}, u32[]{:S(2)}) %collective-permute-start.20) | collective-permute-done | bytes 98336 | tf_op jit(solution)/shard_map/ppermute | solution.py:47
  116.7 0.7 collective-permute-done.21.d
  117.4 0.7 shard_map.106
  118.0 0.4 collective-permute-start.22
  118.4 2.3 %collective-permute-start.23 = (f32[40,384]{1,0:T(8,128)S(1)}, f32[40,384]{1,0:T(8,128)S(1)}, u32[]{:S(2)}, u32[]{:S(2)}) collective-permute-start(f32[40,384]{1,0:T(8,128)S(1)} %get-tuple-element.186), channel_id=1, source_target_pairs={{0,2},{1,3},{2,0},{3,1},{4,6},{5,7},{6,4},{7,5},{8,10},{9,11},{10,... | collective-permute-start | bytes 184328 | tf_op jit(solution)/shard_map/ppermute | solution.py:47
  120.7 4.8 %collective-permute-done.22.b = f32[40,384]{1,0:T(8,128)S(1)} collective-permute-done((f32[40,384]{1,0:T(8,128)S(1)}, f32[40,384]{1,0:T(8,128)S(1)}, u32[]{:S(2)}, u32[]{:S(2)}) %collective-permute-start.22) | collective-permute-done | bytes 61472 | tf_op jit(solution)/shard_map/ppermute | solution.py:47
  125.5 0.6 collective-permute-done.24.d
  126.1 0.7 shard_map.107
  126.8 1.8 %collective-permute-start.28 = (f32[8,128]{1,0:T(8,128)S(1)}, f32[8,128]{1,0:T(8,128)S(1)}, u32[]{:S(2)}, u32[]{:S(2)}) collective-permute-start(f32[8,128]{1,0:T(8,128)S(1)} %shard_map.107), channel_id=1, source_target_pairs={{0,8},{1,9},{2,10},{3,11},{4,12},{5,13},{6,14},{7,15},{8,0},{9,1},... | collective-permute-start | bytes 12296 | tf_op jit(solution)/shard_map/ppermute | solution.py:47
  128.6 2.0 %collective-permute-start.26 = (f32[8,128]{1,0:T(8,128)S(1)}, f32[8,128]{1,0:T(8,128)S(1)}, u32[]{:S(2)}, u32[]{:S(2)}) collective-permute-start(f32[8,128]{1,0:T(8,128)S(1)} %shard_map.107), channel_id=1, source_target_pairs={{0,4},{1,5},{2,6},{3,7},{4,8},{5,9},{6,10},{7,11},{8,12},{9,13},{1... | collective-permute-start | bytes 12296 | tf_op jit(solution)/shard_map/ppermute | solution.py:47
  130.6 1.3 collective-permute-start.27
  132.0 1.4 collective-permute-done.26
  133.4 0.8 collective-permute-done.27
  134.2 2.6 %collective-permute-start.31 = (f32[8,128]{1,0:T(8,128)S(1)}, f32[8,128]{1,0:T(8,128)S(1)}, u32[]{:S(2)}, u32[]{:S(2)}) collective-permute-start(f32[8,128]{1,0:T(8,128)S(1)} %add_add_fusion.1), channel_id=1, source_target_pairs={{0,64},{16,80},{32,96},{48,112},{64,0},{80,16},{96,32},{112,48},{1... | collective-permute-start | bytes 12296 | tf_op jit(solution)/shard_map/ppermute | solution.py:47
  136.8 1.0 collective-permute-start.29
  137.8 2.2 %collective-permute-start.30 = (f32[8,128]{1,0:T(8,128)S(1)}, f32[8,128]{1,0:T(8,128)S(1)}, u32[]{:S(2)}, u32[]{:S(2)}) collective-permute-start(f32[8,128]{1,0:T(8,128)S(1)} %add_add_fusion.1), channel_id=1, source_target_pairs={{0,96},{16,112},{32,0},{48,16},{64,32},{80,48},{96,64},{112,80},{1... | collective-permute-start | bytes 12296 | tf_op jit(solution)/shard_map/ppermute | solution.py:47
  140.0 7.0 %collective-permute-start.25 = (f32[24,384]{1,0:T(8,128)S(1)}, f32[24,384]{1,0:T(8,128)S(1)}, u32[]{:S(2)}, u32[]{:S(2)}) collective-permute-start(f32[24,384]{1,0:T(8,128)S(1)} %get-tuple-element.188), channel_id=1, source_target_pairs={{0,0},{1,32},{2,64},{3,96},{4,1},{5,33},{6,65},{7,97},{8,2},{9,34}... | collective-permute-start | bytes 110600 | tf_op jit(solution)/shard_map/ppermute | solution.py:523
  147.2 0.9 fusion
  148.1 0.3 collective-permute-done.32
  148.3 1.8 %collective-permute-done.25.rows_out = f32[24,384]{1,0:T(8,128)S(1)} collective-permute-done((f32[24,384]{1,0:T(8,128)S(1)}, f32[24,384]{1,0:T(8,128)S(1)}, u32[]{:S(2)}, u32[]{:S(2)}) %collective-permute-start.25) | collective-permute-done | bytes 36896 | tf_op jit(solution)/shard_map/ppermute | solution.py:523
  150.1 1.2 shard_map.108
  (44 shorter events, 0.9 us)
Async XLA Ops:
  0.6 25.0 %copy-start = (bf16[768,1536]{1,0:T(8,128)(2,1)S(1)}, bf16[768,1536]{1,0:T(8,128)(2,1)}, u32[]{:S(2)}) copy-start(bf16[768,1536]{1,0:T(8,128)(2,1)} %param.9) | copy-start | bytes 7077892
  0.6 1.1 copy-start.3
  1.8 0.7 copy-start.5
  2.6 27.1 %copy-start.6 = (f32[1,24,256]{2,1,0:T(8,128)S(1)}, f32[1,24,256]{2,1,0:T(8,128)}, u32[]{:S(2)}) copy-start(f32[1,24,256]{2,1,0:T(8,128)} %param.8) | copy-start | bytes 73732
  2.6 20.0 %collective-permute-start = (f32[264,768]{1,0:T(8,128)S(1)}, f32[264,768]{1,0:T(8,128)}, u32[]{:S(2)}, u32[]{:S(2)}) collective-permute-start(f32[264,768]{1,0:T(8,128)S(1)} %shard_map.93), channel_id=1, source_target_pairs={{0,1},{1,2},{2,3},{3,0},{4,5},{5,6},{6,7},{7,4},{8,9},{9,10},{10,1... | collective-permute-start | bytes 2433032 | tf_op jit(solution)/shard_map/ppermute | solution.py:47
  3.1 21.0 %collective-permute-start.2 = (f32[264,768]{1,0:T(8,128)S(1)}, f32[264,768]{1,0:T(8,128)S(1)}, u32[]{:S(2)}, u32[]{:S(2)}) collective-permute-start(f32[264,768]{1,0:T(8,128)S(1)} %shard_map.93), channel_id=1, source_target_pairs={{0,3},{1,0},{2,1},{3,2},{4,7},{5,4},{6,5},{7,6},{8,11},{9,8},{10,9... | collective-permute-start | bytes 2433032 | tf_op jit(solution)/shard_map/ppermute | solution.py:47
  22.6 21.9 %collective-permute-start.1 = (f32[264,768]{1,0:T(8,128)}, f32[264,768]{1,0:T(8,128)S(1)}, u32[]{:S(2)}, u32[]{:S(2)}) collective-permute-start(f32[264,768]{1,0:T(8,128)} %collective-permute-done.t3), channel_id=1, source_target_pairs={{0,1},{1,2},{2,3},{3,0},{4,5},{5,6},{6,7},{7,4},{8,9},{9,10},{10,1... | collective-permute-start | bytes 2433032 | tf_op jit(solution)/shard_map/ppermute | solution.py:47
  24.1 0.9 copy-start.7
  25.0 19.5 %collective-permute-start.3 = (f32[256,768]{1,0:T(8,128)}, f32[256,768]{1,0:T(8,128)}, u32[]{:S(2)}, u32[]{:S(2)}) collective-permute-start(f32[256,768]{1,0:T(8,128)} %bitcast_convert_fusion), channel_id=1, source_target_pairs={{0,3},{1,0},{2,1},{3,2},{4,7},{5,4},{6,5},{7,6},{8,11},{9,8},{10,9... | collective-permute-start | bytes 2359304 | tf_op jit(solution)/shard_map/ppermute | solution.py:47
  25.5 4.1 %copy-start.2 = (bf16[768,256]{1,0:T(8,128)(2,1)S(1)}, bf16[768,256]{1,0:T(8,128)(2,1)}, u32[]{:S(2)}) copy-start(bf16[768,256]{1,0:T(8,128)(2,1)} %w_bc.5) | copy-start | bytes 1179652
  25.5 4.1 %copy-start.4 = (bf16[1,256,768]{2,1,0:T(8,128)(2,1)S(1)}, bf16[1,256,768]{2,1,0:T(8,128)(2,1)}, u32[]{:S(2)}) copy-start(bf16[1,256,768]{2,1,0:T(8,128)(2,1)} %param.6) | copy-start | bytes 1179652
  25.5 4.1 %copy-start.8 = (f32[264,768]{1,0:T(8,128)S(1)}, f32[264,768]{1,0:T(8,128)}, u32[]{:S(2)}) copy-start(f32[264,768]{1,0:T(8,128)} %copy-done.7) | copy-start | bytes 2433028
  26.9 31.7 %collective-permute-start.4 = (f32[256,768]{1,0:T(8,128)}, f32[256,768]{1,0:T(8,128)S(1)}, u32[]{:S(2)}, u32[]{:S(2)}) collective-permute-start(f32[256,768]{1,0:T(8,128)} %bitcast_convert_fusion), channel_id=1, source_target_pairs={{0,1},{1,2},{2,3},{3,0},{4,5},{5,6},{6,7},{7,4},{8,9},{9,10},{10,1... | collective-permute-start | bytes 2359304 | tf_op jit(solution)/shard_map/ppermute | solution.py:47
  44.5 18.5 %collective-permute-start.5 = (f32[256,768]{1,0:T(8,128)}, f32[256,768]{1,0:T(8,128)S(1)}, u32[]{:S(2)}, u32[]{:S(2)}) collective-permute-start(f32[256,768]{1,0:T(8,128)} %collective-permute-done.3.c1), channel_id=1, source_target_pairs={{0,3},{1,0},{2,1},{3,2},{4,7},{5,4},{6,5},{7,6},{8,11},{9,8},{10,9... | collective-permute-start | bytes 2359304 | tf_op jit(solution)/shard_map/ppermute | solution.py:47
  47.5 21.4 %collective-permute-start.9 = (f32[136,384]{1,0:T(8,128)S(1)}, f32[136,384]{1,0:T(8,128)S(1)}, u32[]{:S(2)}, u32[]{:S(2)}) collective-permute-start(f32[136,384]{1,0:T(8,128)S(1)} %get-tuple-element.154), channel_id=1, source_target_pairs={{0,4},{1,5},{2,6},{3,7},{4,8},{5,9},{6,10},{7,11},{8,12},{9,13},{1... | collective-permute-start | bytes 626696 | tf_op jit(solution)/shard_map/ppermute | solution.py:47
  49.4 21.5 %collective-permute-start.10 = (f32[136,384]{1,0:T(8,128)S(1)}, f32[136,384]{1,0:T(8,128)S(1)}, u32[]{:S(2)}, u32[]{:S(2)}) collective-permute-start(f32[136,384]{1,0:T(8,128)S(1)} %get-tuple-element.155), channel_id=1, source_target_pairs={{0,12},{1,13},{2,14},{3,15},{4,0},{5,1},{6,2},{7,3},{8,4},{9,5},{1... | collective-permute-start | bytes 626696 | tf_op jit(solution)/shard_map/ppermute | solution.py:47
  50.9 20.0 %collective-permute-start.11 = (f32[136,384]{1,0:T(8,128)S(1)}, f32[136,384]{1,0:T(8,128)S(1)}, u32[]{:S(2)}, u32[]{:S(2)}) collective-permute-start(f32[136,384]{1,0:T(8,128)S(1)} %get-tuple-element.156), channel_id=1, source_target_pairs={{0,8},{1,9},{2,10},{3,11},{4,12},{5,13},{6,14},{7,15},{8,0},{9,1},... | collective-permute-start | bytes 626696 | tf_op jit(solution)/shard_map/ppermute | solution.py:47
  53.0 1.5 %copy-start.1 = (bf16[1,256,768]{2,1,0:T(8,128)(2,1)S(1)}, bf16[1,256,768]{2,1,0:T(8,128)(2,1)}, u32[]{:S(2)}) copy-start(bf16[1,256,768]{2,1,0:T(8,128)(2,1)} %param.7) | copy-start | bytes 1179652
  65.1 10.8 %collective-permute-start.6 = (f32[136,384]{1,0:T(8,128)S(1)}, f32[136,384]{1,0:T(8,128)S(1)}, u32[]{:S(2)}, u32[]{:S(2)}) collective-permute-start(f32[136,384]{1,0:T(8,128)S(1)} %get-tuple-element.144), channel_id=1, source_target_pairs={{0,4},{1,5},{2,6},{3,7},{4,8},{5,9},{6,10},{7,11},{8,12},{9,13},{1... | collective-permute-start | bytes 626696 | tf_op jit(solution)/shard_map/ppermute | solution.py:47
  67.2 8.8 %collective-permute-start.7 = (f32[136,384]{1,0:T(8,128)S(1)}, f32[136,384]{1,0:T(8,128)S(1)}, u32[]{:S(2)}, u32[]{:S(2)}) collective-permute-start(f32[136,384]{1,0:T(8,128)S(1)} %get-tuple-element.145), channel_id=1, source_target_pairs={{0,12},{1,13},{2,14},{3,15},{4,0},{5,1},{6,2},{7,3},{8,4},{9,5},{1... | collective-permute-start | bytes 626696 | tf_op jit(solution)/shard_map/ppermute | solution.py:47
  69.0 7.6 %collective-permute-start.8 = (f32[136,384]{1,0:T(8,128)S(1)}, f32[136,384]{1,0:T(8,128)S(1)}, u32[]{:S(2)}, u32[]{:S(2)}) collective-permute-start(f32[136,384]{1,0:T(8,128)S(1)} %get-tuple-element.146), channel_id=1, source_target_pairs={{0,8},{1,9},{2,10},{3,11},{4,12},{5,13},{6,14},{7,15},{8,0},{9,1},... | collective-permute-start | bytes 626696 | tf_op jit(solution)/shard_map/ppermute | solution.py:47
  80.5 3.5 %collective-permute-start.15 = (f32[384,1024]{1,0:T(8,128)S(1)}, f32[384,1024]{1,0:T(8,128)S(1)}, u32[]{:S(2)}, u32[]{:S(2)}) collective-permute-start(f32[384,1024]{1,0:T(8,128)S(1)} %get-tuple-element.175), channel_id=1, source_target_pairs={{0,16},{16,0},{32,48},{48,32},{64,80},{80,64},{96,112},{112,96},{1... | collective-permute-start | bytes 4718600 | tf_op jit(solution)/shard_map/ppermute | solution.py:47
  82.5 20.0 %collective-permute-start.12 = (f32[256,768]{1,0:T(8,128)S(1)}, f32[256,768]{1,0:T(8,128)S(1)}, u32[]{:S(2)}, u32[]{:S(2)}) collective-permute-start(f32[256,768]{1,0:T(8,128)S(1)} %get-tuple-element.170), channel_id=1, source_target_pairs={{0,1},{1,2},{2,3},{3,0},{4,5},{5,6},{6,7},{7,4},{8,9},{9,10},{10,1... | collective-permute-start | bytes 2359304 | tf_op jit(solution)/shard_map/ppermute | solution.py:47
  84.8 21.7 %collective-permute-start.16 = (f32[96,1024]{1,0:T(8,128)S(1)}, f32[96,1024]{1,0:T(8,128)S(1)}, u32[]{:S(2)}, u32[]{:S(2)}) collective-permute-start(f32[96,1024]{1,0:T(8,128)S(1)} %get-tuple-element.177), channel_id=1, source_target_pairs={{0,4},{1,5},{2,6},{3,7},{4,8},{5,9},{6,10},{7,11},{8,12},{9,13},{1... | collective-permute-start | bytes 1179656 | tf_op jit(solution)/shard_map/ppermute | solution.py:47
  86.0 20.5 %collective-permute-start.17 = (f32[96,1024]{1,0:T(8,128)S(1)}, f32[96,1024]{1,0:T(8,128)S(1)}, u32[]{:S(2)}, u32[]{:S(2)}) collective-permute-start(f32[96,1024]{1,0:T(8,128)S(1)} %get-tuple-element.178), channel_id=1, source_target_pairs={{0,8},{1,9},{2,10},{3,11},{4,12},{5,13},{6,14},{7,15},{8,0},{9,1},... | collective-permute-start | bytes 1179656 | tf_op jit(solution)/shard_map/ppermute | solution.py:47
  88.3 18.1 %collective-permute-start.18 = (f32[96,1024]{1,0:T(8,128)S(1)}, f32[96,1024]{1,0:T(8,128)S(1)}, u32[]{:S(2)}, u32[]{:S(2)}) collective-permute-start(f32[96,1024]{1,0:T(8,128)S(1)} %get-tuple-element.179), channel_id=1, source_target_pairs={{0,12},{1,13},{2,14},{3,15},{4,0},{5,1},{6,2},{7,3},{8,4},{9,5},{1... | collective-permute-start | bytes 1179656 | tf_op jit(solution)/shard_map/ppermute | solution.py:47
  102.5 44.7 %collective-permute-start.14 = (f32[256,768]{1,0:T(8,128)S(1)}, f32[256,768]{1,0:T(8,128)S(1)}, u32[]{:S(2)}, u32[]{:S(2)}) collective-permute-start(f32[256,768]{1,0:T(8,128)S(1)} %get-tuple-element.173), channel_id=1, source_target_pairs={{0,3},{1,0},{2,1},{3,2},{4,7},{5,4},{6,5},{7,6},{8,11},{9,8},{10,9... | collective-permute-start | bytes 2359304 | tf_op jit(solution)/shard_map/ppermute | solution.py:47
  103.2 44.0 %collective-permute-start.13 = (f32[256,768]{1,0:T(8,128)S(1)}, f32[256,768]{1,0:T(8,128)S(1)}, u32[]{:S(2)}, u32[]{:S(2)}) collective-permute-start(f32[256,768]{1,0:T(8,128)S(1)} %shard_map.103), channel_id=1, source_target_pairs={{0,1},{1,2},{2,3},{3,0},{4,5},{5,6},{6,7},{7,4},{8,9},{9,10},{10,1... | collective-permute-start | bytes 2359304 | tf_op jit(solution)/shard_map/ppermute | solution.py:47
  107.2 7.8 %collective-permute-start.19 = (f32[24,1024]{1,0:T(8,128)S(1)}, f32[24,1024]{1,0:T(8,128)S(1)}, u32[]{:S(2)}, u32[]{:S(2)}) collective-permute-start(f32[24,1024]{1,0:T(8,128)S(1)} %get-tuple-element.181), channel_id=1, source_target_pairs={{0,32},{16,48},{32,64},{48,80},{64,96},{80,112},{96,0},{112,16},{1... | collective-permute-start | bytes 294920 | tf_op jit(solution)/shard_map/ppermute | solution.py:47
  109.2 7.5 %collective-permute-start.20 = (f32[24,1024]{1,0:T(8,128)S(1)}, f32[24,1024]{1,0:T(8,128)S(1)}, u32[]{:S(2)}, u32[]{:S(2)}) collective-permute-start(f32[24,1024]{1,0:T(8,128)S(1)} %get-tuple-element.182), channel_id=1, source_target_pairs={{0,64},{16,80},{32,96},{48,112},{64,0},{80,16},{96,32},{112,48},{1... | collective-permute-start | bytes 294920 | tf_op jit(solution)/shard_map/ppermute | solution.py:47
  112.7 4.6 %collective-permute-start.21 = (f32[24,1024]{1,0:T(8,128)S(1)}, f32[24,1024]{1,0:T(8,128)S(1)}, u32[]{:S(2)}, u32[]{:S(2)}) collective-permute-start(f32[24,1024]{1,0:T(8,128)S(1)} %get-tuple-element.183), channel_id=1, source_target_pairs={{0,96},{16,112},{32,0},{48,16},{64,32},{80,48},{96,64},{112,80},{1... | collective-permute-start | bytes 294920 | tf_op jit(solution)/shard_map/ppermute | solution.py:47
  118.0 7.5 %collective-permute-start.22 = (f32[40,384]{1,0:T(8,128)S(1)}, f32[40,384]{1,0:T(8,128)S(1)}, u32[]{:S(2)}, u32[]{:S(2)}) collective-permute-start(f32[40,384]{1,0:T(8,128)S(1)} %get-tuple-element.185), channel_id=1, source_target_pairs={{0,1},{1,2},{2,3},{3,0},{4,5},{5,6},{6,7},{7,4},{8,9},{9,10},{10,1... | collective-permute-start | bytes 184328 | tf_op jit(solution)/shard_map/ppermute | solution.py:47
  118.4 7.1 %collective-permute-start.23 = (f32[40,384]{1,0:T(8,128)S(1)}, f32[40,384]{1,0:T(8,128)S(1)}, u32[]{:S(2)}, u32[]{:S(2)}) collective-permute-start(f32[40,384]{1,0:T(8,128)S(1)} %get-tuple-element.186), channel_id=1, source_target_pairs={{0,2},{1,3},{2,0},{3,1},{4,6},{5,7},{6,4},{7,5},{8,10},{9,11},{10,... | collective-permute-start | bytes 184328 | tf_op jit(solution)/shard_map/ppermute | solution.py:47
  120.7 5.4 %collective-permute-start.24 = (f32[40,384]{1,0:T(8,128)S(1)}, f32[40,384]{1,0:T(8,128)S(1)}, u32[]{:S(2)}, u32[]{:S(2)}) collective-permute-start(f32[40,384]{1,0:T(8,128)S(1)} %get-tuple-element.187), channel_id=1, source_target_pairs={{0,3},{1,0},{2,1},{3,2},{4,7},{5,4},{6,5},{7,6},{8,11},{9,8},{10,9... | collective-permute-start | bytes 184328 | tf_op jit(solution)/shard_map/ppermute | solution.py:47
  126.8 5.2 %collective-permute-start.28 = (f32[8,128]{1,0:T(8,128)S(1)}, f32[8,128]{1,0:T(8,128)S(1)}, u32[]{:S(2)}, u32[]{:S(2)}) collective-permute-start(f32[8,128]{1,0:T(8,128)S(1)} %shard_map.107), channel_id=1, source_target_pairs={{0,8},{1,9},{2,10},{3,11},{4,12},{5,13},{6,14},{7,15},{8,0},{9,1},... | collective-permute-start | bytes 12296 | tf_op jit(solution)/shard_map/ppermute | solution.py:47
  128.6 4.8 %collective-permute-start.26 = (f32[8,128]{1,0:T(8,128)S(1)}, f32[8,128]{1,0:T(8,128)S(1)}, u32[]{:S(2)}, u32[]{:S(2)}) collective-permute-start(f32[8,128]{1,0:T(8,128)S(1)} %shard_map.107), channel_id=1, source_target_pairs={{0,4},{1,5},{2,6},{3,7},{4,8},{5,9},{6,10},{7,11},{8,12},{9,13},{1... | collective-permute-start | bytes 12296 | tf_op jit(solution)/shard_map/ppermute | solution.py:47
  130.6 3.6 %collective-permute-start.27 = (f32[8,128]{1,0:T(8,128)S(1)}, f32[8,128]{1,0:T(8,128)S(1)}, u32[]{:S(2)}, u32[]{:S(2)}) collective-permute-start(f32[8,128]{1,0:T(8,128)S(1)} %shard_map.107), channel_id=1, source_target_pairs={{0,12},{1,13},{2,14},{3,15},{4,0},{5,1},{6,2},{7,3},{8,4},{9,5},{1... | collective-permute-start | bytes 12296 | tf_op jit(solution)/shard_map/ppermute | solution.py:47
  134.2 5.9 %collective-permute-start.31 = (f32[8,128]{1,0:T(8,128)S(1)}, f32[8,128]{1,0:T(8,128)S(1)}, u32[]{:S(2)}, u32[]{:S(2)}) collective-permute-start(f32[8,128]{1,0:T(8,128)S(1)} %add_add_fusion.1), channel_id=1, source_target_pairs={{0,64},{16,80},{32,96},{48,112},{64,0},{80,16},{96,32},{112,48},{1... | collective-permute-start | bytes 12296 | tf_op jit(solution)/shard_map/ppermute | solution.py:47
  136.8 10.3 %collective-permute-start.29 = (f32[8,128]{1,0:T(8,128)S(1)}, f32[8,128]{1,0:T(8,128)S(1)}, u32[]{:S(2)}, u32[]{:S(2)}) collective-permute-start(f32[8,128]{1,0:T(8,128)S(1)} %add_add_fusion.1), channel_id=1, source_target_pairs={{0,32},{16,48},{32,64},{48,80},{64,96},{80,112},{96,0},{112,16},{1... | collective-permute-start | bytes 12296 | tf_op jit(solution)/shard_map/ppermute | solution.py:47
  137.8 9.3 %collective-permute-start.30 = (f32[8,128]{1,0:T(8,128)S(1)}, f32[8,128]{1,0:T(8,128)S(1)}, u32[]{:S(2)}, u32[]{:S(2)}) collective-permute-start(f32[8,128]{1,0:T(8,128)S(1)} %add_add_fusion.1), channel_id=1, source_target_pairs={{0,96},{16,112},{32,0},{48,16},{64,32},{80,48},{96,64},{112,80},{1... | collective-permute-start | bytes 12296 | tf_op jit(solution)/shard_map/ppermute | solution.py:47
  140.0 10.1 %collective-permute-start.25 = (f32[24,384]{1,0:T(8,128)S(1)}, f32[24,384]{1,0:T(8,128)S(1)}, u32[]{:S(2)}, u32[]{:S(2)}) collective-permute-start(f32[24,384]{1,0:T(8,128)S(1)} %get-tuple-element.188), channel_id=1, source_target_pairs={{0,0},{1,32},{2,64},{3,96},{4,1},{5,33},{6,65},{7,97},{8,2},{9,34}... | collective-permute-start | bytes 110600 | tf_op jit(solution)/shard_map/ppermute | solution.py:523
  147.1 1.2 collective-permute-start.32

commit v8 on v6

--- a/solution.py
+++ b/solution.py
@@ -254,7 +254,11 @@
 
 
 def blocks():
-    return [(j, j // 4 % 2, (4 * (j % 4) + j // 8) * 24) for j in range(2 * NZ * NY)]
+    rows = []
+    for j in range(2 * NZ * NY):
+        z, c, y = j // 8, j // 4 % 2, j % 4
+        rows.append((j, c, 24 * (4 * y + z if c == 0 else 4 * z + y)))
+    return rows
 
 
 def inner_kernel(
@@ -422,18 +426,30 @@
 
 
 def deal(at, which, terms, rows, cols):
-    axis = {2: "y", 3: "z"}[which]
     p0, p1, p2, p3 = call(
         functools.partial(deal_kernel, which), [((rows, cols), F32)] * 4, [((4, rows, cols), F32)], [at, *terms]
     )
-    r_2 = move(p2, axis, 2)
-    return [p0, move(p1, axis, 1), r_2, move(p3, axis, 3)]
+
+    def send(value, step):
+        lanes, pairs = NX * NY, []
+        for r in range(2 * NZ):
+            for i in range(lanes):
+                if (r % 2 == 0) == (which == 4):
+                    to = r * lanes + (i + step * NX) % lanes
+                else:
+                    to = (r + 2 * step) % (2 * NZ) * lanes + i
+                pairs.append((r * lanes + i, to))
+        return lax.ppermute(value, ("rec", "seq"), pairs)
+
+    r_2 = send(p2, 2)
+    return [p0, send(p1, 1), r_2, send(p3, 3)]
 
 
 def body(tokens, cotangent, log_decay, w_in, w_bc, w_out):
     seq, rec = lax.axis_index("seq"), lax.axis_index("rec")
     x = seq % NX
-    at = jnp.stack([x, rec % 2, seq // NX, rec // 2]).astype(jnp.int32)
+    core, y, z = rec % 2, seq // NX, rec // 2
+    at = jnp.stack([x, core, y, z, jnp.where(core == 0, y, z), jnp.where(core == 0, z, y)]).astype(jnp.int32)
     tie = lax.optimization_barrier
 
     (t0,) = pl.pallas_call(
@@ -510,7 +526,7 @@
         2 * 1024 * (WIDE * DM + 4 * NS * HC),
     )
     got = move(send, "c", 1)
-    terms = deal(at, 2, [keep, got], 96, ALL)
+    terms = deal(at, 4, [keep, got], 96, ALL)
     whole, half = ((SEG, DM), F32), ((HALF, DM), F32)
     d0, d1, d2a, d2b, d3 = call(
         tokens_kernel, [whole, whole, half, half, whole], [], [at, dz, wi, w_bc], 2 * 1024 * WIDE * DM
@@ -519,7 +535,7 @@
     s1, s3 = call(pass_kernel, [whole, whole], [], [at, d1, d3, r_a, r_b])
     m1, m3 = move(s1, "x", 1), move(s3, "x", -1)
     d_tok = (d0 + m1 + m3).astype(BF16)
-    terms = deal(at, 3, terms, 24, ALL)
+    terms = deal(at, 5, terms, 24, ALL)
     p0, p1, p2, p3, rows_out = call(
         cut_kernel, [((40, HC), F32)] * 4 + [((24, HC), F32)], [], [at, *terms]
     )

time: 151 us -> 147 us (0.974); the launches traced: 151 us -> 145 us
  waiting for transfers between devices: 55.8 us -> 46.4 us
  starting transfers between devices: 52.2 us -> 55.5 us
    ppermute x33 -> x27, waiting for transfers between devices: 51.7 us -> 40.5 us  [move(): return lax.ppermute(value, name, pairs)]
    ppermute x0 -> x6, starting transfers between devices: none -> 11 us  [send(): return lax.ppermute(value, ('rec', 'seq'), pairs)]
    ppermute x33 -> x27, starting transfers between devices: 48.1 us -> 38.2 us  [move(): return lax.ppermute(value, name, pairs)]
    ppermute x0 -> x6, waiting for transfers between devices: none -> 3.82 us  [send(): return lax.ppermute(value, ('rec', 'seq'), pairs)]
    ppermute x1, starting transfers between devices: 4.08 us -> 6.32 us  [body(): rows_out = lax.ppermute(rows_out, ('rec', 'seq'), pairs)]
    ppermute x1, waiting for transfers between devices: 4.09 us -> 2.08 us  [body(): rows_out = lax.ppermute(rows_out, ('rec', 'seq'), pairs)]
  transfers between devices with their start and end apart: 34 -> 34, of which waited for: 20 -> 18; matrix products, arithmetic and copies ran while one was open for 3% -> 3% of each run, Pallas kernels for 20% -> 21%
where the time goes in v8:
time: 147 us; the launch traced here: 145 us
  starting transfers between devices  55.5 us (38%)
  waiting for transfers between devices  46.4 us (32%)
  Pallas kernels  34.9 us (24%)
  local copies, waits for them, and re-layouts  4.16 us (3%)
  other arithmetic  2.84 us (2%)
    ppermute x27, waiting for transfers between devices, move(): return lax.ppermute(value, name, pairs)  40.5 us
    ppermute x27, starting transfers between devices, move(): return lax.ppermute(value, name, pairs)  38.2 us
    pallas_call x15, Pallas kernels, call(): pl.pallas_call(kernel, out_shape=[jax.ShapeDtypeStruct(*o) for o in outs]...  34.9 us
    ppermute x6, starting transfers between devices, send(): return lax.ppermute(value, ('rec', 'seq'), pairs)  11 us
    ppermute x1, starting transfers between devices, body(): rows_out = lax.ppermute(rows_out, ('rec', 'seq'), pairs)  6.32 us
    ppermute x6, waiting for transfers between devices, send(): return lax.ppermute(value, ('rec', 'seq'), pairs)  3.82 us
  transfers between devices with their start and end apart: 34, of which 18 were waited for; matrix products, arithmetic and copies ran while one was open for 3% of the time, Pallas kernels for 21%

profile of v8, /device:TPU:6, one launch (start us, length us, event | category | flops | bytes accessed | tf_op | source)
XLA Modules:
  0.0 144.8 jit_solution(14307440778825661610)
XLA Ops:
  0.7 1.1 copy-done.4
  1.8 0.7 copy-done.6
  2.6 0.5 collective-permute-start
  3.1 1.6 %collective-permute-start.2 = (f32[264,768]{1,0:T(8,128)S(1)}, f32[264,768]{1,0:T(8,128)S(1)}, u32[]{:S(2)}, u32[]{:S(2)}) collective-permute-start(f32[264,768]{1,0:T(8,128)S(1)} %shard_map.93), channel_id=1, source_target_pairs={{0,3},{1,0},{2,1},{3,2},{4,7},{5,4},{6,5},{7,6},{8,11},{9,8},{10,9... | collective-permute-start | bytes 2433032 | tf_op jit(solution)/shard_map/ppermute | solution.py:48
  4.7 1.9 %bitcast_convert_fusion = f32[256,768]{1,0:T(8,128)} fusion(bf16[1,256,768]{2,1,0:T(8,128)(2,1)} %param.7), kind=kLoop, calls=%fused_computation.6 | loop fusion | flops 196608 | bytes 1179648 | tf_op jit(solution)/shard_map/convert_element_type | solution.py:462
  6.6 16.0 %collective-permute-done.t3 = f32[264,768]{1,0:T(8,128)} collective-permute-done((f32[264,768]{1,0:T(8,128)S(1)}, f32[264,768]{1,0:T(8,128)}, u32[]{:S(2)}, u32[]{:S(2)}) %collective-permute-start) | collective-permute-done | bytes 811040 | tf_op jit(solution)/shard_map/ppermute | solution.py:48
  22.6 1.5 %collective-permute-start.1 = (f32[264,768]{1,0:T(8,128)}, f32[264,768]{1,0:T(8,128)S(1)}, u32[]{:S(2)}, u32[]{:S(2)}) collective-permute-start(f32[264,768]{1,0:T(8,128)} %collective-permute-done.t3), channel_id=1, source_target_pairs={{0,1},{1,2},{2,3},{3,0},{4,5},{5,6},{6,7},{7,4},{8,9},{9,10},{10,1... | collective-permute-start | bytes 2433032 | tf_op jit(solution)/shard_map/ppermute | solution.py:48
  24.1 0.9 copy-done.8
  25.0 0.5 collective-permute-start.3
  25.7 1.2 constant_dynamic-slice_fusion.w_out
  26.9 2.8 %collective-permute-start.4 = (f32[256,768]{1,0:T(8,128)}, f32[256,768]{1,0:T(8,128)S(1)}, u32[]{:S(2)}, u32[]{:S(2)}) collective-permute-start(f32[256,768]{1,0:T(8,128)} %bitcast_convert_fusion), channel_id=1, source_target_pairs={{0,1},{1,2},{2,3},{3,0},{4,5},{5,6},{6,7},{7,4},{8,9},{9,10},{10,1... | collective-permute-start | bytes 2359304 | tf_op jit(solution)/shard_map/ppermute | solution.py:48
  29.7 6.6 %shard_map.94 = (f32[3,8,256]{2,1,0:T(8,128)S(1)}, f32[3,8,256]{2,1,0:T(8,128)S(1)}, f32[3,256,384]{2,1,0:T(8,128)S(1)}, f32[3,256,384]{2,1,0:T(8,128)S(1)}, bf1...) custom-call(s32[6]{0:T(128)S(1)} %stack.27.at, ...), custom_call_target="tpu_custom_call" | custom-call | flops 905969664 | bytes 3022872 | tf_op jit(solution)/shard_map/pallas_call | solution.py:412
  36.3 3.5 %shard_map.95 = (bf16[3,6,256,256]{3,2,1,0:T(8,128)(2,1)S(1)}, bf16[3,6,256,256]{3,2,1,0:T(8,128)(2,1)S(1)}, f32[3,256,384]{2,1,0:T(8,128)S(1)}) custom-call(s32[6]{0:T(128)S(1)} %stack.27.at, f32[3,8,256]{2,1,0:T(8,128)S(1)} %get-tuple-element.118.cirow.refs_0_, f32[3,8,256]{2,1,0:T(8,128)S(1)} %get-tuple-element.119.cerow.refs_1_, ...), custom_call_target="tpu_custom_call" | custom-call | flops 301989888 | bytes 3391512 | tf_op jit(solution)/shard_map/pallas_call | solution.py:412
  39.8 4.7 %collective-permute-done.3.c1 = f32[256,768]{1,0:T(8,128)} collective-permute-done((f32[256,768]{1,0:T(8,128)}, f32[256,768]{1,0:T(8,128)}, u32[]{:S(2)}, u32[]{:S(2)}) %collective-permute-start.3) | collective-permute-done | bytes 786464 | tf_op jit(solution)/shard_map/ppermute | solution.py:48
  44.6 2.9 %shard_map.96 = (f32[4,8,256]{2,1,0:T(8,128)S(1)}, f32[4,8,256]{2,1,0:T(8,128)S(1)}, f32[4,256,384]{2,1,0:T(8,128)S(1)}, f32[4,256,384]{2,1,0:T(8,128)S(1)}, bf1...) custom-call(s32[6]{0:T(128)S(1)} %stack.27.at, ...), custom_call_target="tpu_custom_call" | custom-call | flops 301989888 | bytes 8724504 | tf_op jit(solution)/shard_map/pallas_call | solution.py:412
  47.5 1.8 %collective-permute-start.9 = (f32[136,384]{1,0:T(8,128)S(1)}, f32[136,384]{1,0:T(8,128)S(1)}, u32[]{:S(2)}, u32[]{:S(2)}) collective-permute-start(f32[136,384]{1,0:T(8,128)S(1)} %get-tuple-element.155), channel_id=1, source_target_pairs={{0,4},{1,5},{2,6},{3,7},{4,8},{5,9},{6,10},{7,11},{8,12},{9,13},{1... | collective-permute-start | bytes 626696 | tf_op jit(solution)/shard_map/ppermute | solution.py:48
  49.4 1.5 %collective-permute-start.10 = (f32[136,384]{1,0:T(8,128)S(1)}, f32[136,384]{1,0:T(8,128)S(1)}, u32[]{:S(2)}, u32[]{:S(2)}) collective-permute-start(f32[136,384]{1,0:T(8,128)S(1)} %get-tuple-element.156), channel_id=1, source_target_pairs={{0,12},{1,13},{2,14},{3,15},{4,0},{5,1},{6,2},{7,3},{8,4},{9,5},{1... | collective-permute-start | bytes 626696 | tf_op jit(solution)/shard_map/ppermute | solution.py:48
  50.9 2.1 %collective-permute-start.11 = (f32[136,384]{1,0:T(8,128)S(1)}, f32[136,384]{1,0:T(8,128)S(1)}, u32[]{:S(2)}, u32[]{:S(2)}) collective-permute-start(f32[136,384]{1,0:T(8,128)S(1)} %get-tuple-element.157), channel_id=1, source_target_pairs={{0,8},{1,9},{2,10},{3,11},{4,12},{5,13},{6,14},{7,15},{8,0},{9,1},... | collective-permute-start | bytes 626696 | tf_op jit(solution)/shard_map/ppermute | solution.py:48
  53.0 1.5 %shard_map.98 = (bf16[1,6,256,256]{3,2,1,0:T(8,128)(2,1)S(1)}, bf16[1,6,256,256]{3,2,1,0:T(8,128)(2,1)S(1)}, f32[1,256,384]{2,1,0:T(8,128)S(1)}) custom-call(s32[6]{0:T(128)S(1)} %stack.27.at, f32[4,8,256]{2,1,0:T(8,128)S(1)} %get-tuple-element.135.cirow, f32[4,8,256]{2,1,0:T(8,128)S(1)} %get-tuple-element.136.cerow, ...), custom_call_target="tpu_custom_call" | custom-call | flops 100663296 | bytes 4522008 | tf_op jit(solution)/shard_map/pallas_call | solution.py:412
  54.6 2.5 %shard_map.97 = (bf16[2,256,768]{2,1,0:T(8,128)(2,1)S(1)}, bf16[2,256,384]{2,1,0:T(8,128)(2,1)S(1)}, bf16[2,256,768]{2,1,0:T(8,128)(2,1)S(1)}, f32[2,128,768]{2,1,0:T(8,128)S(1)}) custom-call(s32[6]{0:T(128)S(1)} %stack.27.at, bf16[256,768]{1,0:T(8,128)(2,1)S(1)} %bitcast.12, f32[256,768]{1,0:T(8,128)} %collective-permute-done.3.c1, ...), custom_call_target="tpu_custom_call" | custom-call | flops 402653184 | bytes 5439512 | tf_op jit(solution)/shard_map/pallas_call | solution.py:412
  57.1 1.5 %collective-permute-done.4.c2 = f32[256,768]{1,0:T(8,128)S(1)} collective-permute-done((f32[256,768]{1,0:T(8,128)}, f32[256,768]{1,0:T(8,128)S(1)}, u32[]{:S(2)}, u32[]{:S(2)}) %collective-permute-start.4) | collective-permute-done | bytes 786464 | tf_op jit(solution)/shard_map/ppermute | solution.py:48
  58.6 4.4 %collective-permute-done.5.c3 = f32[256,768]{1,0:T(8,128)S(1)} collective-permute-done((f32[256,768]{1,0:T(8,128)}, f32[256,768]{1,0:T(8,128)S(1)}, u32[]{:S(2)}, u32[]{:S(2)}) %collective-permute-start.5) | collective-permute-done | bytes 786464 | tf_op jit(solution)/shard_map/ppermute | solution.py:48
  63.0 2.1 %shard_map.99 = (bf16[2,256,768]{2,1,0:T(8,128)(2,1)S(1)}, bf16[2,256,384]{2,1,0:T(8,128)(2,1)S(1)}, bf16[2,256,768]{2,1,0:T(8,128)(2,1)S(1)}, f32[2,4,128,384]{...) custom-call(s32[6]{0:T(128)S(1)} %stack.27.at, ...), custom_call_target="tpu_custom_call" | custom-call | flops 402653184 | bytes 6619160 | tf_op jit(solution)/shard_map/pallas_call | solution.py:412
  65.1 2.1 %collective-permute-start.6 = (f32[136,384]{1,0:T(8,128)S(1)}, f32[136,384]{1,0:T(8,128)S(1)}, u32[]{:S(2)}, u32[]{:S(2)}) collective-permute-start(f32[136,384]{1,0:T(8,128)S(1)} %get-tuple-element.145), channel_id=1, source_target_pairs={{0,4},{1,5},{2,6},{3,7},{4,8},{5,9},{6,10},{7,11},{8,12},{9,13},{1... | collective-permute-start | bytes 626696 | tf_op jit(solution)/shard_map/ppermute | solution.py:48
  67.2 1.7 %collective-permute-start.7 = (f32[136,384]{1,0:T(8,128)S(1)}, f32[136,384]{1,0:T(8,128)S(1)}, u32[]{:S(2)}, u32[]{:S(2)}) collective-permute-start(f32[136,384]{1,0:T(8,128)S(1)} %get-tuple-element.146), channel_id=1, source_target_pairs={{0,12},{1,13},{2,14},{3,15},{4,0},{5,1},{6,2},{7,3},{8,4},{9,5},{1... | collective-permute-start | bytes 626696 | tf_op jit(solution)/shard_map/ppermute | solution.py:48
  68.9 1.9 %collective-permute-start.8 = (f32[136,384]{1,0:T(8,128)S(1)}, f32[136,384]{1,0:T(8,128)S(1)}, u32[]{:S(2)}, u32[]{:S(2)}) collective-permute-start(f32[136,384]{1,0:T(8,128)S(1)} %get-tuple-element.147), channel_id=1, source_target_pairs={{0,8},{1,9},{2,10},{3,11},{4,12},{5,13},{6,14},{7,15},{8,0},{9,1},... | collective-permute-start | bytes 626696 | tf_op jit(solution)/shard_map/ppermute | solution.py:48
  70.9 5.1 %shard_map.100 = (f32[2,384,384]{2,1,0:T(8,128)S(1)}, f32[4,256,384]{2,1,0:T(8,128)S(1)}, f32[4,256,128]{2,1,0:T(8,128)S(1)}, f32[4,256,128]{2,1,0:T(8,128)S(1)}) custom-call(s32[6]{0:T(128)S(1)} %stack.27.at, bf16[4,256,384]{2,1,0:T(8,128)(2,1)S(1)} %get-tuple-element.137.xs, bf16[4,256,256]{2,1,0:T(8,128)(2,1)S(1)} %get-tuple-element.129.bc, ...), custom_call_target="tpu_custom_call" | custom-call | flops 2214592512 | bytes 18452504 | tf_op jit(solution)/shard_map/pallas_call | solution.py:412
  76.0 0.5 collective-permute-done.8.r_2
  76.5 4.0 %shard_map.101 = (f32[384,1024]{1,0:T(8,128)S(1)}, f32[384,1024]{1,0:T(8,128)S(1)}, bf16[4,256,640]{2,1,0:T(8,128)(2,1)S(1)}) custom-call(s32[6]{0:T(128)S(1)} %stack.27.at, bf16[4,256,768]{2,1,0:T(8,128)(2,1)S(1)} %get-tuple-element.127.tokb, bf16[4,256,768]{2,1,0:T(8,128)(2,1)S(1)} %get-tuple-element.128.xfr, ...), custom_call_target="tpu_custom_call" | custom-call | flops 1409286144 | bytes 12816408 | tf_op jit(solution)/shard_map/pallas_call | solution.py:412
  80.6 1.9 %shard_map.102 = (f32[256,768]{1,0:T(8,128)S(1)}, f32[256,768]{1,0:T(8,128)S(1)}, f32[128,768]{1,0:T(8,128)S(1)}, f32[128,768]{1,0:T(8,128)S(1)}, f32[256,768]{1,0:T(8,128)S(1)}) custom-call(s32[6]{0:T(128)S(1)} %stack.27.at, bf16[4,256,640]{2,1,0:T(8,128)(2,1)S(1)} %get-tuple-element.168.dz, bf16[768,384]{1,0:T(8,128)(2,1)S(1)} %constant_dynamic-slice_fusion.1.w_in, ...), custom_call_target="tpu_custom_call" | custom-call | flops 1006632960 | bytes 2293784 | tf_op jit(solution)/shard_map/pallas_call | solution.py:412
  82.6 2.0 %collective-permute-start.13 = (f32[128,768]{1,0:T(8,128)S(1)}, f32[128,768]{1,0:T(8,128)S(1)}, u32[]{:S(2)}, u32[]{:S(2)}) collective-permute-start(f32[128,768]{1,0:T(8,128)S(1)} %get-tuple-element.173), channel_id=1, source_target_pairs={{0,3},{1,0},{2,1},{3,2},{4,7},{5,4},{6,5},{7,6},{8,11},{9,8},{10,9... | collective-permute-start | bytes 1179656 | tf_op jit(solution)/shard_map/ppermute | solution.py:48
  84.6 0.8 shard_map.104
  85.4 1.2 collective-permute-start.17
  86.6 2.4 %collective-permute-start.18 = (f32[96,1024]{1,0:T(8,128)S(1)}, f32[96,1024]{1,0:T(8,128)S(1)}, u32[]{:S(2)}, u32[]{:S(2)}) collective-permute-start(f32[96,1024]{1,0:T(8,128)S(1)} %get-tuple-element.180), channel_id=1, source_target_pairs={{0,8},{1,9},{2,10},{3,11},{4,12},{5,13},{6,14},{7,15},{8,0},{9,1},... | collective-permute-start | bytes 1179656 | tf_op jit(solution)/shard_map/ppermute | solution.py:442
  89.0 0.8 collective-permute-start.19
  89.8 4.3 %collective-permute-done.12.r_a = f32[128,768]{1,0:T(8,128)S(1)} collective-permute-done((f32[128,768]{1,0:T(8,128)S(1)}, f32[128,768]{1,0:T(8,128)S(1)}, u32[]{:S(2)}, u32[]{:S(2)}) %collective-permute-start.12) | collective-permute-done | bytes 393248 | tf_op jit(solution)/shard_map/ppermute | solution.py:48
  94.1 1.3 collective-permute-done.13.r_b
  95.4 0.7 shard_map.103
  96.1 0.5 collective-permute-start.15
  96.6 2.8 %collective-permute-start.14 = (f32[256,768]{1,0:T(8,128)S(1)}, f32[256,768]{1,0:T(8,128)S(1)}, u32[]{:S(2)}, u32[]{:S(2)}) collective-permute-start(f32[256,768]{1,0:T(8,128)S(1)} %get-tuple-element.174), channel_id=1, source_target_pairs={{0,1},{1,2},{2,3},{3,0},{4,5},{5,6},{6,7},{7,4},{8,9},{9,10},{10,1... | collective-permute-start | bytes 2359304 | tf_op jit(solution)/shard_map/ppermute | solution.py:48
  99.6 0.7 shard_map.105
  100.3 2.0 %collective-permute-start.20 = (f32[24,1024]{1,0:T(8,128)S(1)}, f32[24,1024]{1,0:T(8,128)S(1)}, u32[]{:S(2)}, u32[]{:S(2)}) collective-permute-start(f32[24,1024]{1,0:T(8,128)S(1)} %get-tuple-element.183), channel_id=1, source_target_pairs={{0,32},{1,33},{2,34},{3,35},{4,36},{5,37},{6,38},{7,39},{8,40},{9,... | collective-permute-start | bytes 294920 | tf_op jit(solution)/shard_map/ppermute | solution.py:442
  102.3 3.6 %collective-permute-start.21 = (f32[24,1024]{1,0:T(8,128)S(1)}, f32[24,1024]{1,0:T(8,128)S(1)}, u32[]{:S(2)}, u32[]{:S(2)}) collective-permute-start(f32[24,1024]{1,0:T(8,128)S(1)} %get-tuple-element.184), channel_id=1, source_target_pairs={{0,64},{1,65},{2,66},{3,67},{4,68},{5,69},{6,70},{7,71},{8,72},{9,... | collective-permute-start | bytes 294920 | tf_op jit(solution)/shard_map/ppermute | solution.py:442
  105.9 1.0 collective-permute-start.22
  107.0 2.5 %collective-permute-done.21.c = f32[24,1024]{1,0:T(8,128)S(1)} collective-permute-done((f32[24,1024]{1,0:T(8,128)S(1)}, f32[24,1024]{1,0:T(8,128)S(1)}, u32[]{:S(2)}, u32[]{:S(2)}) %collective-permute-start.21) | collective-permute-done | bytes 98336 | tf_op jit(solution)/shard_map/ppermute | solution.py:442
  109.5 1.0 collective-permute-done.22.d
  110.5 0.7 shard_map.106
  111.2 1.4 collective-permute-start.23
  112.5 0.8 collective-permute-start.24
  113.5 4.9 %collective-permute-done.23.b = f32[40,384]{1,0:T(8,128)S(1)} collective-permute-done((f32[40,384]{1,0:T(8,128)S(1)}, f32[40,384]{1,0:T(8,128)S(1)}, u32[]{:S(2)}, u32[]{:S(2)}) %collective-permute-start.23) | collective-permute-done | bytes 61472 | tf_op jit(solution)/shard_map/ppermute | solution.py:48
  118.4 0.7 collective-permute-done.25.d
  119.2 0.7 shard_map.107
  119.8 2.0 %collective-permute-start.29 = (f32[8,128]{1,0:T(8,128)S(1)}, f32[8,128]{1,0:T(8,128)S(1)}, u32[]{:S(2)}, u32[]{:S(2)}) collective-permute-start(f32[8,128]{1,0:T(8,128)S(1)} %shard_map.107), channel_id=1, source_target_pairs={{0,8},{1,9},{2,10},{3,11},{4,12},{5,13},{6,14},{7,15},{8,0},{9,1},... | collective-permute-start | bytes 12296 | tf_op jit(solution)/shard_map/ppermute | solution.py:48
  121.8 1.6 %collective-permute-start.27 = (f32[8,128]{1,0:T(8,128)S(1)}, f32[8,128]{1,0:T(8,128)S(1)}, u32[]{:S(2)}, u32[]{:S(2)}) collective-permute-start(f32[8,128]{1,0:T(8,128)S(1)} %shard_map.107), channel_id=1, source_target_pairs={{0,4},{1,5},{2,6},{3,7},{4,8},{5,9},{6,10},{7,11},{8,12},{9,13},{1... | collective-permute-start | bytes 12296 | tf_op jit(solution)/shard_map/ppermute | solution.py:48
  123.4 1.7 %collective-permute-start.28 = (f32[8,128]{1,0:T(8,128)S(1)}, f32[8,128]{1,0:T(8,128)S(1)}, u32[]{:S(2)}, u32[]{:S(2)}) collective-permute-start(f32[8,128]{1,0:T(8,128)S(1)} %shard_map.107), channel_id=1, source_target_pairs={{0,12},{1,13},{2,14},{3,15},{4,0},{5,1},{6,2},{7,3},{8,4},{9,5},{1... | collective-permute-start | bytes 12296 | tf_op jit(solution)/shard_map/ppermute | solution.py:48
  125.2 1.4 collective-permute-done.27
  126.6 0.3 collective-permute-done.28
  127.0 3.6 %collective-permute-start.32 = (f32[8,128]{1,0:T(8,128)S(1)}, f32[8,128]{1,0:T(8,128)S(1)}, u32[]{:S(2)}, u32[]{:S(2)}) collective-permute-start(f32[8,128]{1,0:T(8,128)S(1)} %add_add_fusion.1), channel_id=1, source_target_pairs={{0,64},{16,80},{32,96},{48,112},{64,0},{80,16},{96,32},{112,48},{1... | collective-permute-start | bytes 12296 | tf_op jit(solution)/shard_map/ppermute | solution.py:48
  130.6 1.0 collective-permute-start.30
  131.6 2.2 %collective-permute-start.31 = (f32[8,128]{1,0:T(8,128)S(1)}, f32[8,128]{1,0:T(8,128)S(1)}, u32[]{:S(2)}, u32[]{:S(2)}) collective-permute-start(f32[8,128]{1,0:T(8,128)S(1)} %add_add_fusion.1), channel_id=1, source_target_pairs={{0,96},{16,112},{32,0},{48,16},{64,32},{80,48},{96,64},{112,80},{1... | collective-permute-start | bytes 12296 | tf_op jit(solution)/shard_map/ppermute | solution.py:48
  133.8 6.3 %collective-permute-start.26 = (f32[24,384]{1,0:T(8,128)S(1)}, f32[24,384]{1,0:T(8,128)S(1)}, u32[]{:S(2)}, u32[]{:S(2)}) collective-permute-start(f32[24,384]{1,0:T(8,128)S(1)} %get-tuple-element.190), channel_id=1, source_target_pairs={{0,0},{1,32},{2,64},{3,96},{4,1},{5,33},{6,65},{7,97},{8,2},{9,34}... | collective-permute-start | bytes 110600 | tf_op jit(solution)/shard_map/ppermute | solution.py:545
  140.4 0.9 fusion
  141.5 2.1 %collective-permute-done.26.rows_out = f32[24,384]{1,0:T(8,128)S(1)} collective-permute-done((f32[24,384]{1,0:T(8,128)S(1)}, f32[24,384]{1,0:T(8,128)S(1)}, u32[]{:S(2)}, u32[]{:S(2)}) %collective-permute-start.26) | collective-permute-done | bytes 36896 | tf_op jit(solution)/shard_map/ppermute | solution.py:545
  143.5 1.2 shard_map.108
  (48 shorter events, 1.6 us)
Async XLA Ops:
  0.6 25.0 %copy-start = (bf16[768,1536]{1,0:T(8,128)(2,1)S(1)}, bf16[768,1536]{1,0:T(8,128)(2,1)}, u32[]{:S(2)}) copy-start(bf16[768,1536]{1,0:T(8,128)(2,1)} %param.9) | copy-start | bytes 7077892
  0.6 1.1 copy-start.4
  1.8 0.7 copy-start.6
  2.6 27.1 %copy-start.7 = (f32[1,24,256]{2,1,0:T(8,128)S(1)}, f32[1,24,256]{2,1,0:T(8,128)}, u32[]{:S(2)}) copy-start(f32[1,24,256]{2,1,0:T(8,128)} %param.8) | copy-start | bytes 73732
  2.6 20.0 %collective-permute-start = (f32[264,768]{1,0:T(8,128)S(1)}, f32[264,768]{1,0:T(8,128)}, u32[]{:S(2)}, u32[]{:S(2)}) collective-permute-start(f32[264,768]{1,0:T(8,128)S(1)} %shard_map.93), channel_id=1, source_target_pairs={{0,1},{1,2},{2,3},{3,0},{4,5},{5,6},{6,7},{7,4},{8,9},{9,10},{10,1... | collective-permute-start | bytes 2433032 | tf_op jit(solution)/shard_map/ppermute | solution.py:48
  3.1 21.0 %collective-permute-start.2 = (f32[264,768]{1,0:T(8,128)S(1)}, f32[264,768]{1,0:T(8,128)S(1)}, u32[]{:S(2)}, u32[]{:S(2)}) collective-permute-start(f32[264,768]{1,0:T(8,128)S(1)} %shard_map.93), channel_id=1, source_target_pairs={{0,3},{1,0},{2,1},{3,2},{4,7},{5,4},{6,5},{7,6},{8,11},{9,8},{10,9... | collective-permute-start | bytes 2433032 | tf_op jit(solution)/shard_map/ppermute | solution.py:48
  22.6 21.9 %collective-permute-start.1 = (f32[264,768]{1,0:T(8,128)}, f32[264,768]{1,0:T(8,128)S(1)}, u32[]{:S(2)}, u32[]{:S(2)}) collective-permute-start(f32[264,768]{1,0:T(8,128)} %collective-permute-done.t3), channel_id=1, source_target_pairs={{0,1},{1,2},{2,3},{3,0},{4,5},{5,6},{6,7},{7,4},{8,9},{9,10},{10,1... | collective-permute-start | bytes 2433032 | tf_op jit(solution)/shard_map/ppermute | solution.py:48
  24.1 0.9 copy-start.8
  25.0 19.5 %collective-permute-start.3 = (f32[256,768]{1,0:T(8,128)}, f32[256,768]{1,0:T(8,128)}, u32[]{:S(2)}, u32[]{:S(2)}) collective-permute-start(f32[256,768]{1,0:T(8,128)} %bitcast_convert_fusion), channel_id=1, source_target_pairs={{0,3},{1,0},{2,1},{3,2},{4,7},{5,4},{6,5},{7,6},{8,11},{9,8},{10,9... | collective-permute-start | bytes 2359304 | tf_op jit(solution)/shard_map/ppermute | solution.py:48
  25.6 4.1 %copy-start.3 = (bf16[768,256]{1,0:T(8,128)(2,1)S(1)}, bf16[768,256]{1,0:T(8,128)(2,1)}, u32[]{:S(2)}) copy-start(bf16[768,256]{1,0:T(8,128)(2,1)} %w_bc.5) | copy-start | bytes 1179652
  25.6 4.1 %copy-start.5 = (bf16[1,256,768]{2,1,0:T(8,128)(2,1)S(1)}, bf16[1,256,768]{2,1,0:T(8,128)(2,1)}, u32[]{:S(2)}) copy-start(bf16[1,256,768]{2,1,0:T(8,128)(2,1)} %param.6) | copy-start | bytes 1179652
  25.6 4.1 %copy-start.9 = (f32[264,768]{1,0:T(8,128)S(1)}, f32[264,768]{1,0:T(8,128)}, u32[]{:S(2)}) copy-start(f32[264,768]{1,0:T(8,128)} %copy-done.8) | copy-start | bytes 2433028
  26.9 31.7 %collective-permute-start.4 = (f32[256,768]{1,0:T(8,128)}, f32[256,768]{1,0:T(8,128)S(1)}, u32[]{:S(2)}, u32[]{:S(2)}) collective-permute-start(f32[256,768]{1,0:T(8,128)} %bitcast_convert_fusion), channel_id=1, source_target_pairs={{0,1},{1,2},{2,3},{3,0},{4,5},{5,6},{6,7},{7,4},{8,9},{9,10},{10,1... | collective-permute-start | bytes 2359304 | tf_op jit(solution)/shard_map/ppermute | solution.py:48
  44.5 18.5 %collective-permute-start.5 = (f32[256,768]{1,0:T(8,128)}, f32[256,768]{1,0:T(8,128)S(1)}, u32[]{:S(2)}, u32[]{:S(2)}) collective-permute-start(f32[256,768]{1,0:T(8,128)} %collective-permute-done.3.c1), channel_id=1, source_target_pairs={{0,3},{1,0},{2,1},{3,2},{4,7},{5,4},{6,5},{7,6},{8,11},{9,8},{10,9... | collective-permute-start | bytes 2359304 | tf_op jit(solution)/shard_map/ppermute | solution.py:48
  47.5 21.4 %collective-permute-start.9 = (f32[136,384]{1,0:T(8,128)S(1)}, f32[136,384]{1,0:T(8,128)S(1)}, u32[]{:S(2)}, u32[]{:S(2)}) collective-permute-start(f32[136,384]{1,0:T(8,128)S(1)} %get-tuple-element.155), channel_id=1, source_target_pairs={{0,4},{1,5},{2,6},{3,7},{4,8},{5,9},{6,10},{7,11},{8,12},{9,13},{1... | collective-permute-start | bytes 626696 | tf_op jit(solution)/shard_map/ppermute | solution.py:48
  49.4 21.5 %collective-permute-start.10 = (f32[136,384]{1,0:T(8,128)S(1)}, f32[136,384]{1,0:T(8,128)S(1)}, u32[]{:S(2)}, u32[]{:S(2)}) collective-permute-start(f32[136,384]{1,0:T(8,128)S(1)} %get-tuple-element.156), channel_id=1, source_target_pairs={{0,12},{1,13},{2,14},{3,15},{4,0},{5,1},{6,2},{7,3},{8,4},{9,5},{1... | collective-permute-start | bytes 626696 | tf_op jit(solution)/shard_map/ppermute | solution.py:48
  50.9 20.0 %collective-permute-start.11 = (f32[136,384]{1,0:T(8,128)S(1)}, f32[136,384]{1,0:T(8,128)S(1)}, u32[]{:S(2)}, u32[]{:S(2)}) collective-permute-start(f32[136,384]{1,0:T(8,128)S(1)} %get-tuple-element.157), channel_id=1, source_target_pairs={{0,8},{1,9},{2,10},{3,11},{4,12},{5,13},{6,14},{7,15},{8,0},{9,1},... | collective-permute-start | bytes 626696 | tf_op jit(solution)/shard_map/ppermute | solution.py:48
  53.0 1.5 %copy-start.2 = (bf16[1,256,768]{2,1,0:T(8,128)(2,1)S(1)}, bf16[1,256,768]{2,1,0:T(8,128)(2,1)}, u32[]{:S(2)}) copy-start(bf16[1,256,768]{2,1,0:T(8,128)(2,1)} %param.7) | copy-start | bytes 1179652
  65.1 10.8 %collective-permute-start.6 = (f32[136,384]{1,0:T(8,128)S(1)}, f32[136,384]{1,0:T(8,128)S(1)}, u32[]{:S(2)}, u32[]{:S(2)}) collective-permute-start(f32[136,384]{1,0:T(8,128)S(1)} %get-tuple-element.145), channel_id=1, source_target_pairs={{0,4},{1,5},{2,6},{3,7},{4,8},{5,9},{6,10},{7,11},{8,12},{9,13},{1... | collective-permute-start | bytes 626696 | tf_op jit(solution)/shard_map/ppermute | solution.py:48
  67.2 8.8 %collective-permute-start.7 = (f32[136,384]{1,0:T(8,128)S(1)}, f32[136,384]{1,0:T(8,128)S(1)}, u32[]{:S(2)}, u32[]{:S(2)}) collective-permute-start(f32[136,384]{1,0:T(8,128)S(1)} %get-tuple-element.146), channel_id=1, source_target_pairs={{0,12},{1,13},{2,14},{3,15},{4,0},{5,1},{6,2},{7,3},{8,4},{9,5},{1... | collective-permute-start | bytes 626696 | tf_op jit(solution)/shard_map/ppermute | solution.py:48
  68.9 7.6 %collective-permute-start.8 = (f32[136,384]{1,0:T(8,128)S(1)}, f32[136,384]{1,0:T(8,128)S(1)}, u32[]{:S(2)}, u32[]{:S(2)}) collective-permute-start(f32[136,384]{1,0:T(8,128)S(1)} %get-tuple-element.147), channel_id=1, source_target_pairs={{0,8},{1,9},{2,10},{3,11},{4,12},{5,13},{6,14},{7,15},{8,0},{9,1},... | collective-permute-start | bytes 626696 | tf_op jit(solution)/shard_map/ppermute | solution.py:48
  80.5 4.1 %collective-permute-start.16 = (f32[384,1024]{1,0:T(8,128)S(1)}, f32[384,1024]{1,0:T(8,128)S(1)}, u32[]{:S(2)}, u32[]{:S(2)}) collective-permute-start(f32[384,1024]{1,0:T(8,128)S(1)} %get-tuple-element.177), channel_id=1, source_target_pairs={{0,16},{16,0},{32,48},{48,32},{64,80},{80,64},{96,112},{112,96},{1... | collective-permute-start | bytes 4718600 | tf_op jit(solution)/shard_map/ppermute | solution.py:48
  82.5 11.6 %collective-permute-start.12 = (f32[128,768]{1,0:T(8,128)S(1)}, f32[128,768]{1,0:T(8,128)S(1)}, u32[]{:S(2)}, u32[]{:S(2)}) collective-permute-start(f32[128,768]{1,0:T(8,128)S(1)} %get-tuple-element.172), channel_id=1, source_target_pairs={{0,1},{1,2},{2,3},{3,0},{4,5},{5,6},{6,7},{7,4},{8,9},{9,10},{10,1... | collective-permute-start | bytes 1179656 | tf_op jit(solution)/shard_map/ppermute | solution.py:48
  82.6 12.8 %collective-permute-start.13 = (f32[128,768]{1,0:T(8,128)S(1)}, f32[128,768]{1,0:T(8,128)S(1)}, u32[]{:S(2)}, u32[]{:S(2)}) collective-permute-start(f32[128,768]{1,0:T(8,128)S(1)} %get-tuple-element.173), channel_id=1, source_target_pairs={{0,3},{1,0},{2,1},{3,2},{4,7},{5,4},{6,5},{7,6},{8,11},{9,8},{10,9... | collective-permute-start | bytes 1179656 | tf_op jit(solution)/shard_map/ppermute | solution.py:48
  85.4 14.0 %collective-permute-start.17 = (f32[96,1024]{1,0:T(8,128)S(1)}, f32[96,1024]{1,0:T(8,128)S(1)}, u32[]{:S(2)}, u32[]{:S(2)}) collective-permute-start(f32[96,1024]{1,0:T(8,128)S(1)} %get-tuple-element.179), channel_id=1, source_target_pairs={{0,4},{1,5},{2,6},{3,7},{4,8},{5,9},{6,10},{7,11},{8,12},{9,13},{1... | collective-permute-start | bytes 1179656 | tf_op jit(solution)/shard_map/ppermute | solution.py:442
  86.6 12.7 %collective-permute-start.18 = (f32[96,1024]{1,0:T(8,128)S(1)}, f32[96,1024]{1,0:T(8,128)S(1)}, u32[]{:S(2)}, u32[]{:S(2)}) collective-permute-start(f32[96,1024]{1,0:T(8,128)S(1)} %get-tuple-element.180), channel_id=1, source_target_pairs={{0,8},{1,9},{2,10},{3,11},{4,12},{5,13},{6,14},{7,15},{8,0},{9,1},... | collective-permute-start | bytes 1179656 | tf_op jit(solution)/shard_map/ppermute | solution.py:442
  89.0 10.6 %collective-permute-start.19 = (f32[96,1024]{1,0:T(8,128)S(1)}, f32[96,1024]{1,0:T(8,128)S(1)}, u32[]{:S(2)}, u32[]{:S(2)}) collective-permute-start(f32[96,1024]{1,0:T(8,128)S(1)} %get-tuple-element.181), channel_id=1, source_target_pairs={{0,12},{1,13},{2,14},{3,15},{4,0},{5,1},{6,2},{7,3},{8,4},{9,5},{1... | collective-permute-start | bytes 1179656 | tf_op jit(solution)/shard_map/ppermute | solution.py:442
  96.1 44.3 %collective-permute-start.15 = (f32[256,768]{1,0:T(8,128)S(1)}, f32[256,768]{1,0:T(8,128)S(1)}, u32[]{:S(2)}, u32[]{:S(2)}) collective-permute-start(f32[256,768]{1,0:T(8,128)S(1)} %get-tuple-element.175), channel_id=1, source_target_pairs={{0,3},{1,0},{2,1},{3,2},{4,7},{5,4},{6,5},{7,6},{8,11},{9,8},{10,9... | collective-permute-start | bytes 2359304 | tf_op jit(solution)/shard_map/ppermute | solution.py:48
  96.6 43.8 %collective-permute-start.14 = (f32[256,768]{1,0:T(8,128)S(1)}, f32[256,768]{1,0:T(8,128)S(1)}, u32[]{:S(2)}, u32[]{:S(2)}) collective-permute-start(f32[256,768]{1,0:T(8,128)S(1)} %get-tuple-element.174), channel_id=1, source_target_pairs={{0,1},{1,2},{2,3},{3,0},{4,5},{5,6},{6,7},{7,4},{8,9},{9,10},{10,1... | collective-permute-start | bytes 2359304 | tf_op jit(solution)/shard_map/ppermute | solution.py:48
  100.3 6.7 %collective-permute-start.20 = (f32[24,1024]{1,0:T(8,128)S(1)}, f32[24,1024]{1,0:T(8,128)S(1)}, u32[]{:S(2)}, u32[]{:S(2)}) collective-permute-start(f32[24,1024]{1,0:T(8,128)S(1)} %get-tuple-element.183), channel_id=1, source_target_pairs={{0,32},{1,33},{2,34},{3,35},{4,36},{5,37},{6,38},{7,39},{8,40},{9,... | collective-permute-start | bytes 294920 | tf_op jit(solution)/shard_map/ppermute | solution.py:442
  102.3 7.2 %collective-permute-start.21 = (f32[24,1024]{1,0:T(8,128)S(1)}, f32[24,1024]{1,0:T(8,128)S(1)}, u32[]{:S(2)}, u32[]{:S(2)}) collective-permute-start(f32[24,1024]{1,0:T(8,128)S(1)} %get-tuple-element.184), channel_id=1, source_target_pairs={{0,64},{1,65},{2,66},{3,67},{4,68},{5,69},{6,70},{7,71},{8,72},{9,... | collective-permute-start | bytes 294920 | tf_op jit(solution)/shard_map/ppermute | solution.py:442
  105.9 4.6 %collective-permute-start.22 = (f32[24,1024]{1,0:T(8,128)S(1)}, f32[24,1024]{1,0:T(8,128)S(1)}, u32[]{:S(2)}, u32[]{:S(2)}) collective-permute-start(f32[24,1024]{1,0:T(8,128)S(1)} %get-tuple-element.185), channel_id=1, source_target_pairs={{0,96},{1,97},{2,98},{3,99},{4,100},{5,101},{6,102},{7,103},{8,104... | collective-permute-start | bytes 294920 | tf_op jit(solution)/shard_map/ppermute | solution.py:442
  111.2 7.3 %collective-permute-start.23 = (f32[40,384]{1,0:T(8,128)S(1)}, f32[40,384]{1,0:T(8,128)S(1)}, u32[]{:S(2)}, u32[]{:S(2)}) collective-permute-start(f32[40,384]{1,0:T(8,128)S(1)} %get-tuple-element.187), channel_id=1, source_target_pairs={{0,1},{1,2},{2,3},{3,0},{4,5},{5,6},{6,7},{7,4},{8,9},{9,10},{10,1... | collective-permute-start | bytes 184328 | tf_op jit(solution)/shard_map/ppermute | solution.py:48
  112.5 5.9 %collective-permute-start.24 = (f32[40,384]{1,0:T(8,128)S(1)}, f32[40,384]{1,0:T(8,128)S(1)}, u32[]{:S(2)}, u32[]{:S(2)}) collective-permute-start(f32[40,384]{1,0:T(8,128)S(1)} %get-tuple-element.188), channel_id=1, source_target_pairs={{0,2},{1,3},{2,0},{3,1},{4,6},{5,7},{6,4},{7,5},{8,10},{9,11},{10,... | collective-permute-start | bytes 184328 | tf_op jit(solution)/shard_map/ppermute | solution.py:48
  113.3 5.9 %collective-permute-start.25 = (f32[40,384]{1,0:T(8,128)S(1)}, f32[40,384]{1,0:T(8,128)S(1)}, u32[]{:S(2)}, u32[]{:S(2)}) collective-permute-start(f32[40,384]{1,0:T(8,128)S(1)} %get-tuple-element.189), channel_id=1, source_target_pairs={{0,3},{1,0},{2,1},{3,2},{4,7},{5,4},{6,5},{7,6},{8,11},{9,8},{10,9... | collective-permute-start | bytes 184328 | tf_op jit(solution)/shard_map/ppermute | solution.py:48
  119.2 25.6 %copy-start.1 = (bf16[768,1536]{1,0:T(8,128)(2,1)S(1)}, bf16[768,1536]{1,0:T(8,128)(2,1)}, u32[]{:S(2)}) copy-start(bf16[768,1536]{1,0:T(8,128)(2,1)} %param.9) | copy-start | bytes 7077892
  119.8 5.4 %collective-permute-start.29 = (f32[8,128]{1,0:T(8,128)S(1)}, f32[8,128]{1,0:T(8,128)S(1)}, u32[]{:S(2)}, u32[]{:S(2)}) collective-permute-start(f32[8,128]{1,0:T(8,128)S(1)} %shard_map.107), channel_id=1, source_target_pairs={{0,8},{1,9},{2,10},{3,11},{4,12},{5,13},{6,14},{7,15},{8,0},{9,1},... | collective-permute-start | bytes 12296 | tf_op jit(solution)/shard_map/ppermute | solution.py:48
  121.8 4.8 %collective-permute-start.27 = (f32[8,128]{1,0:T(8,128)S(1)}, f32[8,128]{1,0:T(8,128)S(1)}, u32[]{:S(2)}, u32[]{:S(2)}) collective-permute-start(f32[8,128]{1,0:T(8,128)S(1)} %shard_map.107), channel_id=1, source_target_pairs={{0,4},{1,5},{2,6},{3,7},{4,8},{5,9},{6,10},{7,11},{8,12},{9,13},{1... | collective-permute-start | bytes 12296 | tf_op jit(solution)/shard_map/ppermute | solution.py:48
  123.4 3.6 %collective-permute-start.28 = (f32[8,128]{1,0:T(8,128)S(1)}, f32[8,128]{1,0:T(8,128)S(1)}, u32[]{:S(2)}, u32[]{:S(2)}) collective-permute-start(f32[8,128]{1,0:T(8,128)S(1)} %shard_map.107), channel_id=1, source_target_pairs={{0,12},{1,13},{2,14},{3,15},{4,0},{5,1},{6,2},{7,3},{8,4},{9,5},{1... | collective-permute-start | bytes 12296 | tf_op jit(solution)/shard_map/ppermute | solution.py:48
  127.0 6.9 %collective-permute-start.32 = (f32[8,128]{1,0:T(8,128)S(1)}, f32[8,128]{1,0:T(8,128)S(1)}, u32[]{:S(2)}, u32[]{:S(2)}) collective-permute-start(f32[8,128]{1,0:T(8,128)S(1)} %add_add_fusion.1), channel_id=1, source_target_pairs={{0,64},{16,80},{32,96},{48,112},{64,0},{80,16},{96,32},{112,48},{1... | collective-permute-start | bytes 12296 | tf_op jit(solution)/shard_map/ppermute | solution.py:48
  130.6 9.6 %collective-permute-start.30 = (f32[8,128]{1,0:T(8,128)S(1)}, f32[8,128]{1,0:T(8,128)S(1)}, u32[]{:S(2)}, u32[]{:S(2)}) collective-permute-start(f32[8,128]{1,0:T(8,128)S(1)} %add_add_fusion.1), channel_id=1, source_target_pairs={{0,32},{16,48},{32,64},{48,80},{64,96},{80,112},{96,0},{112,16},{1... | collective-permute-start | bytes 12296 | tf_op jit(solution)/shard_map/ppermute | solution.py:48
  131.6 8.6 %collective-permute-start.31 = (f32[8,128]{1,0:T(8,128)S(1)}, f32[8,128]{1,0:T(8,128)S(1)}, u32[]{:S(2)}, u32[]{:S(2)}) collective-permute-start(f32[8,128]{1,0:T(8,128)S(1)} %add_add_fusion.1), channel_id=1, source_target_pairs={{0,96},{16,112},{32,0},{48,16},{64,32},{80,48},{96,64},{112,80},{1... | collective-permute-start | bytes 12296 | tf_op jit(solution)/shard_map/ppermute | solution.py:48
  133.8 9.7 %collective-permute-start.26 = (f32[24,384]{1,0:T(8,128)S(1)}, f32[24,384]{1,0:T(8,128)S(1)}, u32[]{:S(2)}, u32[]{:S(2)}) collective-permute-start(f32[24,384]{1,0:T(8,128)S(1)} %get-tuple-element.190), channel_id=1, source_target_pairs={{0,0},{1,32},{2,64},{3,96},{4,1},{5,33},{6,65},{7,97},{8,2},{9,34}... | collective-permute-start | bytes 110600 | tf_op jit(solution)/shard_map/ppermute | solution.py:545
  140.2 1.2 collective-permute-start.33

commit v9 on v8

--- a/solution.py
+++ b/solution.py
@@ -141,14 +141,16 @@
         ce[k] = exact(before, spread, 0, 0)
 
 
-def tok_part(at, toks, own, first, w_in, w_bc, cirow, cerow, ci, ce, tokb, xs, xfr, bc, ends, la):
+def tok_part(at, toks, own, first, w_in, w_bc, cirow, cerow, ci, ce, tokt, xs, xfr, bc, ends, la, tokb):
     decays(at[0], toks, own, first, cirow, cerow, ci, ce, la)
     for k, t in enumerate(toks, first):
-        tokb[k] = t[:SEG].astype(BF16)
+        v = t[:SEG].astype(BF16)
+        tokb[k - first] = v
+        tokt[:, SEG * k : SEG * k + SEG] = v.T
 
     def segment(i, _):
         k = first + i
-        t = tokb[k]
+        t = tokb[i]
         xv = dot(t, w_in[...], 1, 0).astype(BF16)
         bv = dot(t, w_bc[...], 1, 0).astype(BF16)
         xs[k] = xv
@@ -168,11 +170,14 @@
 
 
 def tok_kernel_b(at, t2, w_in, w_bc, *refs):
-    given, full, (pre, s_p, s_m, s_2, ends, la) = refs[:9], refs[9:17], refs[17:]
+    given, full, (pre, s_p, s_m, s_2, ends, la, tokb) = refs[:9], refs[9:17], refs[17:]
     full = (*full, ends)
     for a, b in zip(given, full, strict=True):
-        b[: NX - 1] = a[...]
-    tok_part(at, (t2,), None, NX - 1, w_in, w_bc, *full, la)
+        if len(a.shape) == 2:
+            b[:, : a.shape[1]] = a[...]
+        else:
+            b[: NX - 1] = a[...]
+    tok_part(at, (t2,), None, NX - 1, w_in, w_bc, *full, la, tokb)
     x, y, ci = at[0], at[2], full[2]
     up = row_scan(range(NX), ends, FIRST, ci, x, pre, 0)
     down = row_scan(reversed(range(NX)), ends, SECOND, ci, x, pre, 1)
@@ -311,7 +316,7 @@
 
 
 def outer_kernel(
-    at, tokb, xfr, bc, ci, ce, pre, r_p, r_m, r_2, dxi, dci, dbi, g_out, keep, send, dz, ds, g
+    at, tokt, xfr, bc, ci, ce, pre, r_p, r_m, r_2, dxi, dci, dbi, g_out, keep, send, dz, ds, g
 ):
     x, core, y_at = at[0], at[1], at[2]
     up, down = from_rows(r_p, r_m, r_2, y_at)
@@ -329,7 +334,7 @@
         return 0
 
     lax.fori_loop(0, NX, segment, 0)
-    raw = dot(tokb[...].reshape(NX * SEG, DM), dz[...].reshape(NX * SEG, WIDE), 0, 0)
+    raw = dot(tokt[...], dz[...].reshape(NX * SEG, WIDE), 1, 0)
     for j, c, row in blocks():
         g[c, row : row + 24, :] = raw[24 * j : 24 * j + 24, :]
     for out, c in ((keep, core), (send, 1 - core)):
@@ -337,16 +342,19 @@
         out[:, WIDE:] = g_out[c]
 
 
-def tokens_kernel(at, dz, w_in, w_bc, d0, d1, d2a, d2b, d3):
-    def tokens_of(k):
-        return dot(dz[k, :, :HC], w_in[...], 1, 1) + dot(dz[k, :, HC:], w_bc[...], 1, 1)
-
-    d = tokens_of(3)
+def tokens_of(k, dz, w_in, w_bc):
+    return dot(dz[k, :, :HC], w_in[...], 1, 1) + dot(dz[k, :, HC:], w_bc[...], 1, 1)
+
+
+def far_kernel(at, dz, w_in, w_bc, d2a, d2b):
+    d = tokens_of(3, dz, w_in, w_bc)
     d2a[...] = d[:HALF]
     d2b[...] = d[HALF:]
-    d1[...] = tokens_of(1)
-    d3[...] = tokens_of(2)
-    d0[...] = tokens_of(0)
+
+
+def tokens_kernel(at, dz, w_in, w_bc, d0, d1, d3):
+    for k, d in enumerate((d0, d1, d3)):
+        d[...] = tokens_of(k, dz, w_in, w_bc)
 
 
 def pass_kernel(at, d1, d3, r_a, r_b, s1, s3):
@@ -475,7 +483,7 @@
     def of_tokens(n):
         return [
             ((n, 8, SEG), F32), ((n, 8, SEG), F32), ((n, SEG, HC), F32), ((n, SEG, HC), F32),
-            ((n, SEG, DM), BF16), ((n, SEG, HC), BF16), ((n, SEG, 2 * HC), BF16), ((n, SEG, 2 * NS), BF16),
+            ((DM, n * SEG), BF16), ((n, SEG, HC), BF16), ((n, SEG, 2 * HC), BF16), ((n, SEG, 2 * NS), BF16),
         ]
 
     def ends(n):
@@ -484,7 +492,7 @@
     flops = 2 * SEG * (DM * (HC + 2 * NS) + NS * 2 * HC)
     row = ((8, SEG), F32)
     three = call(
-        tok_kernel_a, [*of_tokens(3), ends(3)], [row], [at, tokens[0], log_decay[0], t1, t3, wi, w_bc], 3 * flops
+        tok_kernel_a, [*of_tokens(3), ends(3)], [row, ((3, SEG, DM), BF16)], [at, tokens[0], log_decay[0], t1, t3, wi, w_bc], 3 * flops
     )
     def mats(n):
         return [((n, NH, SEG, SEG), BF16), ((n, NH, SEG, SEG), BF16), ((n, SEG, HC), F32)]
@@ -496,8 +504,8 @@
     t2, c1, *both = tie((t2, c1, *three, *mats_a))
     three, mats_a = both[:9], both[9:]
     c2 = move(c1, "x", -1)
-    cirow, cerow, ci, ce, tokb, xs, xfr, bc, pre_s, *s_rows = call(
-        tok_kernel_b, [*of_tokens(4), edges, tall, tall, tall], [ends(4), row], [at, t2, wi, w_bc, *three], flops
+    cirow, cerow, ci, ce, tokt, xs, xfr, bc, pre_s, *s_rows = call(
+        tok_kernel_b, [*of_tokens(4), edges, tall, tall, tall], [ends(4), row, ((1, SEG, DM), BF16)], [at, t2, wi, w_bc, *three], flops
     )
     q_rows = rows_exchange(*s_rows)
     two = [((2, SEG, DM), BF16), ((2, SEG, HC), BF16), ((2, SEG, 2 * HC), BF16)]
@@ -522,15 +530,16 @@
         outer_kernel,
         [((ROWS, ALL), F32), ((ROWS, ALL), F32), ((NX, SEG, WIDE), BF16)],
         [((NX, NS, 2 * HC), BF16), ((2, ROWS, WIDE), F32)],
-        [at, tokb, xfr, bc, ci, ce, pre_d, *p_rows, dxi, dci, dbi, g_out],
+        [at, tokt, xfr, bc, ci, ce, pre_d, *p_rows, dxi, dci, dbi, g_out],
         2 * 1024 * (WIDE * DM + 4 * NS * HC),
     )
     got = move(send, "c", 1)
     terms = deal(at, 4, [keep, got], 96, ALL)
     whole, half = ((SEG, DM), F32), ((HALF, DM), F32)
-    d0, d1, d2a, d2b, d3 = call(
-        tokens_kernel, [whole, whole, half, half, whole], [], [at, dz, wi, w_bc], 2 * 1024 * WIDE * DM
-    )
+    flops = 2 * SEG * WIDE * DM
+    d2a, d2b = call(far_kernel, [half, half], [], [at, dz, wi, w_bc], flops)
+    terms[0], dz_later = tie((terms[0], dz))
+    d0, d1, d3 = call(tokens_kernel, [whole] * 3, [], [at, dz_later, wi, w_bc], 3 * flops)
     r_a, r_b = move(d2a, "x", 1), move(d2b, "x", -1)
     s1, s3 = call(pass_kernel, [whole, whole], [], [at, d1, d3, r_a, r_b])
     m1, m3 = move(s1, "x", 1), move(s3, "x", -1)

time: 147 us -> 147 us (level)
    pallas_call x15 -> x16, Pallas kernels: 34.9 us -> 35.7 us  [call(): pl.pallas_call(kernel, out_shape=[jax.ShapeDtypeStruct(*o) for o in outs]...]
  transfers between devices with their start and end apart: 34 -> 34, of which waited for: 18 -> 19; matrix products, arithmetic and copies ran while one was open for 3% -> 2% of each run, Pallas kernels for 21% -> 22%
where the time goes in v9:
time: 147 us; the launch traced here: 144 us
  starting transfers between devices  55.1 us (37%)
  waiting for transfers between devices  45.5 us (31%)
  Pallas kernels  35.7 us (24%)
  local copies, waits for them, and re-layouts  4.15 us (3%)
  other arithmetic  2.87 us (2%)
    ppermute x27, waiting for transfers between devices, move(): return lax.ppermute(value, name, pairs)  39.3 us
    ppermute x27, starting transfers between devices, move(): return lax.ppermute(value, name, pairs)  37.8 us
    pallas_call x16, Pallas kernels, call(): pl.pallas_call(kernel, out_shape=[jax.ShapeDtypeStruct(*o) for o in outs]...  35.7 us
    ppermute x6, starting transfers between devices, send(): return lax.ppermute(value, ('rec', 'seq'), pairs)  11 us
    ppermute x1, starting transfers between devices, body(): rows_out = lax.ppermute(rows_out, ('rec', 'seq'), pairs)  6.33 us
    ppermute x6, waiting for transfers between devices, send(): return lax.ppermute(value, ('rec', 'seq'), pairs)  4.08 us
  transfers between devices with their start and end apart: 34, of which 19 were waited for; matrix products, arithmetic and copies ran while one was open for 2% of the time, Pallas kernels for 22%

profile of v9, /device:TPU:6, one launch (start us, length us, event | category | flops | bytes accessed | tf_op | source)
XLA Modules:
  0.0 144.2 jit_solution(11055563872937701002)
XLA Ops:
  0.7 1.1 copy-done.4
  1.8 0.7 copy-done.6
  3.1 1.6 %collective-permute-start.2 = (f32[264,768]{1,0:T(8,128)S(1)}, f32[264,768]{1,0:T(8,128)S(1)}, u32[]{:S(2)}, u32[]{:S(2)}) collective-permute-start(f32[264,768]{1,0:T(8,128)S(1)} %shard_map.93), channel_id=1, source_target_pairs={{0,3},{1,0},{2,1},{3,2},{4,7},{5,4},{6,5},{7,6},{8,11},{9,8},{10,9... | collective-permute-start | bytes 2433032 | tf_op jit(solution)/shard_map/ppermute | solution.py:48
  4.7 2.0 %bitcast_convert_fusion = f32[256,768]{1,0:T(8,128)} fusion(bf16[1,256,768]{2,1,0:T(8,128)(2,1)} %param.7), kind=kLoop, calls=%fused_computation.6 | loop fusion | flops 196608 | bytes 1179648 | tf_op jit(solution)/shard_map/convert_element_type | solution.py:470
  6.7 15.9 %collective-permute-done.t3 = f32[264,768]{1,0:T(8,128)} collective-permute-done((f32[264,768]{1,0:T(8,128)S(1)}, f32[264,768]{1,0:T(8,128)}, u32[]{:S(2)}, u32[]{:S(2)}) %collective-permute-start) | collective-permute-done | bytes 811040 | tf_op jit(solution)/shard_map/ppermute | solution.py:48
  22.6 1.5 %collective-permute-start.1 = (f32[264,768]{1,0:T(8,128)}, f32[264,768]{1,0:T(8,128)}, u32[]{:S(2)}, u32[]{:S(2)}) collective-permute-start(f32[264,768]{1,0:T(8,128)} %collective-permute-done.t3), channel_id=1, source_target_pairs={{0,1},{1,2},{2,3},{3,0},{4,5},{5,6},{6,7},{7,4},{8,9},{9,10},{10,1... | collective-permute-start | bytes 2433032 | tf_op jit(solution)/shard_map/ppermute | solution.py:48
  24.1 0.9 copy-done.8
  25.0 0.5 collective-permute-start.3
  25.7 1.2 constant_dynamic-slice_fusion.w_out
  26.9 2.8 %collective-permute-start.4 = (f32[256,768]{1,0:T(8,128)}, f32[256,768]{1,0:T(8,128)S(1)}, u32[]{:S(2)}, u32[]{:S(2)}) collective-permute-start(f32[256,768]{1,0:T(8,128)} %bitcast_convert_fusion), channel_id=1, source_target_pairs={{0,1},{1,2},{2,3},{3,0},{4,5},{5,6},{6,7},{7,4},{8,9},{9,10},{10,1... | collective-permute-start | bytes 2359304 | tf_op jit(solution)/shard_map/ppermute | solution.py:48
  29.7 6.6 %shard_map.94 = (f32[3,8,256]{2,1,0:T(8,128)S(1)}, f32[3,8,256]{2,1,0:T(8,128)S(1)}, f32[3,256,384]{2,1,0:T(8,128)S(1)}, f32[3,256,384]{2,1,0:T(8,128)S(1)}, bf1...) custom-call(s32[6]{0:T(128)S(1)} %stack.27.at, ...), custom_call_target="tpu_custom_call" | custom-call | flops 905969664 | bytes 3022872 | tf_op jit(solution)/shard_map/pallas_call | solution.py:420
  36.3 3.5 %shard_map.95 = (bf16[3,6,256,256]{3,2,1,0:T(8,128)(2,1)S(1)}, bf16[3,6,256,256]{3,2,1,0:T(8,128)(2,1)S(1)}, f32[3,256,384]{2,1,0:T(8,128)S(1)}) custom-call(s32[6]{0:T(128)S(1)} %stack.27.at, f32[3,8,256]{2,1,0:T(8,128)S(1)} %get-tuple-element.120.cirow.refs_0_, f32[3,8,256]{2,1,0:T(8,128)S(1)} %get-tuple-element.121.cerow.refs_1_, ...), custom_call_target="tpu_custom_call" | custom-call | flops 301989888 | bytes 3391512 | tf_op jit(solution)/shard_map/pallas_call | solution.py:420
  39.8 4.6 %collective-permute-done.3.c1 = f32[256,768]{1,0:T(8,128)S(1)} collective-permute-done((f32[256,768]{1,0:T(8,128)}, f32[256,768]{1,0:T(8,128)S(1)}, u32[]{:S(2)}, u32[]{:S(2)}) %collective-permute-start.3) | collective-permute-done | bytes 786464 | tf_op jit(solution)/shard_map/ppermute | solution.py:48
  44.7 3.5 %shard_map.96 = (f32[4,8,256]{2,1,0:T(8,128)S(1)}, f32[4,8,256]{2,1,0:T(8,128)S(1)}, f32[4,256,384]{2,1,0:T(8,128)S(1)}, f32[4,256,384]{2,1,0:T(8,128)S(1)}, bf1...) custom-call(s32[6]{0:T(128)S(1)} %stack.27.at, ...), custom_call_target="tpu_custom_call" | custom-call | flops 301989888 | bytes 8724504 | tf_op jit(solution)/shard_map/pallas_call | solution.py:420
  48.3 1.6 %collective-permute-start.9 = (f32[136,384]{1,0:T(8,128)S(1)}, f32[136,384]{1,0:T(8,128)S(1)}, u32[]{:S(2)}, u32[]{:S(2)}) collective-permute-start(f32[136,384]{1,0:T(8,128)S(1)} %get-tuple-element.157), channel_id=1, source_target_pairs={{0,4},{1,5},{2,6},{3,7},{4,8},{5,9},{6,10},{7,11},{8,12},{9,13},{1... | collective-permute-start | bytes 626696 | tf_op jit(solution)/shard_map/ppermute | solution.py:48
  49.9 1.7 %collective-permute-start.10 = (f32[136,384]{1,0:T(8,128)S(1)}, f32[136,384]{1,0:T(8,128)S(1)}, u32[]{:S(2)}, u32[]{:S(2)}) collective-permute-start(f32[136,384]{1,0:T(8,128)S(1)} %get-tuple-element.158), channel_id=1, source_target_pairs={{0,12},{1,13},{2,14},{3,15},{4,0},{5,1},{6,2},{7,3},{8,4},{9,5},{1... | collective-permute-start | bytes 626696 | tf_op jit(solution)/shard_map/ppermute | solution.py:48
  51.6 2.0 %collective-permute-start.11 = (f32[136,384]{1,0:T(8,128)S(1)}, f32[136,384]{1,0:T(8,128)S(1)}, u32[]{:S(2)}, u32[]{:S(2)}) collective-permute-start(f32[136,384]{1,0:T(8,128)S(1)} %get-tuple-element.159), channel_id=1, source_target_pairs={{0,8},{1,9},{2,10},{3,11},{4,12},{5,13},{6,14},{7,15},{8,0},{9,1},... | collective-permute-start | bytes 626696 | tf_op jit(solution)/shard_map/ppermute | solution.py:48
  53.5 1.5 %shard_map.98 = (bf16[1,6,256,256]{3,2,1,0:T(8,128)(2,1)S(1)}, bf16[1,6,256,256]{3,2,1,0:T(8,128)(2,1)S(1)}, f32[1,256,384]{2,1,0:T(8,128)S(1)}) custom-call(s32[6]{0:T(128)S(1)} %stack.27.at, f32[4,8,256]{2,1,0:T(8,128)S(1)} %get-tuple-element.137.cirow, f32[4,8,256]{2,1,0:T(8,128)S(1)} %get-tuple-element.138.cerow, ...), custom_call_target="tpu_custom_call" | custom-call | flops 100663296 | bytes 4522008 | tf_op jit(solution)/shard_map/pallas_call | solution.py:420
  55.1 1.9 %shard_map.97 = (bf16[2,256,768]{2,1,0:T(8,128)(2,1)S(1)}, bf16[2,256,384]{2,1,0:T(8,128)(2,1)S(1)}, bf16[2,256,768]{2,1,0:T(8,128)(2,1)S(1)}, f32[2,128,768]{2,1,0:T(8,128)S(1)}) custom-call(s32[6]{0:T(128)S(1)} %stack.27.at, bf16[256,768]{1,0:T(8,128)(2,1)S(1)} %bitcast.12, f32[256,768]{1,0:T(8,128)S(1)} %collective-permute-done.3.c1, ...), custom_call_target="tpu_custom_call" | custom-call | flops 402653184 | bytes 5439512 | tf_op jit(solution)/shard_map/pallas_call | solution.py:420
  57.0 1.6 %collective-permute-done.4.c2 = f32[256,768]{1,0:T(8,128)S(1)} collective-permute-done((f32[256,768]{1,0:T(8,128)}, f32[256,768]{1,0:T(8,128)S(1)}, u32[]{:S(2)}, u32[]{:S(2)}) %collective-permute-start.4) | collective-permute-done | bytes 786464 | tf_op jit(solution)/shard_map/ppermute | solution.py:48
  58.6 4.1 %collective-permute-done.5.c3 = f32[256,768]{1,0:T(8,128)S(1)} collective-permute-done((f32[256,768]{1,0:T(8,128)S(1)}, f32[256,768]{1,0:T(8,128)S(1)}, u32[]{:S(2)}, u32[]{:S(2)}) %collective-permute-start.5) | collective-permute-done | bytes 786464 | tf_op jit(solution)/shard_map/ppermute | solution.py:48
  62.7 2.1 %shard_map.99 = (bf16[2,256,768]{2,1,0:T(8,128)(2,1)S(1)}, bf16[2,256,384]{2,1,0:T(8,128)(2,1)S(1)}, bf16[2,256,768]{2,1,0:T(8,128)(2,1)S(1)}, f32[2,4,128,384]{...) custom-call(s32[6]{0:T(128)S(1)} %stack.27.at, ...), custom_call_target="tpu_custom_call" | custom-call | flops 402653184 | bytes 6619160 | tf_op jit(solution)/shard_map/pallas_call | solution.py:420
  64.8 2.1 %collective-permute-start.6 = (f32[136,384]{1,0:T(8,128)S(1)}, f32[136,384]{1,0:T(8,128)S(1)}, u32[]{:S(2)}, u32[]{:S(2)}) collective-permute-start(f32[136,384]{1,0:T(8,128)S(1)} %get-tuple-element.147), channel_id=1, source_target_pairs={{0,4},{1,5},{2,6},{3,7},{4,8},{5,9},{6,10},{7,11},{8,12},{9,13},{1... | collective-permute-start | bytes 626696 | tf_op jit(solution)/shard_map/ppermute | solution.py:48
  66.9 1.7 %collective-permute-start.7 = (f32[136,384]{1,0:T(8,128)S(1)}, f32[136,384]{1,0:T(8,128)S(1)}, u32[]{:S(2)}, u32[]{:S(2)}) collective-permute-start(f32[136,384]{1,0:T(8,128)S(1)} %get-tuple-element.148), channel_id=1, source_target_pairs={{0,12},{1,13},{2,14},{3,15},{4,0},{5,1},{6,2},{7,3},{8,4},{9,5},{1... | collective-permute-start | bytes 626696 | tf_op jit(solution)/shard_map/ppermute | solution.py:48
  68.6 1.9 %collective-permute-start.8 = (f32[136,384]{1,0:T(8,128)S(1)}, f32[136,384]{1,0:T(8,128)S(1)}, u32[]{:S(2)}, u32[]{:S(2)}) collective-permute-start(f32[136,384]{1,0:T(8,128)S(1)} %get-tuple-element.149), channel_id=1, source_target_pairs={{0,8},{1,9},{2,10},{3,11},{4,12},{5,13},{6,14},{7,15},{8,0},{9,1},... | collective-permute-start | bytes 626696 | tf_op jit(solution)/shard_map/ppermute | solution.py:48
  70.6 5.1 %shard_map.100 = (f32[2,384,384]{2,1,0:T(8,128)S(1)}, f32[4,256,384]{2,1,0:T(8,128)S(1)}, f32[4,256,128]{2,1,0:T(8,128)S(1)}, f32[4,256,128]{2,1,0:T(8,128)S(1)}) custom-call(s32[6]{0:T(128)S(1)} %stack.27.at, bf16[4,256,384]{2,1,0:T(8,128)(2,1)S(1)} %get-tuple-element.139.xs, bf16[4,256,256]{2,1,0:T(8,128)(2,1)S(1)} %get-tuple-element.131.bc, ...), custom_call_target="tpu_custom_call" | custom-call | flops 2214592512 | bytes 18452504 | tf_op jit(solution)/shard_map/pallas_call | solution.py:420
  75.7 0.5 collective-permute-done.8.r_2
  76.2 3.9 %shard_map.101 = (f32[384,1024]{1,0:T(8,128)S(1)}, f32[384,1024]{1,0:T(8,128)S(1)}, bf16[4,256,640]{2,1,0:T(8,128)(2,1)S(1)}) custom-call(s32[6]{0:T(128)S(1)} %stack.27.at, bf16[768,1024]{1,0:T(8,128)(2,1)S(1)} %get-tuple-element.129.tokt, bf16[4,256,768]{2,1,0:T(8,128)(2,1)S(1)} %get-tuple-element.130.xfr, bf16[4,256,256]{2,1,0:T(8,128)(2,1)S(1)} %get-tuple-element.131.bc, ...), custom_call_target="tpu_custom_call" | custom-call | flops 1409286144 | bytes 12816408 | tf_op jit(solution)/shard_map/pallas_call | solution.py:420
  80.2 1.0 shard_map.104
  81.4 2.0 %collective-permute-start.14 = (f32[128,768]{1,0:T(8,128)S(1)}, f32[128,768]{1,0:T(8,128)S(1)}, u32[]{:S(2)}, u32[]{:S(2)}) collective-permute-start(f32[128,768]{1,0:T(8,128)S(1)} %get-tuple-element.179), channel_id=1, source_target_pairs={{0,3},{1,0},{2,1},{3,2},{4,7},{5,4},{6,5},{7,6},{8,11},{9,8},{10,9... | collective-permute-start | bytes 1179656 | tf_op jit(solution)/shard_map/ppermute | solution.py:48
  83.6 0.8 shard_map.102
  84.4 1.2 collective-permute-start.17
  85.6 2.4 %collective-permute-start.18 = (f32[96,1024]{1,0:T(8,128)S(1)}, f32[96,1024]{1,0:T(8,128)S(1)}, u32[]{:S(2)}, u32[]{:S(2)}) collective-permute-start(f32[96,1024]{1,0:T(8,128)S(1)} %get-tuple-element.184), channel_id=1, source_target_pairs={{0,8},{1,9},{2,10},{3,11},{4,12},{5,13},{6,14},{7,15},{8,0},{9,1},... | collective-permute-start | bytes 1179656 | tf_op jit(solution)/shard_map/ppermute | solution.py:450
  88.0 0.8 collective-permute-start.19
  88.8 1.7 %shard_map.103 = (f32[256,768]{1,0:T(8,128)S(1)}, f32[256,768]{1,0:T(8,128)S(1)}, f32[256,768]{1,0:T(8,128)S(1)}) custom-call(s32[6]{0:T(128)S(1)} %stack.27.at, bf16[4,256,640]{2,1,0:T(8,128)(2,1)S(1)} %get-tuple-element.174.dz, bf16[768,384]{1,0:T(8,128)(2,1)S(1)} %constant_dynamic-slice_fusion.1.w_in, bf16[768,256]{1,0:T(8,128)(2,1)S(1)} %copy-done.2), custom_call_target="tpu_custom_call" | custom-call | flops 754974720 | bytes 2293784 | tf_op jit(solution)/shard_map/pallas_call | solution.py:420
  90.5 2.4 %collective-permute-done.13.r_a = f32[128,768]{1,0:T(8,128)S(1)} collective-permute-done((f32[128,768]{1,0:T(8,128)S(1)}, f32[128,768]{1,0:T(8,128)S(1)}, u32[]{:S(2)}, u32[]{:S(2)}) %collective-permute-start.13) | collective-permute-done | bytes 393248 | tf_op jit(solution)/shard_map/ppermute | solution.py:48
  92.9 1.3 collective-permute-done.14.r_b
  94.2 0.7 shard_map.105
  94.8 0.5 collective-permute-start.16
  95.4 2.8 %collective-permute-start.15 = (f32[256,768]{1,0:T(8,128)S(1)}, f32[256,768]{1,0:T(8,128)S(1)}, u32[]{:S(2)}, u32[]{:S(2)}) collective-permute-start(f32[256,768]{1,0:T(8,128)S(1)} %get-tuple-element.180), channel_id=1, source_target_pairs={{0,1},{1,2},{2,3},{3,0},{4,5},{5,6},{6,7},{7,4},{8,9},{9,10},{10,1... | collective-permute-start | bytes 2359304 | tf_op jit(solution)/shard_map/ppermute | solution.py:48
  98.6 0.7 shard_map.106
  99.3 2.0 %collective-permute-start.20 = (f32[24,1024]{1,0:T(8,128)S(1)}, f32[24,1024]{1,0:T(8,128)S(1)}, u32[]{:S(2)}, u32[]{:S(2)}) collective-permute-start(f32[24,1024]{1,0:T(8,128)S(1)} %get-tuple-element.187), channel_id=1, source_target_pairs={{0,32},{1,33},{2,34},{3,35},{4,36},{5,37},{6,38},{7,39},{8,40},{9,... | collective-permute-start | bytes 294920 | tf_op jit(solution)/shard_map/ppermute | solution.py:450
  101.3 3.6 %collective-permute-start.21 = (f32[24,1024]{1,0:T(8,128)S(1)}, f32[24,1024]{1,0:T(8,128)S(1)}, u32[]{:S(2)}, u32[]{:S(2)}) collective-permute-start(f32[24,1024]{1,0:T(8,128)S(1)} %get-tuple-element.188), channel_id=1, source_target_pairs={{0,64},{1,65},{2,66},{3,67},{4,68},{5,69},{6,70},{7,71},{8,72},{9,... | collective-permute-start | bytes 294920 | tf_op jit(solution)/shard_map/ppermute | solution.py:450
  104.9 1.0 collective-permute-start.22
  106.0 2.5 %collective-permute-done.21.c = f32[24,1024]{1,0:T(8,128)S(1)} collective-permute-done((f32[24,1024]{1,0:T(8,128)S(1)}, f32[24,1024]{1,0:T(8,128)S(1)}, u32[]{:S(2)}, u32[]{:S(2)}) %collective-permute-start.21) | collective-permute-done | bytes 98336 | tf_op jit(solution)/shard_map/ppermute | solution.py:450
  108.5 1.0 collective-permute-done.22.d
  109.5 0.7 shard_map.107
  110.2 1.1 collective-permute-start.23
  111.3 0.8 collective-permute-start.24
  112.3 4.9 %collective-permute-done.23.b = f32[40,384]{1,0:T(8,128)S(1)} collective-permute-done((f32[40,384]{1,0:T(8,128)S(1)}, f32[40,384]{1,0:T(8,128)S(1)}, u32[]{:S(2)}, u32[]{:S(2)}) %collective-permute-start.23) | collective-permute-done | bytes 61472 | tf_op jit(solution)/shard_map/ppermute | solution.py:48
  117.2 0.7 collective-permute-done.25.d
  117.9 0.7 shard_map.108
  118.6 1.8 %collective-permute-start.29 = (f32[8,128]{1,0:T(8,128)S(1)}, f32[8,128]{1,0:T(8,128)S(1)}, u32[]{:S(2)}, u32[]{:S(2)}) collective-permute-start(f32[8,128]{1,0:T(8,128)S(1)} %shard_map.108), channel_id=1, source_target_pairs={{0,8},{1,9},{2,10},{3,11},{4,12},{5,13},{6,14},{7,15},{8,0},{9,1},... | collective-permute-start | bytes 12296 | tf_op jit(solution)/shard_map/ppermute | solution.py:48
  120.4 1.6 %collective-permute-start.27 = (f32[8,128]{1,0:T(8,128)S(1)}, f32[8,128]{1,0:T(8,128)S(1)}, u32[]{:S(2)}, u32[]{:S(2)}) collective-permute-start(f32[8,128]{1,0:T(8,128)S(1)} %shard_map.108), channel_id=1, source_target_pairs={{0,4},{1,5},{2,6},{3,7},{4,8},{5,9},{6,10},{7,11},{8,12},{9,13},{1... | collective-permute-start | bytes 12296 | tf_op jit(solution)/shard_map/ppermute | solution.py:48
  121.9 1.7 %collective-permute-start.28 = (f32[8,128]{1,0:T(8,128)S(1)}, f32[8,128]{1,0:T(8,128)S(1)}, u32[]{:S(2)}, u32[]{:S(2)}) collective-permute-start(f32[8,128]{1,0:T(8,128)S(1)} %shard_map.108), channel_id=1, source_target_pairs={{0,12},{1,13},{2,14},{3,15},{4,0},{5,1},{6,2},{7,3},{8,4},{9,5},{1... | collective-permute-start | bytes 12296 | tf_op jit(solution)/shard_map/ppermute | solution.py:48
  123.8 1.4 collective-permute-done.27
  125.5 3.6 %collective-permute-start.32 = (f32[8,128]{1,0:T(8,128)S(1)}, f32[8,128]{1,0:T(8,128)S(1)}, u32[]{:S(2)}, u32[]{:S(2)}) collective-permute-start(f32[8,128]{1,0:T(8,128)S(1)} %add_add_fusion.1), channel_id=1, source_target_pairs={{0,64},{16,80},{32,96},{48,112},{64,0},{80,16},{96,32},{112,48},{1... | collective-permute-start | bytes 12296 | tf_op jit(solution)/shard_map/ppermute | solution.py:48
  129.2 1.0 collective-permute-start.30
  130.2 2.2 %collective-permute-start.31 = (f32[8,128]{1,0:T(8,128)S(1)}, f32[8,128]{1,0:T(8,128)S(1)}, u32[]{:S(2)}, u32[]{:S(2)}) collective-permute-start(f32[8,128]{1,0:T(8,128)S(1)} %add_add_fusion.1), channel_id=1, source_target_pairs={{0,96},{16,112},{32,0},{48,16},{64,32},{80,48},{96,64},{112,80},{1... | collective-permute-start | bytes 12296 | tf_op jit(solution)/shard_map/ppermute | solution.py:48
  132.4 6.3 %collective-permute-start.26 = (f32[24,384]{1,0:T(8,128)S(1)}, f32[24,384]{1,0:T(8,128)S(1)}, u32[]{:S(2)}, u32[]{:S(2)}) collective-permute-start(f32[24,384]{1,0:T(8,128)S(1)} %get-tuple-element.194), channel_id=1, source_target_pairs={{0,0},{1,32},{2,64},{3,96},{4,1},{5,33},{6,65},{7,97},{8,2},{9,34}... | collective-permute-start | bytes 110600 | tf_op jit(solution)/shard_map/ppermute | solution.py:554
  138.9 1.1 collective-permute-done.33
  140.0 2.1 %collective-permute-done.26.rows_out = f32[24,384]{1,0:T(8,128)S(1)} collective-permute-done((f32[24,384]{1,0:T(8,128)S(1)}, f32[24,384]{1,0:T(8,128)S(1)}, u32[]{:S(2)}, u32[]{:S(2)}) %collective-permute-start.26) | collective-permute-done | bytes 36896 | tf_op jit(solution)/shard_map/ppermute | solution.py:554
  142.1 1.2 shard_map.109
  143.3 0.9 fusion
  (49 shorter events, 3.0 us)
Async XLA Ops:
  0.6 25.0 %copy-start = (bf16[768,1536]{1,0:T(8,128)(2,1)S(1)}, bf16[768,1536]{1,0:T(8,128)(2,1)}, u32[]{:S(2)}) copy-start(bf16[768,1536]{1,0:T(8,128)(2,1)} %param.9) | copy-start | bytes 7077892
  0.6 1.1 copy-start.4
  1.8 0.7 copy-start.6
  2.6 27.1 %copy-start.2 = (bf16[768,256]{1,0:T(8,128)(2,1)S(1)}, bf16[768,256]{1,0:T(8,128)(2,1)}, u32[]{:S(2)}) copy-start(bf16[768,256]{1,0:T(8,128)(2,1)} %w_bc.7) | copy-start | bytes 1179652
  2.6 20.0 %collective-permute-start = (f32[264,768]{1,0:T(8,128)S(1)}, f32[264,768]{1,0:T(8,128)}, u32[]{:S(2)}, u32[]{:S(2)}) collective-permute-start(f32[264,768]{1,0:T(8,128)S(1)} %shard_map.93), channel_id=1, source_target_pairs={{0,1},{1,2},{2,3},{3,0},{4,5},{5,6},{6,7},{7,4},{8,9},{9,10},{10,1... | collective-permute-start | bytes 2433032 | tf_op jit(solution)/shard_map/ppermute | solution.py:48
  3.1 21.0 %collective-permute-start.2 = (f32[264,768]{1,0:T(8,128)S(1)}, f32[264,768]{1,0:T(8,128)S(1)}, u32[]{:S(2)}, u32[]{:S(2)}) collective-permute-start(f32[264,768]{1,0:T(8,128)S(1)} %shard_map.93), channel_id=1, source_target_pairs={{0,3},{1,0},{2,1},{3,2},{4,7},{5,4},{6,5},{7,6},{8,11},{9,8},{10,9... | collective-permute-start | bytes 2433032 | tf_op jit(solution)/shard_map/ppermute | solution.py:48
  22.6 21.8 %collective-permute-start.1 = (f32[264,768]{1,0:T(8,128)}, f32[264,768]{1,0:T(8,128)}, u32[]{:S(2)}, u32[]{:S(2)}) collective-permute-start(f32[264,768]{1,0:T(8,128)} %collective-permute-done.t3), channel_id=1, source_target_pairs={{0,1},{1,2},{2,3},{3,0},{4,5},{5,6},{6,7},{7,4},{8,9},{9,10},{10,1... | collective-permute-start | bytes 2433032 | tf_op jit(solution)/shard_map/ppermute | solution.py:48
  24.1 0.9 copy-start.8
  25.0 19.4 %collective-permute-start.3 = (f32[256,768]{1,0:T(8,128)}, f32[256,768]{1,0:T(8,128)S(1)}, u32[]{:S(2)}, u32[]{:S(2)}) collective-permute-start(f32[256,768]{1,0:T(8,128)} %bitcast_convert_fusion), channel_id=1, source_target_pairs={{0,3},{1,0},{2,1},{3,2},{4,7},{5,4},{6,5},{7,6},{8,11},{9,8},{10,9... | collective-permute-start | bytes 2359304 | tf_op jit(solution)/shard_map/ppermute | solution.py:48
  25.6 4.1 %copy-start.5 = (bf16[1,256,768]{2,1,0:T(8,128)(2,1)S(1)}, bf16[1,256,768]{2,1,0:T(8,128)(2,1)}, u32[]{:S(2)}) copy-start(bf16[1,256,768]{2,1,0:T(8,128)(2,1)} %param.6) | copy-start | bytes 1179652
  25.6 4.1 %copy-start.7 = (f32[1,24,256]{2,1,0:T(8,128)S(1)}, f32[1,24,256]{2,1,0:T(8,128)}, u32[]{:S(2)}) copy-start(f32[1,24,256]{2,1,0:T(8,128)} %param.8) | copy-start | bytes 73732
  25.6 4.1 %copy-start.9 = (f32[264,768]{1,0:T(8,128)S(1)}, f32[264,768]{1,0:T(8,128)}, u32[]{:S(2)}) copy-start(f32[264,768]{1,0:T(8,128)} %copy-done.8) | copy-start | bytes 2433028
  26.9 31.7 %collective-permute-start.4 = (f32[256,768]{1,0:T(8,128)}, f32[256,768]{1,0:T(8,128)S(1)}, u32[]{:S(2)}, u32[]{:S(2)}) collective-permute-start(f32[256,768]{1,0:T(8,128)} %bitcast_convert_fusion), channel_id=1, source_target_pairs={{0,1},{1,2},{2,3},{3,0},{4,5},{5,6},{6,7},{7,4},{8,9},{9,10},{10,1... | collective-permute-start | bytes 2359304 | tf_op jit(solution)/shard_map/ppermute | solution.py:48
  44.4 18.3 %collective-permute-start.5 = (f32[256,768]{1,0:T(8,128)S(1)}, f32[256,768]{1,0:T(8,128)S(1)}, u32[]{:S(2)}, u32[]{:S(2)}) collective-permute-start(f32[256,768]{1,0:T(8,128)S(1)} %collective-permute-done.3.c1), channel_id=1, source_target_pairs={{0,3},{1,0},{2,1},{3,2},{4,7},{5,4},{6,5},{7,6},{8,11},{9,8},{10,9... | collective-permute-start | bytes 2359304 | tf_op jit(solution)/shard_map/ppermute | solution.py:48
  48.3 20.4 %collective-permute-start.9 = (f32[136,384]{1,0:T(8,128)S(1)}, f32[136,384]{1,0:T(8,128)S(1)}, u32[]{:S(2)}, u32[]{:S(2)}) collective-permute-start(f32[136,384]{1,0:T(8,128)S(1)} %get-tuple-element.157), channel_id=1, source_target_pairs={{0,4},{1,5},{2,6},{3,7},{4,8},{5,9},{6,10},{7,11},{8,12},{9,13},{1... | collective-permute-start | bytes 626696 | tf_op jit(solution)/shard_map/ppermute | solution.py:48
  49.9 20.7 %collective-permute-start.10 = (f32[136,384]{1,0:T(8,128)S(1)}, f32[136,384]{1,0:T(8,128)S(1)}, u32[]{:S(2)}, u32[]{:S(2)}) collective-permute-start(f32[136,384]{1,0:T(8,128)S(1)} %get-tuple-element.158), channel_id=1, source_target_pairs={{0,12},{1,13},{2,14},{3,15},{4,0},{5,1},{6,2},{7,3},{8,4},{9,5},{1... | collective-permute-start | bytes 626696 | tf_op jit(solution)/shard_map/ppermute | solution.py:48
  51.6 19.0 %collective-permute-start.11 = (f32[136,384]{1,0:T(8,128)S(1)}, f32[136,384]{1,0:T(8,128)S(1)}, u32[]{:S(2)}, u32[]{:S(2)}) collective-permute-start(f32[136,384]{1,0:T(8,128)S(1)} %get-tuple-element.159), channel_id=1, source_target_pairs={{0,8},{1,9},{2,10},{3,11},{4,12},{5,13},{6,14},{7,15},{8,0},{9,1},... | collective-permute-start | bytes 626696 | tf_op jit(solution)/shard_map/ppermute | solution.py:48
  53.5 1.5 %copy-start.3 = (bf16[1,256,768]{2,1,0:T(8,128)(2,1)S(1)}, bf16[1,256,768]{2,1,0:T(8,128)(2,1)}, u32[]{:S(2)}) copy-start(bf16[1,256,768]{2,1,0:T(8,128)(2,1)} %param.7) | copy-start | bytes 1179652
  64.8 10.8 %collective-permute-start.6 = (f32[136,384]{1,0:T(8,128)S(1)}, f32[136,384]{1,0:T(8,128)S(1)}, u32[]{:S(2)}, u32[]{:S(2)}) collective-permute-start(f32[136,384]{1,0:T(8,128)S(1)} %get-tuple-element.147), channel_id=1, source_target_pairs={{0,4},{1,5},{2,6},{3,7},{4,8},{5,9},{6,10},{7,11},{8,12},{9,13},{1... | collective-permute-start | bytes 626696 | tf_op jit(solution)/shard_map/ppermute | solution.py:48
  66.9 8.8 %collective-permute-start.7 = (f32[136,384]{1,0:T(8,128)S(1)}, f32[136,384]{1,0:T(8,128)S(1)}, u32[]{:S(2)}, u32[]{:S(2)}) collective-permute-start(f32[136,384]{1,0:T(8,128)S(1)} %get-tuple-element.148), channel_id=1, source_target_pairs={{0,12},{1,13},{2,14},{3,15},{4,0},{5,1},{6,2},{7,3},{8,4},{9,5},{1... | collective-permute-start | bytes 626696 | tf_op jit(solution)/shard_map/ppermute | solution.py:48
  68.6 7.6 %collective-permute-start.8 = (f32[136,384]{1,0:T(8,128)S(1)}, f32[136,384]{1,0:T(8,128)S(1)}, u32[]{:S(2)}, u32[]{:S(2)}) collective-permute-start(f32[136,384]{1,0:T(8,128)S(1)} %get-tuple-element.149), channel_id=1, source_target_pairs={{0,8},{1,9},{2,10},{3,11},{4,12},{5,13},{6,14},{7,15},{8,0},{9,1},... | collective-permute-start | bytes 626696 | tf_op jit(solution)/shard_map/ppermute | solution.py:48
  80.1 3.5 %collective-permute-start.12 = (f32[384,1024]{1,0:T(8,128)S(1)}, f32[384,1024]{1,0:T(8,128)S(1)}, u32[]{:S(2)}, u32[]{:S(2)}) collective-permute-start(f32[384,1024]{1,0:T(8,128)S(1)} %get-tuple-element.171), channel_id=1, source_target_pairs={{0,16},{16,0},{32,48},{48,32},{64,80},{80,64},{96,112},{112,96},{1... | collective-permute-start | bytes 4718600 | tf_op jit(solution)/shard_map/ppermute | solution.py:48
  81.3 11.6 %collective-permute-start.13 = (f32[128,768]{1,0:T(8,128)S(1)}, f32[128,768]{1,0:T(8,128)S(1)}, u32[]{:S(2)}, u32[]{:S(2)}) collective-permute-start(f32[128,768]{1,0:T(8,128)S(1)} %get-tuple-element.178), channel_id=1, source_target_pairs={{0,1},{1,2},{2,3},{3,0},{4,5},{5,6},{6,7},{7,4},{8,9},{9,10},{10,1... | collective-permute-start | bytes 1179656 | tf_op jit(solution)/shard_map/ppermute | solution.py:48
  81.4 12.8 %collective-permute-start.14 = (f32[128,768]{1,0:T(8,128)S(1)}, f32[128,768]{1,0:T(8,128)S(1)}, u32[]{:S(2)}, u32[]{:S(2)}) collective-permute-start(f32[128,768]{1,0:T(8,128)S(1)} %get-tuple-element.179), channel_id=1, source_target_pairs={{0,3},{1,0},{2,1},{3,2},{4,7},{5,4},{6,5},{7,6},{8,11},{9,8},{10,9... | collective-permute-start | bytes 1179656 | tf_op jit(solution)/shard_map/ppermute | solution.py:48
  84.4 13.7 %collective-permute-start.17 = (f32[96,1024]{1,0:T(8,128)S(1)}, f32[96,1024]{1,0:T(8,128)S(1)}, u32[]{:S(2)}, u32[]{:S(2)}) collective-permute-start(f32[96,1024]{1,0:T(8,128)S(1)} %get-tuple-element.183), channel_id=1, source_target_pairs={{0,4},{1,5},{2,6},{3,7},{4,8},{5,9},{6,10},{7,11},{8,12},{9,13},{1... | collective-permute-start | bytes 1179656 | tf_op jit(solution)/shard_map/ppermute | solution.py:450
  85.6 12.5 %collective-permute-start.18 = (f32[96,1024]{1,0:T(8,128)S(1)}, f32[96,1024]{1,0:T(8,128)S(1)}, u32[]{:S(2)}, u32[]{:S(2)}) collective-permute-start(f32[96,1024]{1,0:T(8,128)S(1)} %get-tuple-element.184), channel_id=1, source_target_pairs={{0,8},{1,9},{2,10},{3,11},{4,12},{5,13},{6,14},{7,15},{8,0},{9,1},... | collective-permute-start | bytes 1179656 | tf_op jit(solution)/shard_map/ppermute | solution.py:450
  88.0 10.6 %collective-permute-start.19 = (f32[96,1024]{1,0:T(8,128)S(1)}, f32[96,1024]{1,0:T(8,128)S(1)}, u32[]{:S(2)}, u32[]{:S(2)}) collective-permute-start(f32[96,1024]{1,0:T(8,128)S(1)} %get-tuple-element.185), channel_id=1, source_target_pairs={{0,12},{1,13},{2,14},{3,15},{4,0},{5,1},{6,2},{7,3},{8,4},{9,5},{1... | collective-permute-start | bytes 1179656 | tf_op jit(solution)/shard_map/ppermute | solution.py:450
  94.8 48.5 %collective-permute-start.16 = (f32[256,768]{1,0:T(8,128)S(1)}, f32[256,768]{1,0:T(8,128)S(1)}, u32[]{:S(2)}, u32[]{:S(2)}) collective-permute-start(f32[256,768]{1,0:T(8,128)S(1)} %get-tuple-element.181), channel_id=1, source_target_pairs={{0,3},{1,0},{2,1},{3,2},{4,7},{5,4},{6,5},{7,6},{8,11},{9,8},{10,9... | collective-permute-start | bytes 2359304 | tf_op jit(solution)/shard_map/ppermute | solution.py:48
  95.4 48.0 %collective-permute-start.15 = (f32[256,768]{1,0:T(8,128)S(1)}, f32[256,768]{1,0:T(8,128)S(1)}, u32[]{:S(2)}, u32[]{:S(2)}) collective-permute-start(f32[256,768]{1,0:T(8,128)S(1)} %get-tuple-element.180), channel_id=1, source_target_pairs={{0,1},{1,2},{2,3},{3,0},{4,5},{5,6},{6,7},{7,4},{8,9},{9,10},{10,1... | collective-permute-start | bytes 2359304 | tf_op jit(solution)/shard_map/ppermute | solution.py:48
  99.3 6.7 %collective-permute-start.20 = (f32[24,1024]{1,0:T(8,128)S(1)}, f32[24,1024]{1,0:T(8,128)S(1)}, u32[]{:S(2)}, u32[]{:S(2)}) collective-permute-start(f32[24,1024]{1,0:T(8,128)S(1)} %get-tuple-element.187), channel_id=1, source_target_pairs={{0,32},{1,33},{2,34},{3,35},{4,36},{5,37},{6,38},{7,39},{8,40},{9,... | collective-permute-start | bytes 294920 | tf_op jit(solution)/shard_map/ppermute | solution.py:450
  101.3 7.2 %collective-permute-start.21 = (f32[24,1024]{1,0:T(8,128)S(1)}, f32[24,1024]{1,0:T(8,128)S(1)}, u32[]{:S(2)}, u32[]{:S(2)}) collective-permute-start(f32[24,1024]{1,0:T(8,128)S(1)} %get-tuple-element.188), channel_id=1, source_target_pairs={{0,64},{1,65},{2,66},{3,67},{4,68},{5,69},{6,70},{7,71},{8,72},{9,... | collective-permute-start | bytes 294920 | tf_op jit(solution)/shard_map/ppermute | solution.py:450
  104.9 4.6 %collective-permute-start.22 = (f32[24,1024]{1,0:T(8,128)S(1)}, f32[24,1024]{1,0:T(8,128)S(1)}, u32[]{:S(2)}, u32[]{:S(2)}) collective-permute-start(f32[24,1024]{1,0:T(8,128)S(1)} %get-tuple-element.189), channel_id=1, source_target_pairs={{0,96},{1,97},{2,98},{3,99},{4,100},{5,101},{6,102},{7,103},{8,104... | collective-permute-start | bytes 294920 | tf_op jit(solution)/shard_map/ppermute | solution.py:450
  110.2 7.0 %collective-permute-start.23 = (f32[40,384]{1,0:T(8,128)S(1)}, f32[40,384]{1,0:T(8,128)S(1)}, u32[]{:S(2)}, u32[]{:S(2)}) collective-permute-start(f32[40,384]{1,0:T(8,128)S(1)} %get-tuple-element.191), channel_id=1, source_target_pairs={{0,1},{1,2},{2,3},{3,0},{4,5},{5,6},{6,7},{7,4},{8,9},{9,10},{10,1... | collective-permute-start | bytes 184328 | tf_op jit(solution)/shard_map/ppermute | solution.py:48
  111.3 5.9 %collective-permute-start.24 = (f32[40,384]{1,0:T(8,128)S(1)}, f32[40,384]{1,0:T(8,128)S(1)}, u32[]{:S(2)}, u32[]{:S(2)}) collective-permute-start(f32[40,384]{1,0:T(8,128)S(1)} %get-tuple-element.192), channel_id=1, source_target_pairs={{0,2},{1,3},{2,0},{3,1},{4,6},{5,7},{6,4},{7,5},{8,10},{9,11},{10,... | collective-permute-start | bytes 184328 | tf_op jit(solution)/shard_map/ppermute | solution.py:48
  112.1 5.8 %collective-permute-start.25 = (f32[40,384]{1,0:T(8,128)S(1)}, f32[40,384]{1,0:T(8,128)S(1)}, u32[]{:S(2)}, u32[]{:S(2)}) collective-permute-start(f32[40,384]{1,0:T(8,128)S(1)} %get-tuple-element.193), channel_id=1, source_target_pairs={{0,3},{1,0},{2,1},{3,2},{4,7},{5,4},{6,5},{7,6},{8,11},{9,8},{10,9... | collective-permute-start | bytes 184328 | tf_op jit(solution)/shard_map/ppermute | solution.py:48
  117.9 26.3 %copy-start.1 = (bf16[768,1536]{1,0:T(8,128)(2,1)S(1)}, bf16[768,1536]{1,0:T(8,128)(2,1)}, u32[]{:S(2)}) copy-start(bf16[768,1536]{1,0:T(8,128)(2,1)} %param.9) | copy-start | bytes 7077892
  118.6 5.2 %collective-permute-start.29 = (f32[8,128]{1,0:T(8,128)S(1)}, f32[8,128]{1,0:T(8,128)S(1)}, u32[]{:S(2)}, u32[]{:S(2)}) collective-permute-start(f32[8,128]{1,0:T(8,128)S(1)} %shard_map.108), channel_id=1, source_target_pairs={{0,8},{1,9},{2,10},{3,11},{4,12},{5,13},{6,14},{7,15},{8,0},{9,1},... | collective-permute-start | bytes 12296 | tf_op jit(solution)/shard_map/ppermute | solution.py:48
  120.4 4.8 %collective-permute-start.27 = (f32[8,128]{1,0:T(8,128)S(1)}, f32[8,128]{1,0:T(8,128)S(1)}, u32[]{:S(2)}, u32[]{:S(2)}) collective-permute-start(f32[8,128]{1,0:T(8,128)S(1)} %shard_map.108), channel_id=1, source_target_pairs={{0,4},{1,5},{2,6},{3,7},{4,8},{5,9},{6,10},{7,11},{8,12},{9,13},{1... | collective-permute-start | bytes 12296 | tf_op jit(solution)/shard_map/ppermute | solution.py:48
  121.9 3.6 %collective-permute-start.28 = (f32[8,128]{1,0:T(8,128)S(1)}, f32[8,128]{1,0:T(8,128)S(1)}, u32[]{:S(2)}, u32[]{:S(2)}) collective-permute-start(f32[8,128]{1,0:T(8,128)S(1)} %shard_map.108), channel_id=1, source_target_pairs={{0,12},{1,13},{2,14},{3,15},{4,0},{5,1},{6,2},{7,3},{8,4},{9,5},{1... | collective-permute-start | bytes 12296 | tf_op jit(solution)/shard_map/ppermute | solution.py:48
  125.5 6.9 %collective-permute-start.32 = (f32[8,128]{1,0:T(8,128)S(1)}, f32[8,128]{1,0:T(8,128)S(1)}, u32[]{:S(2)}, u32[]{:S(2)}) collective-permute-start(f32[8,128]{1,0:T(8,128)S(1)} %add_add_fusion.1), channel_id=1, source_target_pairs={{0,64},{16,80},{32,96},{48,112},{64,0},{80,16},{96,32},{112,48},{1... | collective-permute-start | bytes 12296 | tf_op jit(solution)/shard_map/ppermute | solution.py:48
  129.2 9.6 %collective-permute-start.30 = (f32[8,128]{1,0:T(8,128)S(1)}, f32[8,128]{1,0:T(8,128)S(1)}, u32[]{:S(2)}, u32[]{:S(2)}) collective-permute-start(f32[8,128]{1,0:T(8,128)S(1)} %add_add_fusion.1), channel_id=1, source_target_pairs={{0,32},{16,48},{32,64},{48,80},{64,96},{80,112},{96,0},{112,16},{1... | collective-permute-start | bytes 12296 | tf_op jit(solution)/shard_map/ppermute | solution.py:48
  130.2 8.6 %collective-permute-start.31 = (f32[8,128]{1,0:T(8,128)S(1)}, f32[8,128]{1,0:T(8,128)S(1)}, u32[]{:S(2)}, u32[]{:S(2)}) collective-permute-start(f32[8,128]{1,0:T(8,128)S(1)} %add_add_fusion.1), channel_id=1, source_target_pairs={{0,96},{16,112},{32,0},{48,16},{64,32},{80,48},{96,64},{112,80},{1... | collective-permute-start | bytes 12296 | tf_op jit(solution)/shard_map/ppermute | solution.py:48
  132.4 9.7 %collective-permute-start.26 = (f32[24,384]{1,0:T(8,128)S(1)}, f32[24,384]{1,0:T(8,128)S(1)}, u32[]{:S(2)}, u32[]{:S(2)}) collective-permute-start(f32[24,384]{1,0:T(8,128)S(1)} %get-tuple-element.194), channel_id=1, source_target_pairs={{0,0},{1,32},{2,64},{3,96},{4,1},{5,33},{6,65},{7,97},{8,2},{9,34}... | collective-permute-start | bytes 110600 | tf_op jit(solution)/shard_map/ppermute | solution.py:554
  138.8 1.2 collective-permute-start.33

commit v10 on v9

--- a/solution.py
+++ b/solution.py
@@ -543,7 +543,6 @@
     r_a, r_b = move(d2a, "x", 1), move(d2b, "x", -1)
     s1, s3 = call(pass_kernel, [whole, whole], [], [at, d1, d3, r_a, r_b])
     m1, m3 = move(s1, "x", 1), move(s3, "x", -1)
-    d_tok = (d0 + m1 + m3).astype(BF16)
     terms = deal(at, 5, terms, 24, ALL)
     p0, p1, p2, p3, rows_out = call(
         cut_kernel, [((40, HC), F32)] * 4 + [((24, HC), F32)], [], [at, *terms]
@@ -555,7 +554,10 @@
     (square,) = call(square_kernel, [((8, 128), F32)], [], [at, *pieces])
     for axis in ("y", "z"):
         square = square + (move(square, axis, 1) + move(square, axis, 3) + move(square, axis, 2))
+    square, m1, m3, d0 = tie((square, m1, m3, d0))
+    d_tok = (d0 + m1 + m3).astype(BF16)
     square = square + move(square, "c", 1)
+    square, d_tok = tie((square, d_tok))
     all_in, all_bc, all_out = call(
         last_kernel,
         [((6, NX * HC), F32), ((6, 2 * NS), F32), ((12, DM), F32)],

time: 147 us -> 144 us (0.980); the launches traced: 144 us -> 143 us
  starting transfers between devices: 55.1 us -> 52.4 us
  waiting for transfers between devices: 45.5 us -> 47.4 us
    ppermute x1, starting transfers between devices: 6.33 us -> 4.69 us  [body(): rows_out = lax.ppermute(rows_out, ('rec', 'seq'), pairs)]
    ppermute x1, waiting for transfers between devices: 2.07 us -> 3.68 us  [body(): rows_out = lax.ppermute(rows_out, ('rec', 'seq'), pairs)]
  transfers between devices with their start and end apart: 34 -> 34, of which waited for: 19 -> 21; matrix products, arithmetic and copies ran while one was open for 2% -> 3% of each run, Pallas kernels for 22% -> 21%
where the time goes in v10:
time: 144 us; the launch traced here: 143 us
  starting transfers between devices  52.4 us (36%)
  waiting for transfers between devices  47.4 us (33%)
  Pallas kernels  35.7 us (25%)
  local copies, waits for them, and re-layouts  4.15 us (3%)
  other arithmetic  2.86 us (2%)
    ppermute x27, waiting for transfers between devices, move(): return lax.ppermute(value, name, pairs)  38.4 us
    ppermute x27, starting transfers between devices, move(): return lax.ppermute(value, name, pairs)  36.7 us
    pallas_call x16, Pallas kernels, call(): pl.pallas_call(kernel, out_shape=[jax.ShapeDtypeStruct(*o) for o in outs]...  35.7 us
    ppermute x6, starting transfers between devices, send(): return lax.ppermute(value, ('rec', 'seq'), pairs)  11 us
    ppermute x6, waiting for transfers between devices, send(): return lax.ppermute(value, ('rec', 'seq'), pairs)  5.29 us
    ppermute x1, starting transfers between devices, body(): rows_out = lax.ppermute(rows_out, ('rec', 'seq'), pairs)  4.69 us
    ppermute x1, waiting for transfers between devices, body(): rows_out = lax.ppermute(rows_out, ('rec', 'seq'), pairs)  3.68 us
  transfers between devices with their start and end apart: 34, of which 21 were waited for; matrix products, arithmetic and copies ran while one was open for 3% of the time, Pallas kernels for 21%

profile of v10, /device:TPU:6, one launch (start us, length us, event | category | flops | bytes accessed | tf_op | source)
XLA Modules:
  0.0 143.4 jit_solution(10106574959419446144)
XLA Ops:
  0.7 1.1 copy-done.4
  1.8 0.7 copy-done.6
  3.1 1.6 %collective-permute-start.2 = (f32[264,768]{1,0:T(8,128)S(1)}, f32[264,768]{1,0:T(8,128)S(1)}, u32[]{:S(2)}, u32[]{:S(2)}) collective-permute-start(f32[264,768]{1,0:T(8,128)S(1)} %shard_map.93), channel_id=1, source_target_pairs={{0,3},{1,0},{2,1},{3,2},{4,7},{5,4},{6,5},{7,6},{8,11},{9,8},{10,9... | collective-permute-start | bytes 2433032 | tf_op jit(solution)/shard_map/ppermute | solution.py:48
  4.7 2.0 %bitcast_convert_fusion = f32[256,768]{1,0:T(8,128)} fusion(bf16[1,256,768]{2,1,0:T(8,128)(2,1)} %param.7), kind=kLoop, calls=%fused_computation.5 | loop fusion | flops 196608 | bytes 1179648 | tf_op jit(solution)/shard_map/convert_element_type | solution.py:470
  6.7 15.9 %collective-permute-done.t3 = f32[264,768]{1,0:T(8,128)} collective-permute-done((f32[264,768]{1,0:T(8,128)S(1)}, f32[264,768]{1,0:T(8,128)}, u32[]{:S(2)}, u32[]{:S(2)}) %collective-permute-start) | collective-permute-done | bytes 811040 | tf_op jit(solution)/shard_map/ppermute | solution.py:48
  22.6 1.5 %collective-permute-start.1 = (f32[264,768]{1,0:T(8,128)}, f32[264,768]{1,0:T(8,128)}, u32[]{:S(2)}, u32[]{:S(2)}) collective-permute-start(f32[264,768]{1,0:T(8,128)} %collective-permute-done.t3), channel_id=1, source_target_pairs={{0,1},{1,2},{2,3},{3,0},{4,5},{5,6},{6,7},{7,4},{8,9},{9,10},{10,1... | collective-permute-start | bytes 2433032 | tf_op jit(solution)/shard_map/ppermute | solution.py:48
  24.1 0.9 copy-done.8
  25.0 0.5 collective-permute-start.3
  25.7 1.2 constant_dynamic-slice_fusion.w_out
  26.9 2.8 %collective-permute-start.4 = (f32[256,768]{1,0:T(8,128)}, f32[256,768]{1,0:T(8,128)S(1)}, u32[]{:S(2)}, u32[]{:S(2)}) collective-permute-start(f32[256,768]{1,0:T(8,128)} %bitcast_convert_fusion), channel_id=1, source_target_pairs={{0,1},{1,2},{2,3},{3,0},{4,5},{5,6},{6,7},{7,4},{8,9},{9,10},{10,1... | collective-permute-start | bytes 2359304 | tf_op jit(solution)/shard_map/ppermute | solution.py:48
  29.7 6.6 %shard_map.94 = (f32[3,8,256]{2,1,0:T(8,128)S(1)}, f32[3,8,256]{2,1,0:T(8,128)S(1)}, f32[3,256,384]{2,1,0:T(8,128)S(1)}, f32[3,256,384]{2,1,0:T(8,128)S(1)}, bf1...) custom-call(s32[6]{0:T(128)S(1)} %stack.27.at, ...), custom_call_target="tpu_custom_call" | custom-call | flops 905969664 | bytes 3022872 | tf_op jit(solution)/shard_map/pallas_call | solution.py:420
  36.3 3.5 %shard_map.95 = (bf16[3,6,256,256]{3,2,1,0:T(8,128)(2,1)S(1)}, bf16[3,6,256,256]{3,2,1,0:T(8,128)(2,1)S(1)}, f32[3,256,384]{2,1,0:T(8,128)S(1)}) custom-call(s32[6]{0:T(128)S(1)} %stack.27.at, f32[3,8,256]{2,1,0:T(8,128)S(1)} %get-tuple-element.126.cirow.refs_0_, f32[3,8,256]{2,1,0:T(8,128)S(1)} %get-tuple-element.127.cerow.refs_1_, ...), custom_call_target="tpu_custom_call" | custom-call | flops 301989888 | bytes 3391512 | tf_op jit(solution)/shard_map/pallas_call | solution.py:420
  39.8 4.6 %collective-permute-done.3.c1 = f32[256,768]{1,0:T(8,128)S(1)} collective-permute-done((f32[256,768]{1,0:T(8,128)}, f32[256,768]{1,0:T(8,128)S(1)}, u32[]{:S(2)}, u32[]{:S(2)}) %collective-permute-start.3) | collective-permute-done | bytes 786464 | tf_op jit(solution)/shard_map/ppermute | solution.py:48
  44.7 3.5 %shard_map.96 = (f32[4,8,256]{2,1,0:T(8,128)S(1)}, f32[4,8,256]{2,1,0:T(8,128)S(1)}, f32[4,256,384]{2,1,0:T(8,128)S(1)}, f32[4,256,384]{2,1,0:T(8,128)S(1)}, bf1...) custom-call(s32[6]{0:T(128)S(1)} %stack.27.at, ...), custom_call_target="tpu_custom_call" | custom-call | flops 301989888 | bytes 8724504 | tf_op jit(solution)/shard_map/pallas_call | solution.py:420
  48.3 1.6 %collective-permute-start.9 = (f32[136,384]{1,0:T(8,128)S(1)}, f32[136,384]{1,0:T(8,128)S(1)}, u32[]{:S(2)}, u32[]{:S(2)}) collective-permute-start(f32[136,384]{1,0:T(8,128)S(1)} %get-tuple-element.163), channel_id=1, source_target_pairs={{0,4},{1,5},{2,6},{3,7},{4,8},{5,9},{6,10},{7,11},{8,12},{9,13},{1... | collective-permute-start | bytes 626696 | tf_op jit(solution)/shard_map/ppermute | solution.py:48
  49.9 1.7 %collective-permute-start.10 = (f32[136,384]{1,0:T(8,128)S(1)}, f32[136,384]{1,0:T(8,128)S(1)}, u32[]{:S(2)}, u32[]{:S(2)}) collective-permute-start(f32[136,384]{1,0:T(8,128)S(1)} %get-tuple-element.164), channel_id=1, source_target_pairs={{0,12},{1,13},{2,14},{3,15},{4,0},{5,1},{6,2},{7,3},{8,4},{9,5},{1... | collective-permute-start | bytes 626696 | tf_op jit(solution)/shard_map/ppermute | solution.py:48
  51.6 2.0 %collective-permute-start.11 = (f32[136,384]{1,0:T(8,128)S(1)}, f32[136,384]{1,0:T(8,128)S(1)}, u32[]{:S(2)}, u32[]{:S(2)}) collective-permute-start(f32[136,384]{1,0:T(8,128)S(1)} %get-tuple-element.165), channel_id=1, source_target_pairs={{0,8},{1,9},{2,10},{3,11},{4,12},{5,13},{6,14},{7,15},{8,0},{9,1},... | collective-permute-start | bytes 626696 | tf_op jit(solution)/shard_map/ppermute | solution.py:48
  53.5 1.5 %shard_map.98 = (bf16[1,6,256,256]{3,2,1,0:T(8,128)(2,1)S(1)}, bf16[1,6,256,256]{3,2,1,0:T(8,128)(2,1)S(1)}, f32[1,256,384]{2,1,0:T(8,128)S(1)}) custom-call(s32[6]{0:T(128)S(1)} %stack.27.at, f32[4,8,256]{2,1,0:T(8,128)S(1)} %get-tuple-element.143.cirow, f32[4,8,256]{2,1,0:T(8,128)S(1)} %get-tuple-element.144.cerow, ...), custom_call_target="tpu_custom_call" | custom-call | flops 100663296 | bytes 4522008 | tf_op jit(solution)/shard_map/pallas_call | solution.py:420
  55.1 1.9 %shard_map.97 = (bf16[2,256,768]{2,1,0:T(8,128)(2,1)S(1)}, bf16[2,256,384]{2,1,0:T(8,128)(2,1)S(1)}, bf16[2,256,768]{2,1,0:T(8,128)(2,1)S(1)}, f32[2,128,768]{2,1,0:T(8,128)S(1)}) custom-call(s32[6]{0:T(128)S(1)} %stack.27.at, bf16[256,768]{1,0:T(8,128)(2,1)S(1)} %bitcast.11, f32[256,768]{1,0:T(8,128)S(1)} %collective-permute-done.3.c1, ...), custom_call_target="tpu_custom_call" | custom-call | flops 402653184 | bytes 5439512 | tf_op jit(solution)/shard_map/pallas_call | solution.py:420
  57.0 1.6 %collective-permute-done.4.c2 = f32[256,768]{1,0:T(8,128)S(1)} collective-permute-done((f32[256,768]{1,0:T(8,128)}, f32[256,768]{1,0:T(8,128)S(1)}, u32[]{:S(2)}, u32[]{:S(2)}) %collective-permute-start.4) | collective-permute-done | bytes 786464 | tf_op jit(solution)/shard_map/ppermute | solution.py:48
  58.6 4.1 %collective-permute-done.5.c3 = f32[256,768]{1,0:T(8,128)S(1)} collective-permute-done((f32[256,768]{1,0:T(8,128)S(1)}, f32[256,768]{1,0:T(8,128)S(1)}, u32[]{:S(2)}, u32[]{:S(2)}) %collective-permute-start.5) | collective-permute-done | bytes 786464 | tf_op jit(solution)/shard_map/ppermute | solution.py:48
  62.7 2.1 %shard_map.99 = (bf16[2,256,768]{2,1,0:T(8,128)(2,1)S(1)}, bf16[2,256,384]{2,1,0:T(8,128)(2,1)S(1)}, bf16[2,256,768]{2,1,0:T(8,128)(2,1)S(1)}, f32[2,4,128,384]{...) custom-call(s32[6]{0:T(128)S(1)} %stack.27.at, ...), custom_call_target="tpu_custom_call" | custom-call | flops 402653184 | bytes 6619160 | tf_op jit(solution)/shard_map/pallas_call | solution.py:420
  64.8 2.1 %collective-permute-start.6 = (f32[136,384]{1,0:T(8,128)S(1)}, f32[136,384]{1,0:T(8,128)S(1)}, u32[]{:S(2)}, u32[]{:S(2)}) collective-permute-start(f32[136,384]{1,0:T(8,128)S(1)} %get-tuple-element.153), channel_id=1, source_target_pairs={{0,4},{1,5},{2,6},{3,7},{4,8},{5,9},{6,10},{7,11},{8,12},{9,13},{1... | collective-permute-start | bytes 626696 | tf_op jit(solution)/shard_map/ppermute | solution.py:48
  66.9 1.7 %collective-permute-start.7 = (f32[136,384]{1,0:T(8,128)S(1)}, f32[136,384]{1,0:T(8,128)S(1)}, u32[]{:S(2)}, u32[]{:S(2)}) collective-permute-start(f32[136,384]{1,0:T(8,128)S(1)} %get-tuple-element.154), channel_id=1, source_target_pairs={{0,12},{1,13},{2,14},{3,15},{4,0},{5,1},{6,2},{7,3},{8,4},{9,5},{1... | collective-permute-start | bytes 626696 | tf_op jit(solution)/shard_map/ppermute | solution.py:48
  68.6 1.9 %collective-permute-start.8 = (f32[136,384]{1,0:T(8,128)S(1)}, f32[136,384]{1,0:T(8,128)S(1)}, u32[]{:S(2)}, u32[]{:S(2)}) collective-permute-start(f32[136,384]{1,0:T(8,128)S(1)} %get-tuple-element.155), channel_id=1, source_target_pairs={{0,8},{1,9},{2,10},{3,11},{4,12},{5,13},{6,14},{7,15},{8,0},{9,1},... | collective-permute-start | bytes 626696 | tf_op jit(solution)/shard_map/ppermute | solution.py:48
  70.6 5.1 %shard_map.100 = (f32[2,384,384]{2,1,0:T(8,128)S(1)}, f32[4,256,384]{2,1,0:T(8,128)S(1)}, f32[4,256,128]{2,1,0:T(8,128)S(1)}, f32[4,256,128]{2,1,0:T(8,128)S(1)}) custom-call(s32[6]{0:T(128)S(1)} %stack.27.at, bf16[4,256,384]{2,1,0:T(8,128)(2,1)S(1)} %get-tuple-element.145.xs, bf16[4,256,256]{2,1,0:T(8,128)(2,1)S(1)} %get-tuple-element.137.bc, ...), custom_call_target="tpu_custom_call" | custom-call | flops 2214592512 | bytes 18452504 | tf_op jit(solution)/shard_map/pallas_call | solution.py:420
  76.2 3.9 %shard_map.101 = (f32[384,1024]{1,0:T(8,128)S(1)}, f32[384,1024]{1,0:T(8,128)S(1)}, bf16[4,256,640]{2,1,0:T(8,128)(2,1)S(1)}) custom-call(s32[6]{0:T(128)S(1)} %stack.27.at, bf16[768,1024]{1,0:T(8,128)(2,1)S(1)} %get-tuple-element.135.tokt, bf16[4,256,768]{2,1,0:T(8,128)(2,1)S(1)} %get-tuple-element.136.xfr, bf16[4,256,256]{2,1,0:T(8,128)(2,1)S(1)} %get-tuple-element.137.bc, ...), custom_call_target="tpu_custom_call" | custom-call | flops 1409286144 | bytes 12816408 | tf_op jit(solution)/shard_map/pallas_call | solution.py:420
  80.2 1.0 shard_map.107
  81.4 2.0 %collective-permute-start.29 = (f32[128,768]{1,0:T(8,128)S(1)}, f32[128,768]{1,0:T(8,128)S(1)}, u32[]{:S(2)}, u32[]{:S(2)}) collective-permute-start(f32[128,768]{1,0:T(8,128)S(1)} %get-tuple-element.196), channel_id=1, source_target_pairs={{0,3},{1,0},{2,1},{3,2},{4,7},{5,4},{6,5},{7,6},{8,11},{9,8},{10,9... | collective-permute-start | bytes 1179656 | tf_op jit(solution)/shard_map/ppermute | solution.py:48
  83.6 0.8 shard_map.102
  84.4 1.2 collective-permute-start.13
  85.6 2.4 %collective-permute-start.14 = (f32[96,1024]{1,0:T(8,128)S(1)}, f32[96,1024]{1,0:T(8,128)S(1)}, u32[]{:S(2)}, u32[]{:S(2)}) collective-permute-start(f32[96,1024]{1,0:T(8,128)S(1)} %get-tuple-element.182), channel_id=1, source_target_pairs={{0,8},{1,9},{2,10},{3,11},{4,12},{5,13},{6,14},{7,15},{8,0},{9,1},... | collective-permute-start | bytes 1179656 | tf_op jit(solution)/shard_map/ppermute | solution.py:450
  88.0 0.8 collective-permute-start.15
  88.8 1.7 %shard_map.106 = (f32[256,768]{1,0:T(8,128)S(1)}, f32[256,768]{1,0:T(8,128)S(1)}, f32[256,768]{1,0:T(8,128)S(1)}) custom-call(s32[6]{0:T(128)S(1)} %stack.27.at, bf16[4,256,640]{2,1,0:T(8,128)(2,1)S(1)} %get-tuple-element.192.dz, bf16[768,384]{1,0:T(8,128)(2,1)S(1)} %constant_dynamic-slice_fusion.1.w_in, bf16[768,256]{1,0:T(8,128)(2,1)S(1)} %copy-done.2), custom_call_target="tpu_custom_call" | custom-call | flops 754974720 | bytes 2293784 | tf_op jit(solution)/shard_map/pallas_call | solution.py:420
  90.5 2.4 %collective-permute-done.28.r_a = f32[128,768]{1,0:T(8,128)S(1)} collective-permute-done((f32[128,768]{1,0:T(8,128)S(1)}, f32[128,768]{1,0:T(8,128)S(1)}, u32[]{:S(2)}, u32[]{:S(2)}) %collective-permute-start.28) | collective-permute-done | bytes 393248 | tf_op jit(solution)/shard_map/ppermute | solution.py:48
  92.9 1.3 collective-permute-done.29.r_b
  94.2 0.7 shard_map.108
  95.1 1.8 %collective-permute-start.31 = (f32[256,768]{1,0:T(8,128)S(1)}, f32[256,768]{1,0:T(8,128)S(1)}, u32[]{:S(2)}, u32[]{:S(2)}) collective-permute-start(f32[256,768]{1,0:T(8,128)S(1)} %get-tuple-element.198), channel_id=1, source_target_pairs={{0,3},{1,0},{2,1},{3,2},{4,7},{5,4},{6,5},{7,6},{8,11},{9,8},{10,9... | collective-permute-start | bytes 2359304 | tf_op jit(solution)/shard_map/ppermute | solution.py:48
  96.9 1.0 collective-permute-done.14.refs_2_
  98.0 0.6 collective-permute-done.15.refs_3_
  98.6 0.7 shard_map.103
  99.3 2.0 %collective-permute-start.16 = (f32[24,1024]{1,0:T(8,128)S(1)}, f32[24,1024]{1,0:T(8,128)S(1)}, u32[]{:S(2)}, u32[]{:S(2)}) collective-permute-start(f32[24,1024]{1,0:T(8,128)S(1)} %get-tuple-element.185), channel_id=1, source_target_pairs={{0,32},{1,33},{2,34},{3,35},{4,36},{5,37},{6,38},{7,39},{8,40},{9,... | collective-permute-start | bytes 294920 | tf_op jit(solution)/shard_map/ppermute | solution.py:450
  101.3 3.6 %collective-permute-start.17 = (f32[24,1024]{1,0:T(8,128)S(1)}, f32[24,1024]{1,0:T(8,128)S(1)}, u32[]{:S(2)}, u32[]{:S(2)}) collective-permute-start(f32[24,1024]{1,0:T(8,128)S(1)} %get-tuple-element.186), channel_id=1, source_target_pairs={{0,64},{1,65},{2,66},{3,67},{4,68},{5,69},{6,70},{7,71},{8,72},{9,... | collective-permute-start | bytes 294920 | tf_op jit(solution)/shard_map/ppermute | solution.py:450
  104.9 1.0 collective-permute-start.18
  106.0 2.5 %collective-permute-done.17.c = f32[24,1024]{1,0:T(8,128)S(1)} collective-permute-done((f32[24,1024]{1,0:T(8,128)S(1)}, f32[24,1024]{1,0:T(8,128)S(1)}, u32[]{:S(2)}, u32[]{:S(2)}) %collective-permute-start.17) | collective-permute-done | bytes 98336 | tf_op jit(solution)/shard_map/ppermute | solution.py:450
  108.5 1.0 collective-permute-done.18.d
  109.5 0.7 shard_map.104
  110.2 1.1 collective-permute-start.19
  111.3 0.8 collective-permute-start.20
  112.3 3.8 %collective-permute-done.19.b = f32[40,384]{1,0:T(8,128)S(1)} collective-permute-done((f32[40,384]{1,0:T(8,128)S(1)}, f32[40,384]{1,0:T(8,128)S(1)}, u32[]{:S(2)}, u32[]{:S(2)}) %collective-permute-start.19) | collective-permute-done | bytes 61472 | tf_op jit(solution)/shard_map/ppermute | solution.py:48
  116.0 1.1 collective-permute-done.20.c
  117.1 0.9 collective-permute-done.21.d
  118.0 0.7 shard_map.105
  118.7 1.8 %collective-permute-start.24 = (f32[8,128]{1,0:T(8,128)S(1)}, f32[8,128]{1,0:T(8,128)S(1)}, u32[]{:S(2)}, u32[]{:S(2)}) collective-permute-start(f32[8,128]{1,0:T(8,128)S(1)} %shard_map.105), channel_id=1, source_target_pairs={{0,8},{1,9},{2,10},{3,11},{4,12},{5,13},{6,14},{7,15},{8,0},{9,1},... | collective-permute-start | bytes 12296 | tf_op jit(solution)/shard_map/ppermute | solution.py:48
  120.5 1.4 collective-permute-start.22
  121.9 1.8 %collective-permute-start.23 = (f32[8,128]{1,0:T(8,128)S(1)}, f32[8,128]{1,0:T(8,128)S(1)}, u32[]{:S(2)}, u32[]{:S(2)}) collective-permute-start(f32[8,128]{1,0:T(8,128)S(1)} %shard_map.105), channel_id=1, source_target_pairs={{0,12},{1,13},{2,14},{3,15},{4,0},{5,1},{6,2},{7,3},{8,4},{9,5},{1... | collective-permute-start | bytes 12296 | tf_op jit(solution)/shard_map/ppermute | solution.py:48
  123.9 1.4 collective-permute-done.22
  125.5 3.7 %collective-permute-start.27 = (f32[8,128]{1,0:T(8,128)S(1)}, f32[8,128]{1,0:T(8,128)S(1)}, u32[]{:S(2)}, u32[]{:S(2)}) collective-permute-start(f32[8,128]{1,0:T(8,128)S(1)} %add_add_fusion.1), channel_id=1, source_target_pairs={{0,64},{16,80},{32,96},{48,112},{64,0},{80,16},{96,32},{112,48},{1... | collective-permute-start | bytes 12296 | tf_op jit(solution)/shard_map/ppermute | solution.py:48
  129.3 1.0 collective-permute-start.25
  130.3 2.2 %collective-permute-start.26 = (f32[8,128]{1,0:T(8,128)S(1)}, f32[8,128]{1,0:T(8,128)S(1)}, u32[]{:S(2)}, u32[]{:S(2)}) collective-permute-start(f32[8,128]{1,0:T(8,128)S(1)} %add_add_fusion.1), channel_id=1, source_target_pairs={{0,96},{16,112},{32,0},{48,16},{64,32},{80,48},{96,64},{112,80},{1... | collective-permute-start | bytes 12296 | tf_op jit(solution)/shard_map/ppermute | solution.py:48
  132.5 4.7 %collective-permute-start.33 = (f32[24,384]{1,0:T(8,128)S(1)}, f32[24,384]{1,0:T(8,128)S(1)}, u32[]{:S(2)}, u32[]{:S(2)}) collective-permute-start(f32[24,384]{1,0:T(8,128)S(1)} %get-tuple-element.205), channel_id=1, source_target_pairs={{0,0},{1,32},{2,64},{3,96},{4,1},{5,33},{6,65},{7,97},{8,2},{9,34}... | collective-permute-start | bytes 110600 | tf_op jit(solution)/shard_map/ppermute | solution.py:553
  137.4 0.9 add_convert_fusion
  138.5 3.7 %collective-permute-done.33.rows_out = f32[24,384]{1,0:T(8,128)S(1)} collective-permute-done((f32[24,384]{1,0:T(8,128)S(1)}, f32[24,384]{1,0:T(8,128)S(1)}, u32[]{:S(2)}, u32[]{:S(2)}) %collective-permute-start.33) | collective-permute-done | bytes 36896 | tf_op jit(solution)/shard_map/ppermute | solution.py:553
  142.2 1.2 shard_map.109
  (49 shorter events, 3.4 us)
Async XLA Ops:
  0.6 25.0 %copy-start = (bf16[768,1536]{1,0:T(8,128)(2,1)S(1)}, bf16[768,1536]{1,0:T(8,128)(2,1)}, u32[]{:S(2)}) copy-start(bf16[768,1536]{1,0:T(8,128)(2,1)} %param.9) | copy-start | bytes 7077892
  0.6 1.1 copy-start.4
  1.8 0.7 copy-start.6
  2.6 27.1 %copy-start.2 = (bf16[768,256]{1,0:T(8,128)(2,1)S(1)}, bf16[768,256]{1,0:T(8,128)(2,1)}, u32[]{:S(2)}) copy-start(bf16[768,256]{1,0:T(8,128)(2,1)} %w_bc.7) | copy-start | bytes 1179652
  2.6 20.0 %collective-permute-start = (f32[264,768]{1,0:T(8,128)S(1)}, f32[264,768]{1,0:T(8,128)}, u32[]{:S(2)}, u32[]{:S(2)}) collective-permute-start(f32[264,768]{1,0:T(8,128)S(1)} %shard_map.93), channel_id=1, source_target_pairs={{0,1},{1,2},{2,3},{3,0},{4,5},{5,6},{6,7},{7,4},{8,9},{9,10},{10,1... | collective-permute-start | bytes 2433032 | tf_op jit(solution)/shard_map/ppermute | solution.py:48
  3.1 21.0 %collective-permute-start.2 = (f32[264,768]{1,0:T(8,128)S(1)}, f32[264,768]{1,0:T(8,128)S(1)}, u32[]{:S(2)}, u32[]{:S(2)}) collective-permute-start(f32[264,768]{1,0:T(8,128)S(1)} %shard_map.93), channel_id=1, source_target_pairs={{0,3},{1,0},{2,1},{3,2},{4,7},{5,4},{6,5},{7,6},{8,11},{9,8},{10,9... | collective-permute-start | bytes 2433032 | tf_op jit(solution)/shard_map/ppermute | solution.py:48
  22.6 21.8 %collective-permute-start.1 = (f32[264,768]{1,0:T(8,128)}, f32[264,768]{1,0:T(8,128)}, u32[]{:S(2)}, u32[]{:S(2)}) collective-permute-start(f32[264,768]{1,0:T(8,128)} %collective-permute-done.t3), channel_id=1, source_target_pairs={{0,1},{1,2},{2,3},{3,0},{4,5},{5,6},{6,7},{7,4},{8,9},{9,10},{10,1... | collective-permute-start | bytes 2433032 | tf_op jit(solution)/shard_map/ppermute | solution.py:48
  24.1 0.9 copy-start.8
  25.0 19.4 %collective-permute-start.3 = (f32[256,768]{1,0:T(8,128)}, f32[256,768]{1,0:T(8,128)S(1)}, u32[]{:S(2)}, u32[]{:S(2)}) collective-permute-start(f32[256,768]{1,0:T(8,128)} %bitcast_convert_fusion), channel_id=1, source_target_pairs={{0,3},{1,0},{2,1},{3,2},{4,7},{5,4},{6,5},{7,6},{8,11},{9,8},{10,9... | collective-permute-start | bytes 2359304 | tf_op jit(solution)/shard_map/ppermute | solution.py:48
  25.6 4.1 %copy-start.5 = (bf16[1,256,768]{2,1,0:T(8,128)(2,1)S(1)}, bf16[1,256,768]{2,1,0:T(8,128)(2,1)}, u32[]{:S(2)}) copy-start(bf16[1,256,768]{2,1,0:T(8,128)(2,1)} %param.6) | copy-start | bytes 1179652
  25.6 4.1 %copy-start.7 = (f32[1,24,256]{2,1,0:T(8,128)S(1)}, f32[1,24,256]{2,1,0:T(8,128)}, u32[]{:S(2)}) copy-start(f32[1,24,256]{2,1,0:T(8,128)} %param.8) | copy-start | bytes 73732
  25.6 4.1 %copy-start.9 = (f32[264,768]{1,0:T(8,128)S(1)}, f32[264,768]{1,0:T(8,128)}, u32[]{:S(2)}) copy-start(f32[264,768]{1,0:T(8,128)} %copy-done.8) | copy-start | bytes 2433028
  26.9 31.7 %collective-permute-start.4 = (f32[256,768]{1,0:T(8,128)}, f32[256,768]{1,0:T(8,128)S(1)}, u32[]{:S(2)}, u32[]{:S(2)}) collective-permute-start(f32[256,768]{1,0:T(8,128)} %bitcast_convert_fusion), channel_id=1, source_target_pairs={{0,1},{1,2},{2,3},{3,0},{4,5},{5,6},{6,7},{7,4},{8,9},{9,10},{10,1... | collective-permute-start | bytes 2359304 | tf_op jit(solution)/shard_map/ppermute | solution.py:48
  44.4 18.3 %collective-permute-start.5 = (f32[256,768]{1,0:T(8,128)S(1)}, f32[256,768]{1,0:T(8,128)S(1)}, u32[]{:S(2)}, u32[]{:S(2)}) collective-permute-start(f32[256,768]{1,0:T(8,128)S(1)} %collective-permute-done.3.c1), channel_id=1, source_target_pairs={{0,3},{1,0},{2,1},{3,2},{4,7},{5,4},{6,5},{7,6},{8,11},{9,8},{10,9... | collective-permute-start | bytes 2359304 | tf_op jit(solution)/shard_map/ppermute | solution.py:48
  48.3 20.4 %collective-permute-start.9 = (f32[136,384]{1,0:T(8,128)S(1)}, f32[136,384]{1,0:T(8,128)S(1)}, u32[]{:S(2)}, u32[]{:S(2)}) collective-permute-start(f32[136,384]{1,0:T(8,128)S(1)} %get-tuple-element.163), channel_id=1, source_target_pairs={{0,4},{1,5},{2,6},{3,7},{4,8},{5,9},{6,10},{7,11},{8,12},{9,13},{1... | collective-permute-start | bytes 626696 | tf_op jit(solution)/shard_map/ppermute | solution.py:48
  49.9 20.7 %collective-permute-start.10 = (f32[136,384]{1,0:T(8,128)S(1)}, f32[136,384]{1,0:T(8,128)S(1)}, u32[]{:S(2)}, u32[]{:S(2)}) collective-permute-start(f32[136,384]{1,0:T(8,128)S(1)} %get-tuple-element.164), channel_id=1, source_target_pairs={{0,12},{1,13},{2,14},{3,15},{4,0},{5,1},{6,2},{7,3},{8,4},{9,5},{1... | collective-permute-start | bytes 626696 | tf_op jit(solution)/shard_map/ppermute | solution.py:48
  51.6 19.0 %collective-permute-start.11 = (f32[136,384]{1,0:T(8,128)S(1)}, f32[136,384]{1,0:T(8,128)S(1)}, u32[]{:S(2)}, u32[]{:S(2)}) collective-permute-start(f32[136,384]{1,0:T(8,128)S(1)} %get-tuple-element.165), channel_id=1, source_target_pairs={{0,8},{1,9},{2,10},{3,11},{4,12},{5,13},{6,14},{7,15},{8,0},{9,1},... | collective-permute-start | bytes 626696 | tf_op jit(solution)/shard_map/ppermute | solution.py:48
  53.5 1.5 %copy-start.3 = (bf16[1,256,768]{2,1,0:T(8,128)(2,1)S(1)}, bf16[1,256,768]{2,1,0:T(8,128)(2,1)}, u32[]{:S(2)}) copy-start(bf16[1,256,768]{2,1,0:T(8,128)(2,1)} %param.7) | copy-start | bytes 1179652
  64.8 10.8 %collective-permute-start.6 = (f32[136,384]{1,0:T(8,128)S(1)}, f32[136,384]{1,0:T(8,128)S(1)}, u32[]{:S(2)}, u32[]{:S(2)}) collective-permute-start(f32[136,384]{1,0:T(8,128)S(1)} %get-tuple-element.153), channel_id=1, source_target_pairs={{0,4},{1,5},{2,6},{3,7},{4,8},{5,9},{6,10},{7,11},{8,12},{9,13},{1... | collective-permute-start | bytes 626696 | tf_op jit(solution)/shard_map/ppermute | solution.py:48
  66.9 8.8 %collective-permute-start.7 = (f32[136,384]{1,0:T(8,128)S(1)}, f32[136,384]{1,0:T(8,128)S(1)}, u32[]{:S(2)}, u32[]{:S(2)}) collective-permute-start(f32[136,384]{1,0:T(8,128)S(1)} %get-tuple-element.154), channel_id=1, source_target_pairs={{0,12},{1,13},{2,14},{3,15},{4,0},{5,1},{6,2},{7,3},{8,4},{9,5},{1... | collective-permute-start | bytes 626696 | tf_op jit(solution)/shard_map/ppermute | solution.py:48
  68.6 7.6 %collective-permute-start.8 = (f32[136,384]{1,0:T(8,128)S(1)}, f32[136,384]{1,0:T(8,128)S(1)}, u32[]{:S(2)}, u32[]{:S(2)}) collective-permute-start(f32[136,384]{1,0:T(8,128)S(1)} %get-tuple-element.155), channel_id=1, source_target_pairs={{0,8},{1,9},{2,10},{3,11},{4,12},{5,13},{6,14},{7,15},{8,0},{9,1},... | collective-permute-start | bytes 626696 | tf_op jit(solution)/shard_map/ppermute | solution.py:48
  80.1 3.5 %collective-permute-start.12 = (f32[384,1024]{1,0:T(8,128)S(1)}, f32[384,1024]{1,0:T(8,128)S(1)}, u32[]{:S(2)}, u32[]{:S(2)}) collective-permute-start(f32[384,1024]{1,0:T(8,128)S(1)} %get-tuple-element.177), channel_id=1, source_target_pairs={{0,16},{16,0},{32,48},{48,32},{64,80},{80,64},{96,112},{112,96},{1... | collective-permute-start | bytes 4718600 | tf_op jit(solution)/shard_map/ppermute | solution.py:48
  81.3 11.6 %collective-permute-start.28 = (f32[128,768]{1,0:T(8,128)S(1)}, f32[128,768]{1,0:T(8,128)S(1)}, u32[]{:S(2)}, u32[]{:S(2)}) collective-permute-start(f32[128,768]{1,0:T(8,128)S(1)} %get-tuple-element.195), channel_id=1, source_target_pairs={{0,1},{1,2},{2,3},{3,0},{4,5},{5,6},{6,7},{7,4},{8,9},{9,10},{10,1... | collective-permute-start | bytes 1179656 | tf_op jit(solution)/shard_map/ppermute | solution.py:48
  81.4 12.8 %collective-permute-start.29 = (f32[128,768]{1,0:T(8,128)S(1)}, f32[128,768]{1,0:T(8,128)S(1)}, u32[]{:S(2)}, u32[]{:S(2)}) collective-permute-start(f32[128,768]{1,0:T(8,128)S(1)} %get-tuple-element.196), channel_id=1, source_target_pairs={{0,3},{1,0},{2,1},{3,2},{4,7},{5,4},{6,5},{7,6},{8,11},{9,8},{10,9... | collective-permute-start | bytes 1179656 | tf_op jit(solution)/shard_map/ppermute | solution.py:48
  84.4 12.5 %collective-permute-start.13 = (f32[96,1024]{1,0:T(8,128)S(1)}, f32[96,1024]{1,0:T(8,128)S(1)}, u32[]{:S(2)}, u32[]{:S(2)}) collective-permute-start(f32[96,1024]{1,0:T(8,128)S(1)} %get-tuple-element.181), channel_id=1, source_target_pairs={{0,4},{1,5},{2,6},{3,7},{4,8},{5,9},{6,10},{7,11},{8,12},{9,13},{1... | collective-permute-start | bytes 1179656 | tf_op jit(solution)/shard_map/ppermute | solution.py:450
  85.6 12.3 %collective-permute-start.14 = (f32[96,1024]{1,0:T(8,128)S(1)}, f32[96,1024]{1,0:T(8,128)S(1)}, u32[]{:S(2)}, u32[]{:S(2)}) collective-permute-start(f32[96,1024]{1,0:T(8,128)S(1)} %get-tuple-element.182), channel_id=1, source_target_pairs={{0,8},{1,9},{2,10},{3,11},{4,12},{5,13},{6,14},{7,15},{8,0},{9,1},... | collective-permute-start | bytes 1179656 | tf_op jit(solution)/shard_map/ppermute | solution.py:450
  88.0 10.6 %collective-permute-start.15 = (f32[96,1024]{1,0:T(8,128)S(1)}, f32[96,1024]{1,0:T(8,128)S(1)}, u32[]{:S(2)}, u32[]{:S(2)}) collective-permute-start(f32[96,1024]{1,0:T(8,128)S(1)} %get-tuple-element.183), channel_id=1, source_target_pairs={{0,12},{1,13},{2,14},{3,15},{4,0},{5,1},{6,2},{7,3},{8,4},{9,5},{1... | collective-permute-start | bytes 1179656 | tf_op jit(solution)/shard_map/ppermute | solution.py:450
  94.8 42.4 %collective-permute-start.30 = (f32[256,768]{1,0:T(8,128)S(1)}, f32[256,768]{1,0:T(8,128)S(1)}, u32[]{:S(2)}, u32[]{:S(2)}) collective-permute-start(f32[256,768]{1,0:T(8,128)S(1)} %get-tuple-element.197), channel_id=1, source_target_pairs={{0,1},{1,2},{2,3},{3,0},{4,5},{5,6},{6,7},{7,4},{8,9},{9,10},{10,1... | collective-permute-start | bytes 2359304 | tf_op jit(solution)/shard_map/ppermute | solution.py:48
  95.1 42.2 %collective-permute-start.31 = (f32[256,768]{1,0:T(8,128)S(1)}, f32[256,768]{1,0:T(8,128)S(1)}, u32[]{:S(2)}, u32[]{:S(2)}) collective-permute-start(f32[256,768]{1,0:T(8,128)S(1)} %get-tuple-element.198), channel_id=1, source_target_pairs={{0,3},{1,0},{2,1},{3,2},{4,7},{5,4},{6,5},{7,6},{8,11},{9,8},{10,9... | collective-permute-start | bytes 2359304 | tf_op jit(solution)/shard_map/ppermute | solution.py:48
  99.3 6.7 %collective-permute-start.16 = (f32[24,1024]{1,0:T(8,128)S(1)}, f32[24,1024]{1,0:T(8,128)S(1)}, u32[]{:S(2)}, u32[]{:S(2)}) collective-permute-start(f32[24,1024]{1,0:T(8,128)S(1)} %get-tuple-element.185), channel_id=1, source_target_pairs={{0,32},{1,33},{2,34},{3,35},{4,36},{5,37},{6,38},{7,39},{8,40},{9,... | collective-permute-start | bytes 294920 | tf_op jit(solution)/shard_map/ppermute | solution.py:450
  101.3 7.2 %collective-permute-start.17 = (f32[24,1024]{1,0:T(8,128)S(1)}, f32[24,1024]{1,0:T(8,128)S(1)}, u32[]{:S(2)}, u32[]{:S(2)}) collective-permute-start(f32[24,1024]{1,0:T(8,128)S(1)} %get-tuple-element.186), channel_id=1, source_target_pairs={{0,64},{1,65},{2,66},{3,67},{4,68},{5,69},{6,70},{7,71},{8,72},{9,... | collective-permute-start | bytes 294920 | tf_op jit(solution)/shard_map/ppermute | solution.py:450
  104.9 4.6 %collective-permute-start.18 = (f32[24,1024]{1,0:T(8,128)S(1)}, f32[24,1024]{1,0:T(8,128)S(1)}, u32[]{:S(2)}, u32[]{:S(2)}) collective-permute-start(f32[24,1024]{1,0:T(8,128)S(1)} %get-tuple-element.187), channel_id=1, source_target_pairs={{0,96},{1,97},{2,98},{3,99},{4,100},{5,101},{6,102},{7,103},{8,104... | collective-permute-start | bytes 294920 | tf_op jit(solution)/shard_map/ppermute | solution.py:450
  110.2 5.9 %collective-permute-start.19 = (f32[40,384]{1,0:T(8,128)S(1)}, f32[40,384]{1,0:T(8,128)S(1)}, u32[]{:S(2)}, u32[]{:S(2)}) collective-permute-start(f32[40,384]{1,0:T(8,128)S(1)} %get-tuple-element.189), channel_id=1, source_target_pairs={{0,1},{1,2},{2,3},{3,0},{4,5},{5,6},{6,7},{7,4},{8,9},{9,10},{10,1... | collective-permute-start | bytes 184328 | tf_op jit(solution)/shard_map/ppermute | solution.py:48
  111.3 5.8 %collective-permute-start.20 = (f32[40,384]{1,0:T(8,128)S(1)}, f32[40,384]{1,0:T(8,128)S(1)}, u32[]{:S(2)}, u32[]{:S(2)}) collective-permute-start(f32[40,384]{1,0:T(8,128)S(1)} %get-tuple-element.190), channel_id=1, source_target_pairs={{0,2},{1,3},{2,0},{3,1},{4,6},{5,7},{6,4},{7,5},{8,10},{9,11},{10,... | collective-permute-start | bytes 184328 | tf_op jit(solution)/shard_map/ppermute | solution.py:48
  112.1 6.0 %collective-permute-start.21 = (f32[40,384]{1,0:T(8,128)S(1)}, f32[40,384]{1,0:T(8,128)S(1)}, u32[]{:S(2)}, u32[]{:S(2)}) collective-permute-start(f32[40,384]{1,0:T(8,128)S(1)} %get-tuple-element.191), channel_id=1, source_target_pairs={{0,3},{1,0},{2,1},{3,2},{4,7},{5,4},{6,5},{7,6},{8,11},{9,8},{10,9... | collective-permute-start | bytes 184328 | tf_op jit(solution)/shard_map/ppermute | solution.py:48
  118.0 25.4 %copy-start.1 = (bf16[768,1536]{1,0:T(8,128)(2,1)S(1)}, bf16[768,1536]{1,0:T(8,128)(2,1)}, u32[]{:S(2)}) copy-start(bf16[768,1536]{1,0:T(8,128)(2,1)} %param.9) | copy-start | bytes 7077892
  118.7 5.2 %collective-permute-start.24 = (f32[8,128]{1,0:T(8,128)S(1)}, f32[8,128]{1,0:T(8,128)S(1)}, u32[]{:S(2)}, u32[]{:S(2)}) collective-permute-start(f32[8,128]{1,0:T(8,128)S(1)} %shard_map.105), channel_id=1, source_target_pairs={{0,8},{1,9},{2,10},{3,11},{4,12},{5,13},{6,14},{7,15},{8,0},{9,1},... | collective-permute-start | bytes 12296 | tf_op jit(solution)/shard_map/ppermute | solution.py:48
  120.5 4.8 %collective-permute-start.22 = (f32[8,128]{1,0:T(8,128)S(1)}, f32[8,128]{1,0:T(8,128)S(1)}, u32[]{:S(2)}, u32[]{:S(2)}) collective-permute-start(f32[8,128]{1,0:T(8,128)S(1)} %shard_map.105), channel_id=1, source_target_pairs={{0,4},{1,5},{2,6},{3,7},{4,8},{5,9},{6,10},{7,11},{8,12},{9,13},{1... | collective-permute-start | bytes 12296 | tf_op jit(solution)/shard_map/ppermute | solution.py:48
  121.9 3.6 %collective-permute-start.23 = (f32[8,128]{1,0:T(8,128)S(1)}, f32[8,128]{1,0:T(8,128)S(1)}, u32[]{:S(2)}, u32[]{:S(2)}) collective-permute-start(f32[8,128]{1,0:T(8,128)S(1)} %shard_map.105), channel_id=1, source_target_pairs={{0,12},{1,13},{2,14},{3,15},{4,0},{5,1},{6,2},{7,3},{8,4},{9,5},{1... | collective-permute-start | bytes 12296 | tf_op jit(solution)/shard_map/ppermute | solution.py:48
  125.5 7.0 %collective-permute-start.27 = (f32[8,128]{1,0:T(8,128)S(1)}, f32[8,128]{1,0:T(8,128)S(1)}, u32[]{:S(2)}, u32[]{:S(2)}) collective-permute-start(f32[8,128]{1,0:T(8,128)S(1)} %add_add_fusion.1), channel_id=1, source_target_pairs={{0,64},{16,80},{32,96},{48,112},{64,0},{80,16},{96,32},{112,48},{1... | collective-permute-start | bytes 12296 | tf_op jit(solution)/shard_map/ppermute | solution.py:48
  129.3 7.9 %collective-permute-start.25 = (f32[8,128]{1,0:T(8,128)S(1)}, f32[8,128]{1,0:T(8,128)S(1)}, u32[]{:S(2)}, u32[]{:S(2)}) collective-permute-start(f32[8,128]{1,0:T(8,128)S(1)} %add_add_fusion.1), channel_id=1, source_target_pairs={{0,32},{16,48},{32,64},{48,80},{64,96},{80,112},{96,0},{112,16},{1... | collective-permute-start | bytes 12296 | tf_op jit(solution)/shard_map/ppermute | solution.py:48
  130.3 6.9 %collective-permute-start.26 = (f32[8,128]{1,0:T(8,128)S(1)}, f32[8,128]{1,0:T(8,128)S(1)}, u32[]{:S(2)}, u32[]{:S(2)}) collective-permute-start(f32[8,128]{1,0:T(8,128)S(1)} %add_add_fusion.1), channel_id=1, source_target_pairs={{0,96},{16,112},{32,0},{48,16},{64,32},{80,48},{96,64},{112,80},{1... | collective-permute-start | bytes 12296 | tf_op jit(solution)/shard_map/ppermute | solution.py:48
  132.5 9.7 %collective-permute-start.33 = (f32[24,384]{1,0:T(8,128)S(1)}, f32[24,384]{1,0:T(8,128)S(1)}, u32[]{:S(2)}, u32[]{:S(2)}) collective-permute-start(f32[24,384]{1,0:T(8,128)S(1)} %get-tuple-element.205), channel_id=1, source_target_pairs={{0,0},{1,32},{2,64},{3,96},{4,1},{5,33},{6,65},{7,97},{8,2},{9,34}... | collective-permute-start | bytes 110600 | tf_op jit(solution)/shard_map/ppermute | solution.py:553
  137.3 1.2 collective-permute-start.32

commit v11 on v10

--- a/solution.py
+++ b/solution.py
@@ -552,8 +552,10 @@
     pairs = [(r * lanes + i, 2 * NZ * NY * (i % NX) + r * NY + i // NX) for r in range(2 * NZ) for i in range(lanes)]
     rows_out = lax.ppermute(rows_out, ("rec", "seq"), pairs)
     (square,) = call(square_kernel, [((8, 128), F32)], [], [at, *pieces])
-    for axis in ("y", "z"):
-        square = square + (move(square, axis, 1) + move(square, axis, 3) + move(square, axis, 2))
+    for partner in (lambda i: i ^ 1, lambda i: 3 - i):
+        square = square + lax.ppermute(square, "seq", [(i, partner(i // NX) * NX + i % NX) for i in range(lanes)])
+    for partner in (lambda i: i ^ 1, lambda i: 3 - i):
+        square = square + lax.ppermute(square, "rec", [(r, partner(r // 2) * 2 + r % 2) for r in range(2 * NZ)])
     square, m1, m3, d0 = tie((square, m1, m3, d0))
     d_tok = (d0 + m1 + m3).astype(BF16)
     square = square + move(square, "c", 1)

time: 144 us -> 156 us (1.083)
  waiting for transfers between devices: 47.4 us -> 66.6 us
  starting transfers between devices: 52.4 us -> 45.9 us
    ppermute x27 -> x21, starting transfers between devices: 36.7 us -> 25.2 us  [move(): return lax.ppermute(value, name, pairs)]
    ppermute x6, waiting for transfers between devices: 5.29 us -> 13.4 us  [send(): return lax.ppermute(value, ('rec', 'seq'), pairs)]
    ppermute x0 -> x4, waiting for transfers between devices: none -> 7.82 us  [the longest x2 4.76 us: body(): lax.ppermute(square, 'seq', [(i, partner(i // NX) * NX + i % NX) for i in...]
    ppermute x0 -> x4, starting transfers between devices: none -> 6.5 us  [the longest x2 3.75 us: body(): lax.ppermute(square, 'seq', [(i, partner(i // NX) * NX + i % NX) for i in...]
    ppermute x27 -> x21, waiting for transfers between devices: 38.4 us -> 40.8 us  [move(): return lax.ppermute(value, name, pairs)]
  transfers between devices with their start and end apart: 34 -> 32, of which waited for: 21 -> 22; matrix products, arithmetic and copies ran while one was open for 3% -> 3% of each run, Pallas kernels for 21% -> 19%
where the time goes in v11:
time: 156 us
  waiting for transfers between devices  66.6 us (43%)
  starting transfers between devices  45.9 us (29%)
  Pallas kernels  35.7 us (23%)
  local copies, waits for them, and re-layouts  4.15 us (3%)
  other arithmetic  2.82 us (2%)
    ppermute x21, waiting for transfers between devices, move(): return lax.ppermute(value, name, pairs)  40.8 us
    pallas_call x16, Pallas kernels, call(): pl.pallas_call(kernel, out_shape=[jax.ShapeDtypeStruct(*o) for o in outs]...  35.7 us
    ppermute x21, starting transfers between devices, move(): return lax.ppermute(value, name, pairs)  25.2 us
    ppermute x6, waiting for transfers between devices, send(): return lax.ppermute(value, ('rec', 'seq'), pairs)  13.4 us
    ppermute x6, starting transfers between devices, send(): return lax.ppermute(value, ('rec', 'seq'), pairs)  10.9 us
    ppermute x2, waiting for transfers between devices, body(): lax.ppermute(square, 'seq', [(i, partner(i // NX) * NX + i % NX) for i in...  4.76 us
    ppermute x1, waiting for transfers between devices, body(): rows_out = lax.ppermute(rows_out, ('rec', 'seq'), pairs)  4.54 us
    ppermute x2, starting transfers between devices, body(): lax.ppermute(square, 'seq', [(i, partner(i // NX) * NX + i % NX) for i in...  3.75 us
  transfers between devices with their start and end apart: 32, of which 22 were waited for; matrix products, arithmetic and copies ran while one was open for 3% of the time, Pallas kernels for 19%

profile of v11, /device:TPU:6, one launch (start us, length us, event | category | flops | bytes accessed | tf_op | source)
XLA Modules:
  0.0 156.0 jit_solution(13504423231865798241)
XLA Ops:
  0.7 1.1 copy-done.4
  1.8 0.7 copy-done.6
  3.1 1.6 %collective-permute-start.2 = (f32[264,768]{1,0:T(8,128)S(1)}, f32[264,768]{1,0:T(8,128)S(1)}, u32[]{:S(2)}, u32[]{:S(2)}) collective-permute-start(f32[264,768]{1,0:T(8,128)S(1)} %shard_map.93), channel_id=1, source_target_pairs={{0,3},{1,0},{2,1},{3,2},{4,7},{5,4},{6,5},{7,6},{8,11},{9,8},{10,9... | collective-permute-start | bytes 2433032 | tf_op jit(solution)/shard_map/ppermute | solution.py:48
  4.7 1.9 %bitcast_convert_fusion = f32[256,768]{1,0:T(8,128)} fusion(bf16[1,256,768]{2,1,0:T(8,128)(2,1)} %param.7), kind=kLoop, calls=%fused_computation.3 | loop fusion | flops 196608 | bytes 1179648 | tf_op jit(solution)/shard_map/convert_element_type | solution.py:470
  6.6 15.9 %collective-permute-done.t3 = f32[264,768]{1,0:T(8,128)} collective-permute-done((f32[264,768]{1,0:T(8,128)S(1)}, f32[264,768]{1,0:T(8,128)}, u32[]{:S(2)}, u32[]{:S(2)}) %collective-permute-start) | collective-permute-done | bytes 811040 | tf_op jit(solution)/shard_map/ppermute | solution.py:48
  22.6 1.5 collective-permute-start.1
  24.1 0.9 copy-done.8
  25.7 1.2 constant_dynamic-slice_fusion.w_out
  26.9 2.8 %collective-permute-start.4 = (f32[256,768]{1,0:T(8,128)}, f32[256,768]{1,0:T(8,128)S(1)}, u32[]{:S(2)}, u32[]{:S(2)}) collective-permute-start(f32[256,768]{1,0:T(8,128)} %bitcast_convert_fusion), channel_id=1, source_target_pairs={{0,1},{1,2},{2,3},{3,0},{4,5},{5,6},{6,7},{7,4},{8,9},{9,10},{10,1... | collective-permute-start | bytes 2359304 | tf_op jit(solution)/shard_map/ppermute | solution.py:48
  29.7 6.6 %shard_map.94 = (f32[3,8,256]{2,1,0:T(8,128)S(1)}, f32[3,8,256]{2,1,0:T(8,128)S(1)}, f32[3,256,384]{2,1,0:T(8,128)S(1)}, f32[3,256,384]{2,1,0:T(8,128)S(1)}, bf1...) custom-call(s32[6]{0:T(128)S(1)} %stack.27.at, ...), custom_call_target="tpu_custom_call" | custom-call | flops 905969664 | bytes 3022872 | tf_op jit(solution)/shard_map/pallas_call | solution.py:420
  36.3 3.5 %shard_map.95 = (bf16[3,6,256,256]{3,2,1,0:T(8,128)(2,1)S(1)}, bf16[3,6,256,256]{3,2,1,0:T(8,128)(2,1)S(1)}, f32[3,256,384]{2,1,0:T(8,128)S(1)}) custom-call(s32[6]{0:T(128)S(1)} %stack.27.at, f32[3,8,256]{2,1,0:T(8,128)S(1)} %get-tuple-element.126.cirow.refs_0_, f32[3,8,256]{2,1,0:T(8,128)S(1)} %get-tuple-element.127.cerow.refs_1_, ...), custom_call_target="tpu_custom_call" | custom-call | flops 301989888 | bytes 3391512 | tf_op jit(solution)/shard_map/pallas_call | solution.py:420
  39.8 4.6 %collective-permute-done.3.c1 = f32[256,768]{1,0:T(8,128)S(1)} collective-permute-done((f32[256,768]{1,0:T(8,128)}, f32[256,768]{1,0:T(8,128)S(1)}, u32[]{:S(2)}, u32[]{:S(2)}) %collective-permute-start.3) | collective-permute-done | bytes 786464 | tf_op jit(solution)/shard_map/ppermute | solution.py:48
  44.7 3.5 %shard_map.96 = (f32[4,8,256]{2,1,0:T(8,128)S(1)}, f32[4,8,256]{2,1,0:T(8,128)S(1)}, f32[4,256,384]{2,1,0:T(8,128)S(1)}, f32[4,256,384]{2,1,0:T(8,128)S(1)}, bf1...) custom-call(s32[6]{0:T(128)S(1)} %stack.27.at, ...), custom_call_target="tpu_custom_call" | custom-call | flops 301989888 | bytes 8724504 | tf_op jit(solution)/shard_map/pallas_call | solution.py:420
  48.3 1.6 %collective-permute-start.9 = (f32[136,384]{1,0:T(8,128)S(1)}, f32[136,384]{1,0:T(8,128)S(1)}, u32[]{:S(2)}, u32[]{:S(2)}) collective-permute-start(f32[136,384]{1,0:T(8,128)S(1)} %get-tuple-element.163), channel_id=1, source_target_pairs={{0,4},{1,5},{2,6},{3,7},{4,8},{5,9},{6,10},{7,11},{8,12},{9,13},{1... | collective-permute-start | bytes 626696 | tf_op jit(solution)/shard_map/ppermute | solution.py:48
  49.9 1.7 %collective-permute-start.10 = (f32[136,384]{1,0:T(8,128)S(1)}, f32[136,384]{1,0:T(8,128)S(1)}, u32[]{:S(2)}, u32[]{:S(2)}) collective-permute-start(f32[136,384]{1,0:T(8,128)S(1)} %get-tuple-element.164), channel_id=1, source_target_pairs={{0,12},{1,13},{2,14},{3,15},{4,0},{5,1},{6,2},{7,3},{8,4},{9,5},{1... | collective-permute-start | bytes 626696 | tf_op jit(solution)/shard_map/ppermute | solution.py:48
  51.6 2.0 %collective-permute-start.11 = (f32[136,384]{1,0:T(8,128)S(1)}, f32[136,384]{1,0:T(8,128)S(1)}, u32[]{:S(2)}, u32[]{:S(2)}) collective-permute-start(f32[136,384]{1,0:T(8,128)S(1)} %get-tuple-element.165), channel_id=1, source_target_pairs={{0,8},{1,9},{2,10},{3,11},{4,12},{5,13},{6,14},{7,15},{8,0},{9,1},... | collective-permute-start | bytes 626696 | tf_op jit(solution)/shard_map/ppermute | solution.py:48
  53.5 1.5 shard_map.98
  55.1 1.9 %shard_map.97 = (bf16[2,256,768]{2,1,0:T(8,128)(2,1)S(1)}, bf16[2,256,384]{2,1,0:T(8,128)(2,1)S(1)}, bf16[2,256,768]{2,1,0:T(8,128)(2,1)S(1)}, f32[2,128,768]{2,1,0:T(8,128)S(1)}) custom-call(s32[6]{0:T(128)S(1)} %stack.27.at, bf16[256,768]{1,0:T(8,128)(2,1)S(1)} %bitcast.11, f32[256,768]{1,0:T(8,128)S(1)} %collective-permute-done.3.c1, ...), custom_call_target="tpu_custom_call" | custom-call | flops 402653184 | bytes 5439512 | tf_op jit(solution)/shard_map/pallas_call | solution.py:420
  57.0 1.6 %collective-permute-done.4.c2 = f32[256,768]{1,0:T(8,128)S(1)} collective-permute-done((f32[256,768]{1,0:T(8,128)}, f32[256,768]{1,0:T(8,128)S(1)}, u32[]{:S(2)}, u32[]{:S(2)}) %collective-permute-start.4) | collective-permute-done | bytes 786464 | tf_op jit(solution)/shard_map/ppermute | solution.py:48
  58.6 4.1 %collective-permute-done.5.c3 = f32[256,768]{1,0:T(8,128)S(1)} collective-permute-done((f32[256,768]{1,0:T(8,128)S(1)}, f32[256,768]{1,0:T(8,128)S(1)}, u32[]{:S(2)}, u32[]{:S(2)}) %collective-permute-start.5) | collective-permute-done | bytes 786464 | tf_op jit(solution)/shard_map/ppermute | solution.py:48
  62.7 2.1 %shard_map.99 = (bf16[2,256,768]{2,1,0:T(8,128)(2,1)S(1)}, bf16[2,256,384]{2,1,0:T(8,128)(2,1)S(1)}, bf16[2,256,768]{2,1,0:T(8,128)(2,1)S(1)}, f32[2,4,128,384]{...) custom-call(s32[6]{0:T(128)S(1)} %stack.27.at, ...), custom_call_target="tpu_custom_call" | custom-call | flops 402653184 | bytes 6619160 | tf_op jit(solution)/shard_map/pallas_call | solution.py:420
  64.8 2.1 %collective-permute-start.6 = (f32[136,384]{1,0:T(8,128)S(1)}, f32[136,384]{1,0:T(8,128)S(1)}, u32[]{:S(2)}, u32[]{:S(2)}) collective-permute-start(f32[136,384]{1,0:T(8,128)S(1)} %get-tuple-element.153), channel_id=1, source_target_pairs={{0,4},{1,5},{2,6},{3,7},{4,8},{5,9},{6,10},{7,11},{8,12},{9,13},{1... | collective-permute-start | bytes 626696 | tf_op jit(solution)/shard_map/ppermute | solution.py:48
  66.9 1.7 %collective-permute-start.7 = (f32[136,384]{1,0:T(8,128)S(1)}, f32[136,384]{1,0:T(8,128)S(1)}, u32[]{:S(2)}, u32[]{:S(2)}) collective-permute-start(f32[136,384]{1,0:T(8,128)S(1)} %get-tuple-element.154), channel_id=1, source_target_pairs={{0,12},{1,13},{2,14},{3,15},{4,0},{5,1},{6,2},{7,3},{8,4},{9,5},{1... | collective-permute-start | bytes 626696 | tf_op jit(solution)/shard_map/ppermute | solution.py:48
  68.6 1.9 %collective-permute-start.8 = (f32[136,384]{1,0:T(8,128)S(1)}, f32[136,384]{1,0:T(8,128)S(1)}, u32[]{:S(2)}, u32[]{:S(2)}) collective-permute-start(f32[136,384]{1,0:T(8,128)S(1)} %get-tuple-element.155), channel_id=1, source_target_pairs={{0,8},{1,9},{2,10},{3,11},{4,12},{5,13},{6,14},{7,15},{8,0},{9,1},... | collective-permute-start | bytes 626696 | tf_op jit(solution)/shard_map/ppermute | solution.py:48
  70.6 5.1 %shard_map.100 = (f32[2,384,384]{2,1,0:T(8,128)S(1)}, f32[4,256,384]{2,1,0:T(8,128)S(1)}, f32[4,256,128]{2,1,0:T(8,128)S(1)}, f32[4,256,128]{2,1,0:T(8,128)S(1)}) custom-call(s32[6]{0:T(128)S(1)} %stack.27.at, bf16[4,256,384]{2,1,0:T(8,128)(2,1)S(1)} %get-tuple-element.145.xs, bf16[4,256,256]{2,1,0:T(8,128)(2,1)S(1)} %get-tuple-element.137.bc, ...), custom_call_target="tpu_custom_call" | custom-call | flops 2214592512 | bytes 18452504 | tf_op jit(solution)/shard_map/pallas_call | solution.py:420
  76.2 3.9 %shard_map.101 = (f32[384,1024]{1,0:T(8,128)S(1)}, f32[384,1024]{1,0:T(8,128)S(1)}, bf16[4,256,640]{2,1,0:T(8,128)(2,1)S(1)}) custom-call(s32[6]{0:T(128)S(1)} %stack.27.at, bf16[768,1024]{1,0:T(8,128)(2,1)S(1)} %get-tuple-element.135.tokt, bf16[4,256,768]{2,1,0:T(8,128)(2,1)S(1)} %get-tuple-element.136.xfr, bf16[4,256,256]{2,1,0:T(8,128)(2,1)S(1)} %get-tuple-element.137.bc, ...), custom_call_target="tpu_custom_call" | custom-call | flops 1409286144 | bytes 12816408 | tf_op jit(solution)/shard_map/pallas_call | solution.py:420
  80.2 1.0 shard_map.107
  81.4 2.0 %collective-permute-start.27 = (f32[128,768]{1,0:T(8,128)S(1)}, f32[128,768]{1,0:T(8,128)S(1)}, u32[]{:S(2)}, u32[]{:S(2)}) collective-permute-start(f32[128,768]{1,0:T(8,128)S(1)} %get-tuple-element.196), channel_id=1, source_target_pairs={{0,3},{1,0},{2,1},{3,2},{4,7},{5,4},{6,5},{7,6},{8,11},{9,8},{10,9... | collective-permute-start | bytes 1179656 | tf_op jit(solution)/shard_map/ppermute | solution.py:48
  83.6 0.8 shard_map.102
  84.4 1.7 %shard_map.106 = (f32[256,768]{1,0:T(8,128)S(1)}, f32[256,768]{1,0:T(8,128)S(1)}, f32[256,768]{1,0:T(8,128)S(1)}) custom-call(s32[6]{0:T(128)S(1)} %stack.27.at, bf16[4,256,640]{2,1,0:T(8,128)(2,1)S(1)} %get-tuple-element.192.dz, bf16[768,384]{1,0:T(8,128)(2,1)S(1)} %constant_dynamic-slice_fusion.1.w_in, bf16[768,256]{1,0:T(8,128)(2,1)S(1)} %copy-done.2), custom_call_target="tpu_custom_call" | custom-call | flops 754974720 | bytes 2293784 | tf_op jit(solution)/shard_map/pallas_call | solution.py:420
  86.1 6.8 %collective-permute-done.26.r_a = f32[128,768]{1,0:T(8,128)S(1)} collective-permute-done((f32[128,768]{1,0:T(8,128)S(1)}, f32[128,768]{1,0:T(8,128)S(1)}, u32[]{:S(2)}, u32[]{:S(2)}) %collective-permute-start.26) | collective-permute-done | bytes 393248 | tf_op jit(solution)/shard_map/ppermute | solution.py:48
  92.9 1.3 collective-permute-done.27.r_b
  94.2 0.7 shard_map.108
  95.1 1.8 %collective-permute-start.29 = (f32[256,768]{1,0:T(8,128)S(1)}, f32[256,768]{1,0:T(8,128)S(1)}, u32[]{:S(2)}, u32[]{:S(2)}) collective-permute-start(f32[256,768]{1,0:T(8,128)S(1)} %get-tuple-element.198), channel_id=1, source_target_pairs={{0,3},{1,0},{2,1},{3,2},{4,7},{5,4},{6,5},{7,6},{8,11},{9,8},{10,9... | collective-permute-start | bytes 2359304 | tf_op jit(solution)/shard_map/ppermute | solution.py:48
  96.9 1.1 collective-permute-start.13
  98.1 2.4 %collective-permute-start.14 = (f32[96,1024]{1,0:T(8,128)S(1)}, f32[96,1024]{1,0:T(8,128)S(1)}, u32[]{:S(2)}, u32[]{:S(2)}) collective-permute-start(f32[96,1024]{1,0:T(8,128)S(1)} %get-tuple-element.182), channel_id=1, source_target_pairs={{0,8},{1,9},{2,10},{3,11},{4,12},{5,13},{6,14},{7,15},{8,0},{9,1},... | collective-permute-start | bytes 1179656 | tf_op jit(solution)/shard_map/ppermute | solution.py:450
  100.4 0.8 collective-permute-start.15
  101.3 4.7 %collective-permute-done.13.refs_1_ = f32[96,1024]{1,0:T(8,128)S(1)} collective-permute-done((f32[96,1024]{1,0:T(8,128)S(1)}, f32[96,1024]{1,0:T(8,128)S(1)}, u32[]{:S(2)}, u32[]{:S(2)}) %collective-permute-start.13) | collective-permute-done | bytes 393248 | tf_op jit(solution)/shard_map/ppermute | solution.py:450
  105.9 4.5 %collective-permute-done.14.refs_2_ = f32[96,1024]{1,0:T(8,128)S(1)} collective-permute-done((f32[96,1024]{1,0:T(8,128)S(1)}, f32[96,1024]{1,0:T(8,128)S(1)}, u32[]{:S(2)}, u32[]{:S(2)}) %collective-permute-start.14) | collective-permute-done | bytes 393248 | tf_op jit(solution)/shard_map/ppermute | solution.py:450
  110.4 0.6 collective-permute-done.15.refs_3_
  111.0 0.7 shard_map.103
  111.7 2.0 %collective-permute-start.16 = (f32[24,1024]{1,0:T(8,128)S(1)}, f32[24,1024]{1,0:T(8,128)S(1)}, u32[]{:S(2)}, u32[]{:S(2)}) collective-permute-start(f32[24,1024]{1,0:T(8,128)S(1)} %get-tuple-element.185), channel_id=1, source_target_pairs={{0,32},{1,33},{2,34},{3,35},{4,36},{5,37},{6,38},{7,39},{8,40},{9,... | collective-permute-start | bytes 294920 | tf_op jit(solution)/shard_map/ppermute | solution.py:450
  113.7 3.6 %collective-permute-start.17 = (f32[24,1024]{1,0:T(8,128)S(1)}, f32[24,1024]{1,0:T(8,128)S(1)}, u32[]{:S(2)}, u32[]{:S(2)}) collective-permute-start(f32[24,1024]{1,0:T(8,128)S(1)} %get-tuple-element.186), channel_id=1, source_target_pairs={{0,64},{1,65},{2,66},{3,67},{4,68},{5,69},{6,70},{7,71},{8,72},{9,... | collective-permute-start | bytes 294920 | tf_op jit(solution)/shard_map/ppermute | solution.py:450
  117.3 1.0 collective-permute-start.18
  118.4 2.5 %collective-permute-done.17.c = f32[24,1024]{1,0:T(8,128)S(1)} collective-permute-done((f32[24,1024]{1,0:T(8,128)S(1)}, f32[24,1024]{1,0:T(8,128)S(1)}, u32[]{:S(2)}, u32[]{:S(2)}) %collective-permute-start.17) | collective-permute-done | bytes 98336 | tf_op jit(solution)/shard_map/ppermute | solution.py:450
  120.9 1.0 collective-permute-done.18.d
  121.9 0.7 shard_map.104
  122.6 1.5 collective-permute-start.19
  124.1 1.1 collective-permute-start.20
  125.2 1.7 %collective-permute-done.19.b = f32[40,384]{1,0:T(8,128)S(1)} collective-permute-done((f32[40,384]{1,0:T(8,128)S(1)}, f32[40,384]{1,0:T(8,128)S(1)}, u32[]{:S(2)}, u32[]{:S(2)}) %collective-permute-start.19) | collective-permute-done | bytes 61472 | tf_op jit(solution)/shard_map/ppermute | solution.py:48
  126.9 2.9 %collective-permute-done.20.c = f32[40,384]{1,0:T(8,128)S(1)} collective-permute-done((f32[40,384]{1,0:T(8,128)S(1)}, f32[40,384]{1,0:T(8,128)S(1)}, u32[]{:S(2)}, u32[]{:S(2)}) %collective-permute-start.20) | collective-permute-done | bytes 61472 | tf_op jit(solution)/shard_map/ppermute | solution.py:48
  129.8 0.8 collective-permute-done.21.d
  130.6 0.7 shard_map.105
  131.3 1.1 collective-permute-start.22
  132.4 2.6 %collective-permute-done.22 = f32[8,128]{1,0:T(8,128)S(1)} collective-permute-done((f32[8,128]{1,0:T(8,128)S(1)}, f32[8,128]{1,0:T(8,128)S(1)}, u32[]{:S(2)}, u32[]{:S(2)}) %collective-permute-start.22) | collective-permute-done | bytes 4128 | tf_op jit(solution)/shard_map/ppermute | solution.py:556
  135.0 2.6 %collective-permute-start.23 = (f32[8,128]{1,0:T(8,128)S(1)}, f32[8,128]{1,0:T(8,128)S(1)}, u32[]{:S(2)}, u32[]{:S(2)}) collective-permute-start(f32[8,128]{1,0:T(8,128)S(1)} %add.37), channel_id=1, source_target_pairs={{0,12},{1,13},{2,14},{3,15},{4,8},{5,9},{6,10},{7,11},{8,4},{9,5},... | collective-permute-start | bytes 12296 | tf_op jit(solution)/shard_map/ppermute | solution.py:556
  137.6 2.2 %collective-permute-done.23 = f32[8,128]{1,0:T(8,128)S(1)} collective-permute-done((f32[8,128]{1,0:T(8,128)S(1)}, f32[8,128]{1,0:T(8,128)S(1)}, u32[]{:S(2)}, u32[]{:S(2)}) %collective-permute-start.23) | collective-permute-done | bytes 4128 | tf_op jit(solution)/shard_map/ppermute | solution.py:556
  139.8 0.5 collective-permute-start.24
  140.4 3.1 %collective-permute-done.24 = f32[8,128]{1,0:T(8,128)S(1)} collective-permute-done((f32[8,128]{1,0:T(8,128)S(1)}, f32[8,128]{1,0:T(8,128)S(1)}, u32[]{:S(2)}, u32[]{:S(2)}) %collective-permute-start.24) | collective-permute-done | bytes 4128 | tf_op jit(solution)/shard_map/ppermute | solution.py:558
  143.4 2.2 %collective-permute-start.25 = (f32[8,128]{1,0:T(8,128)S(1)}, f32[8,128]{1,0:T(8,128)S(1)}, u32[]{:S(2)}, u32[]{:S(2)}) collective-permute-start(f32[8,128]{1,0:T(8,128)S(1)} %add.39), channel_id=1, source_target_pairs={{0,96},{16,112},{32,64},{48,80},{64,32},{80,48},{96,0},{112,16},{1... | collective-permute-start | bytes 12296 | tf_op jit(solution)/shard_map/ppermute | solution.py:558
  145.7 3.3 %collective-permute-start.31 = (f32[24,384]{1,0:T(8,128)S(1)}, f32[24,384]{1,0:T(8,128)S(1)}, u32[]{:S(2)}, u32[]{:S(2)}) collective-permute-start(f32[24,384]{1,0:T(8,128)S(1)} %get-tuple-element.205), channel_id=1, source_target_pairs={{0,0},{1,32},{2,64},{3,96},{4,1},{5,33},{6,65},{7,97},{8,2},{9,34}... | collective-permute-start | bytes 110600 | tf_op jit(solution)/shard_map/ppermute | solution.py:553
  149.1 0.9 add_convert_fusion
  150.3 4.5 %collective-permute-done.31.rows_out = f32[24,384]{1,0:T(8,128)S(1)} collective-permute-done((f32[24,384]{1,0:T(8,128)S(1)}, f32[24,384]{1,0:T(8,128)S(1)}, u32[]{:S(2)}, u32[]{:S(2)}) %collective-permute-start.31) | collective-permute-done | bytes 36896 | tf_op jit(solution)/shard_map/ppermute | solution.py:553
  154.8 1.2 shard_map.109
  (47 shorter events, 3.3 us)
Async XLA Ops:
  0.6 25.0 %copy-start = (bf16[768,1536]{1,0:T(8,128)(2,1)S(1)}, bf16[768,1536]{1,0:T(8,128)(2,1)}, u32[]{:S(2)}) copy-start(bf16[768,1536]{1,0:T(8,128)(2,1)} %param.9) | copy-start | bytes 7077892
  0.6 1.1 copy-start.4
  1.8 0.7 copy-start.6
  2.6 27.1 %copy-start.2 = (bf16[768,256]{1,0:T(8,128)(2,1)S(1)}, bf16[768,256]{1,0:T(8,128)(2,1)}, u32[]{:S(2)}) copy-start(bf16[768,256]{1,0:T(8,128)(2,1)} %w_bc.7) | copy-start | bytes 1179652
  2.6 20.0 %collective-permute-start = (f32[264,768]{1,0:T(8,128)S(1)}, f32[264,768]{1,0:T(8,128)}, u32[]{:S(2)}, u32[]{:S(2)}) collective-permute-start(f32[264,768]{1,0:T(8,128)S(1)} %shard_map.93), channel_id=1, source_target_pairs={{0,1},{1,2},{2,3},{3,0},{4,5},{5,6},{6,7},{7,4},{8,9},{9,10},{10,1... | collective-permute-start | bytes 2433032 | tf_op jit(solution)/shard_map/ppermute | solution.py:48
  3.1 21.0 %collective-permute-start.2 = (f32[264,768]{1,0:T(8,128)S(1)}, f32[264,768]{1,0:T(8,128)S(1)}, u32[]{:S(2)}, u32[]{:S(2)}) collective-permute-start(f32[264,768]{1,0:T(8,128)S(1)} %shard_map.93), channel_id=1, source_target_pairs={{0,3},{1,0},{2,1},{3,2},{4,7},{5,4},{6,5},{7,6},{8,11},{9,8},{10,9... | collective-permute-start | bytes 2433032 | tf_op jit(solution)/shard_map/ppermute | solution.py:48
  22.6 21.8 %collective-permute-start.1 = (f32[264,768]{1,0:T(8,128)}, f32[264,768]{1,0:T(8,128)}, u32[]{:S(2)}, u32[]{:S(2)}) collective-permute-start(f32[264,768]{1,0:T(8,128)} %collective-permute-done.t3), channel_id=1, source_target_pairs={{0,1},{1,2},{2,3},{3,0},{4,5},{5,6},{6,7},{7,4},{8,9},{9,10},{10,1... | collective-permute-start | bytes 2433032 | tf_op jit(solution)/shard_map/ppermute | solution.py:48
  24.1 0.9 copy-start.8
  25.0 19.4 %collective-permute-start.3 = (f32[256,768]{1,0:T(8,128)}, f32[256,768]{1,0:T(8,128)S(1)}, u32[]{:S(2)}, u32[]{:S(2)}) collective-permute-start(f32[256,768]{1,0:T(8,128)} %bitcast_convert_fusion), channel_id=1, source_target_pairs={{0,3},{1,0},{2,1},{3,2},{4,7},{5,4},{6,5},{7,6},{8,11},{9,8},{10,9... | collective-permute-start | bytes 2359304 | tf_op jit(solution)/shard_map/ppermute | solution.py:48
  25.6 4.1 %copy-start.5 = (bf16[1,256,768]{2,1,0:T(8,128)(2,1)S(1)}, bf16[1,256,768]{2,1,0:T(8,128)(2,1)}, u32[]{:S(2)}) copy-start(bf16[1,256,768]{2,1,0:T(8,128)(2,1)} %param.6) | copy-start | bytes 1179652
  25.6 4.1 %copy-start.7 = (f32[1,24,256]{2,1,0:T(8,128)S(1)}, f32[1,24,256]{2,1,0:T(8,128)}, u32[]{:S(2)}) copy-start(f32[1,24,256]{2,1,0:T(8,128)} %param.8) | copy-start | bytes 73732
  25.6 4.1 %copy-start.9 = (f32[264,768]{1,0:T(8,128)S(1)}, f32[264,768]{1,0:T(8,128)}, u32[]{:S(2)}) copy-start(f32[264,768]{1,0:T(8,128)} %copy-done.8) | copy-start | bytes 2433028
  26.9 31.7 %collective-permute-start.4 = (f32[256,768]{1,0:T(8,128)}, f32[256,768]{1,0:T(8,128)S(1)}, u32[]{:S(2)}, u32[]{:S(2)}) collective-permute-start(f32[256,768]{1,0:T(8,128)} %bitcast_convert_fusion), channel_id=1, source_target_pairs={{0,1},{1,2},{2,3},{3,0},{4,5},{5,6},{6,7},{7,4},{8,9},{9,10},{10,1... | collective-permute-start | bytes 2359304 | tf_op jit(solution)/shard_map/ppermute | solution.py:48
  44.4 18.3 %collective-permute-start.5 = (f32[256,768]{1,0:T(8,128)S(1)}, f32[256,768]{1,0:T(8,128)S(1)}, u32[]{:S(2)}, u32[]{:S(2)}) collective-permute-start(f32[256,768]{1,0:T(8,128)S(1)} %collective-permute-done.3.c1), channel_id=1, source_target_pairs={{0,3},{1,0},{2,1},{3,2},{4,7},{5,4},{6,5},{7,6},{8,11},{9,8},{10,9... | collective-permute-start | bytes 2359304 | tf_op jit(solution)/shard_map/ppermute | solution.py:48
  48.3 20.4 %collective-permute-start.9 = (f32[136,384]{1,0:T(8,128)S(1)}, f32[136,384]{1,0:T(8,128)S(1)}, u32[]{:S(2)}, u32[]{:S(2)}) collective-permute-start(f32[136,384]{1,0:T(8,128)S(1)} %get-tuple-element.163), channel_id=1, source_target_pairs={{0,4},{1,5},{2,6},{3,7},{4,8},{5,9},{6,10},{7,11},{8,12},{9,13},{1... | collective-permute-start | bytes 626696 | tf_op jit(solution)/shard_map/ppermute | solution.py:48
  49.9 20.7 %collective-permute-start.10 = (f32[136,384]{1,0:T(8,128)S(1)}, f32[136,384]{1,0:T(8,128)S(1)}, u32[]{:S(2)}, u32[]{:S(2)}) collective-permute-start(f32[136,384]{1,0:T(8,128)S(1)} %get-tuple-element.164), channel_id=1, source_target_pairs={{0,12},{1,13},{2,14},{3,15},{4,0},{5,1},{6,2},{7,3},{8,4},{9,5},{1... | collective-permute-start | bytes 626696 | tf_op jit(solution)/shard_map/ppermute | solution.py:48
  51.6 19.0 %collective-permute-start.11 = (f32[136,384]{1,0:T(8,128)S(1)}, f32[136,384]{1,0:T(8,128)S(1)}, u32[]{:S(2)}, u32[]{:S(2)}) collective-permute-start(f32[136,384]{1,0:T(8,128)S(1)} %get-tuple-element.165), channel_id=1, source_target_pairs={{0,8},{1,9},{2,10},{3,11},{4,12},{5,13},{6,14},{7,15},{8,0},{9,1},... | collective-permute-start | bytes 626696 | tf_op jit(solution)/shard_map/ppermute | solution.py:48
  53.5 1.5 copy-start.3
  64.8 10.8 %collective-permute-start.6 = (f32[136,384]{1,0:T(8,128)S(1)}, f32[136,384]{1,0:T(8,128)S(1)}, u32[]{:S(2)}, u32[]{:S(2)}) collective-permute-start(f32[136,384]{1,0:T(8,128)S(1)} %get-tuple-element.153), channel_id=1, source_target_pairs={{0,4},{1,5},{2,6},{3,7},{4,8},{5,9},{6,10},{7,11},{8,12},{9,13},{1... | collective-permute-start | bytes 626696 | tf_op jit(solution)/shard_map/ppermute | solution.py:48
  66.9 8.8 %collective-permute-start.7 = (f32[136,384]{1,0:T(8,128)S(1)}, f32[136,384]{1,0:T(8,128)S(1)}, u32[]{:S(2)}, u32[]{:S(2)}) collective-permute-start(f32[136,384]{1,0:T(8,128)S(1)} %get-tuple-element.154), channel_id=1, source_target_pairs={{0,12},{1,13},{2,14},{3,15},{4,0},{5,1},{6,2},{7,3},{8,4},{9,5},{1... | collective-permute-start | bytes 626696 | tf_op jit(solution)/shard_map/ppermute | solution.py:48
  68.6 7.6 %collective-permute-start.8 = (f32[136,384]{1,0:T(8,128)S(1)}, f32[136,384]{1,0:T(8,128)S(1)}, u32[]{:S(2)}, u32[]{:S(2)}) collective-permute-start(f32[136,384]{1,0:T(8,128)S(1)} %get-tuple-element.155), channel_id=1, source_target_pairs={{0,8},{1,9},{2,10},{3,11},{4,12},{5,13},{6,14},{7,15},{8,0},{9,1},... | collective-permute-start | bytes 626696 | tf_op jit(solution)/shard_map/ppermute | solution.py:48
  80.1 3.5 %collective-permute-start.12 = (f32[384,1024]{1,0:T(8,128)S(1)}, f32[384,1024]{1,0:T(8,128)S(1)}, u32[]{:S(2)}, u32[]{:S(2)}) collective-permute-start(f32[384,1024]{1,0:T(8,128)S(1)} %get-tuple-element.177), channel_id=1, source_target_pairs={{0,16},{16,0},{32,48},{48,32},{64,80},{80,64},{96,112},{112,96},{1... | collective-permute-start | bytes 4718600 | tf_op jit(solution)/shard_map/ppermute | solution.py:48
  81.3 11.6 %collective-permute-start.26 = (f32[128,768]{1,0:T(8,128)S(1)}, f32[128,768]{1,0:T(8,128)S(1)}, u32[]{:S(2)}, u32[]{:S(2)}) collective-permute-start(f32[128,768]{1,0:T(8,128)S(1)} %get-tuple-element.195), channel_id=1, source_target_pairs={{0,1},{1,2},{2,3},{3,0},{4,5},{5,6},{6,7},{7,4},{8,9},{9,10},{10,1... | collective-permute-start | bytes 1179656 | tf_op jit(solution)/shard_map/ppermute | solution.py:48
  81.4 12.8 %collective-permute-start.27 = (f32[128,768]{1,0:T(8,128)S(1)}, f32[128,768]{1,0:T(8,128)S(1)}, u32[]{:S(2)}, u32[]{:S(2)}) collective-permute-start(f32[128,768]{1,0:T(8,128)S(1)} %get-tuple-element.196), channel_id=1, source_target_pairs={{0,3},{1,0},{2,1},{3,2},{4,7},{5,4},{6,5},{7,6},{8,11},{9,8},{10,9... | collective-permute-start | bytes 1179656 | tf_op jit(solution)/shard_map/ppermute | solution.py:48
  94.8 54.2 %collective-permute-start.28 = (f32[256,768]{1,0:T(8,128)S(1)}, f32[256,768]{1,0:T(8,128)S(1)}, u32[]{:S(2)}, u32[]{:S(2)}) collective-permute-start(f32[256,768]{1,0:T(8,128)S(1)} %get-tuple-element.197), channel_id=1, source_target_pairs={{0,1},{1,2},{2,3},{3,0},{4,5},{5,6},{6,7},{7,4},{8,9},{9,10},{10,1... | collective-permute-start | bytes 2359304 | tf_op jit(solution)/shard_map/ppermute | solution.py:48
  95.1 53.9 %collective-permute-start.29 = (f32[256,768]{1,0:T(8,128)S(1)}, f32[256,768]{1,0:T(8,128)S(1)}, u32[]{:S(2)}, u32[]{:S(2)}) collective-permute-start(f32[256,768]{1,0:T(8,128)S(1)} %get-tuple-element.198), channel_id=1, source_target_pairs={{0,3},{1,0},{2,1},{3,2},{4,7},{5,4},{6,5},{7,6},{8,11},{9,8},{10,9... | collective-permute-start | bytes 2359304 | tf_op jit(solution)/shard_map/ppermute | solution.py:48
  96.9 9.0 %collective-permute-start.13 = (f32[96,1024]{1,0:T(8,128)S(1)}, f32[96,1024]{1,0:T(8,128)S(1)}, u32[]{:S(2)}, u32[]{:S(2)}) collective-permute-start(f32[96,1024]{1,0:T(8,128)S(1)} %get-tuple-element.181), channel_id=1, source_target_pairs={{0,4},{1,5},{2,6},{3,7},{4,8},{5,9},{6,10},{7,11},{8,12},{9,13},{1... | collective-permute-start | bytes 1179656 | tf_op jit(solution)/shard_map/ppermute | solution.py:450
  98.1 12.3 %collective-permute-start.14 = (f32[96,1024]{1,0:T(8,128)S(1)}, f32[96,1024]{1,0:T(8,128)S(1)}, u32[]{:S(2)}, u32[]{:S(2)}) collective-permute-start(f32[96,1024]{1,0:T(8,128)S(1)} %get-tuple-element.182), channel_id=1, source_target_pairs={{0,8},{1,9},{2,10},{3,11},{4,12},{5,13},{6,14},{7,15},{8,0},{9,1},... | collective-permute-start | bytes 1179656 | tf_op jit(solution)/shard_map/ppermute | solution.py:450
  100.4 10.6 %collective-permute-start.15 = (f32[96,1024]{1,0:T(8,128)S(1)}, f32[96,1024]{1,0:T(8,128)S(1)}, u32[]{:S(2)}, u32[]{:S(2)}) collective-permute-start(f32[96,1024]{1,0:T(8,128)S(1)} %get-tuple-element.183), channel_id=1, source_target_pairs={{0,12},{1,13},{2,14},{3,15},{4,0},{5,1},{6,2},{7,3},{8,4},{9,5},{1... | collective-permute-start | bytes 1179656 | tf_op jit(solution)/shard_map/ppermute | solution.py:450
  111.7 6.7 %collective-permute-start.16 = (f32[24,1024]{1,0:T(8,128)S(1)}, f32[24,1024]{1,0:T(8,128)S(1)}, u32[]{:S(2)}, u32[]{:S(2)}) collective-permute-start(f32[24,1024]{1,0:T(8,128)S(1)} %get-tuple-element.185), channel_id=1, source_target_pairs={{0,32},{1,33},{2,34},{3,35},{4,36},{5,37},{6,38},{7,39},{8,40},{9,... | collective-permute-start | bytes 294920 | tf_op jit(solution)/shard_map/ppermute | solution.py:450
  113.7 7.2 %collective-permute-start.17 = (f32[24,1024]{1,0:T(8,128)S(1)}, f32[24,1024]{1,0:T(8,128)S(1)}, u32[]{:S(2)}, u32[]{:S(2)}) collective-permute-start(f32[24,1024]{1,0:T(8,128)S(1)} %get-tuple-element.186), channel_id=1, source_target_pairs={{0,64},{1,65},{2,66},{3,67},{4,68},{5,69},{6,70},{7,71},{8,72},{9,... | collective-permute-start | bytes 294920 | tf_op jit(solution)/shard_map/ppermute | solution.py:450
  117.3 4.6 %collective-permute-start.18 = (f32[24,1024]{1,0:T(8,128)S(1)}, f32[24,1024]{1,0:T(8,128)S(1)}, u32[]{:S(2)}, u32[]{:S(2)}) collective-permute-start(f32[24,1024]{1,0:T(8,128)S(1)} %get-tuple-element.187), channel_id=1, source_target_pairs={{0,96},{1,97},{2,98},{3,99},{4,100},{5,101},{6,102},{7,103},{8,104... | collective-permute-start | bytes 294920 | tf_op jit(solution)/shard_map/ppermute | solution.py:450
  122.6 4.3 %collective-permute-start.19 = (f32[40,384]{1,0:T(8,128)S(1)}, f32[40,384]{1,0:T(8,128)S(1)}, u32[]{:S(2)}, u32[]{:S(2)}) collective-permute-start(f32[40,384]{1,0:T(8,128)S(1)} %get-tuple-element.189), channel_id=1, source_target_pairs={{0,1},{1,2},{2,3},{3,0},{4,5},{5,6},{6,7},{7,4},{8,9},{9,10},{10,1... | collective-permute-start | bytes 184328 | tf_op jit(solution)/shard_map/ppermute | solution.py:48
  124.1 5.7 %collective-permute-start.20 = (f32[40,384]{1,0:T(8,128)S(1)}, f32[40,384]{1,0:T(8,128)S(1)}, u32[]{:S(2)}, u32[]{:S(2)}) collective-permute-start(f32[40,384]{1,0:T(8,128)S(1)} %get-tuple-element.190), channel_id=1, source_target_pairs={{0,2},{1,3},{2,0},{3,1},{4,6},{5,7},{6,4},{7,5},{8,10},{9,11},{10,... | collective-permute-start | bytes 184328 | tf_op jit(solution)/shard_map/ppermute | solution.py:48
  125.2 5.4 %collective-permute-start.21 = (f32[40,384]{1,0:T(8,128)S(1)}, f32[40,384]{1,0:T(8,128)S(1)}, u32[]{:S(2)}, u32[]{:S(2)}) collective-permute-start(f32[40,384]{1,0:T(8,128)S(1)} %get-tuple-element.191), channel_id=1, source_target_pairs={{0,3},{1,0},{2,1},{3,2},{4,7},{5,4},{6,5},{7,6},{8,11},{9,8},{10,9... | collective-permute-start | bytes 184328 | tf_op jit(solution)/shard_map/ppermute | solution.py:48
  130.6 25.4 %copy-start.1 = (bf16[768,1536]{1,0:T(8,128)(2,1)S(1)}, bf16[768,1536]{1,0:T(8,128)(2,1)}, u32[]{:S(2)}) copy-start(bf16[768,1536]{1,0:T(8,128)(2,1)} %param.9) | copy-start | bytes 7077892
  131.3 3.7 %collective-permute-start.22 = (f32[8,128]{1,0:T(8,128)S(1)}, f32[8,128]{1,0:T(8,128)S(1)}, u32[]{:S(2)}, u32[]{:S(2)}) collective-permute-start(f32[8,128]{1,0:T(8,128)S(1)} %shard_map.105), channel_id=1, source_target_pairs={{0,4},{1,5},{2,6},{3,7},{4,0},{5,1},{6,2},{7,3},{8,12},{9,13},{10,... | collective-permute-start | bytes 12296 | tf_op jit(solution)/shard_map/ppermute | solution.py:556
  135.0 4.8 %collective-permute-start.23 = (f32[8,128]{1,0:T(8,128)S(1)}, f32[8,128]{1,0:T(8,128)S(1)}, u32[]{:S(2)}, u32[]{:S(2)}) collective-permute-start(f32[8,128]{1,0:T(8,128)S(1)} %add.37), channel_id=1, source_target_pairs={{0,12},{1,13},{2,14},{3,15},{4,8},{5,9},{6,10},{7,11},{8,4},{9,5},... | collective-permute-start | bytes 12296 | tf_op jit(solution)/shard_map/ppermute | solution.py:556
  139.8 3.6 %collective-permute-start.24 = (f32[8,128]{1,0:T(8,128)S(1)}, f32[8,128]{1,0:T(8,128)S(1)}, u32[]{:S(2)}, u32[]{:S(2)}) collective-permute-start(f32[8,128]{1,0:T(8,128)S(1)} %add.38), channel_id=1, source_target_pairs={{0,32},{16,48},{32,0},{48,16},{64,96},{80,112},{96,64},{112,80},{1... | collective-permute-start | bytes 12296 | tf_op jit(solution)/shard_map/ppermute | solution.py:558
  143.4 5.5 %collective-permute-start.25 = (f32[8,128]{1,0:T(8,128)S(1)}, f32[8,128]{1,0:T(8,128)S(1)}, u32[]{:S(2)}, u32[]{:S(2)}) collective-permute-start(f32[8,128]{1,0:T(8,128)S(1)} %add.39), channel_id=1, source_target_pairs={{0,96},{16,112},{32,64},{48,80},{64,32},{80,48},{96,0},{112,16},{1... | collective-permute-start | bytes 12296 | tf_op jit(solution)/shard_map/ppermute | solution.py:558
  145.7 9.2 %collective-permute-start.31 = (f32[24,384]{1,0:T(8,128)S(1)}, f32[24,384]{1,0:T(8,128)S(1)}, u32[]{:S(2)}, u32[]{:S(2)}) collective-permute-start(f32[24,384]{1,0:T(8,128)S(1)} %get-tuple-element.205), channel_id=1, source_target_pairs={{0,0},{1,32},{2,64},{3,96},{4,1},{5,33},{6,65},{7,97},{8,2},{9,34}... | collective-permute-start | bytes 110600 | tf_op jit(solution)/shard_map/ppermute | solution.py:553
  149.0 1.2 collective-permute-start.30

commit v12 on v10

--- a/solution.py
+++ b/solution.py
@@ -554,6 +554,7 @@
     (square,) = call(square_kernel, [((8, 128), F32)], [], [at, *pieces])
     for axis in ("y", "z"):
         square = square + (move(square, axis, 1) + move(square, axis, 3) + move(square, axis, 2))
+        square, rows_out = tie((square, rows_out))
     square, m1, m3, d0 = tie((square, m1, m3, d0))
     d_tok = (d0 + m1 + m3).astype(BF16)
     square = square + move(square, "c", 1)

time: 144 us -> 148 us (1.028); the launches traced: 143 us -> 146 us
  starting transfers between devices: 52.4 us -> 55.7 us
    ppermute x1, starting transfers between devices: 4.69 us -> 6.71 us  [body(): rows_out = lax.ppermute(rows_out, ('rec', 'seq'), pairs)]
  transfers between devices with their start and end apart: 34 -> 34, of which waited for: 21 -> 20; matrix products, arithmetic and copies ran while one was open for 3% -> 3% of each run, Pallas kernels for 21% -> 21%
where the time goes in v12:
time: 148 us; the launch traced here: 146 us
  starting transfers between devices  55.7 us (38%)
  waiting for transfers between devices  46.5 us (31%)
  Pallas kernels  35.7 us (24%)
  local copies, waits for them, and re-layouts  4.15 us (3%)
  other arithmetic  2.87 us (2%)
    ppermute x27, waiting for transfers between devices, move(): return lax.ppermute(value, name, pairs)  38.5 us
    ppermute x27, starting transfers between devices, move(): return lax.ppermute(value, name, pairs)  38 us
    pallas_call x16, Pallas kernels, call(): pl.pallas_call(kernel, out_shape=[jax.ShapeDtypeStruct(*o) for o in outs]...  35.7 us
    ppermute x6, starting transfers between devices, send(): return lax.ppermute(value, ('rec', 'seq'), pairs)  11 us
    ppermute x1, starting transfers between devices, body(): rows_out = lax.ppermute(rows_out, ('rec', 'seq'), pairs)  6.71 us
    ppermute x6, waiting for transfers between devices, send(): return lax.ppermute(value, ('rec', 'seq'), pairs)  5.29 us
  transfers between devices with their start and end apart: 34, of which 20 were waited for; matrix products, arithmetic and copies ran while one was open for 3% of the time, Pallas kernels for 21%

profile of v12, /device:TPU:6, one launch (start us, length us, event | category | flops | bytes accessed | tf_op | source)
XLA Modules:
  0.0 145.9 jit_solution(8918751167647775008)
XLA Ops:
  0.7 1.1 copy-done.4
  1.8 0.7 copy-done.6
  3.1 1.6 %collective-permute-start.2 = (f32[264,768]{1,0:T(8,128)S(1)}, f32[264,768]{1,0:T(8,128)S(1)}, u32[]{:S(2)}, u32[]{:S(2)}) collective-permute-start(f32[264,768]{1,0:T(8,128)S(1)} %shard_map.93), channel_id=1, source_target_pairs={{0,3},{1,0},{2,1},{3,2},{4,7},{5,4},{6,5},{7,6},{8,11},{9,8},{10,9... | collective-permute-start | bytes 2433032 | tf_op jit(solution)/shard_map/ppermute | solution.py:48
  4.7 2.0 %bitcast_convert_fusion = f32[256,768]{1,0:T(8,128)} fusion(bf16[1,256,768]{2,1,0:T(8,128)(2,1)} %param.7), kind=kLoop, calls=%fused_computation.5 | loop fusion | flops 196608 | bytes 1179648 | tf_op jit(solution)/shard_map/convert_element_type | solution.py:470
  6.7 15.9 %collective-permute-done.t3 = f32[264,768]{1,0:T(8,128)} collective-permute-done((f32[264,768]{1,0:T(8,128)S(1)}, f32[264,768]{1,0:T(8,128)}, u32[]{:S(2)}, u32[]{:S(2)}) %collective-permute-start) | collective-permute-done | bytes 811040 | tf_op jit(solution)/shard_map/ppermute | solution.py:48
  22.6 1.5 %collective-permute-start.1 = (f32[264,768]{1,0:T(8,128)}, f32[264,768]{1,0:T(8,128)}, u32[]{:S(2)}, u32[]{:S(2)}) collective-permute-start(f32[264,768]{1,0:T(8,128)} %collective-permute-done.t3), channel_id=1, source_target_pairs={{0,1},{1,2},{2,3},{3,0},{4,5},{5,6},{6,7},{7,4},{8,9},{9,10},{10,1... | collective-permute-start | bytes 2433032 | tf_op jit(solution)/shard_map/ppermute | solution.py:48
  24.1 0.9 copy-done.8
  25.0 0.5 collective-permute-start.3
  25.7 1.2 constant_dynamic-slice_fusion.w_out
  26.9 2.8 %collective-permute-start.4 = (f32[256,768]{1,0:T(8,128)}, f32[256,768]{1,0:T(8,128)S(1)}, u32[]{:S(2)}, u32[]{:S(2)}) collective-permute-start(f32[256,768]{1,0:T(8,128)} %bitcast_convert_fusion), channel_id=1, source_target_pairs={{0,1},{1,2},{2,3},{3,0},{4,5},{5,6},{6,7},{7,4},{8,9},{9,10},{10,1... | collective-permute-start | bytes 2359304 | tf_op jit(solution)/shard_map/ppermute | solution.py:48
  29.7 6.6 %shard_map.94 = (f32[3,8,256]{2,1,0:T(8,128)S(1)}, f32[3,8,256]{2,1,0:T(8,128)S(1)}, f32[3,256,384]{2,1,0:T(8,128)S(1)}, f32[3,256,384]{2,1,0:T(8,128)S(1)}, bf1...) custom-call(s32[6]{0:T(128)S(1)} %stack.27.at, ...), custom_call_target="tpu_custom_call" | custom-call | flops 905969664 | bytes 3022872 | tf_op jit(solution)/shard_map/pallas_call | solution.py:420
  36.3 3.5 %shard_map.95 = (bf16[3,6,256,256]{3,2,1,0:T(8,128)(2,1)S(1)}, bf16[3,6,256,256]{3,2,1,0:T(8,128)(2,1)S(1)}, f32[3,256,384]{2,1,0:T(8,128)S(1)}) custom-call(s32[6]{0:T(128)S(1)} %stack.27.at, f32[3,8,256]{2,1,0:T(8,128)S(1)} %get-tuple-element.130.cirow.refs_0_, f32[3,8,256]{2,1,0:T(8,128)S(1)} %get-tuple-element.131.cerow.refs_1_, ...), custom_call_target="tpu_custom_call" | custom-call | flops 301989888 | bytes 3391512 | tf_op jit(solution)/shard_map/pallas_call | solution.py:420
  39.8 4.6 %collective-permute-done.3.c1 = f32[256,768]{1,0:T(8,128)S(1)} collective-permute-done((f32[256,768]{1,0:T(8,128)}, f32[256,768]{1,0:T(8,128)S(1)}, u32[]{:S(2)}, u32[]{:S(2)}) %collective-permute-start.3) | collective-permute-done | bytes 786464 | tf_op jit(solution)/shard_map/ppermute | solution.py:48
  44.7 3.5 %shard_map.96 = (f32[4,8,256]{2,1,0:T(8,128)S(1)}, f32[4,8,256]{2,1,0:T(8,128)S(1)}, f32[4,256,384]{2,1,0:T(8,128)S(1)}, f32[4,256,384]{2,1,0:T(8,128)S(1)}, bf1...) custom-call(s32[6]{0:T(128)S(1)} %stack.27.at, ...), custom_call_target="tpu_custom_call" | custom-call | flops 301989888 | bytes 8724504 | tf_op jit(solution)/shard_map/pallas_call | solution.py:420
  48.3 1.6 %collective-permute-start.9 = (f32[136,384]{1,0:T(8,128)S(1)}, f32[136,384]{1,0:T(8,128)S(1)}, u32[]{:S(2)}, u32[]{:S(2)}) collective-permute-start(f32[136,384]{1,0:T(8,128)S(1)} %get-tuple-element.167), channel_id=1, source_target_pairs={{0,4},{1,5},{2,6},{3,7},{4,8},{5,9},{6,10},{7,11},{8,12},{9,13},{1... | collective-permute-start | bytes 626696 | tf_op jit(solution)/shard_map/ppermute | solution.py:48
  49.9 1.7 %collective-permute-start.10 = (f32[136,384]{1,0:T(8,128)S(1)}, f32[136,384]{1,0:T(8,128)S(1)}, u32[]{:S(2)}, u32[]{:S(2)}) collective-permute-start(f32[136,384]{1,0:T(8,128)S(1)} %get-tuple-element.168), channel_id=1, source_target_pairs={{0,12},{1,13},{2,14},{3,15},{4,0},{5,1},{6,2},{7,3},{8,4},{9,5},{1... | collective-permute-start | bytes 626696 | tf_op jit(solution)/shard_map/ppermute | solution.py:48
  51.6 2.0 %collective-permute-start.11 = (f32[136,384]{1,0:T(8,128)S(1)}, f32[136,384]{1,0:T(8,128)S(1)}, u32[]{:S(2)}, u32[]{:S(2)}) collective-permute-start(f32[136,384]{1,0:T(8,128)S(1)} %get-tuple-element.169), channel_id=1, source_target_pairs={{0,8},{1,9},{2,10},{3,11},{4,12},{5,13},{6,14},{7,15},{8,0},{9,1},... | collective-permute-start | bytes 626696 | tf_op jit(solution)/shard_map/ppermute | solution.py:48
  53.5 1.5 %shard_map.98 = (bf16[1,6,256,256]{3,2,1,0:T(8,128)(2,1)S(1)}, bf16[1,6,256,256]{3,2,1,0:T(8,128)(2,1)S(1)}, f32[1,256,384]{2,1,0:T(8,128)S(1)}) custom-call(s32[6]{0:T(128)S(1)} %stack.27.at, f32[4,8,256]{2,1,0:T(8,128)S(1)} %get-tuple-element.147.cirow, f32[4,8,256]{2,1,0:T(8,128)S(1)} %get-tuple-element.148.cerow, ...), custom_call_target="tpu_custom_call" | custom-call | flops 100663296 | bytes 4522008 | tf_op jit(solution)/shard_map/pallas_call | solution.py:420
  55.1 1.9 %shard_map.97 = (bf16[2,256,768]{2,1,0:T(8,128)(2,1)S(1)}, bf16[2,256,384]{2,1,0:T(8,128)(2,1)S(1)}, bf16[2,256,768]{2,1,0:T(8,128)(2,1)S(1)}, f32[2,128,768]{2,1,0:T(8,128)S(1)}) custom-call(s32[6]{0:T(128)S(1)} %stack.27.at, bf16[256,768]{1,0:T(8,128)(2,1)S(1)} %bitcast.11, f32[256,768]{1,0:T(8,128)S(1)} %collective-permute-done.3.c1, ...), custom_call_target="tpu_custom_call" | custom-call | flops 402653184 | bytes 5439512 | tf_op jit(solution)/shard_map/pallas_call | solution.py:420
  57.0 1.6 %collective-permute-done.4.c2 = f32[256,768]{1,0:T(8,128)S(1)} collective-permute-done((f32[256,768]{1,0:T(8,128)}, f32[256,768]{1,0:T(8,128)S(1)}, u32[]{:S(2)}, u32[]{:S(2)}) %collective-permute-start.4) | collective-permute-done | bytes 786464 | tf_op jit(solution)/shard_map/ppermute | solution.py:48
  58.6 4.1 %collective-permute-done.5.c3 = f32[256,768]{1,0:T(8,128)S(1)} collective-permute-done((f32[256,768]{1,0:T(8,128)S(1)}, f32[256,768]{1,0:T(8,128)S(1)}, u32[]{:S(2)}, u32[]{:S(2)}) %collective-permute-start.5) | collective-permute-done | bytes 786464 | tf_op jit(solution)/shard_map/ppermute | solution.py:48
  62.7 2.1 %shard_map.99 = (bf16[2,256,768]{2,1,0:T(8,128)(2,1)S(1)}, bf16[2,256,384]{2,1,0:T(8,128)(2,1)S(1)}, bf16[2,256,768]{2,1,0:T(8,128)(2,1)S(1)}, f32[2,4,128,384]{...) custom-call(s32[6]{0:T(128)S(1)} %stack.27.at, ...), custom_call_target="tpu_custom_call" | custom-call | flops 402653184 | bytes 6619160 | tf_op jit(solution)/shard_map/pallas_call | solution.py:420
  64.8 2.1 %collective-permute-start.6 = (f32[136,384]{1,0:T(8,128)S(1)}, f32[136,384]{1,0:T(8,128)S(1)}, u32[]{:S(2)}, u32[]{:S(2)}) collective-permute-start(f32[136,384]{1,0:T(8,128)S(1)} %get-tuple-element.157), channel_id=1, source_target_pairs={{0,4},{1,5},{2,6},{3,7},{4,8},{5,9},{6,10},{7,11},{8,12},{9,13},{1... | collective-permute-start | bytes 626696 | tf_op jit(solution)/shard_map/ppermute | solution.py:48
  66.9 1.7 %collective-permute-start.7 = (f32[136,384]{1,0:T(8,128)S(1)}, f32[136,384]{1,0:T(8,128)S(1)}, u32[]{:S(2)}, u32[]{:S(2)}) collective-permute-start(f32[136,384]{1,0:T(8,128)S(1)} %get-tuple-element.158), channel_id=1, source_target_pairs={{0,12},{1,13},{2,14},{3,15},{4,0},{5,1},{6,2},{7,3},{8,4},{9,5},{1... | collective-permute-start | bytes 626696 | tf_op jit(solution)/shard_map/ppermute | solution.py:48
  68.6 1.9 %collective-permute-start.8 = (f32[136,384]{1,0:T(8,128)S(1)}, f32[136,384]{1,0:T(8,128)S(1)}, u32[]{:S(2)}, u32[]{:S(2)}) collective-permute-start(f32[136,384]{1,0:T(8,128)S(1)} %get-tuple-element.159), channel_id=1, source_target_pairs={{0,8},{1,9},{2,10},{3,11},{4,12},{5,13},{6,14},{7,15},{8,0},{9,1},... | collective-permute-start | bytes 626696 | tf_op jit(solution)/shard_map/ppermute | solution.py:48
  70.6 5.1 %shard_map.100 = (f32[2,384,384]{2,1,0:T(8,128)S(1)}, f32[4,256,384]{2,1,0:T(8,128)S(1)}, f32[4,256,128]{2,1,0:T(8,128)S(1)}, f32[4,256,128]{2,1,0:T(8,128)S(1)}) custom-call(s32[6]{0:T(128)S(1)} %stack.27.at, bf16[4,256,384]{2,1,0:T(8,128)(2,1)S(1)} %get-tuple-element.149.xs, bf16[4,256,256]{2,1,0:T(8,128)(2,1)S(1)} %get-tuple-element.141.bc, ...), custom_call_target="tpu_custom_call" | custom-call | flops 2214592512 | bytes 18452504 | tf_op jit(solution)/shard_map/pallas_call | solution.py:420
  75.7 0.5 collective-permute-done.8.r_2
  76.2 3.9 %shard_map.101 = (f32[384,1024]{1,0:T(8,128)S(1)}, f32[384,1024]{1,0:T(8,128)S(1)}, bf16[4,256,640]{2,1,0:T(8,128)(2,1)S(1)}) custom-call(s32[6]{0:T(128)S(1)} %stack.27.at, bf16[768,1024]{1,0:T(8,128)(2,1)S(1)} %get-tuple-element.139.tokt, bf16[4,256,768]{2,1,0:T(8,128)(2,1)S(1)} %get-tuple-element.140.xfr, bf16[4,256,256]{2,1,0:T(8,128)(2,1)S(1)} %get-tuple-element.141.bc, ...), custom_call_target="tpu_custom_call" | custom-call | flops 1409286144 | bytes 12816408 | tf_op jit(solution)/shard_map/pallas_call | solution.py:420
  80.2 1.0 shard_map.107
  81.4 2.0 %collective-permute-start.30 = (f32[128,768]{1,0:T(8,128)S(1)}, f32[128,768]{1,0:T(8,128)S(1)}, u32[]{:S(2)}, u32[]{:S(2)}) collective-permute-start(f32[128,768]{1,0:T(8,128)S(1)} %get-tuple-element.204), channel_id=1, source_target_pairs={{0,3},{1,0},{2,1},{3,2},{4,7},{5,4},{6,5},{7,6},{8,11},{9,8},{10,9... | collective-permute-start | bytes 1179656 | tf_op jit(solution)/shard_map/ppermute | solution.py:48
  83.6 0.8 shard_map.102
  84.4 1.2 collective-permute-start.13
  85.6 2.4 %collective-permute-start.14 = (f32[96,1024]{1,0:T(8,128)S(1)}, f32[96,1024]{1,0:T(8,128)S(1)}, u32[]{:S(2)}, u32[]{:S(2)}) collective-permute-start(f32[96,1024]{1,0:T(8,128)S(1)} %get-tuple-element.186), channel_id=1, source_target_pairs={{0,8},{1,9},{2,10},{3,11},{4,12},{5,13},{6,14},{7,15},{8,0},{9,1},... | collective-permute-start | bytes 1179656 | tf_op jit(solution)/shard_map/ppermute | solution.py:450
  88.0 0.8 collective-permute-start.15
  88.8 1.7 %shard_map.106 = (f32[256,768]{1,0:T(8,128)S(1)}, f32[256,768]{1,0:T(8,128)S(1)}, f32[256,768]{1,0:T(8,128)S(1)}) custom-call(s32[6]{0:T(128)S(1)} %stack.27.at, bf16[4,256,640]{2,1,0:T(8,128)(2,1)S(1)} %get-tuple-element.200.dz, bf16[768,384]{1,0:T(8,128)(2,1)S(1)} %constant_dynamic-slice_fusion.1.w_in, bf16[768,256]{1,0:T(8,128)(2,1)S(1)} %copy-done.2), custom_call_target="tpu_custom_call" | custom-call | flops 754974720 | bytes 2293784 | tf_op jit(solution)/shard_map/pallas_call | solution.py:420
  90.5 2.4 %collective-permute-done.29.r_a = f32[128,768]{1,0:T(8,128)S(1)} collective-permute-done((f32[128,768]{1,0:T(8,128)S(1)}, f32[128,768]{1,0:T(8,128)S(1)}, u32[]{:S(2)}, u32[]{:S(2)}) %collective-permute-start.29) | collective-permute-done | bytes 393248 | tf_op jit(solution)/shard_map/ppermute | solution.py:48
  92.9 1.3 collective-permute-done.30.r_b
  94.2 0.7 shard_map.108
  95.1 1.8 %collective-permute-start.32 = (f32[256,768]{1,0:T(8,128)S(1)}, f32[256,768]{1,0:T(8,128)S(1)}, u32[]{:S(2)}, u32[]{:S(2)}) collective-permute-start(f32[256,768]{1,0:T(8,128)S(1)} %get-tuple-element.206), channel_id=1, source_target_pairs={{0,3},{1,0},{2,1},{3,2},{4,7},{5,4},{6,5},{7,6},{8,11},{9,8},{10,9... | collective-permute-start | bytes 2359304 | tf_op jit(solution)/shard_map/ppermute | solution.py:48
  96.9 1.0 collective-permute-done.14.refs_2_
  98.0 0.6 collective-permute-done.15.refs_3_
  98.6 0.7 shard_map.103
  99.3 2.0 %collective-permute-start.16 = (f32[24,1024]{1,0:T(8,128)S(1)}, f32[24,1024]{1,0:T(8,128)S(1)}, u32[]{:S(2)}, u32[]{:S(2)}) collective-permute-start(f32[24,1024]{1,0:T(8,128)S(1)} %get-tuple-element.189), channel_id=1, source_target_pairs={{0,32},{1,33},{2,34},{3,35},{4,36},{5,37},{6,38},{7,39},{8,40},{9,... | collective-permute-start | bytes 294920 | tf_op jit(solution)/shard_map/ppermute | solution.py:450
  101.3 3.6 %collective-permute-start.17 = (f32[24,1024]{1,0:T(8,128)S(1)}, f32[24,1024]{1,0:T(8,128)S(1)}, u32[]{:S(2)}, u32[]{:S(2)}) collective-permute-start(f32[24,1024]{1,0:T(8,128)S(1)} %get-tuple-element.190), channel_id=1, source_target_pairs={{0,64},{1,65},{2,66},{3,67},{4,68},{5,69},{6,70},{7,71},{8,72},{9,... | collective-permute-start | bytes 294920 | tf_op jit(solution)/shard_map/ppermute | solution.py:450
  104.9 1.0 collective-permute-start.18
  106.0 2.5 %collective-permute-done.17.c = f32[24,1024]{1,0:T(8,128)S(1)} collective-permute-done((f32[24,1024]{1,0:T(8,128)S(1)}, f32[24,1024]{1,0:T(8,128)S(1)}, u32[]{:S(2)}, u32[]{:S(2)}) %collective-permute-start.17) | collective-permute-done | bytes 98336 | tf_op jit(solution)/shard_map/ppermute | solution.py:450
  108.5 1.0 collective-permute-done.18.d
  109.5 0.7 shard_map.104
  110.2 1.1 collective-permute-start.19
  111.3 0.8 collective-permute-start.20
  112.3 3.8 %collective-permute-done.19.b = f32[40,384]{1,0:T(8,128)S(1)} collective-permute-done((f32[40,384]{1,0:T(8,128)S(1)}, f32[40,384]{1,0:T(8,128)S(1)}, u32[]{:S(2)}, u32[]{:S(2)}) %collective-permute-start.19) | collective-permute-done | bytes 61472 | tf_op jit(solution)/shard_map/ppermute | solution.py:48
  116.0 1.1 collective-permute-done.20.c
  117.1 0.9 collective-permute-done.21.d
  118.0 0.7 shard_map.105
  118.7 1.8 %collective-permute-start.24 = (f32[8,128]{1,0:T(8,128)S(1)}, f32[8,128]{1,0:T(8,128)S(1)}, u32[]{:S(2)}, u32[]{:S(2)}) collective-permute-start(f32[8,128]{1,0:T(8,128)S(1)} %shard_map.105), channel_id=1, source_target_pairs={{0,8},{1,9},{2,10},{3,11},{4,12},{5,13},{6,14},{7,15},{8,0},{9,1},... | collective-permute-start | bytes 12296 | tf_op jit(solution)/shard_map/ppermute | solution.py:48
  120.5 1.4 collective-permute-start.22
  121.9 1.8 %collective-permute-start.23 = (f32[8,128]{1,0:T(8,128)S(1)}, f32[8,128]{1,0:T(8,128)S(1)}, u32[]{:S(2)}, u32[]{:S(2)}) collective-permute-start(f32[8,128]{1,0:T(8,128)S(1)} %shard_map.105), channel_id=1, source_target_pairs={{0,12},{1,13},{2,14},{3,15},{4,0},{5,1},{6,2},{7,3},{8,4},{9,5},{1... | collective-permute-start | bytes 12296 | tf_op jit(solution)/shard_map/ppermute | solution.py:48
  123.9 6.7 %collective-permute-start.25 = (f32[24,384]{1,0:T(8,128)S(1)}, f32[24,384]{1,0:T(8,128)S(1)}, u32[]{:S(2)}, u32[]{:S(2)}) collective-permute-start(f32[24,384]{1,0:T(8,128)S(1)} %get-tuple-element.196), channel_id=1, source_target_pairs={{0,0},{1,32},{2,64},{3,96},{4,1},{5,33},{6,65},{7,97},{8,2},{9,34}... | collective-permute-start | bytes 110600 | tf_op jit(solution)/shard_map/ppermute | solution.py:553
  130.7 2.8 %collective-permute-done.25.rows_out = f32[24,384]{1,0:T(8,128)S(1)} collective-permute-done((f32[24,384]{1,0:T(8,128)S(1)}, f32[24,384]{1,0:T(8,128)S(1)}, u32[]{:S(2)}, u32[]{:S(2)}) %collective-permute-start.25) | collective-permute-done | bytes 36896 | tf_op jit(solution)/shard_map/ppermute | solution.py:553
  133.5 5.1 %collective-permute-start.28 = (f32[8,128]{1,0:T(8,128)S(1)}, f32[8,128]{1,0:T(8,128)S(1)}, u32[]{:S(2)}, u32[]{:S(2)}) collective-permute-start(f32[8,128]{1,0:T(8,128)S(1)} %add_add_fusion.1), channel_id=1, source_target_pairs={{0,64},{16,80},{32,96},{48,112},{64,0},{80,16},{96,32},{112,48},{1... | collective-permute-start | bytes 12296 | tf_op jit(solution)/shard_map/ppermute | solution.py:48
  138.5 3.2 %collective-permute-start.27 = (f32[8,128]{1,0:T(8,128)S(1)}, f32[8,128]{1,0:T(8,128)S(1)}, u32[]{:S(2)}, u32[]{:S(2)}) collective-permute-start(f32[8,128]{1,0:T(8,128)S(1)} %add_add_fusion.1), channel_id=1, source_target_pairs={{0,96},{16,112},{32,0},{48,16},{64,32},{80,48},{96,64},{112,80},{1... | collective-permute-start | bytes 12296 | tf_op jit(solution)/shard_map/ppermute | solution.py:48
  141.8 1.6 %collective-permute-done.26 = f32[8,128]{1,0:T(8,128)S(1)} collective-permute-done((f32[8,128]{1,0:T(8,128)S(1)}, f32[8,128]{1,0:T(8,128)S(1)}, u32[]{:S(2)}, u32[]{:S(2)}) %collective-permute-start.26) | collective-permute-done | bytes 4128 | tf_op jit(solution)/shard_map/ppermute | solution.py:48
  143.5 0.9 add_convert_fusion
  144.6 1.2 shard_map.109
  (49 shorter events, 2.6 us)
Async XLA Ops:
  0.6 25.0 %copy-start = (bf16[768,1536]{1,0:T(8,128)(2,1)S(1)}, bf16[768,1536]{1,0:T(8,128)(2,1)}, u32[]{:S(2)}) copy-start(bf16[768,1536]{1,0:T(8,128)(2,1)} %param.9) | copy-start | bytes 7077892
  0.6 1.1 copy-start.4
  1.8 0.7 copy-start.6
  2.6 27.1 %copy-start.2 = (bf16[768,256]{1,0:T(8,128)(2,1)S(1)}, bf16[768,256]{1,0:T(8,128)(2,1)}, u32[]{:S(2)}) copy-start(bf16[768,256]{1,0:T(8,128)(2,1)} %w_bc.7) | copy-start | bytes 1179652
  2.6 20.0 %collective-permute-start = (f32[264,768]{1,0:T(8,128)S(1)}, f32[264,768]{1,0:T(8,128)}, u32[]{:S(2)}, u32[]{:S(2)}) collective-permute-start(f32[264,768]{1,0:T(8,128)S(1)} %shard_map.93), channel_id=1, source_target_pairs={{0,1},{1,2},{2,3},{3,0},{4,5},{5,6},{6,7},{7,4},{8,9},{9,10},{10,1... | collective-permute-start | bytes 2433032 | tf_op jit(solution)/shard_map/ppermute | solution.py:48
  3.1 21.0 %collective-permute-start.2 = (f32[264,768]{1,0:T(8,128)S(1)}, f32[264,768]{1,0:T(8,128)S(1)}, u32[]{:S(2)}, u32[]{:S(2)}) collective-permute-start(f32[264,768]{1,0:T(8,128)S(1)} %shard_map.93), channel_id=1, source_target_pairs={{0,3},{1,0},{2,1},{3,2},{4,7},{5,4},{6,5},{7,6},{8,11},{9,8},{10,9... | collective-permute-start | bytes 2433032 | tf_op jit(solution)/shard_map/ppermute | solution.py:48
  22.6 21.8 %collective-permute-start.1 = (f32[264,768]{1,0:T(8,128)}, f32[264,768]{1,0:T(8,128)}, u32[]{:S(2)}, u32[]{:S(2)}) collective-permute-start(f32[264,768]{1,0:T(8,128)} %collective-permute-done.t3), channel_id=1, source_target_pairs={{0,1},{1,2},{2,3},{3,0},{4,5},{5,6},{6,7},{7,4},{8,9},{9,10},{10,1... | collective-permute-start | bytes 2433032 | tf_op jit(solution)/shard_map/ppermute | solution.py:48
  24.1 0.9 copy-start.8
  25.0 19.4 %collective-permute-start.3 = (f32[256,768]{1,0:T(8,128)}, f32[256,768]{1,0:T(8,128)S(1)}, u32[]{:S(2)}, u32[]{:S(2)}) collective-permute-start(f32[256,768]{1,0:T(8,128)} %bitcast_convert_fusion), channel_id=1, source_target_pairs={{0,3},{1,0},{2,1},{3,2},{4,7},{5,4},{6,5},{7,6},{8,11},{9,8},{10,9... | collective-permute-start | bytes 2359304 | tf_op jit(solution)/shard_map/ppermute | solution.py:48
  25.6 4.1 %copy-start.5 = (bf16[1,256,768]{2,1,0:T(8,128)(2,1)S(1)}, bf16[1,256,768]{2,1,0:T(8,128)(2,1)}, u32[]{:S(2)}) copy-start(bf16[1,256,768]{2,1,0:T(8,128)(2,1)} %param.6) | copy-start | bytes 1179652
  25.6 4.1 %copy-start.7 = (f32[1,24,256]{2,1,0:T(8,128)S(1)}, f32[1,24,256]{2,1,0:T(8,128)}, u32[]{:S(2)}) copy-start(f32[1,24,256]{2,1,0:T(8,128)} %param.8) | copy-start | bytes 73732
  25.6 4.1 %copy-start.9 = (f32[264,768]{1,0:T(8,128)S(1)}, f32[264,768]{1,0:T(8,128)}, u32[]{:S(2)}) copy-start(f32[264,768]{1,0:T(8,128)} %copy-done.8) | copy-start | bytes 2433028
  26.9 31.7 %collective-permute-start.4 = (f32[256,768]{1,0:T(8,128)}, f32[256,768]{1,0:T(8,128)S(1)}, u32[]{:S(2)}, u32[]{:S(2)}) collective-permute-start(f32[256,768]{1,0:T(8,128)} %bitcast_convert_fusion), channel_id=1, source_target_pairs={{0,1},{1,2},{2,3},{3,0},{4,5},{5,6},{6,7},{7,4},{8,9},{9,10},{10,1... | collective-permute-start | bytes 2359304 | tf_op jit(solution)/shard_map/ppermute | solution.py:48
  44.4 18.3 %collective-permute-start.5 = (f32[256,768]{1,0:T(8,128)S(1)}, f32[256,768]{1,0:T(8,128)S(1)}, u32[]{:S(2)}, u32[]{:S(2)}) collective-permute-start(f32[256,768]{1,0:T(8,128)S(1)} %collective-permute-done.3.c1), channel_id=1, source_target_pairs={{0,3},{1,0},{2,1},{3,2},{4,7},{5,4},{6,5},{7,6},{8,11},{9,8},{10,9... | collective-permute-start | bytes 2359304 | tf_op jit(solution)/shard_map/ppermute | solution.py:48
  48.3 20.4 %collective-permute-start.9 = (f32[136,384]{1,0:T(8,128)S(1)}, f32[136,384]{1,0:T(8,128)S(1)}, u32[]{:S(2)}, u32[]{:S(2)}) collective-permute-start(f32[136,384]{1,0:T(8,128)S(1)} %get-tuple-element.167), channel_id=1, source_target_pairs={{0,4},{1,5},{2,6},{3,7},{4,8},{5,9},{6,10},{7,11},{8,12},{9,13},{1... | collective-permute-start | bytes 626696 | tf_op jit(solution)/shard_map/ppermute | solution.py:48
  49.9 20.7 %collective-permute-start.10 = (f32[136,384]{1,0:T(8,128)S(1)}, f32[136,384]{1,0:T(8,128)S(1)}, u32[]{:S(2)}, u32[]{:S(2)}) collective-permute-start(f32[136,384]{1,0:T(8,128)S(1)} %get-tuple-element.168), channel_id=1, source_target_pairs={{0,12},{1,13},{2,14},{3,15},{4,0},{5,1},{6,2},{7,3},{8,4},{9,5},{1... | collective-permute-start | bytes 626696 | tf_op jit(solution)/shard_map/ppermute | solution.py:48
  51.6 19.0 %collective-permute-start.11 = (f32[136,384]{1,0:T(8,128)S(1)}, f32[136,384]{1,0:T(8,128)S(1)}, u32[]{:S(2)}, u32[]{:S(2)}) collective-permute-start(f32[136,384]{1,0:T(8,128)S(1)} %get-tuple-element.169), channel_id=1, source_target_pairs={{0,8},{1,9},{2,10},{3,11},{4,12},{5,13},{6,14},{7,15},{8,0},{9,1},... | collective-permute-start | bytes 626696 | tf_op jit(solution)/shard_map/ppermute | solution.py:48
  53.5 1.5 %copy-start.3 = (bf16[1,256,768]{2,1,0:T(8,128)(2,1)S(1)}, bf16[1,256,768]{2,1,0:T(8,128)(2,1)}, u32[]{:S(2)}) copy-start(bf16[1,256,768]{2,1,0:T(8,128)(2,1)} %param.7) | copy-start | bytes 1179652
  64.8 10.8 %collective-permute-start.6 = (f32[136,384]{1,0:T(8,128)S(1)}, f32[136,384]{1,0:T(8,128)S(1)}, u32[]{:S(2)}, u32[]{:S(2)}) collective-permute-start(f32[136,384]{1,0:T(8,128)S(1)} %get-tuple-element.157), channel_id=1, source_target_pairs={{0,4},{1,5},{2,6},{3,7},{4,8},{5,9},{6,10},{7,11},{8,12},{9,13},{1... | collective-permute-start | bytes 626696 | tf_op jit(solution)/shard_map/ppermute | solution.py:48
  66.9 8.8 %collective-permute-start.7 = (f32[136,384]{1,0:T(8,128)S(1)}, f32[136,384]{1,0:T(8,128)S(1)}, u32[]{:S(2)}, u32[]{:S(2)}) collective-permute-start(f32[136,384]{1,0:T(8,128)S(1)} %get-tuple-element.158), channel_id=1, source_target_pairs={{0,12},{1,13},{2,14},{3,15},{4,0},{5,1},{6,2},{7,3},{8,4},{9,5},{1... | collective-permute-start | bytes 626696 | tf_op jit(solution)/shard_map/ppermute | solution.py:48
  68.6 7.6 %collective-permute-start.8 = (f32[136,384]{1,0:T(8,128)S(1)}, f32[136,384]{1,0:T(8,128)S(1)}, u32[]{:S(2)}, u32[]{:S(2)}) collective-permute-start(f32[136,384]{1,0:T(8,128)S(1)} %get-tuple-element.159), channel_id=1, source_target_pairs={{0,8},{1,9},{2,10},{3,11},{4,12},{5,13},{6,14},{7,15},{8,0},{9,1},... | collective-permute-start | bytes 626696 | tf_op jit(solution)/shard_map/ppermute | solution.py:48
  80.1 3.5 %collective-permute-start.12 = (f32[384,1024]{1,0:T(8,128)S(1)}, f32[384,1024]{1,0:T(8,128)S(1)}, u32[]{:S(2)}, u32[]{:S(2)}) collective-permute-start(f32[384,1024]{1,0:T(8,128)S(1)} %get-tuple-element.181), channel_id=1, source_target_pairs={{0,16},{16,0},{32,48},{48,32},{64,80},{80,64},{96,112},{112,96},{1... | collective-permute-start | bytes 4718600 | tf_op jit(solution)/shard_map/ppermute | solution.py:48
  81.3 11.6 %collective-permute-start.29 = (f32[128,768]{1,0:T(8,128)S(1)}, f32[128,768]{1,0:T(8,128)S(1)}, u32[]{:S(2)}, u32[]{:S(2)}) collective-permute-start(f32[128,768]{1,0:T(8,128)S(1)} %get-tuple-element.203), channel_id=1, source_target_pairs={{0,1},{1,2},{2,3},{3,0},{4,5},{5,6},{6,7},{7,4},{8,9},{9,10},{10,1... | collective-permute-start | bytes 1179656 | tf_op jit(solution)/shard_map/ppermute | solution.py:48
  81.4 12.8 %collective-permute-start.30 = (f32[128,768]{1,0:T(8,128)S(1)}, f32[128,768]{1,0:T(8,128)S(1)}, u32[]{:S(2)}, u32[]{:S(2)}) collective-permute-start(f32[128,768]{1,0:T(8,128)S(1)} %get-tuple-element.204), channel_id=1, source_target_pairs={{0,3},{1,0},{2,1},{3,2},{4,7},{5,4},{6,5},{7,6},{8,11},{9,8},{10,9... | collective-permute-start | bytes 1179656 | tf_op jit(solution)/shard_map/ppermute | solution.py:48
  84.4 12.5 %collective-permute-start.13 = (f32[96,1024]{1,0:T(8,128)S(1)}, f32[96,1024]{1,0:T(8,128)S(1)}, u32[]{:S(2)}, u32[]{:S(2)}) collective-permute-start(f32[96,1024]{1,0:T(8,128)S(1)} %get-tuple-element.185), channel_id=1, source_target_pairs={{0,4},{1,5},{2,6},{3,7},{4,8},{5,9},{6,10},{7,11},{8,12},{9,13},{1... | collective-permute-start | bytes 1179656 | tf_op jit(solution)/shard_map/ppermute | solution.py:450
  85.6 12.3 %collective-permute-start.14 = (f32[96,1024]{1,0:T(8,128)S(1)}, f32[96,1024]{1,0:T(8,128)S(1)}, u32[]{:S(2)}, u32[]{:S(2)}) collective-permute-start(f32[96,1024]{1,0:T(8,128)S(1)} %get-tuple-element.186), channel_id=1, source_target_pairs={{0,8},{1,9},{2,10},{3,11},{4,12},{5,13},{6,14},{7,15},{8,0},{9,1},... | collective-permute-start | bytes 1179656 | tf_op jit(solution)/shard_map/ppermute | solution.py:450
  88.0 10.6 %collective-permute-start.15 = (f32[96,1024]{1,0:T(8,128)S(1)}, f32[96,1024]{1,0:T(8,128)S(1)}, u32[]{:S(2)}, u32[]{:S(2)}) collective-permute-start(f32[96,1024]{1,0:T(8,128)S(1)} %get-tuple-element.187), channel_id=1, source_target_pairs={{0,12},{1,13},{2,14},{3,15},{4,0},{5,1},{6,2},{7,3},{8,4},{9,5},{1... | collective-permute-start | bytes 1179656 | tf_op jit(solution)/shard_map/ppermute | solution.py:450
  94.8 48.5 %collective-permute-start.31 = (f32[256,768]{1,0:T(8,128)S(1)}, f32[256,768]{1,0:T(8,128)S(1)}, u32[]{:S(2)}, u32[]{:S(2)}) collective-permute-start(f32[256,768]{1,0:T(8,128)S(1)} %get-tuple-element.205), channel_id=1, source_target_pairs={{0,1},{1,2},{2,3},{3,0},{4,5},{5,6},{6,7},{7,4},{8,9},{9,10},{10,1... | collective-permute-start | bytes 2359304 | tf_op jit(solution)/shard_map/ppermute | solution.py:48
  95.1 48.3 %collective-permute-start.32 = (f32[256,768]{1,0:T(8,128)S(1)}, f32[256,768]{1,0:T(8,128)S(1)}, u32[]{:S(2)}, u32[]{:S(2)}) collective-permute-start(f32[256,768]{1,0:T(8,128)S(1)} %get-tuple-element.206), channel_id=1, source_target_pairs={{0,3},{1,0},{2,1},{3,2},{4,7},{5,4},{6,5},{7,6},{8,11},{9,8},{10,9... | collective-permute-start | bytes 2359304 | tf_op jit(solution)/shard_map/ppermute | solution.py:48
  99.3 6.7 %collective-permute-start.16 = (f32[24,1024]{1,0:T(8,128)S(1)}, f32[24,1024]{1,0:T(8,128)S(1)}, u32[]{:S(2)}, u32[]{:S(2)}) collective-permute-start(f32[24,1024]{1,0:T(8,128)S(1)} %get-tuple-element.189), channel_id=1, source_target_pairs={{0,32},{1,33},{2,34},{3,35},{4,36},{5,37},{6,38},{7,39},{8,40},{9,... | collective-permute-start | bytes 294920 | tf_op jit(solution)/shard_map/ppermute | solution.py:450
  101.3 7.2 %collective-permute-start.17 = (f32[24,1024]{1,0:T(8,128)S(1)}, f32[24,1024]{1,0:T(8,128)S(1)}, u32[]{:S(2)}, u32[]{:S(2)}) collective-permute-start(f32[24,1024]{1,0:T(8,128)S(1)} %get-tuple-element.190), channel_id=1, source_target_pairs={{0,64},{1,65},{2,66},{3,67},{4,68},{5,69},{6,70},{7,71},{8,72},{9,... | collective-permute-start | bytes 294920 | tf_op jit(solution)/shard_map/ppermute | solution.py:450
  104.9 4.6 %collective-permute-start.18 = (f32[24,1024]{1,0:T(8,128)S(1)}, f32[24,1024]{1,0:T(8,128)S(1)}, u32[]{:S(2)}, u32[]{:S(2)}) collective-permute-start(f32[24,1024]{1,0:T(8,128)S(1)} %get-tuple-element.191), channel_id=1, source_target_pairs={{0,96},{1,97},{2,98},{3,99},{4,100},{5,101},{6,102},{7,103},{8,104... | collective-permute-start | bytes 294920 | tf_op jit(solution)/shard_map/ppermute | solution.py:450
  110.2 5.9 %collective-permute-start.19 = (f32[40,384]{1,0:T(8,128)S(1)}, f32[40,384]{1,0:T(8,128)S(1)}, u32[]{:S(2)}, u32[]{:S(2)}) collective-permute-start(f32[40,384]{1,0:T(8,128)S(1)} %get-tuple-element.193), channel_id=1, source_target_pairs={{0,1},{1,2},{2,3},{3,0},{4,5},{5,6},{6,7},{7,4},{8,9},{9,10},{10,1... | collective-permute-start | bytes 184328 | tf_op jit(solution)/shard_map/ppermute | solution.py:48
  111.3 5.8 %collective-permute-start.20 = (f32[40,384]{1,0:T(8,128)S(1)}, f32[40,384]{1,0:T(8,128)S(1)}, u32[]{:S(2)}, u32[]{:S(2)}) collective-permute-start(f32[40,384]{1,0:T(8,128)S(1)} %get-tuple-element.194), channel_id=1, source_target_pairs={{0,2},{1,3},{2,0},{3,1},{4,6},{5,7},{6,4},{7,5},{8,10},{9,11},{10,... | collective-permute-start | bytes 184328 | tf_op jit(solution)/shard_map/ppermute | solution.py:48
  112.1 6.0 %collective-permute-start.21 = (f32[40,384]{1,0:T(8,128)S(1)}, f32[40,384]{1,0:T(8,128)S(1)}, u32[]{:S(2)}, u32[]{:S(2)}) collective-permute-start(f32[40,384]{1,0:T(8,128)S(1)} %get-tuple-element.195), channel_id=1, source_target_pairs={{0,3},{1,0},{2,1},{3,2},{4,7},{5,4},{6,5},{7,6},{8,11},{9,8},{10,9... | collective-permute-start | bytes 184328 | tf_op jit(solution)/shard_map/ppermute | solution.py:48
  118.0 27.8 %copy-start.1 = (bf16[768,1536]{1,0:T(8,128)(2,1)S(1)}, bf16[768,1536]{1,0:T(8,128)(2,1)}, u32[]{:S(2)}) copy-start(bf16[768,1536]{1,0:T(8,128)(2,1)} %param.9) | copy-start | bytes 7077892
  118.7 5.2 %collective-permute-start.24 = (f32[8,128]{1,0:T(8,128)S(1)}, f32[8,128]{1,0:T(8,128)S(1)}, u32[]{:S(2)}, u32[]{:S(2)}) collective-permute-start(f32[8,128]{1,0:T(8,128)S(1)} %shard_map.105), channel_id=1, source_target_pairs={{0,8},{1,9},{2,10},{3,11},{4,12},{5,13},{6,14},{7,15},{8,0},{9,1},... | collective-permute-start | bytes 12296 | tf_op jit(solution)/shard_map/ppermute | solution.py:48
  120.5 10.1 %collective-permute-start.22 = (f32[8,128]{1,0:T(8,128)S(1)}, f32[8,128]{1,0:T(8,128)S(1)}, u32[]{:S(2)}, u32[]{:S(2)}) collective-permute-start(f32[8,128]{1,0:T(8,128)S(1)} %shard_map.105), channel_id=1, source_target_pairs={{0,4},{1,5},{2,6},{3,7},{4,8},{5,9},{6,10},{7,11},{8,12},{9,13},{1... | collective-permute-start | bytes 12296 | tf_op jit(solution)/shard_map/ppermute | solution.py:48
  121.9 8.7 %collective-permute-start.23 = (f32[8,128]{1,0:T(8,128)S(1)}, f32[8,128]{1,0:T(8,128)S(1)}, u32[]{:S(2)}, u32[]{:S(2)}) collective-permute-start(f32[8,128]{1,0:T(8,128)S(1)} %shard_map.105), channel_id=1, source_target_pairs={{0,12},{1,13},{2,14},{3,15},{4,0},{5,1},{6,2},{7,3},{8,4},{9,5},{1... | collective-permute-start | bytes 12296 | tf_op jit(solution)/shard_map/ppermute | solution.py:48
  123.9 9.6 %collective-permute-start.25 = (f32[24,384]{1,0:T(8,128)S(1)}, f32[24,384]{1,0:T(8,128)S(1)}, u32[]{:S(2)}, u32[]{:S(2)}) collective-permute-start(f32[24,384]{1,0:T(8,128)S(1)} %get-tuple-element.196), channel_id=1, source_target_pairs={{0,0},{1,32},{2,64},{3,96},{4,1},{5,33},{6,65},{7,97},{8,2},{9,34}... | collective-permute-start | bytes 110600 | tf_op jit(solution)/shard_map/ppermute | solution.py:553
  133.5 8.3 %collective-permute-start.28 = (f32[8,128]{1,0:T(8,128)S(1)}, f32[8,128]{1,0:T(8,128)S(1)}, u32[]{:S(2)}, u32[]{:S(2)}) collective-permute-start(f32[8,128]{1,0:T(8,128)S(1)} %add_add_fusion.1), channel_id=1, source_target_pairs={{0,64},{16,80},{32,96},{48,112},{64,0},{80,16},{96,32},{112,48},{1... | collective-permute-start | bytes 12296 | tf_op jit(solution)/shard_map/ppermute | solution.py:48
  138.5 4.8 %collective-permute-start.26 = (f32[8,128]{1,0:T(8,128)S(1)}, f32[8,128]{1,0:T(8,128)S(1)}, u32[]{:S(2)}, u32[]{:S(2)}) collective-permute-start(f32[8,128]{1,0:T(8,128)S(1)} %add_add_fusion.1), channel_id=1, source_target_pairs={{0,32},{16,48},{32,64},{48,80},{64,96},{80,112},{96,0},{112,16},{1... | collective-permute-start | bytes 12296 | tf_op jit(solution)/shard_map/ppermute | solution.py:48
  138.5 4.8 %collective-permute-start.27 = (f32[8,128]{1,0:T(8,128)S(1)}, f32[8,128]{1,0:T(8,128)S(1)}, u32[]{:S(2)}, u32[]{:S(2)}) collective-permute-start(f32[8,128]{1,0:T(8,128)S(1)} %add_add_fusion.1), channel_id=1, source_target_pairs={{0,96},{16,112},{32,0},{48,16},{64,32},{80,48},{96,64},{112,80},{1... | collective-permute-start | bytes 12296 | tf_op jit(solution)/shard_map/ppermute | solution.py:48
  143.4 1.2 collective-permute-start.33
